TPU v7x, 256 devices: a whole 4x4x8 slice. The times are simulated.
256 devices in a mesh: dp: 4 (over x), table: 32 (over y, z), col: 2 (over core).
Axes of the slice: x: 4, y: 4, z: 8, core: 2. Of those that a mesh axis runs over, the one named last changes fastest.
Arguments:
- table: float32 [131072, 768], P(('dp', 'table'), 'col'), may hold values from -6 to 6
- accum: float32 [131072], P(('dp', 'table')), may hold values from 0.05 to 0.5
- serve_rows: int32 [128, 512], P(('dp', 'table')), may hold values from 0 to 1023, as said below
- seed_slot: int32 [1024], P(('dp', 'table')), may hold values from 0 to 511
- hop1_slot: int32 [1024, 15], P(('dp', 'table')), may hold values from 0 to 511
- hop2_slot: int32 [1024, 15, 10], P(('dp', 'table')), may hold values from 0 to 511
- hop1_rel: int32 [1024, 15], P(('dp', 'table')), may hold values from 0 to 1
- hop2_rel: int32 [1024, 15, 10], P(('dp', 'table')), may hold values from 0 to 1
- cotangent: bfloat16 [1024, 1024], P(('dp', 'table')), may hold values from -24 to 24
- w_first: bfloat16 [3, 768, 1024], P(None, 'col'), may hold values from -0.5 to 0.5
- w_second: bfloat16 [3, 1024, 1024], replicated, may hold values from -0.109375 to 0.109375
Outputs:
- new_table: float32 [131072, 768], P(('dp', 'table'), 'col')
- new_accum: float32 [131072], P(('dp', 'table'))
- grad_first: float32 [3, 768, 1024], P(None, 'col', ('dp', 'table'))
- grad_second: float32 [3, 1024, 1024], P(None, 'col', ('dp', 'table'))
Inputs may be any that keep to these rules, and one draw needn't show every extreme that they name: `serve_rows`: the 4 entries of one owner for one fetching index are distinct rows.
All inputs are finite; a program needn't handle non-finite values.
Results may differ from a plain program's by a relative error of at most 0.0065.
Values may be sent and summed in bfloat16 or wider, within the bound.
No kernel may reach another device: no remote copies, remote signals or barrier semaphores. Data moves between devices by JAX's collectives and lax.ppermute only.
A program may use at most 128 MiB of HBM per device.

v0:
```python
import jax
import jax.numpy as jnp
from jax import lax
from jax.sharding import PartitionSpec as P

LEARNING_RATE = 0.1


def relation_means(features, relation, relations):
    matches = relation[..., None] == jnp.arange(relations, dtype=jnp.int32)
    onehot = matches.astype(jnp.float32)
    counts = jnp.sum(onehot, axis=-2)
    inverse = 1.0 / jnp.maximum(counts, 1.0)
    totals = jnp.einsum(
        "...kr,...kc->...rc",
        matches.astype(jnp.bfloat16),
        features,
        preferred_element_type=jnp.float32,
    )
    return ((totals * inverse[..., None]).astype(jnp.bfloat16), onehot * inverse[..., None, :])


def silu_slope(values):
    sigma = jax.nn.sigmoid(values)
    return sigma * (1.0 + values * (1.0 - sigma))


def body(
    table,
    accum,
    serve_rows,
    seed_slot,
    hop1_slot,
    hop2_slot,
    hop1_rel,
    hop2_rel,
    cotangent,
    w_first,
    w_second,
):
    owners = lax.axis_size(("dp", "table"))
    columns = table.shape[1]
    per_owner = serve_rows.shape[1] // owners
    seed_count = seed_slot.shape[0]
    fanout = hop1_slot.shape[1]
    relations = w_first.shape[0] - 1
    hidden_units = w_second.shape[1]
    half_units = hidden_units // lax.axis_size("col")
    col_start = lax.axis_index("col") * half_units
    local_rows = serve_rows.reshape(owners, per_owner)
    outgoing = table[local_rows].astype(jnp.bfloat16)
    fetched = lax.all_to_all(
        outgoing, ("dp", "table"), split_axis=0, concat_axis=0, tiled=True
    ).reshape(owners * per_owner, columns)
    x_seed = fetched[seed_slot]
    x_hop_one = fetched[hop1_slot]
    x_hop_two = fetched[hop2_slot]
    mean_one, spread_one = relation_means(x_hop_one, hop1_rel, relations)
    mean_two, spread_two = relation_means(x_hop_two, hop2_rel, relations)
    self_in = jnp.concatenate([x_seed, x_hop_one.reshape(-1, columns)], 0)
    mean_in = jnp.concatenate([mean_one, mean_two.reshape(-1, relations, columns)], 0)
    layer_in = jnp.concatenate([self_in[:, None], mean_in], 1)
    partial_pre = jnp.einsum("nkc,kch->nh", layer_in, w_first, preferred_element_type=jnp.float32)
    pre_act = lax.psum(partial_pre, "col")
    hidden = jax.nn.silu(pre_act).astype(jnp.bfloat16)
    h_seed = hidden[:seed_count]
    h_hop = hidden[seed_count:].reshape(seed_count, fanout, hidden_units)
    mean_hidden, unused = relation_means(h_hop, hop1_rel, relations)
    second_in = jnp.concatenate([h_seed[:, None], mean_hidden], 1)
    own_in = lax.dynamic_slice_in_dim(second_in, col_start, half_units, 2)
    back_second = jnp.einsum("so,kho->skh", cotangent, w_second, preferred_element_type=jnp.float32)
    back_hop = jnp.einsum("sar,srh->sah", spread_one, back_second[:, 1:])
    back_hidden = jnp.concatenate([back_second[:, 0], back_hop.reshape(-1, hidden_units)], 0)
    back_pre = (back_hidden * silu_slope(pre_act)).astype(jnp.bfloat16)
    grad_two = jnp.einsum("skh,so->kho", own_in, cotangent, preferred_element_type=jnp.float32)
    grad_one = jnp.einsum("nkc,nh->kch", layer_in, back_pre, preferred_element_type=jnp.float32)
    grad_one, grad_two = (
        lax.psum_scatter(grad_one, ("dp", "table"), scatter_dimension=2, tiled=True),
        lax.psum_scatter(grad_two, ("dp", "table"), scatter_dimension=2, tiled=True),
    )
    back_in = jnp.einsum("nh,kch->nkc", back_pre, w_first, preferred_element_type=jnp.float32)
    back_seed = back_in[:seed_count, 0]
    back_self = back_in[seed_count:, 0].reshape(seed_count, fanout, columns)
    back_mean_one = back_in[:seed_count, 1:]
    back_mean_two = back_in[seed_count:, 1:].reshape(seed_count, fanout, relations, columns)
    hop_one_grad = back_self + jnp.einsum("sar,src->sac", spread_one, back_mean_one)
    hop_two_grad = jnp.einsum("sabr,sarc->sabc", spread_two, back_mean_two)
    slot_grad = jnp.zeros((owners * per_owner, columns), jnp.float32)
    slot_grad = slot_grad.at[seed_slot].add(back_seed)
    slot_grad = slot_grad.at[hop1_slot.reshape(-1)].add(hop_one_grad.reshape(-1, columns))
    slot_grad = slot_grad.at[hop2_slot.reshape(-1)].add(hop_two_grad.reshape(-1, columns))
    slot_grad = slot_grad.reshape(owners, per_owner, columns)
    arrived = lax.all_to_all(slot_grad, ("dp", "table"), split_axis=0, concat_axis=0, tiled=True)
    row_grad = jnp.zeros((table.shape[0], columns), jnp.float32)
    row_grad = row_grad.at[serve_rows.reshape(-1)].add(arrived.reshape(-1, columns))
    squares = lax.psum(jnp.sum(row_grad * row_grad, axis=1), "col")
    new_accum = accum + squares / (columns * lax.axis_size("col"))
    new_table = table - LEARNING_RATE * row_grad * lax.rsqrt(new_accum)[:, None]
    return (new_table, new_accum, grad_one, grad_two)


def solution(mesh):
    placed = (
        P(("dp", "table"), "col"),
        P(("dp", "table")),
        P(("dp", "table"), None),
        P(("dp", "table")),
        P(("dp", "table"), None),
        P(("dp", "table"), None, None),
        P(("dp", "table"), None),
        P(("dp", "table"), None, None),
        P(("dp", "table"), None),
        P(None, "col", None),
        P(),
    )
    return jax.shard_map(
        body,
        mesh=mesh,
        in_specs=placed,
        out_specs=(
            P(("dp", "table"), "col"),
            P(("dp", "table")),
            P(None, "col", ("dp", "table")),
            P(None, "col", ("dp", "table")),
        ),
        check_vma=False,
    )
```

profile of v0, /device:TPU:8, one launch (start us, length us, event | category | flops | bytes accessed | tf_op | source)
XLA Modules:
  0.0 1601.6 jit_solution(12795002116366240641)
XLA Ops:
  7.2 0.5 broadcast.161
  7.7 1.5 reduce.5
  9.5 3.2 gather_fusion
  12.8 0.8 reshape.267
  13.6 15.3 all-to-all-start
  29.0 0.5 copy-done.15
  29.7 0.1 copy.25
  30.2 0.2 convert_reduce_fusion
  30.5 14.3 all-to-all-done
  44.9 0.6 gather_fusion.1
  45.5 0.8 gather_fusion.2
  46.4 0.1 fusion.1
  46.6 4.6 gather_fusion.3
  51.2 2.7 reshape.220
  53.9 1.8 fusion
  55.8 0.7 copy-done.1
  56.4 1.3 convolution_bitcast_fusion
  57.8 4.5 fusion.25
  62.4 0.6 copy-done.6
  63.0 0.4 fusion.14
  63.4 0.8 slice_bitcast_fusion
  64.2 18.5 %all-reduce.2.cloned.1.call-done = f32[128,1024]{1,0:T(8,128)} async-done(((f32[128,1024]{1,0:T(8,128)}), f32[128,1024]{1,0:T(8,128)}) %all-reduce.2.cloned.1.call-update) | async-done | bytes 524304 | tf_op jit(solution)/shard_map/psum | solution.py:64
  82.7 2.0 multiply_convert_fusion
  84.7 3.0 fusion.7
  87.9 0.8 copy-done.4
  88.8 0.2 fusion.29
  89.1 3.7 fusion.21
  93.0 0.1 reshape.189
  93.2 0.9 fusion.9
  94.1 0.8 copy-done.3
  94.9 0.1 copy.30
  95.1 0.3 convolution_add_fusion
  95.4 1.2 scatter_custom_fusion
  96.6 3.9 fusion.11
  100.5 3.3 reshape.247
  103.8 1.6 scatter_fusion
  105.4 10.5 scatter_fusion.1
  115.9 1.1 reshape.192
  117.0 13.8 all-to-all-start.1
  130.8 25.0 %all-to-all-done.1 = f32[128,4,384]{2,1,0:T(4,128)S(1)} async-done(((f32[128,4,384]{2,1,0:T(4,128)}), f32[128,4,384]{2,1,0:T(4,128)S(1)}, u32[]{:S(2)}, u32[]{:S(2)}) %all-to-all-start.1) | async-done | bytes 786464 | tf_op jit(solution)/shard_map/all_to_all | solution.py:93
  155.8 1.2 reshape.255
  157.0 5.4 scatter_custom_fusion.3
  162.3 1.6 multiply_reduce_fusion
  164.0 2.5 psum.15
  166.4 0.6 rsqrt_multiply_fusion
  167.0 3.3 multiply_subtract_fusion
  170.3 736.9 %reduce-scatter.3.cloned.1.call-done = f32[3,384,8]{1,2,0:T(8,128)} async-done(((f32[3,384,1024]{1,2,0:T(8,128)}), f32[3,384,8]{1,2,0:T(8,128)}) %reduce-scatter.3.cloned.1.call-update) | async-done | bytes 36880 | tf_op jit(solution)/shard_map/reduce_scatter | solution.py:78
  907.2 687.8 %reduce-scatter.5.cloned.1.call-done = f32[3,512,8]{1,2,0:T(8,128)} async-done(((f32[3,512,1024]{1,2,0:T(8,128)}), f32[3,512,8]{1,2,0:T(8,128)}) %reduce-scatter.5.cloned.1.call-update) | async-done | bytes 49168 | tf_op jit(solution)/shard_map/reduce_scatter | solution.py:79
  (73 shorter events, 1.8 us)
Async XLA Ops:
  7.2 49.3 %copy-start = (bf16[3,384,1024]{2,1,0:T(8,128)(2,1)S(1)}, bf16[3,384,1024]{2,1,0:T(8,128)(2,1)}, u32[]{:S(2)}) copy-start(bf16[3,384,1024]{2,1,0:T(8,128)(2,1)} %param.20) | copy-start | bytes 7077892
  12.7 16.3 %copy-start.16 = (s32[8]{0:T(128)S(1)}, s32[8]{0:T(128)}, u32[]{:S(2)}) copy-start(s32[8]{0:T(128)} %param.14) | copy-start | bytes 100
  12.7 16.8 %copy-start.12 = (s32[8,15]{1,0:T(8,128)S(1)}, s32[8,15]{1,0:T(8,128)}, u32[]{:S(2)}) copy-start(s32[8,15]{1,0:T(8,128)} %param.15) | copy-start | bytes 1444
  12.7 16.9 %copy-start.8 = (s32[8,15,10]{1,0,2:T(8,128)S(1)}, s32[8,15,10]{1,0,2:T(8,128)}, u32[]{:S(2)}) copy-start(s32[8,15,10]{1,0,2:T(8,128)} %param.16) | copy-start | bytes 14404
  12.7 17.2 %copy-start.11 = (s32[8,15,10]{1,0,2:T(8,128)S(1)}, s32[8,15,10]{1,0,2:T(8,128)}, u32[]{:S(2)}) copy-start(s32[8,15,10]{1,0,2:T(8,128)} %param.18) | copy-start | bytes 14404
  12.7 17.4 %copy-start.10 = (s32[8,15]{1,0:T(8,128)S(1)}, s32[8,15]{1,0:T(8,128)}, u32[]{:S(2)}) copy-start(s32[8,15]{1,0:T(8,128)} %param.17) | copy-start | bytes 1444
  13.6 31.2 %all-to-all-start = ((bf16[128,4,384]{2,1,0:T(4,128)(2,1)}), bf16[128,4,384]{2,1,0:T(4,128)(2,1)S(1)}, u32[]{:S(2)}, u32[]{:S(2)}) async-start(bf16[128,4,384]{2,1,0:T(4,128)(2,1)} %reshape.267), calls=%async_computation | async-start | bytes 786432 | tf_op jit(solution)/shard_map/all_to_all | solution.py:52
  29.0 53.8 %all-reduce.2.cloned.1.call-start = ((), (), s32[]{:S(2)}) async-start(), calls=%async_computation.4 | async-start | bytes 1048576 | tf_op jit(solution)/shard_map/psum | solution.py:64
  29.0 0.5 copy-start.15
  30.1 23.8 %copy-start.5 = (s32[8,15,10]{2,1,0:T(8,128)}, s32[8,15,10]{2,1,0:T(8,128)S(1)}, u32[]{:S(2)}) copy-start(s32[8,15,10]{2,1,0:T(8,128)S(1)} %copy.24) | copy-start | bytes 14404
  30.5 23.4 %copy-start.7 = (f32[8,15,2]{2,1,0:T(8,128)}, f32[8,15,2]{2,1,0:T(8,128)S(1)}, u32[]{:S(2)}) copy-start(f32[8,15,2]{2,1,0:T(8,128)S(1)} %maximum_divide_fusion) | copy-start | bytes 2884
  55.8 0.7 copy-start.1
  56.4 1.4 copy-start.9
  57.8 849.5 %reduce-scatter.3.cloned.1.call-start = ((), (), s32[]{:S(2)}) async-start(), calls=%async_computation.5 | async-start | bytes 4755456 | tf_op jit(solution)/shard_map/reduce_scatter | solution.py:78
  62.3 0.6 copy-start.6
  63.4 21.3 %copy-start.2 = (bf16[120,2,384]{2,0,1:T(8,128)(2,1)S(1)}, bf16[120,2,384]{2,0,1:T(8,128)(2,1)}, u32[]{:S(2)}) copy-start(bf16[120,2,384]{2,0,1:T(8,128)(2,1)} %copy-done.1) | copy-start | bytes 552964
  87.7 0.9 copy-start.4
  87.8 1507.3 %reduce-scatter.5.cloned.1.call-start = ((), (), s32[]{:S(2)}) async-start(), calls=%async_computation.6 | async-start | bytes 6340608 | tf_op jit(solution)/shard_map/reduce_scatter | solution.py:79
  94.0 0.8 copy-start.3
  115.9 14.9 copy-start.13
  117.0 38.8 %all-to-all-start.1 = ((f32[128,4,384]{2,1,0:T(4,128)}), f32[128,4,384]{2,1,0:T(4,128)S(1)}, u32[]{:S(2)}, u32[]{:S(2)}) async-start(f32[128,4,384]{2,1,0:T(4,128)} %reshape.192), calls=%async_computation.1 | async-start | bytes 1572864 | tf_op jit(solution)/shard_map/all_to_all | solution.py:93
  157.0 9.5 copy-start.14
Sparse Core Ops, SparseCore 0:
  57.9 24.7 all-reduce.1
  89.9 817.2 reduce-scatter.2
  910.3 684.6 reduce-scatter.4
where the time goes:
time: 1620 us; the launch traced here: 1600 us
  waiting for transfers between devices  1480 us (91%)
  starting transfers between devices  29.2 us (2%)
  other arithmetic  28.1 us (2%)
  local copies, waits for them, and re-layouts  24.9 us (2%)
  matrix products  20.1 us (1%)
    reduce_scatter x1, waiting for transfers between devices, body(): lax.psum_scatter(grad_one, ('dp', 'table'), scatter_dimension=2, tiled=True)  737 us
    reduce_scatter x1, waiting for transfers between devices, body(): lax.psum_scatter(grad_two, ('dp', 'table'), scatter_dimension=2, tiled=True)  688 us
  transfers between devices with their start and end apart: 5, of which 5 were waited for; matrix products, arithmetic and copies ran while one was open for 3% of the time, Pallas kernels for 0%

commit v1 on v0

v1 whole, which is shorter than its diff:
```python
import functools
import jax
import jax.numpy as jnp
from jax import lax
from jax.experimental import pallas as pl
from jax.experimental.pallas import tpu as pltpu
from jax.sharding import Mesh
from jax.sharding import PartitionSpec as P

LEARNING_RATE = 0.1
BF16 = jnp.bfloat16
F32 = jnp.float32
LANES = 128
SEED_ROWS = 32
COT_ROWS = 16


def matmul(a, b, contract=(1, 0)):
    dims = (((contract[0],), (contract[1],)), ((), ()))
    return lax.dot_general(a, b, dims, preferred_element_type=F32)


def row_to_column(row):
    return jnp.transpose(jnp.broadcast_to(row, (LANES, LANES)))[:, 0:1]


def column_to_row(column):
    return jnp.transpose(jnp.broadcast_to(column, (LANES, LANES)))[0:1, :]


def call(kernel, outs, operands, flops, smem=0, scratch=()):
    moved = sum(o.size * o.dtype.itemsize for o in list(operands) + list(outs))
    specs = [pl.BlockSpec(memory_space=pltpu.SMEM)] * smem
    specs += [pl.BlockSpec(memory_space=pltpu.VMEM)] * (len(operands) - smem)
    return pl.pallas_call(
        kernel,
        out_shape=tuple(outs),
        in_specs=specs,
        out_specs=tuple(pl.BlockSpec(memory_space=pltpu.VMEM) for _ in outs),
        scratch_shapes=list(scratch),
        compiler_params=pltpu.CompilerParams(vmem_limit_bytes=40 * 1024 * 1024),
        cost_estimate=pl.CostEstimate(flops=flops, bytes_accessed=moved, transcendentals=0),
    )(*operands)


def shaped(shape, dtype):
    return jax.ShapeDtypeStruct(shape, dtype)


def serve_kernel(serve_ref, table_ref, out_ref):
    rows = table_ref[...].astype(BF16)
    lanes = lax.broadcasted_iota(jnp.int32, (LANES, rows.shape[0]), 1)
    for block in range(out_ref.shape[0] // LANES):
        span = slice(block * LANES, (block + 1) * LANES)
        wanted = row_to_column(serve_ref[:, span])
        onehot = jnp.where(wanted == lanes, 1.0, 0.0).astype(BF16)
        out_ref[span, :] = matmul(onehot, rows).astype(BF16)


def index_kernel(idx_ref, cot_ref, w2_ref, ct_ref, c_ref, inv_ref, et_ref, e_ref, back_ref, spread):
    nodes = idx_ref.shape[0]
    slots = ct_ref.shape[1]
    seeds = cot_ref.shape[0]
    neighbours = idx_ref.shape[1] - 2
    lanes = lax.broadcasted_iota(jnp.int32, (nodes, 2 * slots), 1)
    idx = idx_ref[...]
    counts = jnp.zeros((nodes, 2 * slots), F32)
    for j in range(1, 1 + neighbours):
        counts = counts + jnp.where(idx[:, j : j + 1] == lanes, 1.0, 0.0)
    own = jnp.where(idx[:, 0:1] == lanes[:, :slots], 1.0, 0.0)
    parts = (own, counts[:, :slots], counts[:, slots:])
    spread[...] = jnp.zeros(spread.shape, F32)
    for k, part in enumerate(parts):
        span = slice(k * nodes, (k + 1) * nodes)
        ct_ref[span, :] = part.astype(BF16)
        c_ref[:, span] = jnp.transpose(part).astype(BF16)
        if k == 0:
            inverse = jnp.ones((nodes, 1), F32)
        else:
            inverse = 1.0 / jnp.maximum(jnp.sum(part, axis=1, keepdims=True), 1.0)
        inv_ref[span, :] = jnp.broadcast_to(inverse, (nodes, LANES))
        back = matmul(cot_ref[...], w2_ref[k], (1, 1))
        spread[k * seeds : (k + 1) * seeds, :] = back * inverse[:seeds]
    groups = lax.broadcasted_iota(jnp.int32, (nodes, LANES), 1)
    member = jnp.where(idx[:, neighbours + 1 : neighbours + 2] == groups, 1.0, 0.0)
    et_ref[...] = member.astype(BF16)
    e_ref[...] = jnp.transpose(member)[:SEED_ROWS].astype(BF16)
    whole = spread[...]
    high = whole.astype(BF16)
    low = (whole - high.astype(F32)).astype(BF16)
    back_ref[...] = matmul(member.astype(BF16), high) + matmul(member.astype(BF16), low)


def first_kernel(fetched_ref, ct_ref, inv_ref, w1_ref, layer_ref, partial_ref):
    layers = w1_ref.shape[0]
    nodes = partial_ref.shape[0]
    total = None
    for k in range(layers):
        span = slice(k * nodes, (k + 1) * nodes)
        summed = matmul(ct_ref[span, :], fetched_ref[...])
        layer = (summed * inv_ref[span, 0:1]).astype(BF16)
        layer_ref[span, :] = layer
        term = matmul(layer, w1_ref[k])
        total = term if total is None else total + term
    partial_ref[...] = total


def hidden_kernel(place_ref, mine_ref, other_ref, back_ref, e_ref, inv_ref, c_ref, w1_ref, cot_ref,
                  pack_ref, slot_ref):
    layers = w1_ref.shape[0]
    nodes = mine_ref.shape[0]
    width = pack_ref.shape[2]
    seeds = cot_ref.shape[0]
    values = mine_ref[...] + other_ref[...]
    sigma = jax.nn.sigmoid(values)
    hidden = (values * sigma).astype(BF16)
    slope = sigma * (1.0 + values * (1.0 - sigma))
    back = (back_ref[...] * slope).astype(BF16)
    scale = jnp.concatenate(
        [inv_ref[k * nodes : k * nodes + seeds, 0:1] for k in range(layers)]
        + [jnp.zeros((SEED_ROWS - layers * seeds, 1), F32)],
        0,
    )
    second = matmul(e_ref[...], hidden) * scale
    half = second.shape[1] // 2
    second = jnp.where(place_ref[0] == 0, second[:, :half], second[:, half:])
    cot = cot_ref[...].astype(F32)
    cot = jnp.concatenate([cot, jnp.zeros((COT_ROWS - seeds, cot.shape[1]), F32)], 0)
    for j in range(pack_ref.shape[0]):
        span = slice(j * width, (j + 1) * width)
        pack_ref[j, :nodes, :] = back[:, span]
        for part in range(half // width):
            first = nodes + part * SEED_ROWS
            pack_ref[j, first : first + SEED_ROWS, :] = second[
                :, part * width : (part + 1) * width
            ].astype(BF16)
        first = nodes + half // width * SEED_ROWS
        pack_ref[j, first : first + COT_ROWS, :] = cot[:, span].astype(BF16)
    total = None
    for k in range(layers):
        span = slice(k * nodes, (k + 1) * nodes)
        back_in = matmul(back, w1_ref[k], (1, 1)) * inv_ref[span, 0:1]
        term = matmul(c_ref[:, span], back_in.astype(BF16))
        total = term if total is None else total + term
    slot_ref[...] = total.astype(BF16)


def weight_kernel(place_ref, *refs):
    count = place_ref.shape[0] - 2
    layers_in = refs[:count]
    pack_ref = refs[count]
    outs = refs[count + 1 : -1]
    total = refs[-1]
    width = pack_ref.shape[2]
    columns = layers_in[0].shape[1]
    nodes = LANES
    relations = layers_in[0].shape[0] // nodes
    half = (total.shape[1] // relations) - columns
    seeds = SEED_ROWS // (relations + 1)
    packs = [pack_ref.at[place_ref[2 + d]] for d in range(count)]
    left = jnp.concatenate([p[:nodes, :] for p in packs], 0)
    pieces = half // width
    first = nodes + pieces * SEED_ROWS
    cots = jnp.concatenate([p[first : first + COT_ROWS, :].astype(F32)[:seeds] for p in packs], 0)
    seconds = [
        jnp.concatenate(
            [p[nodes + part * SEED_ROWS : nodes + (part + 1) * SEED_ROWS, :].astype(F32) for part in range(pieces)],
            1,
        )
        for p in packs
    ]
    for k in range(relations):
        right = jnp.concatenate([r[k * nodes : (k + 1) * nodes, :] for r in layers_in], 0)
        total[:, k * columns : (k + 1) * columns] = matmul(left, right, (0, 0))
        right = jnp.concatenate([s[k * seeds : (k + 1) * seeds] for s in seconds], 0).astype(BF16)
        start = relations * columns + k * half
        total[:, start : start + half] = matmul(cots.astype(BF16), right, (0, 0))
    rows = outs[0].shape[0]
    for d, out in enumerate(outs):
        target = lax.rem(place_ref[1] + d, len(outs))
        block = total[pl.ds(pl.multiple_of(target * rows, rows), rows), :]
        out[...] = block.astype(out.dtype)


def row_kernel(serve_ref, arrived_ref, grad_ref, square_ref):
    rows = lax.broadcasted_iota(jnp.int32, (LANES, serve_ref.shape[1]), 0)
    arrived = arrived_ref[...]
    for block in range(grad_ref.shape[0] // LANES):
        span = slice(block * LANES, (block + 1) * LANES)
        onehot = jnp.where(serve_ref[...] == rows + block * LANES, 1.0, 0.0).astype(BF16)
        grad = matmul(onehot, arrived)
        grad_ref[span, :] = grad
        square_ref[block : block + 1, :] = column_to_row(jnp.sum(grad * grad, axis=1, keepdims=True))


def update_kernel(columns, table_ref, grad_ref, accum_ref, mine_ref, other_ref, table_out, accum_out):
    accum = accum_ref[...] + (mine_ref[...] + other_ref[...]) / columns
    accum_out[...] = accum
    inverse = lax.rsqrt(accum)
    for block in range(accum.shape[0]):
        span = slice(block * LANES, (block + 1) * LANES)
        scale = row_to_column(inverse[block : block + 1, :])
        table_out[span, :] = table_ref[span, :] - LEARNING_RATE * grad_ref[span, :] * scale


def shift(array, axis, by):
    size = lax.axis_size(axis)
    return lax.ppermute(array, axis, [(i, (i + by) % size) for i in range(size)])


def body(
    table,
    accum,
    serve_rows,
    seed_slot,
    hop1_slot,
    hop2_slot,
    hop1_rel,
    hop2_rel,
    cotangent,
    w_first,
    w_second,
):
    everyone = ("dp", "y", "z")
    owners = lax.axis_size(everyone)
    table_rows, columns = table.shape
    slots = serve_rows.shape[1]
    seeds, fanout = hop1_slot.shape
    fanout_two = hop2_slot.shape[2]
    nodes = seeds + seeds * fanout
    layers, hidden_units = w_second.shape[:2]
    half = hidden_units // 2
    n_x, n_y, n_z = (lax.axis_size(a) for a in everyone)
    x, y = lax.axis_index("dp"), lax.axis_index("y")
    width = hidden_units // n_x

    outgoing = call(
        serve_kernel, [shaped((slots, columns), BF16)], (serve_rows, table), 2 * slots * table_rows * columns
    )[0]
    fetched = lax.all_to_all(
        outgoing.reshape(owners, slots // owners, columns), everyone, split_axis=0, concat_axis=0, tiled=True
    ).reshape(slots, columns)

    key_one = hop1_slot + slots * hop1_rel
    key_two = (hop2_slot + slots * hop2_rel).reshape(seeds * fanout, fanout_two)
    seed_ids = jnp.arange(seeds, dtype=jnp.int32)[:, None]
    group = (seeds * (1 + hop1_rel) + seed_ids).reshape(-1, 1)
    spare = jnp.full((seeds * fanout, fanout - fanout_two), -1, jnp.int32)
    idx = jnp.concatenate(
        [
            jnp.concatenate([seed_slot[:, None], key_one, seed_ids], 1),
            jnp.concatenate([hop1_slot.reshape(-1, 1), key_two, spare, group], 1),
        ],
        0,
    )
    ct, c, inverse, member_t, member, back_hidden = call(
        index_kernel,
        [
            shaped((layers * nodes, slots), BF16),
            shaped((slots, layers * nodes), BF16),
            shaped((layers * nodes, LANES), F32),
            shaped((nodes, LANES), BF16),
            shaped((SEED_ROWS, nodes), BF16),
            shaped((nodes, hidden_units), F32),
        ],
        (idx, cotangent, w_second),
        2 * layers * seeds * hidden_units * hidden_units,
        scratch=[pltpu.VMEM((LANES, hidden_units), F32)],
    )

    layer_in, partial_pre = call(
        first_kernel,
        [shaped((layers * nodes, columns), BF16), shaped((nodes, hidden_units), F32)],
        (fetched, ct, inverse, w_first),
        2 * layers * nodes * columns * (slots + hidden_units),
    )
    other_pre = shift(partial_pre, "col", 1)
    layer_parts = [layer_in] + [shift(layer_in, "dp", d) for d in range(1, n_x)]

    pack_rows = nodes + half // width * SEED_ROWS + COT_ROWS
    pack, slot_grad = call(
        hidden_kernel,
        [shaped((n_x, pack_rows, width), BF16), shaped((slots, columns), BF16)],
        (
            lax.axis_index("col").reshape(1),
            partial_pre,
            other_pre,
            back_hidden,
            member,
            inverse,
            c,
            w_first,
            cotangent,
        ),
        2 * layers * nodes * columns * (slots + hidden_units),
        smem=1,
    )
    pack = lax.all_to_all(pack, "dp", split_axis=0, concat_axis=0, tiled=True)
    arrived = lax.all_to_all(
        slot_grad.reshape(owners, slots // owners, columns), everyone, split_axis=0, concat_axis=0, tiled=True
    ).reshape(slots, columns)

    grad_columns = layers * (columns + half)
    place = jnp.stack([jnp.int32(0), y] + [lax.rem(x + n_x - d, n_x) for d in range(n_x)]).astype(jnp.int32)
    block_rows = width // n_y
    blocks = call(
        weight_kernel,
        [shaped((block_rows, grad_columns), F32 if d == 0 else BF16) for d in range(n_y)],
        (place, *layer_parts, pack),
        2 * n_x * nodes * width * grad_columns,
        smem=1,
        scratch=[pltpu.VMEM((width, grad_columns), F32)],
    )
    grads = blocks[0]
    for d in range(1, n_y):
        grads = grads + shift(blocks[d], "y", d).astype(F32)
    grads = grads.astype(BF16).reshape(n_z, block_rows // n_z, grad_columns)
    grads = lax.all_to_all(grads, "z", split_axis=0, concat_axis=0, tiled=True)
    grads = jnp.sum(grads.astype(F32), axis=0)
    grad_one = grads[:, : layers * columns].reshape(-1, layers, columns).transpose(1, 2, 0)
    grad_two = grads[:, layers * columns :].reshape(-1, layers, half).transpose(1, 2, 0)

    row_grad, squares = call(
        row_kernel,
        [shaped((table_rows, columns), F32), shaped((table_rows // LANES, LANES), F32)],
        (serve_rows, arrived),
        2 * slots * table_rows * columns,
    )
    other_squares = shift(squares, "col", 1)
    new_table, new_accum = call(
        functools.partial(update_kernel, 2 * columns),
        [shaped((table_rows, columns), F32), shaped((table_rows // LANES, LANES), F32)],
        (table, row_grad, accum.reshape(-1, LANES), squares, other_squares),
        3 * table_rows * columns,
    )
    return (new_table, new_accum.reshape(-1), grad_one, grad_two)


def solution(mesh):
    n_dp, n_table, n_col = (mesh.shape[a] for a in ("dp", "table", "col"))
    n_y = 4 if n_table % 4 == 0 and n_table > 4 else 2
    fine = Mesh(mesh.devices.reshape(n_dp, n_y, n_table // n_y, n_col), ("dp", "y", "z", "col"))
    rows = ("dp", "y", "z")
    placed = (
        P(rows, "col"),
        P(rows),
        P(rows, None),
        P(rows),
        P(rows, None),
        P(rows, None, None),
        P(rows, None),
        P(rows, None, None),
        P(rows, None),
        P(None, "col", None),
        P(),
    )
    return jax.shard_map(
        body,
        mesh=fine,
        in_specs=placed,
        out_specs=(P(rows, "col"), P(rows), P(None, "col", rows), P(None, "col", rows)),
        check_vma=False,
    )
```

time: 1620 us -> 122 us (0.08)
  waiting for transfers between devices: 1480 us -> 47.8 us
  other arithmetic: 28.1 us -> 2.1 us
  matrix products: 20.1 us -> 0 us
    reduce_scatter x2 -> x0, waiting for transfers between devices: 1420 us -> none  [the longest x1 737 us: body(): lax.psum_scatter(grad_one, ('dp', 'table'), scatter_dimension=2, tiled=True)]
    ppermute x0 -> x8, waiting for transfers between devices: none -> 28.1 us  [shift(): lax.ppermute(array, axis, [(i, (i + by) % size) for i in range(size)])]
    dot_general x11 -> x0, matrix products: 20.1 us -> none  [the longest x1 4.51 us: body(): jnp.einsum('so,kho->skh', cotangent, w_second, preferred_element_type=jnp...]
    all_to_all x2 -> x4, waiting for transfers between devices: 39.3 us -> 19.7 us  [the longest x1 8.02 us: body(): lax.all_to_all(outgoing.reshape(owners, slots // owners, columns), everyo...]
    scatter-add x4 -> x0, other arithmetic: 18.6 us -> none  [the longest x1 10.5 us: body(): slot_grad.at[hop2_slot.reshape(-1)].add(hop_two_grad.reshape(-1, columns))]
    psum x1 -> x0, waiting for transfers between devices: 18.5 us -> none  [body(): pre_act = lax.psum(partial_pre, 'col')]
  transfers between devices with their start and end apart: 5 -> 12, of which waited for: 5 -> 9; matrix products, arithmetic and copies ran while one was open for 3% -> 3% of each run, Pallas kernels for 0% -> 4%
where the time goes in v1:
time: 122 us; the launch traced here: 120 us
  waiting for transfers between devices  47.8 us (39%)
  starting transfers between devices  41.3 us (34%)
  local copies, waits for them, and re-layouts  14.8 us (12%)
  Pallas kernels  12.8 us (10%)
  other arithmetic  2.1 us (2%)
    ppermute x8, waiting for transfers between devices, shift(): lax.ppermute(array, axis, [(i, (i + by) % size) for i in range(size)])  28.1 us
    all_to_all x1, starting transfers between devices, body(): lax.all_to_all(outgoing.reshape(owners, slots // owners, columns), everyo...  15.8 us
    pallas_call x7, Pallas kernels, call(): pl.pallas_call(kernel, out_shape=tuple(outs), in_specs=specs, out_specs=t...  12.8 us
    ppermute x8, starting transfers between devices, shift(): lax.ppermute(array, axis, [(i, (i + by) % size) for i in range(size)])  11.3 us
    unnamed x38, local copies, waits for them, and re-layouts  10.1 us
    all_to_all x1, waiting for transfers between devices, body(): lax.all_to_all(outgoing.reshape(owners, slots // owners, columns), everyo...  8.02 us
    all_to_all x1, waiting for transfers between devices, body(): grads = lax.all_to_all(grads, 'z', split_axis=0, concat_axis=0, tiled=True)  7.71 us
    all_to_all x1, starting transfers between devices, body(): lax.all_to_all(slot_grad.reshape(owners, slots // owners, columns), every...  7.41 us
  transfers between devices with their start and end apart: 12, of which 9 were waited for; matrix products, arithmetic and copies ran while one was open for 3% of the time, Pallas kernels for 4%

profile of v1, /device:TPU:8, one launch (start us, length us, event | category | flops | bytes accessed | tf_op | source)
XLA Modules:
  0.0 119.6 jit_solution(288658141171434272)
XLA Ops:
  0.6 1.4 %copy-done.2 = f32[1024,384]{1,0:T(8,128)S(1)} copy-done((f32[1024,384]{1,0:T(8,128)S(1)}, f32[1024,384]{1,0:T(8,128)}, u32[]{:S(2)}) %copy-start.2) | copy-done | bytes 1572888
  2.0 0.7 copy-done.10
  2.8 0.9 shard_map.138
  3.7 0.8 reshape.48
  4.5 15.8 %all-to-all-start = ((bf16[128,4,384]{2,1,0:T(4,128)(2,1)}), bf16[128,4,384]{2,1,0:T(4,128)(2,1)}, u32[]{:S(2)}, u32[]{:S(2)}) async-start(bf16[128,4,384]{2,1,0:T(4,128)(2,1)} %reshape.48), calls=%async_computation | async-start | bytes 786432 | tf_op jit(solution)/shard_map/all_to_all | solution.py:240
  20.3 0.1 reshape.50
  20.4 0.1 reshape.52
  20.5 0.1 reshape.51
  20.7 0.1 copy.30
  20.8 0.1 copy.29
  20.9 0.1 pad_add_fusion.idx_ref
  21.0 2.8 %copy-done.1 = bf16[3,1024,1024]{2,1,0:T(8,128)(2,1)S(1)} copy-done((bf16[3,1024,1024]{2,1,0:T(8,128)(2,1)S(1)}, bf16[3,1024,1024]{2,1,0:T(8,128)(2,1)}, u32[]{:S(2)}) %copy-start.1) | copy-done | bytes 6291480
  23.8 2.5 %shard_map.139 = (bf16[384,512]{1,0:T(8,128)(2,1)S(1)}, bf16[512,384]{1,0:T(8,128)(2,1)S(1)}, f32[384,128]{1,0:T(8,128)S(1)}, bf16[128,128]{1,0:T(8,128)(2,1)}, ...) custom-call(s32[128,17]{1,0:T(8,128)S(1)} %pad_add_fusion.idx_ref, bf16[8,1024]{1,0:T(8,128)(2,1)S(1)} %copy-done.8, ...), custom_call_target="tpu_custom_call" | custom-call | flops 50331648 | bytes 7864832 | tf_op jit(solution)/shard_map/pallas_call | solution.py:35
  26.3 0.8 copy-done.4
  27.1 0.7 copy-done.6
  27.8 8.0 %all-to-all-done = bf16[128,4,384]{2,1,0:T(4,128)(2,1)} async-done(((bf16[128,4,384]{2,1,0:T(4,128)(2,1)}), bf16[128,4,384]{2,1,0:T(4,128)(2,1)}, u32[]{:S(2)}, u32[]{:S(2)}) %all-to-all-start) | async-done | bytes 393248 | tf_op jit(solution)/shard_map/all_to_all | solution.py:240
  35.8 1.1 reshape.49.fetched_ref
  36.9 1.0 copy-done.7
  37.9 1.8 %shard_map.140 = (bf16[384,384]{1,0:T(8,128)(2,1)S(1)}, f32[128,1024]{1,0:T(8,128)}) custom-call(bf16[512,384]{1,0:T(8,128)(2,1)S(1)} %reshape.49.fetched_ref, bf16[384,512]{1,0:T(8,128)(2,1)S(1)} %copy-done.7, f32[384,128]{1,0:T(8,128)S(1)} %get-tuple-element.22.inv_ref, bf16[3,384,1024]{2,1,0:T(8,128)(2,1)S(1)} %copy-done), custom_call_target="tpu_custom_call" | custom-call | flops 452984832 | bytes 4161536 | tf_op jit(solution)/shard_map/pallas_call | solution.py:35
  39.7 0.7 copy-done.12
  40.4 2.2 %collective-permute-done.other_ref = f32[128,1024]{1,0:T(8,128)} collective-permute-done((f32[128,1024]{1,0:T(8,128)}, f32[128,1024]{1,0:T(8,128)}, u32[]{:S(2)}, u32[]{:S(2)}) %collective-permute-start) | collective-permute-done | bytes 524320 | tf_op jit(solution)/shard_map/ppermute | solution.py:208
  42.7 1.0 copy-done.5
  43.7 3.5 %shard_map.141 = (bf16[4,208,256]{2,1,0:T(8,128)(2,1)}, bf16[512,384]{1,0:T(8,128)(2,1)S(1)}) custom-call(s32[1]{0:T(128)} %bitcast.place_ref, f32[128,1024]{1,0:T(8,128)} %get-tuple-element.23.mine_ref, f32[128,1024]{1,0:T(8,128)} %collective-permute-done.other_ref, f32[128,1024]{1,0:T(8,128)S(1)} %get-tuple-element.24.back_ref, ...), custom_call_target="tpu_custom_call" | custom-call | flops 452984832 | bytes 5365764 | tf_op jit(solution)/shard_map/pallas_call | solution.py:35
  47.2 3.5 %all-to-all-start.2 = ((bf16[4,208,256]{2,1,0:T(8,128)(2,1)}), bf16[4,208,256]{2,1,0:T(8,128)(2,1)S(1)}, u32[]{:S(2)}, u32[]{:S(2)}) async-start(bf16[4,208,256]{2,1,0:T(8,128)(2,1)} %get-tuple-element.33), calls=%async_computation.2 | async-start | bytes 851968 | tf_op jit(solution)/shard_map/all_to_all | solution.py:298
  50.7 2.0 %collective-permute-start.2 = (bf16[384,384]{1,0:T(8,128)(2,1)}, bf16[384,384]{1,0:T(8,128)(2,1)S(1)}, u32[]{:S(2)}, u32[]{:S(2)}) collective-permute-start(bf16[384,384]{1,0:T(8,128)(2,1)} %copy-done.12), channel_id=1, source_target_pairs={{0,64},{64,128},{128,192},{192,0},{1,65},{65,129},{129,193},{193,1... | collective-permute-start | bytes 884744 | tf_op jit(solution)/shard_map/ppermute | solution.py:208
  52.6 2.7 %collective-permute-start.3 = (bf16[384,384]{1,0:T(8,128)(2,1)}, bf16[384,384]{1,0:T(8,128)(2,1)S(1)}, u32[]{:S(2)}, u32[]{:S(2)}) collective-permute-start(bf16[384,384]{1,0:T(8,128)(2,1)} %copy-done.12), channel_id=1, source_target_pairs={{0,128},{64,192},{128,0},{192,64},{1,129},{65,193},{129,1},{193,65... | collective-permute-start | bytes 884744 | tf_op jit(solution)/shard_map/ppermute | solution.py:208
  55.3 1.5 %collective-permute-start.4 = (bf16[384,384]{1,0:T(8,128)(2,1)}, bf16[384,384]{1,0:T(8,128)(2,1)S(1)}, u32[]{:S(2)}, u32[]{:S(2)}) collective-permute-start(bf16[384,384]{1,0:T(8,128)(2,1)} %copy-done.12), channel_id=1, source_target_pairs={{0,192},{64,0},{128,64},{192,128},{1,193},{65,1},{129,65},{193,129... | collective-permute-start | bytes 884744 | tf_op jit(solution)/shard_map/ppermute | solution.py:208
  56.8 0.1 stack.23.place_ref
  56.9 9.3 %collective-permute-done.2.refs_1_ = bf16[384,384]{1,0:T(8,128)(2,1)S(1)} collective-permute-done((bf16[384,384]{1,0:T(8,128)(2,1)}, bf16[384,384]{1,0:T(8,128)(2,1)S(1)}, u32[]{:S(2)}, u32[]{:S(2)}) %collective-permute-start.2) | collective-permute-done | bytes 294944 | tf_op jit(solution)/shard_map/ppermute | solution.py:208
  66.2 6.1 %collective-permute-done.3.refs_2_ = bf16[384,384]{1,0:T(8,128)(2,1)S(1)} collective-permute-done((bf16[384,384]{1,0:T(8,128)(2,1)}, bf16[384,384]{1,0:T(8,128)(2,1)S(1)}, u32[]{:S(2)}, u32[]{:S(2)}) %collective-permute-start.3) | collective-permute-done | bytes 294944 | tf_op jit(solution)/shard_map/ppermute | solution.py:208
  72.3 1.0 copy-done.13
  73.2 1.7 %shard_map.144 = (f32[64,2688]{1,0:T(8,128)S(1)}, bf16[64,2688]{1,0:T(8,128)(2,1)S(1)}, bf16[64,2688]{1,0:T(8,128)(2,1)S(1)}, bf16[64,2688]{1,0:T(8,128)(2,1)S(1)}) custom-call(s32[6]{0:T(128)S(1)} %stack.23.place_ref, bf16[384,384]{1,0:T(8,128)(2,1)S(1)} %copy-done.13, bf16[384,384]{1,0:T(8,128)(2,1)S(1)} %collective-permute-done.2.refs_1_, ...), custom_call_target="tpu_custom_call" | custom-call | flops 704643072 | bytes 3325976 | tf_op jit(solution)/shard_map/pallas_call | solution.py:35
  74.9 1.3 %collective-permute-start.5 = (bf16[64,2688]{1,0:T(8,128)(2,1)S(1)}, bf16[64,2688]{1,0:T(8,128)(2,1)S(1)}, u32[]{:S(2)}, u32[]{:S(2)}) collective-permute-start(bf16[64,2688]{1,0:T(8,128)(2,1)S(1)} %get-tuple-element.35), channel_id=1, source_target_pairs={{0,16},{16,32},{32,48},{48,0},{1,17},{17,33},{33,49},{49,1},{2,18}... | collective-permute-start | bytes 1032200 | tf_op jit(solution)/shard_map/ppermute | solution.py:208
  76.2 3.8 %collective-permute-start.6 = (bf16[64,2688]{1,0:T(8,128)(2,1)S(1)}, bf16[64,2688]{1,0:T(8,128)(2,1)S(1)}, u32[]{:S(2)}, u32[]{:S(2)}) collective-permute-start(bf16[64,2688]{1,0:T(8,128)(2,1)S(1)} %get-tuple-element.36), channel_id=1, source_target_pairs={{0,32},{16,48},{32,0},{48,16},{1,33},{17,49},{33,1},{49,17},{2,34}... | collective-permute-start | bytes 1032200 | tf_op jit(solution)/shard_map/ppermute | solution.py:208
  80.0 0.8 reshape.53
  80.8 7.4 %all-to-all-start.1 = ((bf16[128,4,384]{2,1,0:T(4,128)(2,1)}), bf16[128,4,384]{2,1,0:T(4,128)(2,1)S(1)}, u32[]{:S(2)}, u32[]{:S(2)}) async-start(bf16[128,4,384]{2,1,0:T(4,128)(2,1)} %reshape.53), calls=%async_computation.1 | async-start | bytes 786432 | tf_op jit(solution)/shard_map/all_to_all | solution.py:299
  88.2 0.7 collective-permute-done.6
  89.0 8.5 %collective-permute-done.7 = bf16[64,2688]{1,0:T(8,128)(2,1)} collective-permute-done((bf16[64,2688]{1,0:T(8,128)(2,1)S(1)}, bf16[64,2688]{1,0:T(8,128)(2,1)}, u32[]{:S(2)}, u32[]{:S(2)}) %collective-permute-start.7) | collective-permute-done | bytes 344096 | tf_op jit(solution)/shard_map/ppermute | solution.py:208
  97.5 1.9 %fusion = bf16[8,8,2688]{2,1,0:T(8,128)(2,1)} fusion(bf16[64,2688]{1,0:T(8,128)(2,1)} %collective-permute-done.7, bf16[64,2688]{1,0:T(8,128)(2,1)S(1)} %collective-permute-done.6, f32[64,2688]{1,0:T(8,128)S(1)} %get-tuple-element.34, bf16[64,2688]{1,0:T(8,128)(2,1)S(1)} %collective-permute-done.5), kind=kLoop, calls=%fused_computation.2 | loop fusion | flops 1204224 | bytes 2064384 | tf_op jit(solution)/shard_map/reshape | solution.py:317
  99.4 4.0 %all-to-all-done.1 = bf16[128,4,384]{2,1,0:T(4,128)(2,1)S(1)} async-done(((bf16[128,4,384]{2,1,0:T(4,128)(2,1)}), bf16[128,4,384]{2,1,0:T(4,128)(2,1)S(1)}, u32[]{:S(2)}, u32[]{:S(2)}) %all-to-all-start.1) | async-done | bytes 393248 | tf_op jit(solution)/shard_map/all_to_all | solution.py:299
  103.4 3.4 %all-to-all-start.3 = ((bf16[8,8,2688]{2,1,0:T(8,128)(2,1)}), bf16[8,8,2688]{2,1,0:T(8,128)(2,1)S(1)}, u32[]{:S(2)}, u32[]{:S(2)}) async-start(bf16[8,8,2688]{2,1,0:T(8,128)(2,1)} %fusion), calls=%async_computation.3 | async-start | bytes 688128 | tf_op jit(solution)/shard_map/all_to_all | solution.py:318
  106.8 0.1 reshape.54.arrived_ref
  106.9 0.9 shard_map.142
  107.9 1.2 collective-permute-done.1.other_ref
  109.0 1.6 %shard_map.143 = (f32[1024,384]{1,0:T(8,128)}, f32[8,128]{1,0:T(8,128)}) custom-call(f32[1024,384]{1,0:T(8,128)S(1)} %copy-done.3, f32[1024,384]{1,0:T(8,128)S(1)} %get-tuple-element.28.grad_ref, f32[8,128]{1,0:T(8,128)S(1)} %bitcast.19, f32[8,128]{1,0:T(8,128)S(1)} %get-tuple-element.29.mine_ref, f32[8,128]{1,0:T(8,128)S(1)} %collective-permute-done.1.other_ref), custom_call_target="tpu_custom_call" | custom-call | flops 1179648 | bytes 4734976 | tf_op jit(solution)/shard_map/pallas_call | solution.py:35
  110.6 7.7 %all-to-all-done.3 = bf16[8,8,2688]{2,1,0:T(8,128)(2,1)S(1)} async-done(((bf16[8,8,2688]{2,1,0:T(8,128)(2,1)}), bf16[8,8,2688]{2,1,0:T(8,128)(2,1)S(1)}, u32[]{:S(2)}, u32[]{:S(2)}) %all-to-all-start.3) | async-done | bytes 344096 | tf_op jit(solution)/shard_map/all_to_all | solution.py:318
  118.4 0.6 slice.9
  119.0 0.6 slice.8
  (42 shorter events, 0.4 us)
Async XLA Ops:
  0.6 1.4 %copy-start.2 = (f32[1024,384]{1,0:T(8,128)S(1)}, f32[1024,384]{1,0:T(8,128)}, u32[]{:S(2)}) copy-start(f32[1024,384]{1,0:T(8,128)} %table_ref.3) | copy-start | bytes 4718596
  2.0 0.7 copy-start.10
  2.7 17.5 %copy-start.16 = (s32[8,15]{1,0:T(8,128)S(1)}, s32[8,15]{1,0:T(8,128)}, u32[]{:S(2)}) copy-start(s32[8,15]{1,0:T(8,128)} %param.15) | copy-start | bytes 1444
  2.7 17.6 %copy-start.17 = (s32[8,15]{1,0:T(8,128)S(1)}, s32[8,15]{1,0:T(8,128)}, u32[]{:S(2)}) copy-start(s32[8,15]{1,0:T(8,128)} %param.17) | copy-start | bytes 1444
  2.7 17.7 %copy-start.14 = (s32[8,15,10]{1,0,2:T(8,128)S(1)}, s32[8,15,10]{1,0,2:T(8,128)}, u32[]{:S(2)}) copy-start(s32[8,15,10]{1,0,2:T(8,128)} %param.16) | copy-start | bytes 14404
  2.7 17.7 %copy-start.15 = (s32[8,15,10]{1,0,2:T(8,128)S(1)}, s32[8,15,10]{1,0,2:T(8,128)}, u32[]{:S(2)}) copy-start(s32[8,15,10]{1,0,2:T(8,128)} %param.18) | copy-start | bytes 14404
  2.7 18.1 %copy-start.18 = (s32[8]{0:T(128)S(1)}, s32[8]{0:T(128)}, u32[]{:S(2)}) copy-start(s32[8]{0:T(128)} %param.14) | copy-start | bytes 100
  2.7 18.3 %copy-start.8 = (bf16[8,1024]{1,0:T(8,128)(2,1)S(1)}, bf16[8,1024]{1,0:T(8,128)(2,1)}, u32[]{:S(2)}) copy-start(bf16[8,1024]{1,0:T(8,128)(2,1)} %cot_ref.3) | copy-start | bytes 49156
  4.5 31.3 %all-to-all-start = ((bf16[128,4,384]{2,1,0:T(4,128)(2,1)}), bf16[128,4,384]{2,1,0:T(4,128)(2,1)}, u32[]{:S(2)}, u32[]{:S(2)}) async-start(bf16[128,4,384]{2,1,0:T(4,128)(2,1)} %reshape.48), calls=%async_computation | async-start | bytes 786432 | tf_op jit(solution)/shard_map/all_to_all | solution.py:240
  21.0 2.8 %copy-start.1 = (bf16[3,1024,1024]{2,1,0:T(8,128)(2,1)S(1)}, bf16[3,1024,1024]{2,1,0:T(8,128)(2,1)}, u32[]{:S(2)}) copy-start(bf16[3,1024,1024]{2,1,0:T(8,128)(2,1)} %w2_ref.1) | copy-start | bytes 18874372
  23.8 13.1 %copy-start = (bf16[3,384,1024]{2,1,0:T(8,128)(2,1)S(1)}, bf16[3,384,1024]{2,1,0:T(8,128)(2,1)}, u32[]{:S(2)}) copy-start(bf16[3,384,1024]{2,1,0:T(8,128)(2,1)} %w1_ref.3) | copy-start | bytes 7077892
  26.3 0.8 copy-start.4
  27.1 0.7 copy-start.6
  36.9 1.0 copy-start.7
  39.7 0.7 copy-start.12
  40.4 2.3 %collective-permute-start = (f32[128,1024]{1,0:T(8,128)}, f32[128,1024]{1,0:T(8,128)}, u32[]{:S(2)}, u32[]{:S(2)}) collective-permute-start(f32[128,1024]{1,0:T(8,128)} %get-tuple-element.23.mine_ref), channel_id=1, source_target_pairs={{0,1},{1,0},{2,3},{3,2},{4,5},{5,4},{6,7},{7,6},{8,9},{9,8},{10,11... | collective-permute-start | bytes 1572872 | tf_op jit(solution)/shard_map/ppermute | solution.py:208
  42.7 1.0 copy-start.5
  47.2 25.1 %all-to-all-start.2 = ((bf16[4,208,256]{2,1,0:T(8,128)(2,1)}), bf16[4,208,256]{2,1,0:T(8,128)(2,1)S(1)}, u32[]{:S(2)}, u32[]{:S(2)}) async-start(bf16[4,208,256]{2,1,0:T(8,128)(2,1)} %get-tuple-element.33), calls=%async_computation.2 | async-start | bytes 851968 | tf_op jit(solution)/shard_map/all_to_all | solution.py:298
  50.7 15.5 %collective-permute-start.2 = (bf16[384,384]{1,0:T(8,128)(2,1)}, bf16[384,384]{1,0:T(8,128)(2,1)S(1)}, u32[]{:S(2)}, u32[]{:S(2)}) collective-permute-start(bf16[384,384]{1,0:T(8,128)(2,1)} %copy-done.12), channel_id=1, source_target_pairs={{0,64},{64,128},{128,192},{192,0},{1,65},{65,129},{129,193},{193,1... | collective-permute-start | bytes 884744 | tf_op jit(solution)/shard_map/ppermute | solution.py:208
  52.6 19.6 %collective-permute-start.3 = (bf16[384,384]{1,0:T(8,128)(2,1)}, bf16[384,384]{1,0:T(8,128)(2,1)S(1)}, u32[]{:S(2)}, u32[]{:S(2)}) collective-permute-start(bf16[384,384]{1,0:T(8,128)(2,1)} %copy-done.12), channel_id=1, source_target_pairs={{0,128},{64,192},{128,0},{192,64},{1,129},{65,193},{129,1},{193,65... | collective-permute-start | bytes 884744 | tf_op jit(solution)/shard_map/ppermute | solution.py:208
  55.3 17.0 %collective-permute-start.4 = (bf16[384,384]{1,0:T(8,128)(2,1)}, bf16[384,384]{1,0:T(8,128)(2,1)S(1)}, u32[]{:S(2)}, u32[]{:S(2)}) collective-permute-start(bf16[384,384]{1,0:T(8,128)(2,1)} %copy-done.12), channel_id=1, source_target_pairs={{0,192},{64,0},{128,64},{192,128},{1,193},{65,1},{129,65},{193,129... | collective-permute-start | bytes 884744 | tf_op jit(solution)/shard_map/ppermute | solution.py:208
  72.3 1.0 copy-start.13
  74.9 13.3 %collective-permute-start.5 = (bf16[64,2688]{1,0:T(8,128)(2,1)S(1)}, bf16[64,2688]{1,0:T(8,128)(2,1)S(1)}, u32[]{:S(2)}, u32[]{:S(2)}) collective-permute-start(bf16[64,2688]{1,0:T(8,128)(2,1)S(1)} %get-tuple-element.35), channel_id=1, source_target_pairs={{0,16},{16,32},{32,48},{48,0},{1,17},{17,33},{33,49},{49,1},{2,18}... | collective-permute-start | bytes 1032200 | tf_op jit(solution)/shard_map/ppermute | solution.py:208
  76.2 12.8 %collective-permute-start.6 = (bf16[64,2688]{1,0:T(8,128)(2,1)S(1)}, bf16[64,2688]{1,0:T(8,128)(2,1)S(1)}, u32[]{:S(2)}, u32[]{:S(2)}) collective-permute-start(bf16[64,2688]{1,0:T(8,128)(2,1)S(1)} %get-tuple-element.36), channel_id=1, source_target_pairs={{0,32},{16,48},{32,0},{48,16},{1,33},{17,49},{33,1},{49,17},{2,34}... | collective-permute-start | bytes 1032200 | tf_op jit(solution)/shard_map/ppermute | solution.py:208
  80.0 17.5 %collective-permute-start.7 = (bf16[64,2688]{1,0:T(8,128)(2,1)S(1)}, bf16[64,2688]{1,0:T(8,128)(2,1)}, u32[]{:S(2)}, u32[]{:S(2)}) collective-permute-start(bf16[64,2688]{1,0:T(8,128)(2,1)S(1)} %get-tuple-element.37), channel_id=1, source_target_pairs={{0,48},{16,0},{32,16},{48,32},{1,49},{17,1},{33,17},{49,33},{2,50}... | collective-permute-start | bytes 1032200 | tf_op jit(solution)/shard_map/ppermute | solution.py:208
  80.8 22.6 %all-to-all-start.1 = ((bf16[128,4,384]{2,1,0:T(4,128)(2,1)}), bf16[128,4,384]{2,1,0:T(4,128)(2,1)S(1)}, u32[]{:S(2)}, u32[]{:S(2)}) async-start(bf16[128,4,384]{2,1,0:T(4,128)(2,1)} %reshape.53), calls=%async_computation.1 | async-start | bytes 786432 | tf_op jit(solution)/shard_map/all_to_all | solution.py:299
  97.5 9.4 %copy-start.11 = (s32[1,512]{1,0:T(1,128)S(1)}, s32[1,512]{1,0:T(1,128)}, u32[]{:S(2)}) copy-start(s32[1,512]{1,0:T(1,128)} %serve_ref.3) | copy-start | bytes 6148
  99.4 9.6 %copy-start.3 = (f32[1024,384]{1,0:T(8,128)S(1)}, f32[1024,384]{1,0:T(8,128)}, u32[]{:S(2)}) copy-start(f32[1024,384]{1,0:T(8,128)} %table_ref.3) | copy-start | bytes 4718596
  99.4 9.6 %copy-start.9 = (f32[1024]{0:T(1024)S(1)}, f32[1024]{0:T(1024)}, u32[]{:S(2)}) copy-start(f32[1024]{0:T(1024)} %param.12) | copy-start | bytes 12292
  103.4 14.9 %all-to-all-start.3 = ((bf16[8,8,2688]{2,1,0:T(8,128)(2,1)}), bf16[8,8,2688]{2,1,0:T(8,128)(2,1)S(1)}, u32[]{:S(2)}, u32[]{:S(2)}) async-start(bf16[8,8,2688]{2,1,0:T(8,128)(2,1)} %fusion), calls=%async_computation.3 | async-start | bytes 688128 | tf_op jit(solution)/shard_map/all_to_all | solution.py:318
  107.8 1.2 %collective-permute-start.1 = (f32[8,128]{1,0:T(8,128)S(1)}, f32[8,128]{1,0:T(8,128)S(1)}, u32[]{:S(2)}, u32[]{:S(2)}) collective-permute-start(f32[8,128]{1,0:T(8,128)S(1)} %get-tuple-element.29.mine_ref), channel_id=1, source_target_pairs={{0,1},{1,0},{2,3},{3,2},{4,5},{5,4},{6,7},{7,6},{8,9},{9,8},{10,11... | collective-permute-start | bytes 12296 | tf_op jit(solution)/shard_map/ppermute | solution.py:208

commit v2 on v1

v2 whole, which is shorter than its diff:
```python
import functools
import jax
import jax.numpy as jnp
from jax import lax
from jax.experimental import pallas as pl
from jax.experimental.pallas import tpu as pltpu
from jax.sharding import Mesh
from jax.sharding import PartitionSpec as P

LEARNING_RATE = 0.1
BF16 = jnp.bfloat16
F32 = jnp.float32
LANES = 128
SEED_ROWS = 32
COT_ROWS = 16


def matmul(a, b, contract=(1, 0)):
    dims = (((contract[0],), (contract[1],)), ((), ()))
    return lax.dot_general(a, b, dims, preferred_element_type=F32)


def row_to_column(row):
    return jnp.transpose(jnp.broadcast_to(row, (LANES, LANES)))[:, 0:1]


def column_to_row(column):
    return jnp.transpose(jnp.broadcast_to(column, (LANES, LANES)))[0:1, :]


class Incoming:
    def __init__(self, source, buffer, semaphore):
        self.buffer, self.waiting = buffer, True
        self.shape = buffer.shape
        self.copy = pltpu.make_async_copy(source, buffer, semaphore)
        self.copy.start()

    def get(self):
        if self.waiting:
            self.copy.wait()
        self.waiting = False
        return self.buffer


class Outgoing:
    def __init__(self, target, buffer, semaphore):
        self.buffer = buffer
        self.copy = pltpu.make_async_copy(buffer, target, semaphore)

    def send(self):
        self.copy.start()


def call(kernel, outs, operands, flops, smem=0, scratch=(), hbm_in=(), hbm_out=(), hbm_raw=()):
    limit = LIMITS.get(getattr(kernel, "func", kernel), 12)
    moved = sum(o.size * o.dtype.itemsize for o in list(operands) + list(outs))
    specs = [
        pl.BlockSpec(memory_space=pltpu.SMEM if i < smem else pltpu.HBM if i in hbm_in else pltpu.VMEM)
        for i in range(len(operands))
    ]
    made = [
        pl.BlockSpec(memory_space=pltpu.HBM if i in hbm_out or i in hbm_raw else pltpu.VMEM)
        for i in range(len(outs))
    ]
    buffers = [pltpu.VMEM(operands[i].shape, operands[i].dtype) for i in hbm_in]
    buffers += [pltpu.VMEM(outs[i].shape, outs[i].dtype) for i in hbm_out]
    semaphores = [pltpu.SemaphoreType.DMA((len(buffers),))] if buffers else []

    def wrapped(*refs):
        refs = list(refs)
        if not buffers:
            kernel(*refs)
            return
        first = len(operands) + len(outs)
        held, sems = refs[first : first + len(buffers)], refs[first + len(buffers)]
        rest = refs[first + len(buffers) + 1 :]
        for j, i in enumerate(hbm_in):
            refs[i] = Incoming(refs[i], held[j], sems.at[j])
        leaving = []
        for j, i in enumerate(hbm_out, len(hbm_in)):
            place = len(operands) + i
            refs[place] = Outgoing(refs[place], held[j], sems.at[j])
            leaving.append(refs[place])
        kernel(*refs[:first], *rest)
        for out in leaving:
            out.copy.wait()

    return pl.pallas_call(
        wrapped,
        out_shape=tuple(outs),
        in_specs=specs,
        out_specs=tuple(made),
        scratch_shapes=buffers + semaphores + list(scratch),
        compiler_params=pltpu.CompilerParams(vmem_limit_bytes=limit * 1024 * 1024),
        cost_estimate=pl.CostEstimate(flops=flops, bytes_accessed=moved, transcendentals=0),
    )(*operands)


def shaped(shape, dtype):
    return jax.ShapeDtypeStruct(shape, dtype)


def serve_kernel(serve_ref, table_ref, out_ref):
    serve_ref = serve_ref.get()
    rows = table_ref.get()[...].astype(BF16)
    lanes = lax.broadcasted_iota(jnp.int32, (LANES, rows.shape[0]), 1)
    owners = LANES // out_ref.shape[1]
    for block in range(serve_ref.shape[1] // LANES):
        wanted = row_to_column(serve_ref[:, block * LANES : (block + 1) * LANES])
        onehot = jnp.where(wanted == lanes, 1.0, 0.0).astype(BF16)
        picked = matmul(onehot, rows).astype(BF16)
        out_ref[block * owners : (block + 1) * owners] = picked.reshape(owners, *out_ref.shape[1:])


def index_kernel(idx_ref, cot_ref, w2_ref, *refs):
    outs, spread = refs[:-1], refs[-1]
    ct_ref, c_ref, inv_ref, e_ref, back_ref = (o.buffer for o in outs)
    nodes = idx_ref.shape[0]
    slots = ct_ref.shape[1]
    seeds = cot_ref.shape[0]
    neighbours = idx_ref.shape[1] - 2
    lanes = lax.broadcasted_iota(jnp.int32, (nodes, 2 * slots), 1)
    idx = idx_ref[...]
    counts = jnp.zeros((nodes, 2 * slots), F32)
    for j in range(1, 1 + neighbours):
        counts = counts + jnp.where(idx[:, j : j + 1] == lanes, 1.0, 0.0)
    own = jnp.where(idx[:, 0:1] == lanes[:, :slots], 1.0, 0.0)
    parts = (own, counts[:, :slots], counts[:, slots:])
    spread[...] = jnp.zeros(spread.shape, F32)
    for k, part in enumerate(parts):
        span = slice(k * nodes, (k + 1) * nodes)
        ct_ref[span, :] = part.astype(BF16)
        c_ref[:, span] = jnp.transpose(part).astype(BF16)
        if k == 0:
            inverse = jnp.ones((nodes, 1), F32)
        else:
            inverse = 1.0 / jnp.maximum(jnp.sum(part, axis=1, keepdims=True), 1.0)
        inv_ref[span, :] = jnp.broadcast_to(inverse, (nodes, LANES))
        back = matmul(cot_ref[...], w2_ref[k], (1, 1))
        spread[k * seeds : (k + 1) * seeds, :] = back * inverse[:seeds]
    groups = lax.broadcasted_iota(jnp.int32, (nodes, LANES), 1)
    member = jnp.where(idx[:, neighbours + 1 : neighbours + 2] == groups, 1.0, 0.0)
    e_ref[...] = jnp.transpose(member)[:SEED_ROWS].astype(BF16)
    whole = spread[...]
    high = whole.astype(BF16)
    low = (whole - high.astype(F32)).astype(BF16)
    for out in outs[:-1]:
        out.send()
    back_ref[...] = matmul(member.astype(BF16), high) + matmul(member.astype(BF16), low)
    outs[-1].send()


def first_kernel(fetched_ref, ct_ref, w1_ref, layer_ref, partial_ref):
    layers = w1_ref.shape[0]
    layer_out, partial_out = layer_ref, partial_ref
    layer_ref, partial_ref = layer_ref.buffer, partial_ref.buffer
    nodes = partial_ref.shape[0]
    fetched = fetched_ref[...].reshape(ct_ref.shape[1], layer_ref.shape[1])
    total = None
    ct_ref = ct_ref.get()
    ones = jnp.ones((ct_ref.shape[1], LANES), BF16)
    for k in range(layers):
        span = slice(k * nodes, (k + 1) * nodes)
        summed = matmul(ct_ref[span, :], fetched)
        inverse = 1.0 / jnp.maximum(matmul(ct_ref[span, :], ones)[:, 0:1], 1.0)
        layer_ref[span, :] = (summed * inverse).astype(BF16)
    layer_out.send()
    for k in range(layers):
        term = matmul(layer_ref[k * nodes : (k + 1) * nodes, :], w1_ref[k])
        total = term if total is None else total + term
    partial_ref[...] = total
    partial_out.send()


def hidden_kernel(place_ref, mine_ref, other_ref, back_ref, e_ref, inv_ref, cot_ref, c_ref, w1_ref, slot_ref, *refs):
    packs, stage, sems = refs[:-2], refs[-2], refs[-1]
    nodes = mine_ref.shape[0]
    width = stage.shape[2]
    seeds = cot_ref.shape[0]
    layers = inv_ref.shape[0] // nodes
    values = mine_ref.get()[...] + other_ref.get()[...]
    back_ref, e_ref, inv_ref = back_ref.get(), e_ref.get(), inv_ref.get()
    sigma = jax.nn.sigmoid(values)
    hidden = (values * sigma).astype(BF16)
    slope = sigma * (1.0 + values * (1.0 - sigma))
    back = (back_ref[...] * slope).astype(BF16)
    scale = jnp.concatenate(
        [inv_ref[k * nodes : k * nodes + seeds, 0:1] for k in range(layers)]
        + [jnp.zeros((SEED_ROWS - layers * seeds, 1), F32)],
        0,
    )
    second = matmul(e_ref[...], hidden) * scale
    half = second.shape[1] // 2
    second = jnp.where(place_ref[0] == 0, second[:, :half], second[:, half:]).astype(BF16)
    cot = cot_ref[...].astype(F32)
    cot = jnp.concatenate([cot, jnp.zeros((COT_ROWS - seeds, cot.shape[1]), F32)], 0).astype(BF16)
    for j in range(len(packs)):
        span = slice(j * width, (j + 1) * width)
        stage[j, :nodes, :] = back[:, span]
        for part in range(half // width):
            first = nodes + part * SEED_ROWS
            stage[j, first : first + SEED_ROWS, :] = second[:, part * width : (part + 1) * width]
        first = nodes + half // width * SEED_ROWS
        stage[j, first : first + COT_ROWS, :] = cot[:, span]
    copies = [
        pltpu.make_async_copy(stage.at[lax.rem(place_ref[1] + d, len(packs))], pack, sems.at[d])
        for d, pack in enumerate(packs)
    ]
    for copy in copies:
        copy.start()
    total = None
    for k in range(layers):
        span = slice(k * nodes, (k + 1) * nodes)
        back_in = matmul(back, w1_ref[k], (1, 1)) * inv_ref[span, 0:1]
        term = matmul(c_ref.get()[:, span], back_in.astype(BF16))
        total = term if total is None else total + term
    slot_ref[...] = total.astype(BF16).reshape(slot_ref.shape)
    for copy in copies:
        copy.wait()


def weight_kernel(place_ref, *refs):
    count = refs[0].shape[0]
    layer_refs = [refs[0].get().at[lax.rem(place_ref[1] + count - d, count)] for d in range(count)]
    pack_refs = (refs[1].get(), *refs[2 : 1 + count])
    own_ref, outs = refs[1 + count], refs[2 + count : -1]
    total = refs[-1]
    width = pack_refs[0].shape[1]
    columns = layer_refs[0].shape[1]
    nodes = LANES
    relations = layer_refs[0].shape[0] // nodes
    rows = own_ref.shape[0]
    left = jnp.concatenate([p[:nodes, :] for p in pack_refs], 0)
    for k in range(relations):
        right = jnp.concatenate([r[k * nodes : (k + 1) * nodes, :] for r in layer_refs], 0)
        total[k] = matmul(left, right, (0, 0))
    pieces = (pack_refs[0].shape[0] - nodes - COT_ROWS) // SEED_ROWS
    half = pieces * width
    seeds = SEED_ROWS // (relations + 1)
    first = nodes + pieces * SEED_ROWS
    cots = jnp.concatenate([p[first : first + COT_ROWS, :].astype(F32)[:seeds] for p in pack_refs], 0)
    seconds = [
        jnp.concatenate(
            [p[nodes + part * SEED_ROWS : nodes + (part + 1) * SEED_ROWS, :].astype(F32) for part in range(pieces)],
            1,
        )
        for p in pack_refs
    ]
    second = jnp.concatenate(
        [jnp.concatenate([s[k * seeds : (k + 1) * seeds] for s in seconds], 0) for k in range(relations)], 1
    ).astype(BF16)
    group = count * seeds
    tail = relations * rows
    for d, out in enumerate(outs):
        target = lax.rem(place_ref[0] + d, len(outs))
        start = pl.multiple_of(target * rows, rows)
        for k in range(relations):
            block = total[k, pl.ds(start, rows), :]
            if d == 0:
                own_ref[:, k * columns : (k + 1) * columns] = block
            else:
                out[k * rows : (k + 1) * rows, :] = block.astype(BF16)
        for piece in range(relations * half // columns):
            out[tail + piece * group : tail + (piece + 1) * group, :] = second[
                :, piece * columns : (piece + 1) * columns
            ]
        chosen = cots[:, :rows]
        for j in range(1, len(outs)):
            chosen = jnp.where(target == j, cots[:, j * rows : (j + 1) * rows], chosen)
        chosen = jnp.concatenate([chosen, jnp.zeros((group, columns - rows), F32)], 1)
        out[out.shape[0] - group :, :] = chosen.astype(BF16)


def group_kernel(relations, own_ref, *refs):
    packs, out_ref = refs[:-1], refs[-1]
    rows = own_ref.shape[0]
    columns = packs[0].shape[1]
    tail = relations * rows
    wide = out_ref.shape[1] - relations * columns
    pieces = wide // columns
    group = (packs[0].shape[0] - tail) // (pieces + 1)
    for k in range(relations):
        span = slice(k * columns, (k + 1) * columns)
        block = own_ref[:, span]
        for pack in packs[1:]:
            block = block + pack[k * rows : (k + 1) * rows, :].astype(F32)
        out_ref[:, span] = block.astype(BF16)
    cots = jnp.concatenate([p[tail + pieces * group :, :] for p in packs], 0)
    for piece in range(pieces):
        first = tail + piece * group
        second = jnp.concatenate([p[first : first + group, :] for p in packs], 0)
        start = (relations + piece) * columns
        out_ref[:, start : start + columns] = matmul(cots, second, (0, 0))[:rows].astype(BF16)


def sum_kernel(parts_ref, one_ref, two_ref):
    total = jnp.sum(parts_ref[...].astype(F32), axis=0)
    start = 0
    for ref in (one_ref, two_ref):
        wide = ref.shape[2]
        for k in range(ref.shape[0]):
            ref[k] = total[:, start : start + wide]
            start += wide


def row_kernel(serve_ref, arrived_ref, grad_ref, square_ref):
    rows = lax.broadcasted_iota(jnp.int32, (LANES, serve_ref.shape[1]), 0)
    arrived = arrived_ref[...].reshape(serve_ref.shape[1], grad_ref.shape[1])
    for block in range(grad_ref.shape[0] // LANES):
        span = slice(block * LANES, (block + 1) * LANES)
        onehot = jnp.where(serve_ref[...] == rows + block * LANES, 1.0, 0.0).astype(BF16)
        grad = matmul(onehot, arrived)
        grad_ref[span, :] = grad
        square_ref[block : block + 1, :] = column_to_row(jnp.sum(grad * grad, axis=1, keepdims=True))


def update_kernel(columns, table_ref, grad_ref, accum_ref, mine_ref, other_ref, table_out, accum_out):
    accum = accum_ref[...] + (mine_ref[...] + other_ref[...]) / columns
    accum_out[...] = accum
    inverse = lax.rsqrt(accum)
    for block in range(accum.shape[0]):
        span = slice(block * LANES, (block + 1) * LANES)
        scale = row_to_column(inverse[block : block + 1, :])
        table_out[span, :] = table_ref[span, :] - LEARNING_RATE * grad_ref[span, :] * scale


def shift(array, axis, by):
    size = lax.axis_size(axis)
    return lax.ppermute(array, axis, [(i, (i + by) % size) for i in range(size)])


LIMITS = {serve_kernel: 60, index_kernel: 60, first_kernel: 50, hidden_kernel: 50}


def body(
    table,
    accum,
    serve_rows,
    seed_slot,
    hop1_slot,
    hop2_slot,
    hop1_rel,
    hop2_rel,
    cotangent,
    w_first,
    w_second,
):
    everyone = ("dp", "y", "z")
    owners = lax.axis_size(everyone)
    table_rows, columns = table.shape
    slots = serve_rows.shape[1]
    seeds, fanout = hop1_slot.shape
    fanout_two = hop2_slot.shape[2]
    nodes = seeds + seeds * fanout
    layers, hidden_units = w_second.shape[:2]
    half = hidden_units // 2
    n_x, n_y, n_z = (lax.axis_size(a) for a in everyone)
    x, y = lax.axis_index("dp"), lax.axis_index("y")
    width = hidden_units // n_x

    blocks_shape = (owners, slots // owners, columns)
    outgoing = call(
        serve_kernel, [shaped(blocks_shape, BF16)], (serve_rows, table), 2 * slots * table_rows * columns, hbm_in=(0, 1)
    )[0]
    fetched = lax.all_to_all(outgoing, everyone, split_axis=0, concat_axis=0, tiled=True)

    key_one = hop1_slot + slots * hop1_rel
    key_two = (hop2_slot + slots * hop2_rel).reshape(seeds * fanout, fanout_two)
    seed_ids = jnp.arange(seeds, dtype=jnp.int32)[:, None]
    group = (seeds * (1 + hop1_rel) + seed_ids).reshape(-1, 1)
    spare = jnp.full((seeds * fanout, fanout - fanout_two), -1, jnp.int32)
    idx = jnp.concatenate(
        [
            jnp.concatenate([seed_slot[:, None], key_one, seed_ids], 1),
            jnp.concatenate([hop1_slot.reshape(-1, 1), key_two, spare, group], 1),
        ],
        0,
    )
    ct, c, inverse, member, back_hidden = call(
        index_kernel,
        [
            shaped((layers * nodes, slots), BF16),
            shaped((slots, layers * nodes), BF16),
            shaped((layers * nodes, LANES), F32),
            shaped((SEED_ROWS, nodes), BF16),
            shaped((nodes, hidden_units), F32),
        ],
        (idx, cotangent, w_second),
        2 * layers * seeds * hidden_units * hidden_units,
        scratch=[pltpu.VMEM((LANES, hidden_units), F32)],
        hbm_out=range(5),
    )

    layer_in, partial_pre = call(
        first_kernel,
        [shaped((layers * nodes, columns), BF16), shaped((nodes, hidden_units), F32)],
        (fetched, ct, w_first),
        2 * layers * nodes * columns * (slots + hidden_units),
        hbm_in=(1,),
        hbm_out=(0, 1),
    )
    other_pre = shift(partial_pre, "col", 1)
    layer_parts = lax.all_gather(layer_in, "dp")

    pack_rows = nodes + half // width * SEED_ROWS + COT_ROWS
    pack_shape = (pack_rows, width)
    slot_grad, *packs = call(
        hidden_kernel,
        [shaped(blocks_shape, BF16)] + [shaped(pack_shape, BF16)] * n_x,
        (
            jnp.stack([lax.axis_index("col"), x]),
            partial_pre,
            other_pre,
            back_hidden,
            member,
            inverse,
            cotangent,
            c,
            w_first,
        ),
        2 * layers * nodes * columns * (slots + hidden_units),
        smem=1,
        scratch=[pltpu.VMEM((n_x, *pack_shape), BF16), pltpu.SemaphoreType.DMA((n_x,))],
        hbm_in=(1, 2, 3, 4, 5, 7),
        hbm_raw=range(1, 1 + n_x),
    )
    packs = [packs[0]] + [shift(packs[d], "dp", d) for d in range(1, n_x)]
    arrived = lax.all_to_all(slot_grad, everyone, split_axis=0, concat_axis=0, tiled=True)

    block_rows = width // n_y
    group_rows = layers * block_rows + (layers * half // columns + 1) * n_x * seeds
    own, *blocks = call(
        weight_kernel,
        [shaped((block_rows, layers * columns), F32)] + [shaped((group_rows, columns), BF16)] * n_y,
        (jnp.stack([y, x]), layer_parts, *packs),
        2 * n_x * nodes * width * layers * columns,
        smem=1,
        scratch=[pltpu.VMEM((layers, width, columns), F32)],
        hbm_in=(1, 2),
    )
    blocks = [blocks[0]] + [shift(blocks[d], "y", d) for d in range(1, n_y)]
    grad_columns = layers * (columns + half)
    grads = call(
        functools.partial(group_kernel, layers),
        [shaped((block_rows, grad_columns), BF16)],
        (own, *blocks),
        2 * n_x * n_y * seeds * block_rows * layers * half,
    )[0]
    grads = grads.reshape(n_z, block_rows // n_z, grad_columns)
    grads = lax.all_to_all(grads, "z", split_axis=0, concat_axis=0, tiled=True)
    grad_one, grad_two = call(
        sum_kernel,
        [shaped((layers, block_rows // n_z, wide), F32) for wide in (columns, half)],
        (grads,),
        block_rows * grad_columns,
    )
    grad_one, grad_two = grad_one.transpose(0, 2, 1), grad_two.transpose(0, 2, 1)

    row_grad, squares = call(
        row_kernel,
        [shaped((table_rows, columns), F32), shaped((table_rows // LANES, LANES), F32)],
        (serve_rows, arrived),
        2 * slots * table_rows * columns,
    )
    other_squares = shift(squares, "col", 1)
    new_table, new_accum = call(
        functools.partial(update_kernel, 2 * columns),
        [shaped((table_rows, columns), F32), shaped((table_rows // LANES, LANES), F32)],
        (table, row_grad, accum.reshape(-1, LANES), squares, other_squares),
        3 * table_rows * columns,
    )
    return (new_table, new_accum.reshape(-1), grad_one, grad_two)


def solution(mesh):
    n_dp, n_table, n_col = (mesh.shape[a] for a in ("dp", "table", "col"))
    n_y = 4 if n_table % 4 == 0 and n_table > 4 else 2
    fine = Mesh(mesh.devices.reshape(n_dp, n_y, n_table // n_y, n_col), ("dp", "y", "z", "col"))
    rows = ("dp", "y", "z")
    placed = (
        P(rows, "col"),
        P(rows),
        P(rows, None),
        P(rows),
        P(rows, None),
        P(rows, None, None),
        P(rows, None),
        P(rows, None, None),
        P(rows, None),
        P(None, "col", None),
        P(),
    )
    return jax.shard_map(
        body,
        mesh=fine,
        in_specs=placed,
        out_specs=(P(rows, "col"), P(rows), P(None, "col", rows), P(None, "col", rows)),
        check_vma=False,
    )
```

time: 122 us -> 125 us (1.025); the launches traced: 120 us -> 124 us
  between operations: 0.84 us -> 14.3 us
  Pallas kernels: 12.8 us -> 22.9 us
  waiting for transfers between devices: 47.8 us -> 37.7 us
  local copies, waits for them, and re-layouts: 14.8 us -> 6.41 us
    pallas_call x7 -> x9, Pallas kernels: 12.8 us -> 22.9 us  [call(): pl.pallas_call(wrapped, out_shape=tuple(outs), in_specs=specs, out_specs=...]
    ppermute x8, waiting for transfers between devices: 28.1 us -> 20.3 us  [shift(): lax.ppermute(array, axis, [(i, (i + by) % size) for i in range(size)])]
    unnamed x38, local copies, waits for them, and re-layouts: 10.1 us -> 5.9 us
    all_to_all x3 -> x2, waiting for transfers between devices: 12 us -> 7.99 us  [the longest x1 7.99 us: body(): lax.all_to_all(outgoing, everyone, split_axis=0, concat_axis=0, tiled=True)]
    all_to_all x1, starting transfers between devices: 3.44 us -> 7.09 us  [body(): grads = lax.all_to_all(grads, 'z', split_axis=0, concat_axis=0, tiled=True)]
    all_to_all x3 -> x2, starting transfers between devices: 26.6 us -> 23.6 us  [the longest x1 15.4 us: body(): lax.all_to_all(outgoing, everyone, split_axis=0, concat_axis=0, tiled=True)]
    reshape x4 -> x0, local copies, waits for them, and re-layouts: 2.87 us -> none  [the longest x1 1.09 us: body(): fetched = lax.all_to_all(outgoing.reshape(owners, slots // owners, column...]
    reshape x1 -> x0, other arithmetic: 1.89 us -> none  [body(): grads = grads.astype(BF16).reshape(n_z, block_rows // n_z, grad_columns)]
  transfers between devices with their start and end apart: 12 -> 12, of which waited for: 9 -> 9; matrix products, arithmetic and copies ran while one was open for 3% -> 1% of each run, Pallas kernels for 4% -> 14%
where the time goes in v2:
time: 125 us; the launch traced here: 124 us
  starting transfers between devices  41.8 us (33%)
  waiting for transfers between devices  37.7 us (30%)
  Pallas kernels  22.9 us (18%)
  between operations  14.3 us (11%)
  local copies, waits for them, and re-layouts  6.41 us (5%)
    pallas_call x9, Pallas kernels, call(): pl.pallas_call(wrapped, out_shape=tuple(outs), in_specs=specs, out_specs=...  22.9 us
    ppermute x8, waiting for transfers between devices, shift(): lax.ppermute(array, axis, [(i, (i + by) % size) for i in range(size)])  20.3 us
    all_to_all x1, starting transfers between devices, body(): lax.all_to_all(outgoing, everyone, split_axis=0, concat_axis=0, tiled=True)  15.4 us
    ppermute x8, starting transfers between devices, shift(): lax.ppermute(array, axis, [(i, (i + by) % size) for i in range(size)])  11.1 us
    all_to_all x1, waiting for transfers between devices, body(): grads = lax.all_to_all(grads, 'z', split_axis=0, concat_axis=0, tiled=True)  9.38 us
    all_to_all x1, starting transfers between devices, body(): lax.all_to_all(slot_grad, everyone, split_axis=0, concat_axis=0, tiled=True)  8.24 us
    all_to_all x1, waiting for transfers between devices, body(): lax.all_to_all(outgoing, everyone, split_axis=0, concat_axis=0, tiled=True)  7.99 us
    all_to_all x1, starting transfers between devices, body(): grads = lax.all_to_all(grads, 'z', split_axis=0, concat_axis=0, tiled=True)  7.09 us
  transfers between devices with their start and end apart: 12, of which 9 were waited for; matrix products, arithmetic and copies ran while one was open for 1% of the time, Pallas kernels for 14%

profile of v2, /device:TPU:8, one launch (start us, length us, event | category | flops | bytes accessed | tf_op | source)
XLA Modules:
  0.0 123.9 jit_solution(16651900747382694366)
XLA Ops:
  7.2 3.1 %shard_map.138 = bf16[128,4,384]{2,1,0:T(4,128)(2,1)} custom-call(s32[1,512]{1,0:T(1,128)} %refs_0_.4, f32[1024,384]{1,0:T(8,128)} %refs_0_.5), custom_call_target="tpu_custom_call" | custom-call | flops 402653184 | bytes 1968128 | tf_op jit(solution)/shard_map/pallas_call | solution.py:88
  10.4 15.4 %all-to-all-start = ((bf16[128,4,384]{2,1,0:T(4,128)(2,1)}), bf16[128,4,384]{2,1,0:T(4,128)(2,1)S(1)}, u32[]{:S(2)}, u32[]{:S(2)}) async-start(bf16[128,4,384]{2,1,0:T(4,128)(2,1)} %shard_map.138), calls=%async_computation | async-start | bytes 786432 | tf_op jit(solution)/shard_map/all_to_all | solution.py:365
  25.7 0.0 all-gather.3.cloned.1.call-start
  25.8 0.1 reshape.26
  25.9 0.1 reshape.28
  26.0 0.1 reshape.27
  26.1 0.1 pad.8.clone
  26.1 0.1 pad_add_fusion.1
  26.2 0.1 copy.30
  26.3 0.1 copy.29
  26.4 0.7 pad_add_fusion.refs_0_
  27.1 6.5 %shard_map.139 = (bf16[384,512]{1,0:T(8,128)(2,1)}, bf16[512,384]{1,0:T(8,128)(2,1)}, f32[384,128]{1,0:T(8,128)}, bf16[32,128]{1,0:T(8,128)(2,1)}, f32[128,1024]{1,0:T(8,128)}) custom-call(s32[128,17]{1,0:T(8,128)} %pad_add_fusion.refs_0_, bf16[8,1024]{1,0:T(8,128)(2,1)} %refs_6_.1, bf16[3,1024,1024]{2,1,0:T(8,128)(2,1)} %refs_2_.2), custom_call_target="tpu_custom_call" | custom-call | flops 50331648 | bytes 7832064 | tf_op jit(solution)/shard_map/pallas_call | solution.py:88
  33.6 8.0 %all-to-all-done.refs_0_ = bf16[128,4,384]{2,1,0:T(4,128)(2,1)S(1)} async-done(((bf16[128,4,384]{2,1,0:T(4,128)(2,1)}), bf16[128,4,384]{2,1,0:T(4,128)(2,1)S(1)}, u32[]{:S(2)}, u32[]{:S(2)}) %all-to-all-start) | async-done | bytes 393248 | tf_op jit(solution)/shard_map/all_to_all | solution.py:365
  41.6 1.0 copy-done.7
  42.6 1.5 %shard_map.140 = (bf16[384,384]{1,0:T(8,128)(2,1)S(1)}, f32[128,1024]{1,0:T(8,128)S(1)}) custom-call(bf16[128,4,384]{2,1,0:T(4,128)(2,1)S(1)} %all-to-all-done.refs_0_, bf16[384,512]{1,0:T(8,128)(2,1)S(1)} %copy-done.7, bf16[3,384,1024]{2,1,0:T(8,128)(2,1)S(1)} %copy-done), custom_call_target="tpu_custom_call" | custom-call | flops 452984832 | bytes 3964928 | tf_op jit(solution)/shard_map/pallas_call | solution.py:88
  44.1 0.8 copy-done.4
  44.9 0.7 copy-done.8
  45.6 0.0 all-gather.3.cloned.1.call-update
  45.7 0.1 collective-permute-start
  45.8 0.1 pad_add_fusion.2.refs_0_
  45.9 2.0 %collective-permute-done.refs_2_ = f32[128,1024]{1,0:T(8,128)S(1)} collective-permute-done((f32[128,1024]{1,0:T(8,128)}, f32[128,1024]{1,0:T(8,128)S(1)}, u32[]{:S(2)}, u32[]{:S(2)}) %collective-permute-start) | collective-permute-done | bytes 524320 | tf_op jit(solution)/shard_map/ppermute | solution.py:329
  47.9 1.0 copy-done.5
  48.9 1.0 copy-done.6
  49.9 5.7 %shard_map.141 = (bf16[128,4,384]{2,1,0:T(4,128)(2,1)}, bf16[208,256]{1,0:T(8,128)(2,1)S(1)}, bf16[208,256]{1,0:T(8,128)(2,1)S(1)}, bf16[208,256]{1,0:T(8,128)(2,1)S(1)}, bf16[208,256]{1,0:T(8,128)(2,1)S(1)}) custom-call(s32[2]{0:T(128)S(1)} %pad_add_fusion.2.refs_0_, f32[128,1024]{1,0:T(8,128)S(1)} %copy-done.5, ...), custom_call_target="tpu_custom_call" | custom-call | flops 452984832 | bytes 5365768 | tf_op jit(solution)/shard_map/pallas_call | solution.py:88
  55.6 8.2 %all-to-all-start.1 = ((bf16[128,4,384]{2,1,0:T(4,128)(2,1)}), bf16[128,4,384]{2,1,0:T(4,128)(2,1)S(1)}, u32[]{:S(2)}, u32[]{:S(2)}) async-start(bf16[128,4,384]{2,1,0:T(4,128)(2,1)} %get-tuple-element.33), calls=%async_computation.1 | async-start | bytes 786432 | tf_op jit(solution)/shard_map/all_to_all | solution.py:428
  63.9 1.8 %collective-permute-start.2 = (bf16[208,256]{1,0:T(8,128)(2,1)S(1)}, bf16[208,256]{1,0:T(8,128)(2,1)S(1)}, u32[]{:S(2)}, u32[]{:S(2)}) collective-permute-start(bf16[208,256]{1,0:T(8,128)(2,1)S(1)} %get-tuple-element.40), channel_id=1, source_target_pairs={{0,64},{64,128},{128,192},{192,0},{1,65},{65,129},{129,193},{193,1... | collective-permute-start | bytes 319496 | tf_op jit(solution)/shard_map/ppermute | solution.py:329
  65.7 3.1 %collective-permute-start.3 = (bf16[208,256]{1,0:T(8,128)(2,1)S(1)}, bf16[208,256]{1,0:T(8,128)(2,1)S(1)}, u32[]{:S(2)}, u32[]{:S(2)}) collective-permute-start(bf16[208,256]{1,0:T(8,128)(2,1)S(1)} %get-tuple-element.41), channel_id=1, source_target_pairs={{0,128},{64,192},{128,0},{192,64},{1,129},{65,193},{129,1},{193,65... | collective-permute-start | bytes 319496 | tf_op jit(solution)/shard_map/ppermute | solution.py:329
  68.8 1.2 %collective-permute-start.4 = (bf16[208,256]{1,0:T(8,128)(2,1)S(1)}, bf16[208,256]{1,0:T(8,128)(2,1)S(1)}, u32[]{:S(2)}, u32[]{:S(2)}) collective-permute-start(bf16[208,256]{1,0:T(8,128)(2,1)S(1)} %get-tuple-element.42), channel_id=1, source_target_pairs={{0,192},{64,0},{128,64},{192,128},{1,193},{65,1},{129,65},{193,129... | collective-permute-start | bytes 319496 | tf_op jit(solution)/shard_map/ppermute | solution.py:329
  70.0 0.1 pad_add_fusion.3.refs_0_
  70.1 1.6 %collective-permute-done.2.refs_3_ = bf16[208,256]{1,0:T(8,128)(2,1)S(1)} collective-permute-done((bf16[208,256]{1,0:T(8,128)(2,1)S(1)}, bf16[208,256]{1,0:T(8,128)(2,1)S(1)}, u32[]{:S(2)}, u32[]{:S(2)}) %collective-permute-start.2) | collective-permute-done | bytes 106528 | tf_op jit(solution)/shard_map/ppermute | solution.py:329
  71.7 5.2 %collective-permute-done.3.refs_4_ = bf16[208,256]{1,0:T(8,128)(2,1)S(1)} collective-permute-done((bf16[208,256]{1,0:T(8,128)(2,1)S(1)}, bf16[208,256]{1,0:T(8,128)(2,1)S(1)}, u32[]{:S(2)}, u32[]{:S(2)}) %collective-permute-start.3) | collective-permute-done | bytes 106528 | tf_op jit(solution)/shard_map/ppermute | solution.py:329
  76.9 1.3 %copy-done.2 = bf16[1536,384]{1,0:T(8,128)(2,1)S(1)} copy-done((bf16[1536,384]{1,0:T(8,128)(2,1)S(1)}, bf16[1536,384]{1,0:T(8,128)(2,1)}, u32[]{:S(2)}) %copy-start.2) | copy-done | bytes 1179672
  78.2 1.7 %shard_map.144 = (f32[64,1152]{1,0:T(8,128)S(1)}, bf16[352,384]{1,0:T(8,128)(2,1)S(1)}, bf16[352,384]{1,0:T(8,128)(2,1)S(1)}, bf16[352,384]{1,0:T(8,128)(2,1)S(1)}, bf16[352,384]{1,0:T(8,128)(2,1)S(1)}) custom-call(s32[2]{0:T(128)S(1)} %pad_add_fusion.3.refs_0_, bf16[4,384,384]{2,1,0:T(8,128)(2,1)S(1)} %bitcast.12, ...), custom_call_target="tpu_custom_call" | custom-call | flops 301989888 | bytes 2981896 | tf_op jit(solution)/shard_map/pallas_call | solution.py:88
  79.9 0.0 copy-start.13
  79.9 1.6 %collective-permute-start.5 = (bf16[352,384]{1,0:T(8,128)(2,1)S(1)}, bf16[352,384]{1,0:T(8,128)(2,1)S(1)}, u32[]{:S(2)}, u32[]{:S(2)}) collective-permute-start(bf16[352,384]{1,0:T(8,128)(2,1)S(1)} %get-tuple-element.45), channel_id=1, source_target_pairs={{0,16},{16,32},{32,48},{48,0},{1,17},{17,33},{33,49},{49,1},{2,18}... | collective-permute-start | bytes 811016 | tf_op jit(solution)/shard_map/ppermute | solution.py:329
  81.5 1.1 collective-permute-start.6
  82.6 2.1 %collective-permute-start.7 = (bf16[352,384]{1,0:T(8,128)(2,1)S(1)}, bf16[352,384]{1,0:T(8,128)(2,1)S(1)}, u32[]{:S(2)}, u32[]{:S(2)}) collective-permute-start(bf16[352,384]{1,0:T(8,128)(2,1)S(1)} %get-tuple-element.47), channel_id=1, source_target_pairs={{0,48},{16,0},{32,16},{48,32},{1,49},{17,1},{33,17},{49,33},{2,50}... | collective-permute-start | bytes 811016 | tf_op jit(solution)/shard_map/ppermute | solution.py:329
  84.7 4.7 %collective-permute-done.5.refs_2_ = bf16[352,384]{1,0:T(8,128)(2,1)S(1)} collective-permute-done((bf16[352,384]{1,0:T(8,128)(2,1)S(1)}, bf16[352,384]{1,0:T(8,128)(2,1)S(1)}, u32[]{:S(2)}, u32[]{:S(2)}) %collective-permute-start.5) | collective-permute-done | bytes 270368 | tf_op jit(solution)/shard_map/ppermute | solution.py:329
  89.4 3.0 %collective-permute-done.6.refs_3_ = bf16[352,384]{1,0:T(8,128)(2,1)S(1)} collective-permute-done((bf16[352,384]{1,0:T(8,128)(2,1)S(1)}, bf16[352,384]{1,0:T(8,128)(2,1)S(1)}, u32[]{:S(2)}, u32[]{:S(2)}) %collective-permute-start.6) | collective-permute-done | bytes 270368 | tf_op jit(solution)/shard_map/ppermute | solution.py:329
  92.5 2.6 %collective-permute-done.7.refs_4_ = bf16[352,384]{1,0:T(8,128)(2,1)S(1)} collective-permute-done((bf16[352,384]{1,0:T(8,128)(2,1)S(1)}, bf16[352,384]{1,0:T(8,128)(2,1)S(1)}, u32[]{:S(2)}, u32[]{:S(2)}) %collective-permute-start.7) | collective-permute-done | bytes 270368 | tf_op jit(solution)/shard_map/ppermute | solution.py:329
  95.0 1.2 shard_map.145
  96.3 7.1 %all-to-all-start.2 = ((bf16[8,8,2688]{2,1,0:T(8,128)(2,1)}), bf16[8,8,2688]{2,1,0:T(8,128)(2,1)S(1)}, u32[]{:S(2)}, u32[]{:S(2)}) async-start(bf16[8,8,2688]{2,1,0:T(8,128)(2,1)} %bitcast.7), calls=%async_computation.2 | async-start | bytes 688128 | tf_op jit(solution)/shard_map/all_to_all | solution.py:450
  103.4 0.9 shard_map.142
  104.2 0.1 collective-permute-start.1
  104.3 1.2 collective-permute-done.1.refs_4_
  105.5 1.6 %shard_map.143 = (f32[1024,384]{1,0:T(8,128)}, f32[8,128]{1,0:T(8,128)}) custom-call(f32[1024,384]{1,0:T(8,128)S(1)} %copy-done.1, f32[1024,384]{1,0:T(8,128)S(1)} %get-tuple-element.34.refs_1_, f32[8,128]{1,0:T(8,128)S(1)} %bitcast.13, f32[8,128]{1,0:T(8,128)S(1)} %get-tuple-element.35.refs_3_, f32[8,128]{1,0:T(8,128)S(1)} %collective-permute-done.1.refs_4_), custom_call_target="tpu_custom_call" | custom-call | flops 1179648 | bytes 4734976 | tf_op jit(solution)/shard_map/pallas_call | solution.py:88
  107.1 9.4 %all-to-all-done.2.refs_0_ = bf16[8,8,2688]{2,1,0:T(8,128)(2,1)S(1)} async-done(((bf16[8,8,2688]{2,1,0:T(8,128)(2,1)}), bf16[8,8,2688]{2,1,0:T(8,128)(2,1)S(1)}, u32[]{:S(2)}, u32[]{:S(2)}) %all-to-all-start.2) | async-done | bytes 344096 | tf_op jit(solution)/shard_map/all_to_all | solution.py:450
  116.4 0.7 shard_map.146
  (38 shorter events, 0.1 us)
Async XLA Ops:
  7.2 18.6 %copy-start.16 = (s32[8,15]{1,0:T(8,128)S(1)}, s32[8,15]{1,0:T(8,128)}, u32[]{:S(2)}) copy-start(s32[8,15]{1,0:T(8,128)} %param.15) | copy-start | bytes 1444
  7.2 18.7 %copy-start.17 = (s32[8,15]{1,0:T(8,128)S(1)}, s32[8,15]{1,0:T(8,128)}, u32[]{:S(2)}) copy-start(s32[8,15]{1,0:T(8,128)} %param.17) | copy-start | bytes 1444
  7.2 18.8 %copy-start.14 = (s32[8,15,10]{1,0,2:T(8,128)S(1)}, s32[8,15,10]{1,0,2:T(8,128)}, u32[]{:S(2)}) copy-start(s32[8,15,10]{1,0,2:T(8,128)} %param.16) | copy-start | bytes 14404
  7.2 18.8 %copy-start.15 = (s32[8,15,10]{1,0,2:T(8,128)S(1)}, s32[8,15,10]{1,0,2:T(8,128)}, u32[]{:S(2)}) copy-start(s32[8,15,10]{1,0,2:T(8,128)} %param.18) | copy-start | bytes 14404
  7.2 19.1 %copy-start.18 = (s32[8]{0:T(128)S(1)}, s32[8]{0:T(128)}, u32[]{:S(2)}) copy-start(s32[8]{0:T(128)} %param.14) | copy-start | bytes 100
  10.4 31.2 %all-to-all-start = ((bf16[128,4,384]{2,1,0:T(4,128)(2,1)}), bf16[128,4,384]{2,1,0:T(4,128)(2,1)S(1)}, u32[]{:S(2)}, u32[]{:S(2)}) async-start(bf16[128,4,384]{2,1,0:T(4,128)(2,1)} %shard_map.138), calls=%async_computation | async-start | bytes 786432 | tf_op jit(solution)/shard_map/all_to_all | solution.py:365
  25.7 51.2 %all-gather.3.cloned.1.call-start = ((), (), s32[]{:S(2)}) async-start(), calls=%async_computation.3 | async-start | bytes 1474560 | tf_op jit(solution)/shard_map/all_gather | solution.py:403
  27.1 14.5 %copy-start = (bf16[3,384,1024]{2,1,0:T(8,128)(2,1)S(1)}, bf16[3,384,1024]{2,1,0:T(8,128)(2,1)}, u32[]{:S(2)}) copy-start(bf16[3,384,1024]{2,1,0:T(8,128)(2,1)} %refs_8_.1) | copy-start | bytes 7077892
  41.6 1.0 copy-start.7
  42.6 5.3 %copy-start.3 = (f32[128,1024]{1,0:T(8,128)S(1)}, f32[128,1024]{1,0:T(8,128)}, u32[]{:S(2)}) copy-start(f32[128,1024]{1,0:T(8,128)} %get-tuple-element.29.refs_3_) | copy-start | bytes 1572868
  42.6 5.3 %copy-start.9 = (f32[384,128]{1,0:T(8,128)S(1)}, f32[384,128]{1,0:T(8,128)}, u32[]{:S(2)}) copy-start(f32[384,128]{1,0:T(8,128)} %get-tuple-element.31.refs_5_) | copy-start | bytes 589828
  42.6 5.3 %copy-start.10 = (bf16[8,1024]{1,0:T(8,128)(2,1)S(1)}, bf16[8,1024]{1,0:T(8,128)(2,1)}, u32[]{:S(2)}) copy-start(bf16[8,1024]{1,0:T(8,128)(2,1)} %refs_6_.1) | copy-start | bytes 49156
  42.6 5.3 %copy-start.11 = (bf16[32,128]{1,0:T(8,128)(2,1)S(1)}, bf16[32,128]{1,0:T(8,128)(2,1)}, u32[]{:S(2)}) copy-start(bf16[32,128]{1,0:T(8,128)(2,1)} %get-tuple-element.30.refs_4_) | copy-start | bytes 24580
  44.1 0.8 copy-start.4
  44.9 0.7 copy-start.8
  45.7 2.2 %collective-permute-start = (f32[128,1024]{1,0:T(8,128)}, f32[128,1024]{1,0:T(8,128)S(1)}, u32[]{:S(2)}, u32[]{:S(2)}) collective-permute-start(f32[128,1024]{1,0:T(8,128)} %copy-done.4), channel_id=1, source_target_pairs={{0,1},{1,0},{2,3},{3,2},{4,5},{5,4},{6,7},{7,6},{8,9},{9,8},{10,11... | collective-permute-start | bytes 1572872 | tf_op jit(solution)/shard_map/ppermute | solution.py:329
  47.9 1.0 copy-start.5
  48.9 1.0 copy-start.6
  55.6 40.6 %all-to-all-start.1 = ((bf16[128,4,384]{2,1,0:T(4,128)(2,1)}), bf16[128,4,384]{2,1,0:T(4,128)(2,1)S(1)}, u32[]{:S(2)}, u32[]{:S(2)}) async-start(bf16[128,4,384]{2,1,0:T(4,128)(2,1)} %get-tuple-element.33), calls=%async_computation.1 | async-start | bytes 786432 | tf_op jit(solution)/shard_map/all_to_all | solution.py:428
  63.9 7.8 %collective-permute-start.2 = (bf16[208,256]{1,0:T(8,128)(2,1)S(1)}, bf16[208,256]{1,0:T(8,128)(2,1)S(1)}, u32[]{:S(2)}, u32[]{:S(2)}) collective-permute-start(bf16[208,256]{1,0:T(8,128)(2,1)S(1)} %get-tuple-element.40), channel_id=1, source_target_pairs={{0,64},{64,128},{128,192},{192,0},{1,65},{65,129},{129,193},{193,1... | collective-permute-start | bytes 319496 | tf_op jit(solution)/shard_map/ppermute | solution.py:329
  65.7 11.3 %collective-permute-start.3 = (bf16[208,256]{1,0:T(8,128)(2,1)S(1)}, bf16[208,256]{1,0:T(8,128)(2,1)S(1)}, u32[]{:S(2)}, u32[]{:S(2)}) collective-permute-start(bf16[208,256]{1,0:T(8,128)(2,1)S(1)} %get-tuple-element.41), channel_id=1, source_target_pairs={{0,128},{64,192},{128,0},{192,64},{1,129},{65,193},{129,1},{193,65... | collective-permute-start | bytes 319496 | tf_op jit(solution)/shard_map/ppermute | solution.py:329
  68.8 8.1 %collective-permute-start.4 = (bf16[208,256]{1,0:T(8,128)(2,1)S(1)}, bf16[208,256]{1,0:T(8,128)(2,1)S(1)}, u32[]{:S(2)}, u32[]{:S(2)}) collective-permute-start(bf16[208,256]{1,0:T(8,128)(2,1)S(1)} %get-tuple-element.42), channel_id=1, source_target_pairs={{0,192},{64,0},{128,64},{192,128},{1,193},{65,1},{129,65},{193,129... | collective-permute-start | bytes 319496 | tf_op jit(solution)/shard_map/ppermute | solution.py:329
  76.9 1.3 %copy-start.2 = (bf16[1536,384]{1,0:T(8,128)(2,1)S(1)}, bf16[1536,384]{1,0:T(8,128)(2,1)}, u32[]{:S(2)}) copy-start(bf16[1536,384]{1,0:T(8,128)(2,1)} %all-gather.3.cloned.1.call-done) | copy-start | bytes 3538948
  79.9 23.4 %copy-start.13 = (s32[1,512]{1,0:T(1,128)S(1)}, s32[1,512]{1,0:T(1,128)}, u32[]{:S(2)}) copy-start(s32[1,512]{1,0:T(1,128)} %refs_0_.4) | copy-start | bytes 6148
  79.9 9.5 %collective-permute-start.5 = (bf16[352,384]{1,0:T(8,128)(2,1)S(1)}, bf16[352,384]{1,0:T(8,128)(2,1)S(1)}, u32[]{:S(2)}, u32[]{:S(2)}) collective-permute-start(bf16[352,384]{1,0:T(8,128)(2,1)S(1)} %get-tuple-element.45), channel_id=1, source_target_pairs={{0,16},{16,32},{32,48},{48,0},{1,17},{17,33},{33,49},{49,1},{2,18}... | collective-permute-start | bytes 811016 | tf_op jit(solution)/shard_map/ppermute | solution.py:329
  81.5 10.9 %collective-permute-start.6 = (bf16[352,384]{1,0:T(8,128)(2,1)S(1)}, bf16[352,384]{1,0:T(8,128)(2,1)S(1)}, u32[]{:S(2)}, u32[]{:S(2)}) collective-permute-start(bf16[352,384]{1,0:T(8,128)(2,1)S(1)} %get-tuple-element.46), channel_id=1, source_target_pairs={{0,32},{16,48},{32,0},{48,16},{1,33},{17,49},{33,1},{49,17},{2,34}... | collective-permute-start | bytes 811016 | tf_op jit(solution)/shard_map/ppermute | solution.py:329
  82.6 12.4 %collective-permute-start.7 = (bf16[352,384]{1,0:T(8,128)(2,1)S(1)}, bf16[352,384]{1,0:T(8,128)(2,1)S(1)}, u32[]{:S(2)}, u32[]{:S(2)}) collective-permute-start(bf16[352,384]{1,0:T(8,128)(2,1)S(1)} %get-tuple-element.47), channel_id=1, source_target_pairs={{0,48},{16,0},{32,16},{48,32},{1,49},{17,1},{33,17},{49,33},{2,50}... | collective-permute-start | bytes 811016 | tf_op jit(solution)/shard_map/ppermute | solution.py:329
  95.0 10.4 %copy-start.1 = (f32[1024,384]{1,0:T(8,128)S(1)}, f32[1024,384]{1,0:T(8,128)}, u32[]{:S(2)}) copy-start(f32[1024,384]{1,0:T(8,128)} %refs_0_.5) | copy-start | bytes 4718596
  95.0 10.4 %copy-start.12 = (f32[1024]{0:T(1024)S(1)}, f32[1024]{0:T(1024)}, u32[]{:S(2)}) copy-start(f32[1024]{0:T(1024)} %param.12) | copy-start | bytes 12292
  96.3 20.2 %all-to-all-start.2 = ((bf16[8,8,2688]{2,1,0:T(8,128)(2,1)}), bf16[8,8,2688]{2,1,0:T(8,128)(2,1)S(1)}, u32[]{:S(2)}, u32[]{:S(2)}) async-start(bf16[8,8,2688]{2,1,0:T(8,128)(2,1)} %bitcast.7), calls=%async_computation.2 | async-start | bytes 688128 | tf_op jit(solution)/shard_map/all_to_all | solution.py:450
  104.2 1.2 collective-permute-start.1
Sparse Core Ops, SparseCore 0:
  45.8 22.3 all-gather.2

commit v3 on v2

--- a/solution.py
+++ b/solution.py
@@ -52,7 +52,8 @@
 
 
 def call(kernel, outs, operands, flops, smem=0, scratch=(), hbm_in=(), hbm_out=(), hbm_raw=()):
-    limit = LIMITS.get(getattr(kernel, "func", kernel), 12)
+    name = getattr(kernel, "func", kernel)
+    limit, flops = LIMITS.get(name, 12), FLOPS.get(name, 10**12)
     moved = sum(o.size * o.dtype.itemsize for o in list(operands) + list(outs))
     specs = [
         pl.BlockSpec(memory_space=pltpu.SMEM if i < smem else pltpu.HBM if i in hbm_in else pltpu.VMEM)
@@ -219,11 +220,9 @@
         copy.wait()
 
 
-def weight_kernel(place_ref, *refs):
-    count = refs[0].shape[0]
-    layer_refs = [refs[0].get().at[lax.rem(place_ref[1] + count - d, count)] for d in range(count)]
-    pack_refs = (refs[1].get(), *refs[2 : 1 + count])
-    own_ref, outs = refs[1 + count], refs[2 + count : -1]
+def weight_kernel(count, place_ref, *refs):
+    layer_refs, pack_refs = refs[:count], refs[count : 2 * count]
+    own_ref, outs = refs[2 * count], refs[2 * count + 1 : -1]
     total = refs[-1]
     width = pack_refs[0].shape[1]
     columns = layer_refs[0].shape[1]
@@ -329,7 +328,8 @@
     return lax.ppermute(array, axis, [(i, (i + by) % size) for i in range(size)])
 
 
-LIMITS = {serve_kernel: 60, index_kernel: 60, first_kernel: 50, hidden_kernel: 50}
+LIMITS = {serve_kernel: 60, index_kernel: 60, first_kernel: 60, hidden_kernel: 50}
+FLOPS = {}
 
 
 def body(
@@ -400,7 +400,7 @@
         hbm_out=(0, 1),
     )
     other_pre = shift(partial_pre, "col", 1)
-    layer_parts = lax.all_gather(layer_in, "dp")
+    layer_parts = [layer_in] + [shift(layer_in, "dp", d) for d in range(1, n_x)]
 
     pack_rows = nodes + half // width * SEED_ROWS + COT_ROWS
     pack_shape = (pack_rows, width)
@@ -430,13 +430,12 @@
     block_rows = width // n_y
     group_rows = layers * block_rows + (layers * half // columns + 1) * n_x * seeds
     own, *blocks = call(
-        weight_kernel,
+        functools.partial(weight_kernel, n_x),
         [shaped((block_rows, layers * columns), F32)] + [shaped((group_rows, columns), BF16)] * n_y,
-        (jnp.stack([y, x]), layer_parts, *packs),
+        (y.reshape(1), *layer_parts, *packs),
         2 * n_x * nodes * width * layers * columns,
         smem=1,
         scratch=[pltpu.VMEM((layers, width, columns), F32)],
-        hbm_in=(1, 2),
     )
     blocks = [blocks[0]] + [shift(blocks[d], "y", d) for d in range(1, n_y)]
     grad_columns = layers * (columns + half)

time: 125 us -> 112 us (0.90)
  between operations: 14.3 us -> 0.91 us
  Pallas kernels: 22.9 us -> 31.5 us
  waiting for transfers between devices: 37.7 us -> 32.3 us
  local copies, waits for them, and re-layouts: 6.41 us -> 2.31 us
    ppermute x8 -> x11, waiting for transfers between devices: 20.3 us -> 7.59 us  [shift(): lax.ppermute(array, axis, [(i, (i + by) % size) for i in range(size)])]
    pallas_call x9, Pallas kernels: 22.9 us -> 31.5 us  [call(): pl.pallas_call(wrapped, out_shape=tuple(outs), in_specs=specs, out_specs=...]
    all_to_all x1, waiting for transfers between devices: 0.01 us -> 6.34 us  [body(): lax.all_to_all(slot_grad, everyone, split_axis=0, concat_axis=0, tiled=True)]
    unnamed x38 -> x34, local copies, waits for them, and re-layouts: 5.9 us -> 1.8 us
    all_to_all x1, starting transfers between devices: 7.09 us -> 5.68 us  [body(): grads = lax.all_to_all(grads, 'z', split_axis=0, concat_axis=0, tiled=True)]
    ppermute x8 -> x11, starting transfers between devices: 11.1 us -> 11.9 us  [shift(): lax.ppermute(array, axis, [(i, (i + by) % size) for i in range(size)])]
  transfers between devices with their start and end apart: 12 -> 14, of which waited for: 9 -> 5; matrix products, arithmetic and copies ran while one was open for 1% -> 1% of each run, Pallas kernels for 14% -> 20%
where the time goes in v3:
time: 112 us; the launch traced here: 110 us
  starting transfers between devices  42.5 us (38%)
  waiting for transfers between devices  32.3 us (29%)
  Pallas kernels  31.5 us (28%)
  local copies, waits for them, and re-layouts  2.31 us (2%)
    pallas_call x9, Pallas kernels, call(): pl.pallas_call(wrapped, out_shape=tuple(outs), in_specs=specs, out_specs=...  31.5 us
    all_to_all x1, starting transfers between devices, body(): lax.all_to_all(outgoing, everyone, split_axis=0, concat_axis=0, tiled=True)  15.8 us
    ppermute x11, starting transfers between devices, shift(): lax.ppermute(array, axis, [(i, (i + by) % size) for i in range(size)])  11.9 us
    all_to_all x1, waiting for transfers between devices, body(): grads = lax.all_to_all(grads, 'z', split_axis=0, concat_axis=0, tiled=True)  10.5 us
    all_to_all x1, starting transfers between devices, body(): lax.all_to_all(slot_grad, everyone, split_axis=0, concat_axis=0, tiled=True)  9.1 us
    all_to_all x1, waiting for transfers between devices, body(): lax.all_to_all(outgoing, everyone, split_axis=0, concat_axis=0, tiled=True)  7.89 us
    ppermute x11, waiting for transfers between devices, shift(): lax.ppermute(array, axis, [(i, (i + by) % size) for i in range(size)])  7.59 us
    all_to_all x1, waiting for transfers between devices, body(): lax.all_to_all(slot_grad, everyone, split_axis=0, concat_axis=0, tiled=True)  6.34 us
  transfers between devices with their start and end apart: 14, of which 5 were waited for; matrix products, arithmetic and copies ran while one was open for 1% of the time, Pallas kernels for 20%

profile of v3, /device:TPU:8, one launch (start us, length us, event | category | flops | bytes accessed | tf_op | source)
XLA Modules:
  0.0 110.4 jit_solution(8088237773684556168)
XLA Ops:
  0.7 3.1 %shard_map.138 = bf16[128,4,384]{2,1,0:T(4,128)(2,1)} custom-call(s32[1,512]{1,0:T(1,128)} %refs_0_.4, f32[1024,384]{1,0:T(8,128)} %refs_0_.5), custom_call_target="tpu_custom_call" | custom-call | flops 999999995904 | bytes 1968128 | tf_op jit(solution)/shard_map/pallas_call | solution.py:89
  3.8 15.8 %all-to-all-start = ((bf16[128,4,384]{2,1,0:T(4,128)(2,1)}), bf16[128,4,384]{2,1,0:T(4,128)(2,1)}, u32[]{:S(2)}, u32[]{:S(2)}) async-start(bf16[128,4,384]{2,1,0:T(4,128)(2,1)} %shard_map.138), calls=%async_computation | async-start | bytes 786432 | tf_op jit(solution)/shard_map/all_to_all | solution.py:365
  19.6 0.1 reshape.29
  19.7 0.1 reshape.31
  19.8 0.1 reshape.30
  19.9 0.1 pad.6.clone
  20.0 0.1 pad_add_fusion.1
  20.0 0.1 copy.30
  20.2 0.1 copy.29
  20.2 0.7 pad_add_fusion.refs_0_
  21.0 6.3 %shard_map.139 = (bf16[384,512]{1,0:T(8,128)(2,1)}, bf16[512,384]{1,0:T(8,128)(2,1)}, f32[384,128]{1,0:T(8,128)}, bf16[32,128]{1,0:T(8,128)(2,1)}, f32[128,1024]{1,0:T(8,128)}) custom-call(s32[128,17]{1,0:T(8,128)} %pad_add_fusion.refs_0_, bf16[8,1024]{1,0:T(8,128)(2,1)} %refs_6_.1, bf16[3,1024,1024]{2,1,0:T(8,128)(2,1)} %refs_2_.2), custom_call_target="tpu_custom_call" | custom-call | flops 999999995904 | bytes 7832064 | tf_op jit(solution)/shard_map/pallas_call | solution.py:89
  27.3 7.9 %all-to-all-done.refs_0_ = bf16[128,4,384]{2,1,0:T(4,128)(2,1)} async-done(((bf16[128,4,384]{2,1,0:T(4,128)(2,1)}), bf16[128,4,384]{2,1,0:T(4,128)(2,1)}, u32[]{:S(2)}, u32[]{:S(2)}) %all-to-all-start) | async-done | bytes 393248 | tf_op jit(solution)/shard_map/all_to_all | solution.py:365
  35.2 0.0 copy-start.11
  35.2 4.7 %shard_map.140 = (bf16[384,384]{1,0:T(8,128)(2,1)}, f32[128,1024]{1,0:T(8,128)}) custom-call(bf16[128,4,384]{2,1,0:T(4,128)(2,1)} %all-to-all-done.refs_0_, bf16[384,512]{1,0:T(8,128)(2,1)} %get-tuple-element.27.refs_1_, bf16[3,384,1024]{2,1,0:T(8,128)(2,1)} %refs_8_.1), custom_call_target="tpu_custom_call" | custom-call | flops 999999995904 | bytes 3964928 | tf_op jit(solution)/shard_map/pallas_call | solution.py:89
  39.9 0.1 collective-permute-start
  40.0 0.1 pad_add_fusion.2.refs_0_
  40.0 0.8 collective-permute-start.2
  40.8 1.6 %collective-permute-start.3 = (bf16[384,384]{1,0:T(8,128)(2,1)}, bf16[384,384]{1,0:T(8,128)(2,1)}, u32[]{:S(2)}, u32[]{:S(2)}) collective-permute-start(bf16[384,384]{1,0:T(8,128)(2,1)} %get-tuple-element.38.refs_1_), channel_id=1, source_target_pairs={{0,128},{64,192},{128,0},{192,64},{1,129},{65,193},{129,1},{193,65... | collective-permute-start | bytes 884744 | tf_op jit(solution)/shard_map/ppermute | solution.py:328
  42.5 1.8 %collective-permute-start.4 = (bf16[384,384]{1,0:T(8,128)(2,1)}, bf16[384,384]{1,0:T(8,128)(2,1)}, u32[]{:S(2)}, u32[]{:S(2)}) collective-permute-start(bf16[384,384]{1,0:T(8,128)(2,1)} %get-tuple-element.38.refs_1_), channel_id=1, source_target_pairs={{0,192},{64,0},{128,64},{192,128},{1,193},{65,1},{129,65},{193,129... | collective-permute-start | bytes 884744 | tf_op jit(solution)/shard_map/ppermute | solution.py:328
  44.2 0.0 collective-permute-done.refs_2_
  44.3 1.0 copy-done.1
  45.3 5.7 %shard_map.141 = (bf16[128,4,384]{2,1,0:T(4,128)(2,1)}, bf16[208,256]{1,0:T(8,128)(2,1)S(1)}, bf16[208,256]{1,0:T(8,128)(2,1)S(1)}, bf16[208,256]{1,0:T(8,128)(2,1)S(1)}, bf16[208,256]{1,0:T(8,128)(2,1)S(1)}) custom-call(s32[2]{0:T(128)S(1)} %pad_add_fusion.2.refs_0_, f32[128,1024]{1,0:T(8,128)S(1)} %copy-done.1, ...), custom_call_target="tpu_custom_call" | custom-call | flops 999999995904 | bytes 5365768 | tf_op jit(solution)/shard_map/pallas_call | solution.py:89
  51.1 0.3 collective-permute-start.5
  51.4 1.9 %collective-permute-start.6 = (bf16[208,256]{1,0:T(8,128)(2,1)S(1)}, bf16[208,256]{1,0:T(8,128)(2,1)S(1)}, u32[]{:S(2)}, u32[]{:S(2)}) collective-permute-start(bf16[208,256]{1,0:T(8,128)(2,1)S(1)} %get-tuple-element.41), channel_id=1, source_target_pairs={{0,128},{64,192},{128,0},{192,64},{1,129},{65,193},{129,1},{193,65... | collective-permute-start | bytes 319496 | tf_op jit(solution)/shard_map/ppermute | solution.py:328
  53.3 4.4 %collective-permute-done.2.refs_2_ = bf16[384,384]{1,0:T(8,128)(2,1)} collective-permute-done((bf16[384,384]{1,0:T(8,128)(2,1)}, bf16[384,384]{1,0:T(8,128)(2,1)}, u32[]{:S(2)}, u32[]{:S(2)}) %collective-permute-start.2) | collective-permute-done | bytes 294944 | tf_op jit(solution)/shard_map/ppermute | solution.py:328
  57.7 0.0 collective-permute-start.7
  57.7 9.1 %all-to-all-start.1 = ((bf16[128,4,384]{2,1,0:T(4,128)(2,1)}), bf16[128,4,384]{2,1,0:T(4,128)(2,1)}, u32[]{:S(2)}, u32[]{:S(2)}) async-start(bf16[128,4,384]{2,1,0:T(4,128)(2,1)} %get-tuple-element.33), calls=%async_computation.1 | async-start | bytes 786432 | tf_op jit(solution)/shard_map/all_to_all | solution.py:428
  66.8 0.0 collective-permute-done.3.refs_3_
  66.8 0.0 collective-permute-done.4.refs_4_
  66.9 0.0 collective-permute-done.6.refs_7_
  66.9 0.0 collective-permute-done.7.refs_8_
  66.9 0.0 copy-start.5
  66.9 2.8 %shard_map.144 = (f32[64,1152]{1,0:T(8,128)S(1)}, bf16[352,384]{1,0:T(8,128)(2,1)S(1)}, bf16[352,384]{1,0:T(8,128)(2,1)}, bf16[352,384]{1,0:T(8,128)(2,1)}, bf16[352,384]{1,0:T(8,128)(2,1)}) custom-call(s32[1]{0:T(128)} %bitcast.5.refs_0_, bf16[384,384]{1,0:T(8,128)(2,1)S(1)} %copy-done.2, bf16[384,384]{1,0:T(8,128)(2,1)} %collective-permute-done.2.refs_2_, ...), custom_call_target="tpu_custom_call" | custom-call | flops 999999995904 | bytes 2981892 | tf_op jit(solution)/shard_map/pallas_call | solution.py:89
  69.7 0.7 copy-done.8
  70.4 1.0 collective-permute-start.10
  71.4 1.0 collective-permute-start.8
  72.5 3.4 %collective-permute-start.9 = (bf16[352,384]{1,0:T(8,128)(2,1)}, bf16[352,384]{1,0:T(8,128)(2,1)}, u32[]{:S(2)}, u32[]{:S(2)}) collective-permute-start(bf16[352,384]{1,0:T(8,128)(2,1)} %get-tuple-element.46), channel_id=1, source_target_pairs={{0,32},{16,48},{32,0},{48,16},{1,33},{17,49},{33,1},{49,17},{2,34}... | collective-permute-start | bytes 811016 | tf_op jit(solution)/shard_map/ppermute | solution.py:328
  75.8 6.3 %all-to-all-done.1.refs_1_ = bf16[128,4,384]{2,1,0:T(4,128)(2,1)} async-done(((bf16[128,4,384]{2,1,0:T(4,128)(2,1)}), bf16[128,4,384]{2,1,0:T(4,128)(2,1)}, u32[]{:S(2)}, u32[]{:S(2)}) %all-to-all-start.1) | async-done | bytes 393248 | tf_op jit(solution)/shard_map/all_to_all | solution.py:428
  82.2 2.5 %shard_map.142 = (f32[1024,384]{1,0:T(8,128)S(1)}, f32[8,128]{1,0:T(8,128)}) custom-call(s32[1,512]{1,0:T(1,128)S(1)} %copy-done.5, bf16[128,4,384]{2,1,0:T(4,128)(2,1)} %all-to-all-done.1.refs_1_), custom_call_target="tpu_custom_call" | custom-call | flops 999999995904 | bytes 1972224 | tf_op jit(solution)/shard_map/pallas_call | solution.py:89
  84.7 0.0 collective-permute-start.1
  84.7 0.0 collective-permute-done.10.refs_4_
  84.7 0.0 collective-permute-done.8.refs_2_
  84.7 3.1 %collective-permute-done.9.refs_3_ = bf16[352,384]{1,0:T(8,128)(2,1)} collective-permute-done((bf16[352,384]{1,0:T(8,128)(2,1)}, bf16[352,384]{1,0:T(8,128)(2,1)}, u32[]{:S(2)}, u32[]{:S(2)}) %collective-permute-start.9) | collective-permute-done | bytes 270368 | tf_op jit(solution)/shard_map/ppermute | solution.py:328
  87.9 2.5 %shard_map.145 = bf16[64,2688]{1,0:T(8,128)(2,1)} custom-call(f32[64,1152]{1,0:T(8,128)S(1)} %get-tuple-element.43.refs_0_, bf16[352,384]{1,0:T(8,128)(2,1)S(1)} %copy-done.9, bf16[352,384]{1,0:T(8,128)(2,1)} %collective-permute-done.8.refs_2_, bf16[352,384]{1,0:T(8,128)(2,1)} %collective-permute-done.9.refs_3_, bf16[352,384]{1,0:T(8,128)(2,1)} %collective-permute-done.10.refs_4_), custom_call_target="tpu_custom_call" | custom-call | flops 999999995904 | bytes 1720320 | tf_op jit(solution)/shard_map/pallas_call | solution.py:89
  90.3 5.7 %all-to-all-start.2 = ((bf16[8,8,2688]{2,1,0:T(8,128)(2,1)}), bf16[8,8,2688]{2,1,0:T(8,128)(2,1)}, u32[]{:S(2)}, u32[]{:S(2)}) async-start(bf16[8,8,2688]{2,1,0:T(8,128)(2,1)} %bitcast.6), calls=%async_computation.2 | async-start | bytes 688128 | tf_op jit(solution)/shard_map/all_to_all | solution.py:449
  96.0 2.3 %shard_map.143 = (f32[1024,384]{1,0:T(8,128)}, f32[8,128]{1,0:T(8,128)}) custom-call(f32[1024,384]{1,0:T(8,128)S(1)} %copy-done, f32[1024,384]{1,0:T(8,128)S(1)} %get-tuple-element.34.refs_1_, f32[8,128]{1,0:T(8,128)S(1)} %bitcast.11, f32[8,128]{1,0:T(8,128)} %get-tuple-element.35.refs_3_, f32[8,128]{1,0:T(8,128)} %collective-permute-done.1.refs_4_), custom_call_target="tpu_custom_call" | custom-call | flops 999999995904 | bytes 4734976 | tf_op jit(solution)/shard_map/pallas_call | solution.py:89
  98.3 10.5 %all-to-all-done.2.refs_0_ = bf16[8,8,2688]{2,1,0:T(8,128)(2,1)} async-done(((bf16[8,8,2688]{2,1,0:T(8,128)(2,1)}), bf16[8,8,2688]{2,1,0:T(8,128)(2,1)}, u32[]{:S(2)}, u32[]{:S(2)}) %all-to-all-start.2) | async-done | bytes 344096 | tf_op jit(solution)/shard_map/all_to_all | solution.py:449
  108.8 1.6 %shard_map.146 = (f32[3,8,384]{2,1,0:T(8,128)}, f32[3,8,512]{2,1,0:T(8,128)}) custom-call(bf16[8,8,2688]{2,1,0:T(8,128)(2,1)} %all-to-all-done.2.refs_0_), custom_call_target="tpu_custom_call" | custom-call | flops 999999995904 | bytes 430080 | tf_op jit(solution)/shard_map/pallas_call | solution.py:89
  (36 shorter events, 0.1 us)
Async XLA Ops:
  0.6 19.0 %copy-start.14 = (s32[8,15]{1,0:T(8,128)S(1)}, s32[8,15]{1,0:T(8,128)}, u32[]{:S(2)}) copy-start(s32[8,15]{1,0:T(8,128)} %param.15) | copy-start | bytes 1444
  0.6 19.1 %copy-start.15 = (s32[8,15]{1,0:T(8,128)S(1)}, s32[8,15]{1,0:T(8,128)}, u32[]{:S(2)}) copy-start(s32[8,15]{1,0:T(8,128)} %param.17) | copy-start | bytes 1444
  0.7 19.1 %copy-start.12 = (s32[8,15,10]{1,0,2:T(8,128)S(1)}, s32[8,15,10]{1,0,2:T(8,128)}, u32[]{:S(2)}) copy-start(s32[8,15,10]{1,0,2:T(8,128)} %param.16) | copy-start | bytes 14404
  0.7 19.1 %copy-start.13 = (s32[8,15,10]{1,0,2:T(8,128)S(1)}, s32[8,15,10]{1,0,2:T(8,128)}, u32[]{:S(2)}) copy-start(s32[8,15,10]{1,0,2:T(8,128)} %param.18) | copy-start | bytes 14404
  0.7 19.5 %copy-start.16 = (s32[8]{0:T(128)S(1)}, s32[8]{0:T(128)}, u32[]{:S(2)}) copy-start(s32[8]{0:T(128)} %param.14) | copy-start | bytes 100
  3.8 31.3 %all-to-all-start = ((bf16[128,4,384]{2,1,0:T(4,128)(2,1)}), bf16[128,4,384]{2,1,0:T(4,128)(2,1)}, u32[]{:S(2)}, u32[]{:S(2)}) async-start(bf16[128,4,384]{2,1,0:T(4,128)(2,1)} %shard_map.138), calls=%async_computation | async-start | bytes 786432 | tf_op jit(solution)/shard_map/all_to_all | solution.py:365
  35.2 9.1 %copy-start.3 = (bf16[8,1024]{1,0:T(8,128)(2,1)S(1)}, bf16[8,1024]{1,0:T(8,128)(2,1)}, u32[]{:S(2)}) copy-start(bf16[8,1024]{1,0:T(8,128)(2,1)} %refs_6_.1) | copy-start | bytes 49156
  35.2 9.1 %copy-start.6 = (f32[128,1024]{1,0:T(8,128)S(1)}, f32[128,1024]{1,0:T(8,128)}, u32[]{:S(2)}) copy-start(f32[128,1024]{1,0:T(8,128)} %get-tuple-element.29.refs_3_) | copy-start | bytes 1572868
  35.2 9.1 %copy-start.7 = (bf16[512,384]{1,0:T(8,128)(2,1)S(1)}, bf16[512,384]{1,0:T(8,128)(2,1)}, u32[]{:S(2)}) copy-start(bf16[512,384]{1,0:T(8,128)(2,1)} %get-tuple-element.32.refs_7_) | copy-start | bytes 1179652
  35.2 9.1 %copy-start.10 = (f32[384,128]{1,0:T(8,128)S(1)}, f32[384,128]{1,0:T(8,128)}, u32[]{:S(2)}) copy-start(f32[384,128]{1,0:T(8,128)} %get-tuple-element.31.refs_5_) | copy-start | bytes 589828
  35.2 9.1 %copy-start.11 = (bf16[32,128]{1,0:T(8,128)(2,1)S(1)}, bf16[32,128]{1,0:T(8,128)(2,1)}, u32[]{:S(2)}) copy-start(bf16[32,128]{1,0:T(8,128)(2,1)} %get-tuple-element.30.refs_4_) | copy-start | bytes 24580
  39.9 4.4 %collective-permute-start = (f32[128,1024]{1,0:T(8,128)}, f32[128,1024]{1,0:T(8,128)S(1)}, u32[]{:S(2)}, u32[]{:S(2)}) collective-permute-start(f32[128,1024]{1,0:T(8,128)} %get-tuple-element.28.refs_1_), channel_id=1, source_target_pairs={{0,1},{1,0},{2,3},{3,2},{4,5},{5,4},{6,7},{7,6},{8,9},{9,8},{10,11... | collective-permute-start | bytes 1572872 | tf_op jit(solution)/shard_map/ppermute | solution.py:328
  40.0 17.7 %collective-permute-start.2 = (bf16[384,384]{1,0:T(8,128)(2,1)}, bf16[384,384]{1,0:T(8,128)(2,1)}, u32[]{:S(2)}, u32[]{:S(2)}) collective-permute-start(bf16[384,384]{1,0:T(8,128)(2,1)} %get-tuple-element.38.refs_1_), channel_id=1, source_target_pairs={{0,64},{64,128},{128,192},{192,0},{1,65},{65,129},{129,193},{193,1... | collective-permute-start | bytes 884744 | tf_op jit(solution)/shard_map/ppermute | solution.py:328
  40.8 26.0 %collective-permute-start.3 = (bf16[384,384]{1,0:T(8,128)(2,1)}, bf16[384,384]{1,0:T(8,128)(2,1)}, u32[]{:S(2)}, u32[]{:S(2)}) collective-permute-start(bf16[384,384]{1,0:T(8,128)(2,1)} %get-tuple-element.38.refs_1_), channel_id=1, source_target_pairs={{0,128},{64,192},{128,0},{192,64},{1,129},{65,193},{129,1},{193,65... | collective-permute-start | bytes 884744 | tf_op jit(solution)/shard_map/ppermute | solution.py:328
  42.5 24.4 %collective-permute-start.4 = (bf16[384,384]{1,0:T(8,128)(2,1)}, bf16[384,384]{1,0:T(8,128)(2,1)}, u32[]{:S(2)}, u32[]{:S(2)}) collective-permute-start(bf16[384,384]{1,0:T(8,128)(2,1)} %get-tuple-element.38.refs_1_), channel_id=1, source_target_pairs={{0,192},{64,0},{128,64},{192,128},{1,193},{65,1},{129,65},{193,129... | collective-permute-start | bytes 884744 | tf_op jit(solution)/shard_map/ppermute | solution.py:328
  44.3 1.0 copy-start.1
  45.3 21.6 %copy-start.2 = (bf16[384,384]{1,0:T(8,128)(2,1)S(1)}, bf16[384,384]{1,0:T(8,128)(2,1)}, u32[]{:S(2)}) copy-start(bf16[384,384]{1,0:T(8,128)(2,1)} %get-tuple-element.38.refs_1_) | copy-start | bytes 884740
  51.1 15.8 %collective-permute-start.5 = (bf16[208,256]{1,0:T(8,128)(2,1)S(1)}, bf16[208,256]{1,0:T(8,128)(2,1)S(1)}, u32[]{:S(2)}, u32[]{:S(2)}) collective-permute-start(bf16[208,256]{1,0:T(8,128)(2,1)S(1)} %get-tuple-element.40), channel_id=1, source_target_pairs={{0,64},{64,128},{128,192},{192,0},{1,65},{65,129},{129,193},{193,1... | collective-permute-start | bytes 319496 | tf_op jit(solution)/shard_map/ppermute | solution.py:328
  51.4 15.5 %collective-permute-start.6 = (bf16[208,256]{1,0:T(8,128)(2,1)S(1)}, bf16[208,256]{1,0:T(8,128)(2,1)S(1)}, u32[]{:S(2)}, u32[]{:S(2)}) collective-permute-start(bf16[208,256]{1,0:T(8,128)(2,1)S(1)} %get-tuple-element.41), channel_id=1, source_target_pairs={{0,128},{64,192},{128,0},{192,64},{1,129},{65,193},{129,1},{193,65... | collective-permute-start | bytes 319496 | tf_op jit(solution)/shard_map/ppermute | solution.py:328
  57.7 9.2 %collective-permute-start.7 = (bf16[208,256]{1,0:T(8,128)(2,1)S(1)}, bf16[208,256]{1,0:T(8,128)(2,1)S(1)}, u32[]{:S(2)}, u32[]{:S(2)}) collective-permute-start(bf16[208,256]{1,0:T(8,128)(2,1)S(1)} %get-tuple-element.42), channel_id=1, source_target_pairs={{0,192},{64,0},{128,64},{192,128},{1,193},{65,1},{129,65},{193,129... | collective-permute-start | bytes 319496 | tf_op jit(solution)/shard_map/ppermute | solution.py:328
  57.7 24.5 %all-to-all-start.1 = ((bf16[128,4,384]{2,1,0:T(4,128)(2,1)}), bf16[128,4,384]{2,1,0:T(4,128)(2,1)}, u32[]{:S(2)}, u32[]{:S(2)}) async-start(bf16[128,4,384]{2,1,0:T(4,128)(2,1)} %get-tuple-element.33), calls=%async_computation.1 | async-start | bytes 786432 | tf_op jit(solution)/shard_map/all_to_all | solution.py:428
  66.9 15.3 %copy-start.5 = (s32[1,512]{1,0:T(1,128)S(1)}, s32[1,512]{1,0:T(1,128)}, u32[]{:S(2)}) copy-start(s32[1,512]{1,0:T(1,128)} %refs_0_.4) | copy-start | bytes 6148
  69.7 0.7 copy-start.8
  70.4 14.3 %collective-permute-start.10 = (bf16[352,384]{1,0:T(8,128)(2,1)}, bf16[352,384]{1,0:T(8,128)(2,1)}, u32[]{:S(2)}, u32[]{:S(2)}) collective-permute-start(bf16[352,384]{1,0:T(8,128)(2,1)} %get-tuple-element.47), channel_id=1, source_target_pairs={{0,48},{16,0},{32,16},{48,32},{1,49},{17,1},{33,17},{49,33},{2,50}... | collective-permute-start | bytes 811016 | tf_op jit(solution)/shard_map/ppermute | solution.py:328
  71.4 13.3 %collective-permute-start.8 = (bf16[352,384]{1,0:T(8,128)(2,1)}, bf16[352,384]{1,0:T(8,128)(2,1)}, u32[]{:S(2)}, u32[]{:S(2)}) collective-permute-start(bf16[352,384]{1,0:T(8,128)(2,1)} %get-tuple-element.45), channel_id=1, source_target_pairs={{0,16},{16,32},{32,48},{48,0},{1,17},{17,33},{33,49},{49,1},{2,18}... | collective-permute-start | bytes 811016 | tf_op jit(solution)/shard_map/ppermute | solution.py:328
  72.5 15.4 %collective-permute-start.9 = (bf16[352,384]{1,0:T(8,128)(2,1)}, bf16[352,384]{1,0:T(8,128)(2,1)}, u32[]{:S(2)}, u32[]{:S(2)}) collective-permute-start(bf16[352,384]{1,0:T(8,128)(2,1)} %get-tuple-element.46), channel_id=1, source_target_pairs={{0,32},{16,48},{32,0},{48,16},{1,33},{17,49},{33,1},{49,17},{2,34}... | collective-permute-start | bytes 811016 | tf_op jit(solution)/shard_map/ppermute | solution.py:328
  82.2 5.7 %copy-start.9 = (bf16[352,384]{1,0:T(8,128)(2,1)S(1)}, bf16[352,384]{1,0:T(8,128)(2,1)}, u32[]{:S(2)}) copy-start(bf16[352,384]{1,0:T(8,128)(2,1)} %copy-done.8) | copy-start | bytes 811012
  84.7 11.3 %collective-permute-start.1 = (f32[8,128]{1,0:T(8,128)}, f32[8,128]{1,0:T(8,128)}, u32[]{:S(2)}, u32[]{:S(2)}) collective-permute-start(f32[8,128]{1,0:T(8,128)} %get-tuple-element.35.refs_3_), channel_id=1, source_target_pairs={{0,1},{1,0},{2,3},{3,2},{4,5},{5,4},{6,7},{7,6},{8,9},{9,8},{10,11... | collective-permute-start | bytes 12296 | tf_op jit(solution)/shard_map/ppermute | solution.py:328
  87.9 8.2 %copy-start = (f32[1024,384]{1,0:T(8,128)S(1)}, f32[1024,384]{1,0:T(8,128)}, u32[]{:S(2)}) copy-start(f32[1024,384]{1,0:T(8,128)} %refs_0_.5) | copy-start | bytes 4718596
  87.9 8.2 %copy-start.4 = (f32[1024]{0:T(1024)S(1)}, f32[1024]{0:T(1024)}, u32[]{:S(2)}) copy-start(f32[1024]{0:T(1024)} %param.12) | copy-start | bytes 12292
  90.3 18.5 %all-to-all-start.2 = ((bf16[8,8,2688]{2,1,0:T(8,128)(2,1)}), bf16[8,8,2688]{2,1,0:T(8,128)(2,1)}, u32[]{:S(2)}, u32[]{:S(2)}) async-start(bf16[8,8,2688]{2,1,0:T(8,128)(2,1)} %bitcast.6), calls=%async_computation.2 | async-start | bytes 688128 | tf_op jit(solution)/shard_map/all_to_all | solution.py:449

commit v4 on v3

--- a/solution.py
+++ b/solution.py
@@ -51,12 +51,12 @@
         self.copy.start()
 
 
-def call(kernel, outs, operands, flops, smem=0, scratch=(), hbm_in=(), hbm_out=(), hbm_raw=()):
+def call(kernel, outs, operands, smem=0, scratch=(), hbm_in=(), hbm_out=(), raw_in=(), hbm_raw=()):
     name = getattr(kernel, "func", kernel)
-    limit, flops = LIMITS.get(name, 12), FLOPS.get(name, 10**12)
+    limit, flops = LIMITS.get(name, 12), COSTS.get(name, 10**12)
     moved = sum(o.size * o.dtype.itemsize for o in list(operands) + list(outs))
     specs = [
-        pl.BlockSpec(memory_space=pltpu.SMEM if i < smem else pltpu.HBM if i in hbm_in else pltpu.VMEM)
+        pl.BlockSpec(memory_space=pltpu.SMEM if i < smem else pltpu.HBM if i in hbm_in or i in raw_in else pltpu.VMEM)
         for i in range(len(operands))
     ]
     made = [
@@ -101,16 +101,14 @@
     return jax.ShapeDtypeStruct(shape, dtype)
 
 
-def serve_kernel(serve_ref, table_ref, out_ref):
-    serve_ref = serve_ref.get()
+def serve_kernel(serve_ref, table_ref, out_ref, onehot):
+    serve = serve_ref.get()[...]
+    lanes = lax.broadcasted_iota(jnp.int32, (LANES, onehot.shape[1]), 1)
+    for block in range(serve.shape[1] // LANES):
+        span = slice(block * LANES, (block + 1) * LANES)
+        onehot[span, :] = jnp.where(row_to_column(serve[:, span]) == lanes, 1.0, 0.0).astype(BF16)
     rows = table_ref.get()[...].astype(BF16)
-    lanes = lax.broadcasted_iota(jnp.int32, (LANES, rows.shape[0]), 1)
-    owners = LANES // out_ref.shape[1]
-    for block in range(serve_ref.shape[1] // LANES):
-        wanted = row_to_column(serve_ref[:, block * LANES : (block + 1) * LANES])
-        onehot = jnp.where(wanted == lanes, 1.0, 0.0).astype(BF16)
-        picked = matmul(onehot, rows).astype(BF16)
-        out_ref[block * owners : (block + 1) * owners] = picked.reshape(owners, *out_ref.shape[1:])
+    out_ref[...] = matmul(onehot[...], rows).astype(BF16).reshape(out_ref.shape)
 
 
 def index_kernel(idx_ref, cot_ref, w2_ref, *refs):
@@ -156,7 +154,7 @@
     layer_out, partial_out = layer_ref, partial_ref
     layer_ref, partial_ref = layer_ref.buffer, partial_ref.buffer
     nodes = partial_ref.shape[0]
-    fetched = fetched_ref[...].reshape(ct_ref.shape[1], layer_ref.shape[1])
+    fetched = fetched_ref.get()[...].reshape(ct_ref.shape[1], layer_ref.shape[1])
     total = None
     ct_ref = ct_ref.get()
     ones = jnp.ones((ct_ref.shape[1], LANES), BF16)
@@ -167,13 +165,13 @@
         layer_ref[span, :] = (summed * inverse).astype(BF16)
     layer_out.send()
     for k in range(layers):
-        term = matmul(layer_ref[k * nodes : (k + 1) * nodes, :], w1_ref[k])
+        term = matmul(layer_ref[k * nodes : (k + 1) * nodes, :], w1_ref.get()[k])
         total = term if total is None else total + term
     partial_ref[...] = total
     partial_out.send()
 
 
-def hidden_kernel(place_ref, mine_ref, other_ref, back_ref, e_ref, inv_ref, cot_ref, c_ref, w1_ref, slot_ref, *refs):
+def hidden_kernel(place_ref, mine_ref, other_ref, back_ref, e_ref, inv_ref, cot_ref, layer_ref, out_ref, *refs):
     packs, stage, sems = refs[:-2], refs[-2], refs[-1]
     nodes = mine_ref.shape[0]
     width = stage.shape[2]
@@ -185,6 +183,7 @@
     hidden = (values * sigma).astype(BF16)
     slope = sigma * (1.0 + values * (1.0 - sigma))
     back = (back_ref[...] * slope).astype(BF16)
+    out_ref[...] = back
     scale = jnp.concatenate(
         [inv_ref[k * nodes : k * nodes + seeds, 0:1] for k in range(layers)]
         + [jnp.zeros((SEED_ROWS - layers * seeds, 1), F32)],
@@ -203,47 +202,68 @@
             stage[j, first : first + SEED_ROWS, :] = second[:, part * width : (part + 1) * width]
         first = nodes + half // width * SEED_ROWS
         stage[j, first : first + COT_ROWS, :] = cot[:, span]
-    copies = [
-        pltpu.make_async_copy(stage.at[lax.rem(place_ref[1] + d, len(packs))], pack, sems.at[d])
-        for d, pack in enumerate(packs)
-    ]
+    moves = []
+    for d, pack in enumerate(packs):
+        chosen = stage.at[lax.rem(place_ref[1] + d, len(packs))]
+        if d != len(packs) // 2:
+            moves.append((chosen, pack))
+            continue
+        start = 0
+        for source in (chosen, layer_ref):
+            rows, wide = source.shape
+            for lane in range(0, wide, LANES):
+                moves.append((source.at[:, lane : lane + LANES], pack.at[start : start + rows, :]))
+                start += rows
+    copies = [pltpu.make_async_copy(source, target, sems.at[i]) for i, (source, target) in enumerate(moves)]
     for copy in copies:
         copy.start()
+    for copy in copies:
+        copy.wait()
+
+
+def slot_kernel(back_ref, inv_ref, c_ref, w1_ref, slot_ref):
+    nodes = back_ref.shape[0]
     total = None
-    for k in range(layers):
+    for k in range(w1_ref.shape[0]):
         span = slice(k * nodes, (k + 1) * nodes)
-        back_in = matmul(back, w1_ref[k], (1, 1)) * inv_ref[span, 0:1]
+        back_in = matmul(back_ref[...], w1_ref.get()[k], (1, 1)) * inv_ref.get()[span, 0:1]
         term = matmul(c_ref.get()[:, span], back_in.astype(BF16))
         total = term if total is None else total + term
     slot_ref[...] = total.astype(BF16).reshape(slot_ref.shape)
-    for copy in copies:
-        copy.wait()
 
 
 def weight_kernel(count, place_ref, *refs):
-    layer_refs, pack_refs = refs[:count], refs[count : 2 * count]
-    own_ref, outs = refs[2 * count], refs[2 * count + 1 : -1]
-    total = refs[-1]
-    width = pack_refs[0].shape[1]
-    columns = layer_refs[0].shape[1]
+    layer_refs, pack_refs = list(refs[: count - 1]), list(refs[count - 1 : 2 * count - 1])
+    own_ref, outs, total = refs[2 * count - 1], refs[2 * count : -1], refs[-1]
+    pack_rows, width = pack_refs[0].shape
+    layer_rows, columns = layer_refs[0].shape
+    layer_parts = [r.get()[...] for r in layer_refs]
+    far = pack_refs[count // 2][...]
+    parts, start = [], 0
+    for rows, wide in ((pack_rows, width), (layer_rows, columns)):
+        lanes = [far[start + i * rows : start + (i + 1) * rows] for i in range(wide // LANES)]
+        parts.append(jnp.concatenate(lanes, 1))
+        start += rows * len(lanes)
+    layer_parts.insert(count // 2, parts[1])
+    packs = [parts[0] if d == count // 2 else ref[...] for d, ref in enumerate(pack_refs)]
     nodes = LANES
-    relations = layer_refs[0].shape[0] // nodes
+    relations = layer_rows // nodes
     rows = own_ref.shape[0]
-    left = jnp.concatenate([p[:nodes, :] for p in pack_refs], 0)
+    left = jnp.concatenate([p[:nodes, :] for p in packs], 0)
     for k in range(relations):
-        right = jnp.concatenate([r[k * nodes : (k + 1) * nodes, :] for r in layer_refs], 0)
+        right = jnp.concatenate([r[k * nodes : (k + 1) * nodes, :] for r in layer_parts], 0)
         total[k] = matmul(left, right, (0, 0))
-    pieces = (pack_refs[0].shape[0] - nodes - COT_ROWS) // SEED_ROWS
+    pieces = (pack_rows - nodes - COT_ROWS) // SEED_ROWS
     half = pieces * width
     seeds = SEED_ROWS // (relations + 1)
     first = nodes + pieces * SEED_ROWS
-    cots = jnp.concatenate([p[first : first + COT_ROWS, :].astype(F32)[:seeds] for p in pack_refs], 0)
+    cots = jnp.concatenate([p[first : first + COT_ROWS, :].astype(F32)[:seeds] for p in packs], 0)
     seconds = [
         jnp.concatenate(
             [p[nodes + part * SEED_ROWS : nodes + (part + 1) * SEED_ROWS, :].astype(F32) for part in range(pieces)],
             1,
         )
-        for p in pack_refs
+        for p in packs
     ]
     second = jnp.concatenate(
         [jnp.concatenate([s[k * seeds : (k + 1) * seeds] for s in seconds], 0) for k in range(relations)], 1
@@ -328,8 +348,8 @@
     return lax.ppermute(array, axis, [(i, (i + by) % size) for i in range(size)])
 
 
-LIMITS = {serve_kernel: 60, index_kernel: 60, first_kernel: 60, hidden_kernel: 50}
-FLOPS = {}
+LIMITS = {serve_kernel: 60, index_kernel: 60, first_kernel: 60, hidden_kernel: 60, slot_kernel: 50}
+COSTS = {update_kernel: 0, group_kernel: 0, row_kernel: 0}
 
 
 def body(
@@ -360,7 +380,7 @@
 
     blocks_shape = (owners, slots // owners, columns)
     outgoing = call(
-        serve_kernel, [shaped(blocks_shape, BF16)], (serve_rows, table), 2 * slots * table_rows * columns, hbm_in=(0, 1)
+        serve_kernel, [shaped(blocks_shape, BF16)], (serve_rows, table), scratch=[pltpu.VMEM((slots, table_rows), BF16)], hbm_in=(0, 1)
     )[0]
     fetched = lax.all_to_all(outgoing, everyone, split_axis=0, concat_axis=0, tiled=True)
 
@@ -386,7 +406,6 @@
             shaped((nodes, hidden_units), F32),
         ],
         (idx, cotangent, w_second),
-        2 * layers * seeds * hidden_units * hidden_units,
         scratch=[pltpu.VMEM((LANES, hidden_units), F32)],
         hbm_out=range(5),
     )
@@ -395,18 +414,19 @@
         first_kernel,
         [shaped((layers * nodes, columns), BF16), shaped((nodes, hidden_units), F32)],
         (fetched, ct, w_first),
-        2 * layers * nodes * columns * (slots + hidden_units),
-        hbm_in=(1,),
+        hbm_in=(0, 1, 2),
         hbm_out=(0, 1),
     )
     other_pre = shift(partial_pre, "col", 1)
-    layer_parts = [layer_in] + [shift(layer_in, "dp", d) for d in range(1, n_x)]
+    layer_parts = [layer_in] + [shift(layer_in, "dp", d) for d in range(1, n_x) if d != n_x // 2]
 
     pack_rows = nodes + half // width * SEED_ROWS + COT_ROWS
     pack_shape = (pack_rows, width)
-    slot_grad, *packs = call(
+    far = n_x // 2
+    far_shape = ((pack_rows * width + layers * nodes * columns) // LANES, LANES)
+    back, *packs = call(
         hidden_kernel,
-        [shaped(blocks_shape, BF16)] + [shaped(pack_shape, BF16)] * n_x,
+        [shaped((nodes, hidden_units), BF16)] + [shaped(far_shape if d == far else pack_shape, BF16) for d in range(n_x)],
         (
             jnp.stack([lax.axis_index("col"), x]),
             partial_pre,
@@ -415,16 +435,17 @@
             member,
             inverse,
             cotangent,
-            c,
-            w_first,
+            layer_in,
         ),
-        2 * layers * nodes * columns * (slots + hidden_units),
         smem=1,
-        scratch=[pltpu.VMEM((n_x, *pack_shape), BF16), pltpu.SemaphoreType.DMA((n_x,))],
-        hbm_in=(1, 2, 3, 4, 5, 7),
+        scratch=[pltpu.VMEM((n_x, *pack_shape), BF16), pltpu.SemaphoreType.DMA((n_x - 1 + (width + columns) // LANES,))],
+        hbm_in=(1, 2, 3, 4, 5),
+        raw_in=(7,),
         hbm_raw=range(1, 1 + n_x),
     )
     packs = [packs[0]] + [shift(packs[d], "dp", d) for d in range(1, n_x)]
+    back, *layer_parts[1:] = lax.optimization_barrier((back, *layer_parts[1:]))
+    slot_grad = call(slot_kernel, [shaped(blocks_shape, BF16)], (back, inverse, c, w_first), hbm_in=(1, 2, 3))[0]
     arrived = lax.all_to_all(slot_grad, everyone, split_axis=0, concat_axis=0, tiled=True)
 
     block_rows = width // n_y
@@ -433,8 +454,8 @@
         functools.partial(weight_kernel, n_x),
         [shaped((block_rows, layers * columns), F32)] + [shaped((group_rows, columns), BF16)] * n_y,
         (y.reshape(1), *layer_parts, *packs),
-        2 * n_x * nodes * width * layers * columns,
         smem=1,
+        hbm_in=range(1, n_x),
         scratch=[pltpu.VMEM((layers, width, columns), F32)],
     )
     blocks = [blocks[0]] + [shift(blocks[d], "y", d) for d in range(1, n_y)]
@@ -443,7 +464,6 @@
         functools.partial(group_kernel, layers),
         [shaped((block_rows, grad_columns), BF16)],
         (own, *blocks),
-        2 * n_x * n_y * seeds * block_rows * layers * half,
     )[0]
     grads = grads.reshape(n_z, block_rows // n_z, grad_columns)
     grads = lax.all_to_all(grads, "z", split_axis=0, concat_axis=0, tiled=True)
@@ -451,7 +471,6 @@
         sum_kernel,
         [shaped((layers, block_rows // n_z, wide), F32) for wide in (columns, half)],
         (grads,),
-        block_rows * grad_columns,
     )
     grad_one, grad_two = grad_one.transpose(0, 2, 1), grad_two.transpose(0, 2, 1)
 
@@ -459,14 +478,12 @@
         row_kernel,
         [shaped((table_rows, columns), F32), shaped((table_rows // LANES, LANES), F32)],
         (serve_rows, arrived),
-        2 * slots * table_rows * columns,
     )
     other_squares = shift(squares, "col", 1)
     new_table, new_accum = call(
         functools.partial(update_kernel, 2 * columns),
         [shaped((table_rows, columns), F32), shaped((table_rows // LANES, LANES), F32)],
         (table, row_grad, accum.reshape(-1, LANES), squares, other_squares),
-        3 * table_rows * columns,
     )
     return (new_table, new_accum.reshape(-1), grad_one, grad_two)
 

time: 112 us -> 116 us (1.036); the launches traced: 110 us -> 116 us
  Pallas kernels: 31.5 us -> 37.5 us
    ppermute x11 -> x10, waiting for transfers between devices: 7.59 us -> 14.6 us  [shift(): lax.ppermute(array, axis, [(i, (i + by) % size) for i in range(size)])]
    all_to_all x1, waiting for transfers between devices: 6.34 us -> 0.01 us  [body(): lax.all_to_all(slot_grad, everyone, split_axis=0, concat_axis=0, tiled=True)]
    pallas_call x9 -> x10, Pallas kernels: 31.5 us -> 37.5 us  [call(): pl.pallas_call(wrapped, out_shape=tuple(outs), in_specs=specs, out_specs=...]
    all_to_all x1, waiting for transfers between devices: 10.5 us -> 8.79 us  [body(): grads = lax.all_to_all(grads, 'z', split_axis=0, concat_axis=0, tiled=True)]
    ppermute x11 -> x10, starting transfers between devices: 11.9 us -> 12 us  [shift(): lax.ppermute(array, axis, [(i, (i + by) % size) for i in range(size)])]
  transfers between devices with their start and end apart: 14 -> 13, of which waited for: 5 -> 6; matrix products, arithmetic and copies ran while one was open for 1% -> 2% of each run, Pallas kernels for 20% -> 26%
where the time goes in v4:
time: 116 us
  starting transfers between devices  42.2 us (36%)
  Pallas kernels  37.5 us (32%)
  waiting for transfers between devices  31.3 us (27%)
  local copies, waits for them, and re-layouts  2.32 us (2%)
  other arithmetic  1.38 us (1%)
    pallas_call x10, Pallas kernels, call(): pl.pallas_call(wrapped, out_shape=tuple(outs), in_specs=specs, out_specs=...  37.5 us
    all_to_all x1, starting transfers between devices, body(): lax.all_to_all(outgoing, everyone, split_axis=0, concat_axis=0, tiled=True)  15.8 us
    ppermute x10, waiting for transfers between devices, shift(): lax.ppermute(array, axis, [(i, (i + by) % size) for i in range(size)])  14.6 us
    ppermute x10, starting transfers between devices, shift(): lax.ppermute(array, axis, [(i, (i + by) % size) for i in range(size)])  12 us
    all_to_all x1, starting transfers between devices, body(): lax.all_to_all(slot_grad, everyone, split_axis=0, concat_axis=0, tiled=True)  9.06 us
    all_to_all x1, waiting for transfers between devices, body(): grads = lax.all_to_all(grads, 'z', split_axis=0, concat_axis=0, tiled=True)  8.79 us
    all_to_all x1, waiting for transfers between devices, body(): lax.all_to_all(outgoing, everyone, split_axis=0, concat_axis=0, tiled=True)  7.89 us
    all_to_all x1, starting transfers between devices, body(): grads = lax.all_to_all(grads, 'z', split_axis=0, concat_axis=0, tiled=True)  5.44 us
  transfers between devices with their start and end apart: 13, of which 6 were waited for; matrix products, arithmetic and copies ran while one was open for 2% of the time, Pallas kernels for 26%

profile of v4, /device:TPU:8, one launch (start us, length us, event | category | flops | bytes accessed | tf_op | source)
XLA Modules:
  0.0 115.6 jit_solution(5834226137652114884)
XLA Ops:
  0.7 2.9 %shard_map.138 = bf16[128,4,384]{2,1,0:T(4,128)(2,1)} custom-call(s32[1,512]{1,0:T(1,128)} %refs_0_.4, f32[1024,384]{1,0:T(8,128)} %refs_0_.5), custom_call_target="tpu_custom_call" | custom-call | flops 999999995904 | bytes 1968128 | tf_op jit(solution)/shard_map/pallas_call | solution.py:89
  3.6 15.8 %all-to-all-start = ((bf16[128,4,384]{2,1,0:T(4,128)(2,1)}), bf16[128,4,384]{2,1,0:T(4,128)(2,1)}, u32[]{:S(2)}, u32[]{:S(2)}) async-start(bf16[128,4,384]{2,1,0:T(4,128)(2,1)} %shard_map.138), calls=%async_computation | async-start | bytes 786432 | tf_op jit(solution)/shard_map/all_to_all | solution.py:385
  19.4 0.1 reshape.29
  19.5 0.1 reshape.31
  19.6 0.1 reshape.30
  19.7 0.1 pad.6.clone
  19.8 0.1 pad_add_fusion.1
  19.9 0.1 copy.30
  20.0 0.1 copy.29
  20.1 0.7 pad_add_fusion.refs_0_
  20.8 6.3 %shard_map.139 = (bf16[384,512]{1,0:T(8,128)(2,1)}, bf16[512,384]{1,0:T(8,128)(2,1)}, f32[384,128]{1,0:T(8,128)}, bf16[32,128]{1,0:T(8,128)(2,1)}, f32[128,1024]{1,0:T(8,128)}) custom-call(s32[128,17]{1,0:T(8,128)} %pad_add_fusion.refs_0_, bf16[8,1024]{1,0:T(8,128)(2,1)} %refs_6_.1, bf16[3,1024,1024]{2,1,0:T(8,128)(2,1)} %refs_2_.2), custom_call_target="tpu_custom_call" | custom-call | flops 999999995904 | bytes 7832064 | tf_op jit(solution)/shard_map/pallas_call | solution.py:89
  27.1 7.9 %all-to-all-done.refs_0_ = bf16[128,4,384]{2,1,0:T(4,128)(2,1)} async-done(((bf16[128,4,384]{2,1,0:T(4,128)(2,1)}), bf16[128,4,384]{2,1,0:T(4,128)(2,1)}, u32[]{:S(2)}, u32[]{:S(2)}) %all-to-all-start) | async-done | bytes 393248 | tf_op jit(solution)/shard_map/all_to_all | solution.py:385
  35.0 3.3 %shard_map.140 = (bf16[384,384]{1,0:T(8,128)(2,1)}, f32[128,1024]{1,0:T(8,128)}) custom-call(bf16[128,4,384]{2,1,0:T(4,128)(2,1)} %all-to-all-done.refs_0_, bf16[384,512]{1,0:T(8,128)(2,1)} %get-tuple-element.30.refs_1_, bf16[3,384,1024]{2,1,0:T(8,128)(2,1)} %refs_3_.1), custom_call_target="tpu_custom_call" | custom-call | flops 999999995904 | bytes 3964928 | tf_op jit(solution)/shard_map/pallas_call | solution.py:89
  38.3 0.1 collective-permute-start
  38.4 0.6 pad_add_fusion.2.refs_0_
  39.0 0.8 collective-permute-start.1
  39.8 2.5 %collective-permute-start.2 = (bf16[384,384]{1,0:T(8,128)(2,1)}, bf16[384,384]{1,0:T(8,128)(2,1)}, u32[]{:S(2)}, u32[]{:S(2)}) collective-permute-start(bf16[384,384]{1,0:T(8,128)(2,1)} %get-tuple-element.35.refs_7_.refs_1_), channel_id=1, source_target_pairs={{0,192},{64,0},{128,64},{192,128},{1,193},{65,1},{129,65},{193,129... | collective-permute-start | bytes 884744 | tf_op jit(solution)/shard_map/ppermute | solution.py:348
  42.3 0.0 collective-permute-done.refs_2_
  42.3 0.8 copy-done.14
  43.1 13.4 %shard_map.141 = (bf16[128,1024]{1,0:T(8,128)(2,1)}, bf16[208,256]{1,0:T(8,128)(2,1)}, bf16[208,256]{1,0:T(8,128)(2,1)}, bf16[1568,128]{1,0:T(8,128)(2,1)}, bf16[208,256]{1,0:T(8,128)(2,1)}) custom-call(s32[2]{0:T(128)} %pad_add_fusion.2.refs_0_, f32[128,1024]{1,0:T(8,128)} %get-tuple-element.31.refs_1_, f32[128,1024]{1,0:T(8,128)} %copy-done.14, ...), custom_call_target="tpu_custom_call" | custom-call | flops 999999995904 | bytes 3072008 | tf_op jit(solution)/shard_map/pallas_call | solution.py:89
  56.5 0.0 collective-permute-done.2.refs_3_
  56.5 0.4 collective-permute-start.5
  57.0 0.5 collective-permute-start.4
  57.5 2.7 %collective-permute-start.6 = (bf16[208,256]{1,0:T(8,128)(2,1)}, bf16[208,256]{1,0:T(8,128)(2,1)}, u32[]{:S(2)}, u32[]{:S(2)}) collective-permute-start(bf16[208,256]{1,0:T(8,128)(2,1)} %get-tuple-element.48), channel_id=1, source_target_pairs={{0,192},{64,0},{128,64},{192,128},{1,193},{65,1},{129,65},{193,129... | collective-permute-start | bytes 319496 | tf_op jit(solution)/shard_map/ppermute | solution.py:348
  60.2 0.9 copy-done.6
  61.2 3.1 %shard_map.142 = bf16[128,4,384]{2,1,0:T(4,128)(2,1)} custom-call(bf16[128,1024]{1,0:T(8,128)(2,1)S(1)} %copy-done.6, f32[384,128]{1,0:T(8,128)S(1)} %copy-done.7, bf16[512,384]{1,0:T(8,128)(2,1)S(1)} %copy-done.5, bf16[3,384,1024]{2,1,0:T(8,128)(2,1)S(1)} %copy-done.3), custom_call_target="tpu_custom_call" | custom-call | flops 999999995904 | bytes 3604480 | tf_op jit(solution)/shard_map/pallas_call | solution.py:89
  64.3 9.1 %all-to-all-start.1 = ((bf16[128,4,384]{2,1,0:T(4,128)(2,1)}), bf16[128,4,384]{2,1,0:T(4,128)(2,1)}, u32[]{:S(2)}, u32[]{:S(2)}) async-start(bf16[128,4,384]{2,1,0:T(4,128)(2,1)} %shard_map.142), calls=%async_computation.1 | async-start | bytes 786432 | tf_op jit(solution)/shard_map/all_to_all | solution.py:449
  73.4 0.0 collective-permute-done.4.refs_5_
  73.4 0.0 collective-permute-done.6.refs_7_
  73.4 3.0 %shard_map.145 = (f32[64,1152]{1,0:T(8,128)S(1)}, bf16[352,384]{1,0:T(8,128)(2,1)S(1)}, bf16[352,384]{1,0:T(8,128)(2,1)S(1)}, bf16[352,384]{1,0:T(8,128)(2,1)S(1)}, bf16[352,384]{1,0:T(8,128)(2,1)S(1)}) custom-call(s32[1]{0:T(128)} %bitcast.5.refs_0_, bf16[384,384]{1,0:T(8,128)(2,1)S(1)} %copy-done.4, bf16[384,384]{1,0:T(8,128)(2,1)} %collective-permute-done.1.refs_2_, ...), custom_call_target="tpu_custom_call" | custom-call | flops 999999995904 | bytes 2981892 | tf_op jit(solution)/shard_map/pallas_call | solution.py:89
  76.4 0.0 copy-start.2
  76.4 0.0 copy-start
  76.4 0.0 copy-start.1
  76.5 1.6 %collective-permute-start.7 = (bf16[352,384]{1,0:T(8,128)(2,1)S(1)}, bf16[352,384]{1,0:T(8,128)(2,1)S(1)}, u32[]{:S(2)}, u32[]{:S(2)}) collective-permute-start(bf16[352,384]{1,0:T(8,128)(2,1)S(1)} %get-tuple-element.51), channel_id=1, source_target_pairs={{0,16},{16,32},{32,48},{48,0},{1,17},{17,33},{33,49},{49,1},{2,18}... | collective-permute-start | bytes 811016 | tf_op jit(solution)/shard_map/ppermute | solution.py:348
  78.1 1.7 %collective-permute-start.8 = (bf16[352,384]{1,0:T(8,128)(2,1)S(1)}, bf16[352,384]{1,0:T(8,128)(2,1)S(1)}, u32[]{:S(2)}, u32[]{:S(2)}) collective-permute-start(bf16[352,384]{1,0:T(8,128)(2,1)S(1)} %get-tuple-element.52), channel_id=1, source_target_pairs={{0,32},{16,48},{32,0},{48,16},{1,33},{17,49},{33,1},{49,17},{2,34}... | collective-permute-start | bytes 811016 | tf_op jit(solution)/shard_map/ppermute | solution.py:348
  79.7 1.6 %collective-permute-start.9 = (bf16[352,384]{1,0:T(8,128)(2,1)S(1)}, bf16[352,384]{1,0:T(8,128)(2,1)S(1)}, u32[]{:S(2)}, u32[]{:S(2)}) collective-permute-start(bf16[352,384]{1,0:T(8,128)(2,1)S(1)} %get-tuple-element.53), channel_id=1, source_target_pairs={{0,48},{16,0},{32,16},{48,32},{1,49},{17,1},{33,17},{49,33},{2,50}... | collective-permute-start | bytes 811016 | tf_op jit(solution)/shard_map/ppermute | solution.py:348
  81.3 6.8 %collective-permute-done.7.refs_2_ = bf16[352,384]{1,0:T(8,128)(2,1)S(1)} collective-permute-done((bf16[352,384]{1,0:T(8,128)(2,1)S(1)}, bf16[352,384]{1,0:T(8,128)(2,1)S(1)}, u32[]{:S(2)}, u32[]{:S(2)}) %collective-permute-start.7) | collective-permute-done | bytes 270368 | tf_op jit(solution)/shard_map/ppermute | solution.py:348
  88.1 2.2 %collective-permute-done.8.refs_3_ = bf16[352,384]{1,0:T(8,128)(2,1)S(1)} collective-permute-done((bf16[352,384]{1,0:T(8,128)(2,1)S(1)}, bf16[352,384]{1,0:T(8,128)(2,1)S(1)}, u32[]{:S(2)}, u32[]{:S(2)}) %collective-permute-start.8) | collective-permute-done | bytes 270368 | tf_op jit(solution)/shard_map/ppermute | solution.py:348
  90.4 4.4 %collective-permute-done.9.refs_4_ = bf16[352,384]{1,0:T(8,128)(2,1)S(1)} collective-permute-done((bf16[352,384]{1,0:T(8,128)(2,1)S(1)}, bf16[352,384]{1,0:T(8,128)(2,1)S(1)}, u32[]{:S(2)}, u32[]{:S(2)}) %collective-permute-start.9) | collective-permute-done | bytes 270368 | tf_op jit(solution)/shard_map/ppermute | solution.py:348
  94.8 1.2 %shard_map.146 = bf16[64,2688]{1,0:T(8,128)(2,1)} custom-call(f32[64,1152]{1,0:T(8,128)S(1)} %get-tuple-element.49.refs_0_, bf16[352,384]{1,0:T(8,128)(2,1)S(1)} %get-tuple-element.50.refs_1_, bf16[352,384]{1,0:T(8,128)(2,1)S(1)} %collective-permute-done.7.refs_2_, bf16[352,384]{1,0:T(8,128)(2,1)S(1)} %collective-permute-done.8.refs_3_, ...), custom_call_target="tpu_custom_call" | custom-call | bytes 1720320 | tf_op jit(solution)/shard_map/pallas_call | solution.py:89
  96.0 0.0 all-to-all-done.1.refs_1_
  96.0 5.4 %all-to-all-start.2 = ((bf16[8,8,2688]{2,1,0:T(8,128)(2,1)}), bf16[8,8,2688]{2,1,0:T(8,128)(2,1)S(1)}, u32[]{:S(2)}, u32[]{:S(2)}) async-start(bf16[8,8,2688]{2,1,0:T(8,128)(2,1)} %bitcast.6), calls=%async_computation.2 | async-start | bytes 688128 | tf_op jit(solution)/shard_map/all_to_all | solution.py:469
  101.5 1.8 %shard_map.143 = (f32[1024,384]{1,0:T(8,128)S(1)}, f32[8,128]{1,0:T(8,128)S(1)}) custom-call(s32[1,512]{1,0:T(1,128)S(1)} %copy-done.2, bf16[128,4,384]{2,1,0:T(4,128)(2,1)} %all-to-all-done.1.refs_1_), custom_call_target="tpu_custom_call" | custom-call | bytes 1972224 | tf_op jit(solution)/shard_map/pallas_call | solution.py:89
  103.3 0.1 collective-permute-start.3
  103.4 1.2 collective-permute-done.3.refs_4_
  104.6 1.6 %shard_map.144 = (f32[1024,384]{1,0:T(8,128)}, f32[8,128]{1,0:T(8,128)}) custom-call(f32[1024,384]{1,0:T(8,128)S(1)} %copy-done, f32[1024,384]{1,0:T(8,128)S(1)} %get-tuple-element.39.refs_1_, f32[8,128]{1,0:T(8,128)S(1)} %bitcast.11, f32[8,128]{1,0:T(8,128)S(1)} %get-tuple-element.40.refs_3_, f32[8,128]{1,0:T(8,128)S(1)} %collective-permute-done.3.refs_4_), custom_call_target="tpu_custom_call" | custom-call | bytes 4734976 | tf_op jit(solution)/shard_map/pallas_call | solution.py:89
  106.1 8.8 %all-to-all-done.2.refs_0_ = bf16[8,8,2688]{2,1,0:T(8,128)(2,1)S(1)} async-done(((bf16[8,8,2688]{2,1,0:T(8,128)(2,1)}), bf16[8,8,2688]{2,1,0:T(8,128)(2,1)S(1)}, u32[]{:S(2)}, u32[]{:S(2)}) %all-to-all-start.2) | async-done | bytes 344096 | tf_op jit(solution)/shard_map/all_to_all | solution.py:469
  114.9 0.7 shard_map.147
  (31 shorter events, 0.1 us)
Async XLA Ops:
  0.6 18.8 %copy-start.11 = (s32[8,15]{1,0:T(8,128)S(1)}, s32[8,15]{1,0:T(8,128)}, u32[]{:S(2)}) copy-start(s32[8,15]{1,0:T(8,128)} %param.15) | copy-start | bytes 1444
  0.6 18.9 %copy-start.12 = (s32[8,15]{1,0:T(8,128)S(1)}, s32[8,15]{1,0:T(8,128)}, u32[]{:S(2)}) copy-start(s32[8,15]{1,0:T(8,128)} %param.17) | copy-start | bytes 1444
  0.7 18.9 %copy-start.9 = (s32[8,15,10]{1,0,2:T(8,128)S(1)}, s32[8,15,10]{1,0,2:T(8,128)}, u32[]{:S(2)}) copy-start(s32[8,15,10]{1,0,2:T(8,128)} %param.16) | copy-start | bytes 14404
  0.7 18.9 %copy-start.10 = (s32[8,15,10]{1,0,2:T(8,128)S(1)}, s32[8,15,10]{1,0,2:T(8,128)}, u32[]{:S(2)}) copy-start(s32[8,15,10]{1,0,2:T(8,128)} %param.18) | copy-start | bytes 14404
  0.7 19.3 %copy-start.13 = (s32[8]{0:T(128)S(1)}, s32[8]{0:T(128)}, u32[]{:S(2)}) copy-start(s32[8]{0:T(128)} %param.14) | copy-start | bytes 100
  3.6 31.3 %all-to-all-start = ((bf16[128,4,384]{2,1,0:T(4,128)(2,1)}), bf16[128,4,384]{2,1,0:T(4,128)(2,1)}, u32[]{:S(2)}, u32[]{:S(2)}) async-start(bf16[128,4,384]{2,1,0:T(4,128)(2,1)} %shard_map.138), calls=%async_computation | async-start | bytes 786432 | tf_op jit(solution)/shard_map/all_to_all | solution.py:385
  38.3 3.9 %collective-permute-start = (f32[128,1024]{1,0:T(8,128)}, f32[128,1024]{1,0:T(8,128)S(1)}, u32[]{:S(2)}, u32[]{:S(2)}) collective-permute-start(f32[128,1024]{1,0:T(8,128)} %get-tuple-element.31.refs_1_), channel_id=1, source_target_pairs={{0,1},{1,0},{2,3},{3,2},{4,5},{5,4},{6,7},{7,6},{8,9},{9,8},{10,11... | collective-permute-start | bytes 1572872 | tf_op jit(solution)/shard_map/ppermute | solution.py:348
  39.0 17.5 %collective-permute-start.1 = (bf16[384,384]{1,0:T(8,128)(2,1)}, bf16[384,384]{1,0:T(8,128)(2,1)}, u32[]{:S(2)}, u32[]{:S(2)}) collective-permute-start(bf16[384,384]{1,0:T(8,128)(2,1)} %get-tuple-element.35.refs_7_.refs_1_), channel_id=1, source_target_pairs={{0,64},{64,128},{128,192},{192,0},{1,65},{65,129},{129,193},{193,1... | collective-permute-start | bytes 884744 | tf_op jit(solution)/shard_map/ppermute | solution.py:348
  39.8 16.7 %collective-permute-start.2 = (bf16[384,384]{1,0:T(8,128)(2,1)}, bf16[384,384]{1,0:T(8,128)(2,1)}, u32[]{:S(2)}, u32[]{:S(2)}) collective-permute-start(bf16[384,384]{1,0:T(8,128)(2,1)} %get-tuple-element.35.refs_7_.refs_1_), channel_id=1, source_target_pairs={{0,192},{64,0},{128,64},{192,128},{1,193},{65,1},{129,65},{193,129... | collective-permute-start | bytes 884744 | tf_op jit(solution)/shard_map/ppermute | solution.py:348
  42.3 0.8 copy-start.14
  43.1 17.2 %copy-start.3 = (bf16[3,384,1024]{2,1,0:T(8,128)(2,1)S(1)}, bf16[3,384,1024]{2,1,0:T(8,128)(2,1)}, u32[]{:S(2)}) copy-start(bf16[3,384,1024]{2,1,0:T(8,128)(2,1)} %refs_3_.1) | copy-start | bytes 7077892
  43.1 17.2 %copy-start.5 = (bf16[512,384]{1,0:T(8,128)(2,1)S(1)}, bf16[512,384]{1,0:T(8,128)(2,1)}, u32[]{:S(2)}) copy-start(bf16[512,384]{1,0:T(8,128)(2,1)} %get-tuple-element.38.refs_2_) | copy-start | bytes 1179652
  43.1 17.2 %copy-start.7 = (f32[384,128]{1,0:T(8,128)S(1)}, f32[384,128]{1,0:T(8,128)}, u32[]{:S(2)}) copy-start(f32[384,128]{1,0:T(8,128)} %get-tuple-element.34.refs_5_.refs_1_) | copy-start | bytes 589828
  56.5 16.9 %collective-permute-start.5 = (bf16[1568,128]{1,0:T(8,128)(2,1)}, bf16[1568,128]{1,0:T(8,128)(2,1)}, u32[]{:S(2)}, u32[]{:S(2)}) collective-permute-start(bf16[1568,128]{1,0:T(8,128)(2,1)} %get-tuple-element.47), channel_id=1, source_target_pairs={{0,128},{64,192},{128,0},{192,64},{1,129},{65,193},{129,1},{193,65... | collective-permute-start | bytes 1204232 | tf_op jit(solution)/shard_map/ppermute | solution.py:348
  57.0 16.4 %collective-permute-start.4 = (bf16[208,256]{1,0:T(8,128)(2,1)}, bf16[208,256]{1,0:T(8,128)(2,1)}, u32[]{:S(2)}, u32[]{:S(2)}) collective-permute-start(bf16[208,256]{1,0:T(8,128)(2,1)} %get-tuple-element.46), channel_id=1, source_target_pairs={{0,64},{64,128},{128,192},{192,0},{1,65},{65,129},{129,193},{193,1... | collective-permute-start | bytes 319496 | tf_op jit(solution)/shard_map/ppermute | solution.py:348
  57.5 15.9 %collective-permute-start.6 = (bf16[208,256]{1,0:T(8,128)(2,1)}, bf16[208,256]{1,0:T(8,128)(2,1)}, u32[]{:S(2)}, u32[]{:S(2)}) collective-permute-start(bf16[208,256]{1,0:T(8,128)(2,1)} %get-tuple-element.48), channel_id=1, source_target_pairs={{0,192},{64,0},{128,64},{192,128},{1,193},{65,1},{129,65},{193,129... | collective-permute-start | bytes 319496 | tf_op jit(solution)/shard_map/ppermute | solution.py:348
  60.2 1.0 copy-start.6
  61.2 12.3 %copy-start.4 = (bf16[384,384]{1,0:T(8,128)(2,1)S(1)}, bf16[384,384]{1,0:T(8,128)(2,1)}, u32[]{:S(2)}) copy-start(bf16[384,384]{1,0:T(8,128)(2,1)} %get-tuple-element.35.refs_7_.refs_1_) | copy-start | bytes 884740
  61.2 12.3 %copy-start.8 = (bf16[208,256]{1,0:T(8,128)(2,1)S(1)}, bf16[208,256]{1,0:T(8,128)(2,1)}, u32[]{:S(2)}) copy-start(bf16[208,256]{1,0:T(8,128)(2,1)} %get-tuple-element.45.refs_4_) | copy-start | bytes 319492
  64.3 31.7 %all-to-all-start.1 = ((bf16[128,4,384]{2,1,0:T(4,128)(2,1)}), bf16[128,4,384]{2,1,0:T(4,128)(2,1)}, u32[]{:S(2)}, u32[]{:S(2)}) async-start(bf16[128,4,384]{2,1,0:T(4,128)(2,1)} %shard_map.142), calls=%async_computation.1 | async-start | bytes 786432 | tf_op jit(solution)/shard_map/all_to_all | solution.py:449
  76.4 25.1 %copy-start.2 = (s32[1,512]{1,0:T(1,128)S(1)}, s32[1,512]{1,0:T(1,128)}, u32[]{:S(2)}) copy-start(s32[1,512]{1,0:T(1,128)} %refs_0_.4) | copy-start | bytes 6148
  76.4 28.1 %copy-start = (f32[1024,384]{1,0:T(8,128)S(1)}, f32[1024,384]{1,0:T(8,128)}, u32[]{:S(2)}) copy-start(f32[1024,384]{1,0:T(8,128)} %refs_0_.5) | copy-start | bytes 4718596
  76.4 28.1 %copy-start.1 = (f32[1024]{0:T(1024)S(1)}, f32[1024]{0:T(1024)}, u32[]{:S(2)}) copy-start(f32[1024]{0:T(1024)} %param.12) | copy-start | bytes 12292
  76.5 11.7 %collective-permute-start.7 = (bf16[352,384]{1,0:T(8,128)(2,1)S(1)}, bf16[352,384]{1,0:T(8,128)(2,1)S(1)}, u32[]{:S(2)}, u32[]{:S(2)}) collective-permute-start(bf16[352,384]{1,0:T(8,128)(2,1)S(1)} %get-tuple-element.51), channel_id=1, source_target_pairs={{0,16},{16,32},{32,48},{48,0},{1,17},{17,33},{33,49},{49,1},{2,18}... | collective-permute-start | bytes 811016 | tf_op jit(solution)/shard_map/ppermute | solution.py:348
  78.1 12.3 %collective-permute-start.8 = (bf16[352,384]{1,0:T(8,128)(2,1)S(1)}, bf16[352,384]{1,0:T(8,128)(2,1)S(1)}, u32[]{:S(2)}, u32[]{:S(2)}) collective-permute-start(bf16[352,384]{1,0:T(8,128)(2,1)S(1)} %get-tuple-element.52), channel_id=1, source_target_pairs={{0,32},{16,48},{32,0},{48,16},{1,33},{17,49},{33,1},{49,17},{2,34}... | collective-permute-start | bytes 811016 | tf_op jit(solution)/shard_map/ppermute | solution.py:348
  79.7 15.1 %collective-permute-start.9 = (bf16[352,384]{1,0:T(8,128)(2,1)S(1)}, bf16[352,384]{1,0:T(8,128)(2,1)S(1)}, u32[]{:S(2)}, u32[]{:S(2)}) collective-permute-start(bf16[352,384]{1,0:T(8,128)(2,1)S(1)} %get-tuple-element.53), channel_id=1, source_target_pairs={{0,48},{16,0},{32,16},{48,32},{1,49},{17,1},{33,17},{49,33},{2,50}... | collective-permute-start | bytes 811016 | tf_op jit(solution)/shard_map/ppermute | solution.py:348
  96.0 18.9 %all-to-all-start.2 = ((bf16[8,8,2688]{2,1,0:T(8,128)(2,1)}), bf16[8,8,2688]{2,1,0:T(8,128)(2,1)S(1)}, u32[]{:S(2)}, u32[]{:S(2)}) async-start(bf16[8,8,2688]{2,1,0:T(8,128)(2,1)} %bitcast.6), calls=%async_computation.2 | async-start | bytes 688128 | tf_op jit(solution)/shard_map/all_to_all | solution.py:469
  103.3 1.2 %collective-permute-start.3 = (f32[8,128]{1,0:T(8,128)S(1)}, f32[8,128]{1,0:T(8,128)S(1)}, u32[]{:S(2)}, u32[]{:S(2)}) collective-permute-start(f32[8,128]{1,0:T(8,128)S(1)} %get-tuple-element.40.refs_3_), channel_id=1, source_target_pairs={{0,1},{1,0},{2,3},{3,2},{4,5},{5,4},{6,7},{7,6},{8,9},{9,8},{10,11... | collective-permute-start | bytes 12296 | tf_op jit(solution)/shard_map/ppermute | solution.py:348

commit v5 on v4

--- a/solution.py
+++ b/solution.py
@@ -51,12 +51,12 @@
         self.copy.start()
 
 
-def call(kernel, outs, operands, smem=0, scratch=(), hbm_in=(), hbm_out=(), raw_in=(), hbm_raw=()):
+def call(kernel, outs, operands, smem=0, scratch=(), hbm_in=(), hbm_out=(), hbm_raw=()):
     name = getattr(kernel, "func", kernel)
     limit, flops = LIMITS.get(name, 12), COSTS.get(name, 10**12)
     moved = sum(o.size * o.dtype.itemsize for o in list(operands) + list(outs))
     specs = [
-        pl.BlockSpec(memory_space=pltpu.SMEM if i < smem else pltpu.HBM if i in hbm_in or i in raw_in else pltpu.VMEM)
+        pl.BlockSpec(memory_space=pltpu.SMEM if i < smem else pltpu.HBM if i in hbm_in else pltpu.VMEM)
         for i in range(len(operands))
     ]
     made = [
@@ -209,7 +209,7 @@
             moves.append((chosen, pack))
             continue
         start = 0
-        for source in (chosen, layer_ref):
+        for source in (chosen, layer_ref.get()):
             rows, wide = source.shape
             for lane in range(0, wide, LANES):
                 moves.append((source.at[:, lane : lane + LANES], pack.at[start : start + rows, :]))
@@ -439,8 +439,7 @@
         ),
         smem=1,
         scratch=[pltpu.VMEM((n_x, *pack_shape), BF16), pltpu.SemaphoreType.DMA((n_x - 1 + (width + columns) // LANES,))],
-        hbm_in=(1, 2, 3, 4, 5),
-        raw_in=(7,),
+        hbm_in=(1, 2, 3, 4, 5, 7),
         hbm_raw=range(1, 1 + n_x),
     )
     packs = [packs[0]] + [shift(packs[d], "dp", d) for d in range(1, n_x)]

time: 116 us -> 110 us (0.948)
  Pallas kernels: 37.5 us -> 28.4 us
  waiting for transfers between devices: 31.3 us -> 33.4 us
  starting transfers between devices: 42.2 us -> 43.5 us
    pallas_call x10, Pallas kernels: 37.5 us -> 28.4 us  [call(): pl.pallas_call(wrapped, out_shape=tuple(outs), in_specs=specs, out_specs=...]
    ppermute x10, waiting for transfers between devices: 14.6 us -> 16.7 us  [shift(): lax.ppermute(array, axis, [(i, (i + by) % size) for i in range(size)])]
  transfers between devices with their start and end apart: 13 -> 13, of which waited for: 6 -> 7; matrix products, arithmetic and copies ran while one was open for 2% -> 2% of each run, Pallas kernels for 26% -> 19%
where the time goes in v5:
time: 110 us
  starting transfers between devices  43.5 us (40%)
  waiting for transfers between devices  33.4 us (30%)
  Pallas kernels  28.4 us (26%)
  local copies, waits for them, and re-layouts  2.32 us (2%)
  other arithmetic  1.38 us (1%)
    pallas_call x10, Pallas kernels, call(): pl.pallas_call(wrapped, out_shape=tuple(outs), in_specs=specs, out_specs=...  28.4 us
    ppermute x10, waiting for transfers between devices, shift(): lax.ppermute(array, axis, [(i, (i + by) % size) for i in range(size)])  16.7 us
    all_to_all x1, starting transfers between devices, body(): lax.all_to_all(outgoing, everyone, split_axis=0, concat_axis=0, tiled=True)  15.8 us
    ppermute x10, starting transfers between devices, shift(): lax.ppermute(array, axis, [(i, (i + by) % size) for i in range(size)])  13 us
    all_to_all x1, starting transfers between devices, body(): lax.all_to_all(slot_grad, everyone, split_axis=0, concat_axis=0, tiled=True)  9.32 us
    all_to_all x1, waiting for transfers between devices, body(): grads = lax.all_to_all(grads, 'z', split_axis=0, concat_axis=0, tiled=True)  8.81 us
    all_to_all x1, waiting for transfers between devices, body(): lax.all_to_all(outgoing, everyone, split_axis=0, concat_axis=0, tiled=True)  7.89 us
    all_to_all x1, starting transfers between devices, body(): grads = lax.all_to_all(grads, 'z', split_axis=0, concat_axis=0, tiled=True)  5.42 us
  transfers between devices with their start and end apart: 13, of which 7 were waited for; matrix products, arithmetic and copies ran while one was open for 2% of the time, Pallas kernels for 19%

profile of v5, /device:TPU:8, one launch (start us, length us, event | category | flops | bytes accessed | tf_op | source)
XLA Modules:
  0.0 109.9 jit_solution(8639557378687759156)
XLA Ops:
  0.7 2.9 %shard_map.138 = bf16[128,4,384]{2,1,0:T(4,128)(2,1)} custom-call(s32[1,512]{1,0:T(1,128)} %refs_0_.4, f32[1024,384]{1,0:T(8,128)} %refs_0_.5), custom_call_target="tpu_custom_call" | custom-call | flops 999999995904 | bytes 1968128 | tf_op jit(solution)/shard_map/pallas_call | solution.py:89
  3.6 15.8 %all-to-all-start = ((bf16[128,4,384]{2,1,0:T(4,128)(2,1)}), bf16[128,4,384]{2,1,0:T(4,128)(2,1)}, u32[]{:S(2)}, u32[]{:S(2)}) async-start(bf16[128,4,384]{2,1,0:T(4,128)(2,1)} %shard_map.138), calls=%async_computation | async-start | bytes 786432 | tf_op jit(solution)/shard_map/all_to_all | solution.py:385
  19.4 0.1 reshape.29
  19.5 0.1 reshape.31
  19.6 0.1 reshape.30
  19.7 0.1 pad.6.clone
  19.8 0.1 pad_add_fusion.1
  19.9 0.1 copy.30
  20.0 0.1 copy.29
  20.1 0.7 pad_add_fusion.refs_0_
  20.8 6.3 %shard_map.139 = (bf16[384,512]{1,0:T(8,128)(2,1)}, bf16[512,384]{1,0:T(8,128)(2,1)}, f32[384,128]{1,0:T(8,128)}, bf16[32,128]{1,0:T(8,128)(2,1)}, f32[128,1024]{1,0:T(8,128)}) custom-call(s32[128,17]{1,0:T(8,128)} %pad_add_fusion.refs_0_, bf16[8,1024]{1,0:T(8,128)(2,1)} %refs_6_.1, bf16[3,1024,1024]{2,1,0:T(8,128)(2,1)} %refs_2_.2), custom_call_target="tpu_custom_call" | custom-call | flops 999999995904 | bytes 7832064 | tf_op jit(solution)/shard_map/pallas_call | solution.py:89
  27.1 7.9 %all-to-all-done.refs_0_ = bf16[128,4,384]{2,1,0:T(4,128)(2,1)} async-done(((bf16[128,4,384]{2,1,0:T(4,128)(2,1)}), bf16[128,4,384]{2,1,0:T(4,128)(2,1)}, u32[]{:S(2)}, u32[]{:S(2)}) %all-to-all-start) | async-done | bytes 393248 | tf_op jit(solution)/shard_map/all_to_all | solution.py:385
  35.0 3.3 %shard_map.140 = (bf16[384,384]{1,0:T(8,128)(2,1)}, f32[128,1024]{1,0:T(8,128)}) custom-call(bf16[128,4,384]{2,1,0:T(4,128)(2,1)} %all-to-all-done.refs_0_, bf16[384,512]{1,0:T(8,128)(2,1)} %get-tuple-element.30.refs_1_, bf16[3,384,1024]{2,1,0:T(8,128)(2,1)} %refs_3_.1), custom_call_target="tpu_custom_call" | custom-call | flops 999999995904 | bytes 3964928 | tf_op jit(solution)/shard_map/pallas_call | solution.py:89
  38.3 0.1 collective-permute-start
  38.4 0.6 pad_add_fusion.2.refs_0_
  39.0 0.8 collective-permute-start.1
  39.8 2.5 %collective-permute-start.2 = (bf16[384,384]{1,0:T(8,128)(2,1)}, bf16[384,384]{1,0:T(8,128)(2,1)}, u32[]{:S(2)}, u32[]{:S(2)}) collective-permute-start(bf16[384,384]{1,0:T(8,128)(2,1)} %get-tuple-element.35.refs_7_.refs_1_), channel_id=1, source_target_pairs={{0,192},{64,0},{128,64},{192,128},{1,193},{65,1},{129,65},{193,129... | collective-permute-start | bytes 884744 | tf_op jit(solution)/shard_map/ppermute | solution.py:348
  42.3 0.8 copy-done.14
  43.1 4.3 %shard_map.141 = (bf16[128,1024]{1,0:T(8,128)(2,1)}, bf16[208,256]{1,0:T(8,128)(2,1)}, bf16[208,256]{1,0:T(8,128)(2,1)}, bf16[1568,128]{1,0:T(8,128)(2,1)}, bf16[208,256]{1,0:T(8,128)(2,1)}) custom-call(s32[2]{0:T(128)} %pad_add_fusion.2.refs_0_, f32[128,1024]{1,0:T(8,128)} %get-tuple-element.31.refs_1_, f32[128,1024]{1,0:T(8,128)} %copy-done.14, ...), custom_call_target="tpu_custom_call" | custom-call | flops 999999995904 | bytes 3072008 | tf_op jit(solution)/shard_map/pallas_call | solution.py:89
  47.4 2.5 %collective-permute-done.1.refs_2_ = bf16[384,384]{1,0:T(8,128)(2,1)} collective-permute-done((bf16[384,384]{1,0:T(8,128)(2,1)}, bf16[384,384]{1,0:T(8,128)(2,1)}, u32[]{:S(2)}, u32[]{:S(2)}) %collective-permute-start.1) | collective-permute-done | bytes 294944 | tf_op jit(solution)/shard_map/ppermute | solution.py:348
  49.9 0.0 collective-permute-done.2.refs_3_
  50.0 1.5 %collective-permute-start.5 = (bf16[1568,128]{1,0:T(8,128)(2,1)}, bf16[1568,128]{1,0:T(8,128)(2,1)}, u32[]{:S(2)}, u32[]{:S(2)}) collective-permute-start(bf16[1568,128]{1,0:T(8,128)(2,1)} %get-tuple-element.47), channel_id=1, source_target_pairs={{0,128},{64,192},{128,0},{192,64},{1,129},{65,193},{129,1},{193,65... | collective-permute-start | bytes 1204232 | tf_op jit(solution)/shard_map/ppermute | solution.py:348
  51.4 2.3 %collective-permute-start.4 = (bf16[208,256]{1,0:T(8,128)(2,1)}, bf16[208,256]{1,0:T(8,128)(2,1)}, u32[]{:S(2)}, u32[]{:S(2)}) collective-permute-start(bf16[208,256]{1,0:T(8,128)(2,1)} %get-tuple-element.46), channel_id=1, source_target_pairs={{0,64},{64,128},{128,192},{192,0},{1,65},{65,129},{129,193},{193,1... | collective-permute-start | bytes 319496 | tf_op jit(solution)/shard_map/ppermute | solution.py:348
  53.8 0.9 collective-permute-start.6
  54.7 0.9 copy-done.6
  55.6 3.1 %shard_map.142 = bf16[128,4,384]{2,1,0:T(4,128)(2,1)} custom-call(bf16[128,1024]{1,0:T(8,128)(2,1)S(1)} %copy-done.6, f32[384,128]{1,0:T(8,128)S(1)} %copy-done.7, bf16[512,384]{1,0:T(8,128)(2,1)S(1)} %copy-done.5, bf16[3,384,1024]{2,1,0:T(8,128)(2,1)S(1)} %copy-done.3), custom_call_target="tpu_custom_call" | custom-call | flops 999999995904 | bytes 3604480 | tf_op jit(solution)/shard_map/pallas_call | solution.py:89
  58.8 9.3 %all-to-all-start.1 = ((bf16[128,4,384]{2,1,0:T(4,128)(2,1)}), bf16[128,4,384]{2,1,0:T(4,128)(2,1)}, u32[]{:S(2)}, u32[]{:S(2)}) async-start(bf16[128,4,384]{2,1,0:T(4,128)(2,1)} %shard_map.142), calls=%async_computation.1 | async-start | bytes 786432 | tf_op jit(solution)/shard_map/all_to_all | solution.py:448
  68.1 0.0 collective-permute-done.4.refs_5_
  68.1 0.0 collective-permute-done.5.refs_6_
  68.2 3.0 %shard_map.145 = (f32[64,1152]{1,0:T(8,128)S(1)}, bf16[352,384]{1,0:T(8,128)(2,1)S(1)}, bf16[352,384]{1,0:T(8,128)(2,1)S(1)}, bf16[352,384]{1,0:T(8,128)(2,1)S(1)}, bf16[352,384]{1,0:T(8,128)(2,1)S(1)}) custom-call(s32[1]{0:T(128)} %bitcast.5.refs_0_, bf16[384,384]{1,0:T(8,128)(2,1)S(1)} %copy-done.4, bf16[384,384]{1,0:T(8,128)(2,1)} %collective-permute-done.1.refs_2_, ...), custom_call_target="tpu_custom_call" | custom-call | flops 999999995904 | bytes 2981892 | tf_op jit(solution)/shard_map/pallas_call | solution.py:89
  71.1 0.0 copy-start.2
  71.2 0.0 copy-start
  71.2 0.0 copy-start.1
  71.2 1.6 %collective-permute-start.7 = (bf16[352,384]{1,0:T(8,128)(2,1)S(1)}, bf16[352,384]{1,0:T(8,128)(2,1)S(1)}, u32[]{:S(2)}, u32[]{:S(2)}) collective-permute-start(bf16[352,384]{1,0:T(8,128)(2,1)S(1)} %get-tuple-element.51), channel_id=1, source_target_pairs={{0,16},{16,32},{32,48},{48,0},{1,17},{17,33},{33,49},{49,1},{2,18}... | collective-permute-start | bytes 811016 | tf_op jit(solution)/shard_map/ppermute | solution.py:348
  72.8 1.6 %collective-permute-start.8 = (bf16[352,384]{1,0:T(8,128)(2,1)S(1)}, bf16[352,384]{1,0:T(8,128)(2,1)S(1)}, u32[]{:S(2)}, u32[]{:S(2)}) collective-permute-start(bf16[352,384]{1,0:T(8,128)(2,1)S(1)} %get-tuple-element.52), channel_id=1, source_target_pairs={{0,32},{16,48},{32,0},{48,16},{1,33},{17,49},{33,1},{49,17},{2,34}... | collective-permute-start | bytes 811016 | tf_op jit(solution)/shard_map/ppermute | solution.py:348
  74.4 1.7 %collective-permute-start.9 = (bf16[352,384]{1,0:T(8,128)(2,1)S(1)}, bf16[352,384]{1,0:T(8,128)(2,1)S(1)}, u32[]{:S(2)}, u32[]{:S(2)}) collective-permute-start(bf16[352,384]{1,0:T(8,128)(2,1)S(1)} %get-tuple-element.53), channel_id=1, source_target_pairs={{0,48},{16,0},{32,16},{48,32},{1,49},{17,1},{33,17},{49,33},{2,50}... | collective-permute-start | bytes 811016 | tf_op jit(solution)/shard_map/ppermute | solution.py:348
  76.1 6.5 %collective-permute-done.7.refs_2_ = bf16[352,384]{1,0:T(8,128)(2,1)S(1)} collective-permute-done((bf16[352,384]{1,0:T(8,128)(2,1)S(1)}, bf16[352,384]{1,0:T(8,128)(2,1)S(1)}, u32[]{:S(2)}, u32[]{:S(2)}) %collective-permute-start.7) | collective-permute-done | bytes 270368 | tf_op jit(solution)/shard_map/ppermute | solution.py:348
  82.6 2.3 %collective-permute-done.8.refs_3_ = bf16[352,384]{1,0:T(8,128)(2,1)S(1)} collective-permute-done((bf16[352,384]{1,0:T(8,128)(2,1)S(1)}, bf16[352,384]{1,0:T(8,128)(2,1)S(1)}, u32[]{:S(2)}, u32[]{:S(2)}) %collective-permute-start.8) | collective-permute-done | bytes 270368 | tf_op jit(solution)/shard_map/ppermute | solution.py:348
  84.9 4.2 %collective-permute-done.9.refs_4_ = bf16[352,384]{1,0:T(8,128)(2,1)S(1)} collective-permute-done((bf16[352,384]{1,0:T(8,128)(2,1)S(1)}, bf16[352,384]{1,0:T(8,128)(2,1)S(1)}, u32[]{:S(2)}, u32[]{:S(2)}) %collective-permute-start.9) | collective-permute-done | bytes 270368 | tf_op jit(solution)/shard_map/ppermute | solution.py:348
  89.1 1.2 %shard_map.146 = bf16[64,2688]{1,0:T(8,128)(2,1)} custom-call(f32[64,1152]{1,0:T(8,128)S(1)} %get-tuple-element.49.refs_0_, bf16[352,384]{1,0:T(8,128)(2,1)S(1)} %get-tuple-element.50.refs_1_, bf16[352,384]{1,0:T(8,128)(2,1)S(1)} %collective-permute-done.7.refs_2_, bf16[352,384]{1,0:T(8,128)(2,1)S(1)} %collective-permute-done.8.refs_3_, ...), custom_call_target="tpu_custom_call" | custom-call | bytes 1720320 | tf_op jit(solution)/shard_map/pallas_call | solution.py:89
  90.3 0.0 all-to-all-done.1.refs_1_
  90.3 5.4 %all-to-all-start.2 = ((bf16[8,8,2688]{2,1,0:T(8,128)(2,1)}), bf16[8,8,2688]{2,1,0:T(8,128)(2,1)S(1)}, u32[]{:S(2)}, u32[]{:S(2)}) async-start(bf16[8,8,2688]{2,1,0:T(8,128)(2,1)} %bitcast.6), calls=%async_computation.2 | async-start | bytes 688128 | tf_op jit(solution)/shard_map/all_to_all | solution.py:468
  95.7 1.8 %shard_map.143 = (f32[1024,384]{1,0:T(8,128)S(1)}, f32[8,128]{1,0:T(8,128)S(1)}) custom-call(s32[1,512]{1,0:T(1,128)S(1)} %copy-done.2, bf16[128,4,384]{2,1,0:T(4,128)(2,1)} %all-to-all-done.1.refs_1_), custom_call_target="tpu_custom_call" | custom-call | bytes 1972224 | tf_op jit(solution)/shard_map/pallas_call | solution.py:89
  97.6 0.1 collective-permute-start.3
  97.7 1.2 %collective-permute-done.3.refs_4_ = f32[8,128]{1,0:T(8,128)S(1)} collective-permute-done((f32[8,128]{1,0:T(8,128)S(1)}, f32[8,128]{1,0:T(8,128)S(1)}, u32[]{:S(2)}, u32[]{:S(2)}) %collective-permute-start.3) | collective-permute-done | bytes 4128 | tf_op jit(solution)/shard_map/ppermute | solution.py:348
  98.8 1.6 %shard_map.144 = (f32[1024,384]{1,0:T(8,128)}, f32[8,128]{1,0:T(8,128)}) custom-call(f32[1024,384]{1,0:T(8,128)S(1)} %copy-done, f32[1024,384]{1,0:T(8,128)S(1)} %get-tuple-element.39.refs_1_, f32[8,128]{1,0:T(8,128)S(1)} %bitcast.11, f32[8,128]{1,0:T(8,128)S(1)} %get-tuple-element.40.refs_3_, f32[8,128]{1,0:T(8,128)S(1)} %collective-permute-done.3.refs_4_), custom_call_target="tpu_custom_call" | custom-call | bytes 4734976 | tf_op jit(solution)/shard_map/pallas_call | solution.py:89
  100.4 8.8 %all-to-all-done.2.refs_0_ = bf16[8,8,2688]{2,1,0:T(8,128)(2,1)S(1)} async-done(((bf16[8,8,2688]{2,1,0:T(8,128)(2,1)}), bf16[8,8,2688]{2,1,0:T(8,128)(2,1)S(1)}, u32[]{:S(2)}, u32[]{:S(2)}) %all-to-all-start.2) | async-done | bytes 344096 | tf_op jit(solution)/shard_map/all_to_all | solution.py:468
  109.2 0.7 shard_map.147
  (31 shorter events, 0.1 us)
Async XLA Ops:
  0.6 18.8 %copy-start.11 = (s32[8,15]{1,0:T(8,128)S(1)}, s32[8,15]{1,0:T(8,128)}, u32[]{:S(2)}) copy-start(s32[8,15]{1,0:T(8,128)} %param.15) | copy-start | bytes 1444
  0.6 18.9 %copy-start.12 = (s32[8,15]{1,0:T(8,128)S(1)}, s32[8,15]{1,0:T(8,128)}, u32[]{:S(2)}) copy-start(s32[8,15]{1,0:T(8,128)} %param.17) | copy-start | bytes 1444
  0.7 18.9 %copy-start.9 = (s32[8,15,10]{1,0,2:T(8,128)S(1)}, s32[8,15,10]{1,0,2:T(8,128)}, u32[]{:S(2)}) copy-start(s32[8,15,10]{1,0,2:T(8,128)} %param.16) | copy-start | bytes 14404
  0.7 18.9 %copy-start.10 = (s32[8,15,10]{1,0,2:T(8,128)S(1)}, s32[8,15,10]{1,0,2:T(8,128)}, u32[]{:S(2)}) copy-start(s32[8,15,10]{1,0,2:T(8,128)} %param.18) | copy-start | bytes 14404
  0.7 19.3 %copy-start.13 = (s32[8]{0:T(128)S(1)}, s32[8]{0:T(128)}, u32[]{:S(2)}) copy-start(s32[8]{0:T(128)} %param.14) | copy-start | bytes 100
  3.6 31.3 %all-to-all-start = ((bf16[128,4,384]{2,1,0:T(4,128)(2,1)}), bf16[128,4,384]{2,1,0:T(4,128)(2,1)}, u32[]{:S(2)}, u32[]{:S(2)}) async-start(bf16[128,4,384]{2,1,0:T(4,128)(2,1)} %shard_map.138), calls=%async_computation | async-start | bytes 786432 | tf_op jit(solution)/shard_map/all_to_all | solution.py:385
  38.3 3.9 %collective-permute-start = (f32[128,1024]{1,0:T(8,128)}, f32[128,1024]{1,0:T(8,128)S(1)}, u32[]{:S(2)}, u32[]{:S(2)}) collective-permute-start(f32[128,1024]{1,0:T(8,128)} %get-tuple-element.31.refs_1_), channel_id=1, source_target_pairs={{0,1},{1,0},{2,3},{3,2},{4,5},{5,4},{6,7},{7,6},{8,9},{9,8},{10,11... | collective-permute-start | bytes 1572872 | tf_op jit(solution)/shard_map/ppermute | solution.py:348
  39.0 10.9 %collective-permute-start.1 = (bf16[384,384]{1,0:T(8,128)(2,1)}, bf16[384,384]{1,0:T(8,128)(2,1)}, u32[]{:S(2)}, u32[]{:S(2)}) collective-permute-start(bf16[384,384]{1,0:T(8,128)(2,1)} %get-tuple-element.35.refs_7_.refs_1_), channel_id=1, source_target_pairs={{0,64},{64,128},{128,192},{192,0},{1,65},{65,129},{129,193},{193,1... | collective-permute-start | bytes 884744 | tf_op jit(solution)/shard_map/ppermute | solution.py:348
  39.8 10.1 %collective-permute-start.2 = (bf16[384,384]{1,0:T(8,128)(2,1)}, bf16[384,384]{1,0:T(8,128)(2,1)}, u32[]{:S(2)}, u32[]{:S(2)}) collective-permute-start(bf16[384,384]{1,0:T(8,128)(2,1)} %get-tuple-element.35.refs_7_.refs_1_), channel_id=1, source_target_pairs={{0,192},{64,0},{128,64},{192,128},{1,193},{65,1},{129,65},{193,129... | collective-permute-start | bytes 884744 | tf_op jit(solution)/shard_map/ppermute | solution.py:348
  42.3 0.8 copy-start.14
  43.1 11.6 %copy-start.3 = (bf16[3,384,1024]{2,1,0:T(8,128)(2,1)S(1)}, bf16[3,384,1024]{2,1,0:T(8,128)(2,1)}, u32[]{:S(2)}) copy-start(bf16[3,384,1024]{2,1,0:T(8,128)(2,1)} %refs_3_.1) | copy-start | bytes 7077892
  43.1 11.6 %copy-start.5 = (bf16[512,384]{1,0:T(8,128)(2,1)S(1)}, bf16[512,384]{1,0:T(8,128)(2,1)}, u32[]{:S(2)}) copy-start(bf16[512,384]{1,0:T(8,128)(2,1)} %get-tuple-element.38.refs_2_) | copy-start | bytes 1179652
  43.1 11.6 %copy-start.7 = (f32[384,128]{1,0:T(8,128)S(1)}, f32[384,128]{1,0:T(8,128)}, u32[]{:S(2)}) copy-start(f32[384,128]{1,0:T(8,128)} %get-tuple-element.34.refs_5_.refs_1_) | copy-start | bytes 589828
  50.0 18.2 %collective-permute-start.5 = (bf16[1568,128]{1,0:T(8,128)(2,1)}, bf16[1568,128]{1,0:T(8,128)(2,1)}, u32[]{:S(2)}, u32[]{:S(2)}) collective-permute-start(bf16[1568,128]{1,0:T(8,128)(2,1)} %get-tuple-element.47), channel_id=1, source_target_pairs={{0,128},{64,192},{128,0},{192,64},{1,129},{65,193},{129,1},{193,65... | collective-permute-start | bytes 1204232 | tf_op jit(solution)/shard_map/ppermute | solution.py:348
  51.4 16.7 %collective-permute-start.4 = (bf16[208,256]{1,0:T(8,128)(2,1)}, bf16[208,256]{1,0:T(8,128)(2,1)}, u32[]{:S(2)}, u32[]{:S(2)}) collective-permute-start(bf16[208,256]{1,0:T(8,128)(2,1)} %get-tuple-element.46), channel_id=1, source_target_pairs={{0,64},{64,128},{128,192},{192,0},{1,65},{65,129},{129,193},{193,1... | collective-permute-start | bytes 319496 | tf_op jit(solution)/shard_map/ppermute | solution.py:348
  53.8 14.4 %collective-permute-start.6 = (bf16[208,256]{1,0:T(8,128)(2,1)}, bf16[208,256]{1,0:T(8,128)(2,1)}, u32[]{:S(2)}, u32[]{:S(2)}) collective-permute-start(bf16[208,256]{1,0:T(8,128)(2,1)} %get-tuple-element.48), channel_id=1, source_target_pairs={{0,192},{64,0},{128,64},{192,128},{1,193},{65,1},{129,65},{193,129... | collective-permute-start | bytes 319496 | tf_op jit(solution)/shard_map/ppermute | solution.py:348
  54.7 1.0 copy-start.6
  55.6 12.5 %copy-start.4 = (bf16[384,384]{1,0:T(8,128)(2,1)S(1)}, bf16[384,384]{1,0:T(8,128)(2,1)}, u32[]{:S(2)}) copy-start(bf16[384,384]{1,0:T(8,128)(2,1)} %get-tuple-element.35.refs_7_.refs_1_) | copy-start | bytes 884740
  55.6 12.5 %copy-start.8 = (bf16[208,256]{1,0:T(8,128)(2,1)S(1)}, bf16[208,256]{1,0:T(8,128)(2,1)}, u32[]{:S(2)}) copy-start(bf16[208,256]{1,0:T(8,128)(2,1)} %get-tuple-element.45.refs_4_) | copy-start | bytes 319492
  58.8 31.5 %all-to-all-start.1 = ((bf16[128,4,384]{2,1,0:T(4,128)(2,1)}), bf16[128,4,384]{2,1,0:T(4,128)(2,1)}, u32[]{:S(2)}, u32[]{:S(2)}) async-start(bf16[128,4,384]{2,1,0:T(4,128)(2,1)} %shard_map.142), calls=%async_computation.1 | async-start | bytes 786432 | tf_op jit(solution)/shard_map/all_to_all | solution.py:448
  71.1 24.6 %copy-start.2 = (s32[1,512]{1,0:T(1,128)S(1)}, s32[1,512]{1,0:T(1,128)}, u32[]{:S(2)}) copy-start(s32[1,512]{1,0:T(1,128)} %refs_0_.4) | copy-start | bytes 6148
  71.2 27.7 %copy-start = (f32[1024,384]{1,0:T(8,128)S(1)}, f32[1024,384]{1,0:T(8,128)}, u32[]{:S(2)}) copy-start(f32[1024,384]{1,0:T(8,128)} %refs_0_.5) | copy-start | bytes 4718596
  71.2 27.6 %copy-start.1 = (f32[1024]{0:T(1024)S(1)}, f32[1024]{0:T(1024)}, u32[]{:S(2)}) copy-start(f32[1024]{0:T(1024)} %param.12) | copy-start | bytes 12292
  71.2 11.4 %collective-permute-start.7 = (bf16[352,384]{1,0:T(8,128)(2,1)S(1)}, bf16[352,384]{1,0:T(8,128)(2,1)S(1)}, u32[]{:S(2)}, u32[]{:S(2)}) collective-permute-start(bf16[352,384]{1,0:T(8,128)(2,1)S(1)} %get-tuple-element.51), channel_id=1, source_target_pairs={{0,16},{16,32},{32,48},{48,0},{1,17},{17,33},{33,49},{49,1},{2,18}... | collective-permute-start | bytes 811016 | tf_op jit(solution)/shard_map/ppermute | solution.py:348
  72.8 12.1 %collective-permute-start.8 = (bf16[352,384]{1,0:T(8,128)(2,1)S(1)}, bf16[352,384]{1,0:T(8,128)(2,1)S(1)}, u32[]{:S(2)}, u32[]{:S(2)}) collective-permute-start(bf16[352,384]{1,0:T(8,128)(2,1)S(1)} %get-tuple-element.52), channel_id=1, source_target_pairs={{0,32},{16,48},{32,0},{48,16},{1,33},{17,49},{33,1},{49,17},{2,34}... | collective-permute-start | bytes 811016 | tf_op jit(solution)/shard_map/ppermute | solution.py:348
  74.4 14.7 %collective-permute-start.9 = (bf16[352,384]{1,0:T(8,128)(2,1)S(1)}, bf16[352,384]{1,0:T(8,128)(2,1)S(1)}, u32[]{:S(2)}, u32[]{:S(2)}) collective-permute-start(bf16[352,384]{1,0:T(8,128)(2,1)S(1)} %get-tuple-element.53), channel_id=1, source_target_pairs={{0,48},{16,0},{32,16},{48,32},{1,49},{17,1},{33,17},{49,33},{2,50}... | collective-permute-start | bytes 811016 | tf_op jit(solution)/shard_map/ppermute | solution.py:348
  90.3 18.9 %all-to-all-start.2 = ((bf16[8,8,2688]{2,1,0:T(8,128)(2,1)}), bf16[8,8,2688]{2,1,0:T(8,128)(2,1)S(1)}, u32[]{:S(2)}, u32[]{:S(2)}) async-start(bf16[8,8,2688]{2,1,0:T(8,128)(2,1)} %bitcast.6), calls=%async_computation.2 | async-start | bytes 688128 | tf_op jit(solution)/shard_map/all_to_all | solution.py:468
  97.6 1.2 %collective-permute-start.3 = (f32[8,128]{1,0:T(8,128)S(1)}, f32[8,128]{1,0:T(8,128)S(1)}, u32[]{:S(2)}, u32[]{:S(2)}) collective-permute-start(f32[8,128]{1,0:T(8,128)S(1)} %get-tuple-element.40.refs_3_), channel_id=1, source_target_pairs={{0,1},{1,0},{2,3},{3,2},{4,5},{5,4},{6,7},{7,6},{8,9},{9,8},{10,11... | collective-permute-start | bytes 12296 | tf_op jit(solution)/shard_map/ppermute | solution.py:348

commit v6 on v5

--- a/solution.py
+++ b/solution.py
@@ -290,8 +290,8 @@
         out[out.shape[0] - group :, :] = chosen.astype(BF16)
 
 
-def group_kernel(relations, own_ref, *refs):
-    packs, out_ref = refs[:-1], refs[-1]
+def group_kernel(relations, count, place_ref, own_ref, *refs):
+    packs, outs, out_ref = refs[:count], refs[count:-1], refs[-1]
     rows = own_ref.shape[0]
     columns = packs[0].shape[1]
     tail = relations * rows
@@ -303,17 +303,24 @@
         block = own_ref[:, span]
         for pack in packs[1:]:
             block = block + pack[k * rows : (k + 1) * rows, :].astype(F32)
-        out_ref[:, span] = block.astype(BF16)
+        out_ref[:, span] = block
     cots = jnp.concatenate([p[tail + pieces * group :, :] for p in packs], 0)
     for piece in range(pieces):
         first = tail + piece * group
         second = jnp.concatenate([p[first : first + group, :] for p in packs], 0)
         start = (relations + piece) * columns
-        out_ref[:, start : start + columns] = matmul(cots, second, (0, 0))[:rows].astype(BF16)
-
-
-def sum_kernel(parts_ref, one_ref, two_ref):
-    total = jnp.sum(parts_ref[...].astype(F32), axis=0)
+        out_ref[:, start : start + columns] = matmul(cots, second, (0, 0))[:rows]
+    part = outs[0].shape[0]
+    for d, out in enumerate(outs):
+        start = pl.multiple_of(lax.rem(place_ref[0] + d, len(outs)) * part, part)
+        out[...] = out_ref[pl.ds(start, part), :].astype(out.dtype)
+
+
+def sum_kernel(*refs):
+    parts, (one_ref, two_ref) = refs[:-2], refs[-2:]
+    total = parts[0][...]
+    for part in parts[1:]:
+        total = total + part[...].astype(F32)
     start = 0
     for ref in (one_ref, two_ref):
         wide = ref.shape[2]
@@ -348,8 +355,8 @@
     return lax.ppermute(array, axis, [(i, (i + by) % size) for i in range(size)])
 
 
-LIMITS = {serve_kernel: 60, index_kernel: 60, first_kernel: 60, hidden_kernel: 60, slot_kernel: 50}
-COSTS = {update_kernel: 0, group_kernel: 0, row_kernel: 0}
+LIMITS = {serve_kernel: 60, index_kernel: 60, first_kernel: 60, hidden_kernel: 60, slot_kernel: 60}
+COSTS = {update_kernel: 0, row_kernel: 0}
 
 
 def body(
@@ -375,7 +382,7 @@
     layers, hidden_units = w_second.shape[:2]
     half = hidden_units // 2
     n_x, n_y, n_z = (lax.axis_size(a) for a in everyone)
-    x, y = lax.axis_index("dp"), lax.axis_index("y")
+    x, y, z = (lax.axis_index(a) for a in everyone)
     width = hidden_units // n_x
 
     blocks_shape = (owners, slots // owners, columns)
@@ -396,6 +403,7 @@
         ],
         0,
     )
+    idx, place, y, z = lax.optimization_barrier((idx, jnp.stack([lax.axis_index("col"), x]), y, z))
     ct, c, inverse, member, back_hidden = call(
         index_kernel,
         [
@@ -428,7 +436,7 @@
         hidden_kernel,
         [shaped((nodes, hidden_units), BF16)] + [shaped(far_shape if d == far else pack_shape, BF16) for d in range(n_x)],
         (
-            jnp.stack([lax.axis_index("col"), x]),
+            place,
             partial_pre,
             other_pre,
             back_hidden,
@@ -442,11 +450,8 @@
         hbm_in=(1, 2, 3, 4, 5, 7),
         hbm_raw=range(1, 1 + n_x),
     )
+    packs, layer_parts = lax.optimization_barrier((packs, layer_parts))
     packs = [packs[0]] + [shift(packs[d], "dp", d) for d in range(1, n_x)]
-    back, *layer_parts[1:] = lax.optimization_barrier((back, *layer_parts[1:]))
-    slot_grad = call(slot_kernel, [shaped(blocks_shape, BF16)], (back, inverse, c, w_first), hbm_in=(1, 2, 3))[0]
-    arrived = lax.all_to_all(slot_grad, everyone, split_axis=0, concat_axis=0, tiled=True)
-
     block_rows = width // n_y
     group_rows = layers * block_rows + (layers * half // columns + 1) * n_x * seeds
     own, *blocks = call(
@@ -457,19 +462,23 @@
         hbm_in=range(1, n_x),
         scratch=[pltpu.VMEM((layers, width, columns), F32)],
     )
+    back, own = lax.optimization_barrier((back, own))
+    slot_grad = call(slot_kernel, [shaped(blocks_shape, BF16)], (back, inverse, c, w_first), hbm_in=(1, 2, 3))[0]
+    arrived = lax.all_to_all(slot_grad, everyone, split_axis=0, concat_axis=0, tiled=True)
+
     blocks = [blocks[0]] + [shift(blocks[d], "y", d) for d in range(1, n_y)]
     grad_columns = layers * (columns + half)
-    grads = call(
-        functools.partial(group_kernel, layers),
-        [shaped((block_rows, grad_columns), BF16)],
-        (own, *blocks),
-    )[0]
-    grads = grads.reshape(n_z, block_rows // n_z, grad_columns)
-    grads = lax.all_to_all(grads, "z", split_axis=0, concat_axis=0, tiled=True)
+    rows = block_rows // n_z
+    own, *parts = call(
+        functools.partial(group_kernel, layers, n_y),
+        [shaped((rows, grad_columns), F32 if d == 0 else BF16) for d in range(n_z)],
+        (z.reshape(1), own, *blocks),
+        smem=1,
+        scratch=[pltpu.VMEM((block_rows, grad_columns), F32)],
+    )
+    parts = [shift(part, "z", d) for d, part in enumerate(parts, 1)]
     grad_one, grad_two = call(
-        sum_kernel,
-        [shaped((layers, block_rows // n_z, wide), F32) for wide in (columns, half)],
-        (grads,),
+        sum_kernel, [shaped((layers, rows, wide), F32) for wide in (columns, half)], (own, *parts)
     )
     grad_one, grad_two = grad_one.transpose(0, 2, 1), grad_two.transpose(0, 2, 1)
 

time: 110 us -> 116 us (1.055)
  the two profiles are of different devices: /device:TPU:8 before, /device:TPU:1 now
where the time goes in v6:
time: 116 us; the launch traced here: 115 us
  starting transfers between devices  56.1 us (48%)
  Pallas kernels  32.1 us (28%)
  waiting for transfers between devices  22 us (19%)
  local copies, waits for them, and re-layouts  3.2 us (3%)
    pallas_call x10, Pallas kernels, call(): pl.pallas_call(wrapped, out_shape=tuple(outs), in_specs=specs, out_specs=...  32.1 us
    ppermute x17, starting transfers between devices, shift(): lax.ppermute(array, axis, [(i, (i + by) % size) for i in range(size)])  30.8 us
    all_to_all x1, starting transfers between devices, body(): lax.all_to_all(outgoing, everyone, split_axis=0, concat_axis=0, tiled=True)  16.8 us
    ppermute x17, waiting for transfers between devices, shift(): lax.ppermute(array, axis, [(i, (i + by) % size) for i in range(size)])  14.1 us
    all_to_all x1, starting transfers between devices, body(): lax.all_to_all(slot_grad, everyone, split_axis=0, concat_axis=0, tiled=True)  8.48 us
    all_to_all x1, waiting for transfers between devices, body(): lax.all_to_all(outgoing, everyone, split_axis=0, concat_axis=0, tiled=True)  7.85 us
  transfers between devices with their start and end apart: 19, of which 4 were waited for; matrix products, arithmetic and copies ran while one was open for 2% of the time, Pallas kernels for 18%

profile of v6, /device:TPU:1, one launch (start us, length us, event | category | flops | bytes accessed | tf_op | source)
XLA Modules:
  0.0 115.0 jit_solution(15969715291350649409)
XLA Ops:
  0.7 2.9 %shard_map.138 = bf16[128,4,384]{2,1,0:T(4,128)(2,1)} custom-call(s32[1,512]{1,0:T(1,128)} %refs_0_.4, f32[1024,384]{1,0:T(8,128)} %refs_0_.5), custom_call_target="tpu_custom_call" | custom-call | flops 999999995904 | bytes 1968128 | tf_op jit(solution)/shard_map/pallas_call | solution.py:89
  3.6 16.8 %all-to-all-start = ((bf16[128,4,384]{2,1,0:T(4,128)(2,1)}), bf16[128,4,384]{2,1,0:T(4,128)(2,1)}, u32[]{:S(2)}, u32[]{:S(2)}) async-start(bf16[128,4,384]{2,1,0:T(4,128)(2,1)} %shard_map.138), calls=%async_computation | async-start | bytes 786432 | tf_op jit(solution)/shard_map/all_to_all | solution.py:392
  20.5 0.1 reshape.29
  20.6 0.1 copy.32
  20.7 0.1 pad_add_fusion
  20.7 0.1 copy.33
  20.8 0.1 reshape.31
  20.9 0.1 reshape.30
  21.0 0.6 pad_add_fusion.1.refs_0_
  21.6 0.1 add_add_fusion
  21.7 0.7 copy.34.refs_0_
  22.4 6.3 %shard_map.139 = (bf16[384,512]{1,0:T(8,128)(2,1)}, bf16[512,384]{1,0:T(8,128)(2,1)}, f32[384,128]{1,0:T(8,128)}, bf16[32,128]{1,0:T(8,128)(2,1)}, f32[128,1024]{1,0:T(8,128)}) custom-call(s32[128,17]{1,0:T(8,128)} %copy.34.refs_0_, bf16[8,1024]{1,0:T(8,128)(2,1)} %refs_6_.1, bf16[3,1024,1024]{2,1,0:T(8,128)(2,1)} %refs_2_.2), custom_call_target="tpu_custom_call" | custom-call | flops 999999995904 | bytes 7832064 | tf_op jit(solution)/shard_map/pallas_call | solution.py:89
  28.8 7.8 %all-to-all-done.refs_0_ = bf16[128,4,384]{2,1,0:T(4,128)(2,1)} async-done(((bf16[128,4,384]{2,1,0:T(4,128)(2,1)}), bf16[128,4,384]{2,1,0:T(4,128)(2,1)}, u32[]{:S(2)}, u32[]{:S(2)}) %all-to-all-start) | async-done | bytes 393248 | tf_op jit(solution)/shard_map/all_to_all | solution.py:392
  36.6 3.3 %shard_map.140 = (bf16[384,384]{1,0:T(8,128)(2,1)}, f32[128,1024]{1,0:T(8,128)}) custom-call(bf16[128,4,384]{2,1,0:T(4,128)(2,1)} %all-to-all-done.refs_0_, bf16[384,512]{1,0:T(8,128)(2,1)} %get-tuple-element.50.refs_1_, bf16[3,384,1024]{2,1,0:T(8,128)(2,1)} %refs_3_.1), custom_call_target="tpu_custom_call" | custom-call | flops 999999995904 | bytes 3964928 | tf_op jit(solution)/shard_map/pallas_call | solution.py:89
  40.0 2.4 %collective-permute-start = (f32[128,1024]{1,0:T(8,128)}, f32[128,1024]{1,0:T(8,128)S(1)}, u32[]{:S(2)}, u32[]{:S(2)}) collective-permute-start(f32[128,1024]{1,0:T(8,128)} %get-tuple-element.51.refs_1_), channel_id=1, source_target_pairs={{0,1},{1,0},{2,3},{3,2},{4,5},{5,4},{6,7},{7,6},{8,9},{9,8},{10,11... | collective-permute-start | bytes 1572872 | tf_op jit(solution)/shard_map/ppermute | solution.py:355
  42.4 2.7 %collective-permute-start.2 = (bf16[384,384]{1,0:T(8,128)(2,1)}, bf16[384,384]{1,0:T(8,128)(2,1)}, u32[]{:S(2)}, u32[]{:S(2)}) collective-permute-start(bf16[384,384]{1,0:T(8,128)(2,1)} %get-tuple-element.62.refs_7_.refs_1_), channel_id=1, source_target_pairs={{0,192},{64,0},{128,64},{192,128},{1,193},{65,1},{129,65},{193,129... | collective-permute-start | bytes 884744 | tf_op jit(solution)/shard_map/ppermute | solution.py:355
  45.1 0.8 copy-done.10
  45.9 4.2 %shard_map.141 = (bf16[128,1024]{1,0:T(8,128)(2,1)}, bf16[208,256]{1,0:T(8,128)(2,1)}, bf16[208,256]{1,0:T(8,128)(2,1)}, bf16[1568,128]{1,0:T(8,128)(2,1)}, bf16[208,256]{1,0:T(8,128)(2,1)}) custom-call(s32[2]{0:T(128)} %pad_add_fusion.1.refs_0_, f32[128,1024]{1,0:T(8,128)} %get-tuple-element.51.refs_1_, f32[128,1024]{1,0:T(8,128)} %copy-done.10, ...), custom_call_target="tpu_custom_call" | custom-call | flops 999999995904 | bytes 3072008 | tf_op jit(solution)/shard_map/pallas_call | solution.py:89
  50.1 2.3 %collective-permute-done.1.refs_2_ = bf16[384,384]{1,0:T(8,128)(2,1)} collective-permute-done((bf16[384,384]{1,0:T(8,128)(2,1)}, bf16[384,384]{1,0:T(8,128)(2,1)}, u32[]{:S(2)}, u32[]{:S(2)}) %collective-permute-start.1) | collective-permute-done | bytes 294944 | tf_op jit(solution)/shard_map/ppermute | solution.py:355
  52.5 1.2 %collective-permute-start.4 = (bf16[1568,128]{1,0:T(8,128)(2,1)}, bf16[1568,128]{1,0:T(8,128)(2,1)S(1)}, u32[]{:S(2)}, u32[]{:S(2)}) collective-permute-start(bf16[1568,128]{1,0:T(8,128)(2,1)} %get-tuple-element.67), channel_id=1, source_target_pairs={{0,128},{64,192},{128,0},{192,64},{1,129},{65,193},{129,1},{193,65... | collective-permute-start | bytes 1204232 | tf_op jit(solution)/shard_map/ppermute | solution.py:355
  53.7 1.7 %collective-permute-start.3 = (bf16[208,256]{1,0:T(8,128)(2,1)}, bf16[208,256]{1,0:T(8,128)(2,1)S(1)}, u32[]{:S(2)}, u32[]{:S(2)}) collective-permute-start(bf16[208,256]{1,0:T(8,128)(2,1)} %get-tuple-element.66), channel_id=1, source_target_pairs={{0,64},{64,128},{128,192},{192,0},{1,65},{65,129},{129,193},{193,1... | collective-permute-start | bytes 319496 | tf_op jit(solution)/shard_map/ppermute | solution.py:355
  55.4 1.0 collective-permute-start.5
  56.4 11.3 %collective-permute-done.3.refs_5_ = bf16[208,256]{1,0:T(8,128)(2,1)S(1)} collective-permute-done((bf16[208,256]{1,0:T(8,128)(2,1)}, bf16[208,256]{1,0:T(8,128)(2,1)S(1)}, u32[]{:S(2)}, u32[]{:S(2)}) %collective-permute-start.3) | collective-permute-done | bytes 106528 | tf_op jit(solution)/shard_map/ppermute | solution.py:355
  67.7 0.9 copy-done.4
  68.6 2.8 %shard_map.142 = (f32[64,1152]{1,0:T(8,128)S(1)}, bf16[352,384]{1,0:T(8,128)(2,1)S(1)}, bf16[352,384]{1,0:T(8,128)(2,1)}, bf16[352,384]{1,0:T(8,128)(2,1)}, bf16[352,384]{1,0:T(8,128)(2,1)}) custom-call(s32[1]{0:T(128)} %bitcast.3.refs_0_, bf16[384,384]{1,0:T(8,128)(2,1)S(1)} %copy-done.3, bf16[384,384]{1,0:T(8,128)(2,1)} %collective-permute-done.1.refs_2_, ...), custom_call_target="tpu_custom_call" | custom-call | flops 999999995904 | bytes 2981892 | tf_op jit(solution)/shard_map/pallas_call | solution.py:89
  71.4 0.3 collective-permute-start.7
  71.7 0.8 collective-permute-start.8
  72.5 1.9 %collective-permute-start.9 = (bf16[352,384]{1,0:T(8,128)(2,1)}, bf16[352,384]{1,0:T(8,128)(2,1)}, u32[]{:S(2)}, u32[]{:S(2)}) collective-permute-start(bf16[352,384]{1,0:T(8,128)(2,1)} %get-tuple-element.81), channel_id=1, source_target_pairs={{0,48},{16,0},{32,16},{48,32},{1,49},{17,1},{33,17},{49,33},{2,50}... | collective-permute-start | bytes 811016 | tf_op jit(solution)/shard_map/ppermute | solution.py:355
  74.4 5.4 %shard_map.143 = bf16[128,4,384]{2,1,0:T(4,128)(2,1)} custom-call(bf16[128,1024]{1,0:T(8,128)(2,1)} %get-tuple-element.70.refs_0_, f32[384,128]{1,0:T(8,128)} %get-tuple-element.54.refs_5_.refs_1_, bf16[512,384]{1,0:T(8,128)(2,1)} %get-tuple-element.71.refs_2_, bf16[3,384,1024]{2,1,0:T(8,128)(2,1)} %refs_3_.1), custom_call_target="tpu_custom_call" | custom-call | flops 999999995904 | bytes 3604480 | tf_op jit(solution)/shard_map/pallas_call | solution.py:89
  79.8 8.5 %all-to-all-start.1 = ((bf16[128,4,384]{2,1,0:T(4,128)(2,1)}), bf16[128,4,384]{2,1,0:T(4,128)(2,1)}, u32[]{:S(2)}, u32[]{:S(2)}) async-start(bf16[128,4,384]{2,1,0:T(4,128)(2,1)} %shard_map.143), calls=%async_computation.1 | async-start | bytes 786432 | tf_op jit(solution)/shard_map/all_to_all | solution.py:467
  88.3 0.0 collective-permute-done.8.refs_4_
  88.3 0.0 copy-start.2
  88.3 1.7 %shard_map.146 = (f32[8,2688]{1,0:T(8,128)S(1)}, bf16[8,2688]{1,0:T(8,128)(2,1)S(1)}, bf16[8,2688]{1,0:T(8,128)(2,1)S(1)}, bf16[8,2688]{1,0:T(8,128)(2,1)S(1)}, ...) custom-call(s32[1]{0:T(128)} %bitcast.6.refs_0_, ...), custom_call_target="tpu_custom_call" | custom-call | flops 999999995904 | bytes 1763332 | tf_op jit(solution)/shard_map/pallas_call | solution.py:89
  90.0 0.6 collective-permute-start.10
  90.6 2.1 %collective-permute-start.11 = (bf16[8,2688]{1,0:T(8,128)(2,1)S(1)}, bf16[8,2688]{1,0:T(8,128)(2,1)S(1)}, u32[]{:S(2)}, u32[]{:S(2)}) collective-permute-start(bf16[8,2688]{1,0:T(8,128)(2,1)S(1)} %get-tuple-element.84), channel_id=1, source_target_pairs={{0,4},{2,6},{4,8},{6,10},{8,12},{10,14},{12,0},{14,2},{1,5},{3,7},... | collective-permute-start | bytes 129032 | tf_op jit(solution)/shard_map/ppermute | solution.py:355
  92.6 2.4 %collective-permute-start.12 = (bf16[8,2688]{1,0:T(8,128)(2,1)S(1)}, bf16[8,2688]{1,0:T(8,128)(2,1)S(1)}, u32[]{:S(2)}, u32[]{:S(2)}) collective-permute-start(bf16[8,2688]{1,0:T(8,128)(2,1)S(1)} %get-tuple-element.85), channel_id=1, source_target_pairs={{0,6},{2,8},{4,10},{6,12},{8,14},{10,0},{12,2},{14,4},{1,7},{3,9},... | collective-permute-start | bytes 129032 | tf_op jit(solution)/shard_map/ppermute | solution.py:355
  95.0 2.1 %collective-permute-start.13 = (bf16[8,2688]{1,0:T(8,128)(2,1)S(1)}, bf16[8,2688]{1,0:T(8,128)(2,1)S(1)}, u32[]{:S(2)}, u32[]{:S(2)}) collective-permute-start(bf16[8,2688]{1,0:T(8,128)(2,1)S(1)} %get-tuple-element.86), channel_id=1, source_target_pairs={{0,8},{2,10},{4,12},{6,14},{8,0},{10,2},{12,4},{14,6},{1,9},{3,11}... | collective-permute-start | bytes 129032 | tf_op jit(solution)/shard_map/ppermute | solution.py:355
  97.1 2.4 %collective-permute-start.14 = (bf16[8,2688]{1,0:T(8,128)(2,1)S(1)}, bf16[8,2688]{1,0:T(8,128)(2,1)S(1)}, u32[]{:S(2)}, u32[]{:S(2)}) collective-permute-start(bf16[8,2688]{1,0:T(8,128)(2,1)S(1)} %get-tuple-element.87), channel_id=1, source_target_pairs={{0,10},{2,12},{4,14},{6,0},{8,2},{10,4},{12,6},{14,8},{1,11},{3,13... | collective-permute-start | bytes 129032 | tf_op jit(solution)/shard_map/ppermute | solution.py:355
  99.5 3.3 %collective-permute-start.15 = (bf16[8,2688]{1,0:T(8,128)(2,1)S(1)}, bf16[8,2688]{1,0:T(8,128)(2,1)S(1)}, u32[]{:S(2)}, u32[]{:S(2)}) collective-permute-start(bf16[8,2688]{1,0:T(8,128)(2,1)S(1)} %get-tuple-element.88), channel_id=1, source_target_pairs={{0,12},{2,14},{4,0},{6,2},{8,4},{10,6},{12,8},{14,10},{1,13},{3,15... | collective-permute-start | bytes 129032 | tf_op jit(solution)/shard_map/ppermute | solution.py:355
  102.8 1.2 %collective-permute-start.16 = (bf16[8,2688]{1,0:T(8,128)(2,1)S(1)}, bf16[8,2688]{1,0:T(8,128)(2,1)S(1)}, u32[]{:S(2)}, u32[]{:S(2)}) collective-permute-start(bf16[8,2688]{1,0:T(8,128)(2,1)S(1)} %get-tuple-element.89), channel_id=1, source_target_pairs={{0,14},{2,0},{4,2},{6,4},{8,6},{10,8},{12,10},{14,12},{1,15},{3,1}... | collective-permute-start | bytes 129032 | tf_op jit(solution)/shard_map/ppermute | solution.py:355
  104.0 2.4 %shard_map.144 = (f32[1024,384]{1,0:T(8,128)S(1)}, f32[8,128]{1,0:T(8,128)}) custom-call(s32[1,512]{1,0:T(1,128)S(1)} %copy-done.2, bf16[128,4,384]{2,1,0:T(4,128)(2,1)} %all-to-all-done.1.refs_1_), custom_call_target="tpu_custom_call" | custom-call | bytes 1972224 | tf_op jit(solution)/shard_map/pallas_call | solution.py:89
  106.5 4.8 %collective-permute-start.6 = (f32[8,128]{1,0:T(8,128)}, f32[8,128]{1,0:T(8,128)}, u32[]{:S(2)}, u32[]{:S(2)}) collective-permute-start(f32[8,128]{1,0:T(8,128)} %get-tuple-element.73.refs_3_), channel_id=1, source_target_pairs={{0,1},{1,0},{2,3},{3,2},{4,5},{5,4},{6,7},{7,6},{8,9},{9,8},{10,11... | collective-permute-start | bytes 12296 | tf_op jit(solution)/shard_map/ppermute | solution.py:355
  111.3 0.0 copy-start
  111.3 0.0 copy-start.1
  111.3 0.7 shard_map.147
  112.0 0.4 collective-permute-done.6.refs_4_
  112.5 0.3 copy-done
  112.8 2.3 %shard_map.145 = (f32[1024,384]{1,0:T(8,128)}, f32[8,128]{1,0:T(8,128)}) custom-call(f32[1024,384]{1,0:T(8,128)S(1)} %copy-done, f32[1024,384]{1,0:T(8,128)S(1)} %get-tuple-element.72.refs_1_, f32[8,128]{1,0:T(8,128)S(1)} %bitcast.11, f32[8,128]{1,0:T(8,128)} %get-tuple-element.73.refs_3_, f32[8,128]{1,0:T(8,128)} %collective-permute-done.6.refs_4_), custom_call_target="tpu_custom_call" | custom-call | bytes 4734976 | tf_op jit(solution)/shard_map/pallas_call | solution.py:89
  (35 shorter events, 0.1 us)
Async XLA Ops:
  0.6 19.8 %copy-start.7 = (s32[8,15]{1,0:T(8,128)S(1)}, s32[8,15]{1,0:T(8,128)}, u32[]{:S(2)}) copy-start(s32[8,15]{1,0:T(8,128)} %param.15) | copy-start | bytes 1444
  0.6 19.9 %copy-start.8 = (s32[8,15]{1,0:T(8,128)S(1)}, s32[8,15]{1,0:T(8,128)}, u32[]{:S(2)}) copy-start(s32[8,15]{1,0:T(8,128)} %param.17) | copy-start | bytes 1444
  0.7 19.9 %copy-start.9 = (s32[8]{0:T(128)S(1)}, s32[8]{0:T(128)}, u32[]{:S(2)}) copy-start(s32[8]{0:T(128)} %param.14) | copy-start | bytes 100
  0.7 20.2 %copy-start.5 = (s32[8,15,10]{1,0,2:T(8,128)S(1)}, s32[8,15,10]{1,0,2:T(8,128)}, u32[]{:S(2)}) copy-start(s32[8,15,10]{1,0,2:T(8,128)} %param.16) | copy-start | bytes 14404
  0.7 20.2 %copy-start.6 = (s32[8,15,10]{1,0,2:T(8,128)S(1)}, s32[8,15,10]{1,0,2:T(8,128)}, u32[]{:S(2)}) copy-start(s32[8,15,10]{1,0,2:T(8,128)} %param.18) | copy-start | bytes 14404
  3.6 33.0 %all-to-all-start = ((bf16[128,4,384]{2,1,0:T(4,128)(2,1)}), bf16[128,4,384]{2,1,0:T(4,128)(2,1)}, u32[]{:S(2)}, u32[]{:S(2)}) async-start(bf16[128,4,384]{2,1,0:T(4,128)(2,1)} %shard_map.138), calls=%async_computation | async-start | bytes 786432 | tf_op jit(solution)/shard_map/all_to_all | solution.py:392
  40.0 5.1 %collective-permute-start = (f32[128,1024]{1,0:T(8,128)}, f32[128,1024]{1,0:T(8,128)S(1)}, u32[]{:S(2)}, u32[]{:S(2)}) collective-permute-start(f32[128,1024]{1,0:T(8,128)} %get-tuple-element.51.refs_1_), channel_id=1, source_target_pairs={{0,1},{1,0},{2,3},{3,2},{4,5},{5,4},{6,7},{7,6},{8,9},{9,8},{10,11... | collective-permute-start | bytes 1572872 | tf_op jit(solution)/shard_map/ppermute | solution.py:355
  42.4 10.1 %collective-permute-start.1 = (bf16[384,384]{1,0:T(8,128)(2,1)}, bf16[384,384]{1,0:T(8,128)(2,1)}, u32[]{:S(2)}, u32[]{:S(2)}) collective-permute-start(bf16[384,384]{1,0:T(8,128)(2,1)} %get-tuple-element.62.refs_7_.refs_1_), channel_id=1, source_target_pairs={{0,64},{64,128},{128,192},{192,0},{1,65},{65,129},{129,193},{193,1... | collective-permute-start | bytes 884744 | tf_op jit(solution)/shard_map/ppermute | solution.py:355
  42.4 10.1 %collective-permute-start.2 = (bf16[384,384]{1,0:T(8,128)(2,1)}, bf16[384,384]{1,0:T(8,128)(2,1)}, u32[]{:S(2)}, u32[]{:S(2)}) collective-permute-start(bf16[384,384]{1,0:T(8,128)(2,1)} %get-tuple-element.62.refs_7_.refs_1_), channel_id=1, source_target_pairs={{0,192},{64,0},{128,64},{192,128},{1,193},{65,1},{129,65},{193,129... | collective-permute-start | bytes 884744 | tf_op jit(solution)/shard_map/ppermute | solution.py:355
  45.1 0.8 copy-start.10
  45.9 21.8 %copy-start.3 = (bf16[384,384]{1,0:T(8,128)(2,1)S(1)}, bf16[384,384]{1,0:T(8,128)(2,1)}, u32[]{:S(2)}) copy-start(bf16[384,384]{1,0:T(8,128)(2,1)} %get-tuple-element.62.refs_7_.refs_1_) | copy-start | bytes 884740
  52.5 15.2 %collective-permute-start.4 = (bf16[1568,128]{1,0:T(8,128)(2,1)}, bf16[1568,128]{1,0:T(8,128)(2,1)S(1)}, u32[]{:S(2)}, u32[]{:S(2)}) collective-permute-start(bf16[1568,128]{1,0:T(8,128)(2,1)} %get-tuple-element.67), channel_id=1, source_target_pairs={{0,128},{64,192},{128,0},{192,64},{1,129},{65,193},{129,1},{193,65... | collective-permute-start | bytes 1204232 | tf_op jit(solution)/shard_map/ppermute | solution.py:355
  53.7 14.0 %collective-permute-start.3 = (bf16[208,256]{1,0:T(8,128)(2,1)}, bf16[208,256]{1,0:T(8,128)(2,1)S(1)}, u32[]{:S(2)}, u32[]{:S(2)}) collective-permute-start(bf16[208,256]{1,0:T(8,128)(2,1)} %get-tuple-element.66), channel_id=1, source_target_pairs={{0,64},{64,128},{128,192},{192,0},{1,65},{65,129},{129,193},{193,1... | collective-permute-start | bytes 319496 | tf_op jit(solution)/shard_map/ppermute | solution.py:355
  55.4 12.3 %collective-permute-start.5 = (bf16[208,256]{1,0:T(8,128)(2,1)}, bf16[208,256]{1,0:T(8,128)(2,1)S(1)}, u32[]{:S(2)}, u32[]{:S(2)}) collective-permute-start(bf16[208,256]{1,0:T(8,128)(2,1)} %get-tuple-element.68), channel_id=1, source_target_pairs={{0,192},{64,0},{128,64},{192,128},{1,193},{65,1},{129,65},{193,129... | collective-permute-start | bytes 319496 | tf_op jit(solution)/shard_map/ppermute | solution.py:355
  67.7 0.9 copy-start.4
  71.4 16.8 %collective-permute-start.7 = (bf16[352,384]{1,0:T(8,128)(2,1)}, bf16[352,384]{1,0:T(8,128)(2,1)}, u32[]{:S(2)}, u32[]{:S(2)}) collective-permute-start(bf16[352,384]{1,0:T(8,128)(2,1)} %get-tuple-element.79), channel_id=1, source_target_pairs={{0,16},{16,32},{32,48},{48,0},{1,17},{17,33},{33,49},{49,1},{2,18}... | collective-permute-start | bytes 811016 | tf_op jit(solution)/shard_map/ppermute | solution.py:355
  71.7 16.6 %collective-permute-start.8 = (bf16[352,384]{1,0:T(8,128)(2,1)}, bf16[352,384]{1,0:T(8,128)(2,1)}, u32[]{:S(2)}, u32[]{:S(2)}) collective-permute-start(bf16[352,384]{1,0:T(8,128)(2,1)} %get-tuple-element.80), channel_id=1, source_target_pairs={{0,32},{16,48},{32,0},{48,16},{1,33},{17,49},{33,1},{49,17},{2,34}... | collective-permute-start | bytes 811016 | tf_op jit(solution)/shard_map/ppermute | solution.py:355
  72.5 15.8 %collective-permute-start.9 = (bf16[352,384]{1,0:T(8,128)(2,1)}, bf16[352,384]{1,0:T(8,128)(2,1)}, u32[]{:S(2)}, u32[]{:S(2)}) collective-permute-start(bf16[352,384]{1,0:T(8,128)(2,1)} %get-tuple-element.81), channel_id=1, source_target_pairs={{0,48},{16,0},{32,16},{48,32},{1,49},{17,1},{33,17},{49,33},{2,50}... | collective-permute-start | bytes 811016 | tf_op jit(solution)/shard_map/ppermute | solution.py:355
  79.8 24.2 %all-to-all-start.1 = ((bf16[128,4,384]{2,1,0:T(4,128)(2,1)}), bf16[128,4,384]{2,1,0:T(4,128)(2,1)}, u32[]{:S(2)}, u32[]{:S(2)}) async-start(bf16[128,4,384]{2,1,0:T(4,128)(2,1)} %shard_map.143), calls=%async_computation.1 | async-start | bytes 786432 | tf_op jit(solution)/shard_map/all_to_all | solution.py:467
  88.3 15.7 %copy-start.2 = (s32[1,512]{1,0:T(1,128)S(1)}, s32[1,512]{1,0:T(1,128)}, u32[]{:S(2)}) copy-start(s32[1,512]{1,0:T(1,128)} %refs_0_.4) | copy-start | bytes 6148
  90.0 9.5 %collective-permute-start.10 = (bf16[8,2688]{1,0:T(8,128)(2,1)S(1)}, bf16[8,2688]{1,0:T(8,128)(2,1)S(1)}, u32[]{:S(2)}, u32[]{:S(2)}) collective-permute-start(bf16[8,2688]{1,0:T(8,128)(2,1)S(1)} %get-tuple-element.83), channel_id=1, source_target_pairs={{0,2},{2,4},{4,6},{6,8},{8,10},{10,12},{12,14},{14,0},{1,3},{3,5},... | collective-permute-start | bytes 129032 | tf_op jit(solution)/shard_map/ppermute | solution.py:355
  90.6 12.3 %collective-permute-start.11 = (bf16[8,2688]{1,0:T(8,128)(2,1)S(1)}, bf16[8,2688]{1,0:T(8,128)(2,1)S(1)}, u32[]{:S(2)}, u32[]{:S(2)}) collective-permute-start(bf16[8,2688]{1,0:T(8,128)(2,1)S(1)} %get-tuple-element.84), channel_id=1, source_target_pairs={{0,4},{2,6},{4,8},{6,10},{8,12},{10,14},{12,0},{14,2},{1,5},{3,7},... | collective-permute-start | bytes 129032 | tf_op jit(solution)/shard_map/ppermute | solution.py:355
  92.6 13.8 %collective-permute-start.12 = (bf16[8,2688]{1,0:T(8,128)(2,1)S(1)}, bf16[8,2688]{1,0:T(8,128)(2,1)S(1)}, u32[]{:S(2)}, u32[]{:S(2)}) collective-permute-start(bf16[8,2688]{1,0:T(8,128)(2,1)S(1)} %get-tuple-element.85), channel_id=1, source_target_pairs={{0,6},{2,8},{4,10},{6,12},{8,14},{10,0},{12,2},{14,4},{1,7},{3,9},... | collective-permute-start | bytes 129032 | tf_op jit(solution)/shard_map/ppermute | solution.py:355
  95.0 16.3 %collective-permute-start.13 = (bf16[8,2688]{1,0:T(8,128)(2,1)S(1)}, bf16[8,2688]{1,0:T(8,128)(2,1)S(1)}, u32[]{:S(2)}, u32[]{:S(2)}) collective-permute-start(bf16[8,2688]{1,0:T(8,128)(2,1)S(1)} %get-tuple-element.86), channel_id=1, source_target_pairs={{0,8},{2,10},{4,12},{6,14},{8,0},{10,2},{12,4},{14,6},{1,9},{3,11}... | collective-permute-start | bytes 129032 | tf_op jit(solution)/shard_map/ppermute | solution.py:355
  97.1 14.2 %collective-permute-start.14 = (bf16[8,2688]{1,0:T(8,128)(2,1)S(1)}, bf16[8,2688]{1,0:T(8,128)(2,1)S(1)}, u32[]{:S(2)}, u32[]{:S(2)}) collective-permute-start(bf16[8,2688]{1,0:T(8,128)(2,1)S(1)} %get-tuple-element.87), channel_id=1, source_target_pairs={{0,10},{2,12},{4,14},{6,0},{8,2},{10,4},{12,6},{14,8},{1,11},{3,13... | collective-permute-start | bytes 129032 | tf_op jit(solution)/shard_map/ppermute | solution.py:355
  99.5 11.8 %collective-permute-start.15 = (bf16[8,2688]{1,0:T(8,128)(2,1)S(1)}, bf16[8,2688]{1,0:T(8,128)(2,1)S(1)}, u32[]{:S(2)}, u32[]{:S(2)}) collective-permute-start(bf16[8,2688]{1,0:T(8,128)(2,1)S(1)} %get-tuple-element.88), channel_id=1, source_target_pairs={{0,12},{2,14},{4,0},{6,2},{8,4},{10,6},{12,8},{14,10},{1,13},{3,15... | collective-permute-start | bytes 129032 | tf_op jit(solution)/shard_map/ppermute | solution.py:355
  102.8 8.5 %collective-permute-start.16 = (bf16[8,2688]{1,0:T(8,128)(2,1)S(1)}, bf16[8,2688]{1,0:T(8,128)(2,1)S(1)}, u32[]{:S(2)}, u32[]{:S(2)}) collective-permute-start(bf16[8,2688]{1,0:T(8,128)(2,1)S(1)} %get-tuple-element.89), channel_id=1, source_target_pairs={{0,14},{2,0},{4,2},{6,4},{8,6},{10,8},{12,10},{14,12},{1,15},{3,1}... | collective-permute-start | bytes 129032 | tf_op jit(solution)/shard_map/ppermute | solution.py:355
  106.5 6.0 %collective-permute-start.6 = (f32[8,128]{1,0:T(8,128)}, f32[8,128]{1,0:T(8,128)}, u32[]{:S(2)}, u32[]{:S(2)}) collective-permute-start(f32[8,128]{1,0:T(8,128)} %get-tuple-element.73.refs_3_), channel_id=1, source_target_pairs={{0,1},{1,0},{2,3},{3,2},{4,5},{5,4},{6,7},{7,6},{8,9},{9,8},{10,11... | collective-permute-start | bytes 12296 | tf_op jit(solution)/shard_map/ppermute | solution.py:355
  111.3 1.4 %copy-start = (f32[1024,384]{1,0:T(8,128)S(1)}, f32[1024,384]{1,0:T(8,128)}, u32[]{:S(2)}) copy-start(f32[1024,384]{1,0:T(8,128)} %refs_0_.5) | copy-start | bytes 4718596
  111.3 1.4 %copy-start.1 = (f32[1024]{0:T(1024)S(1)}, f32[1024]{0:T(1024)}, u32[]{:S(2)}) copy-start(f32[1024]{0:T(1024)} %param.12) | copy-start | bytes 12292

commit v7 on v5

--- a/solution.py
+++ b/solution.py
@@ -95,6 +95,10 @@
         compiler_params=pltpu.CompilerParams(vmem_limit_bytes=limit * 1024 * 1024),
         cost_estimate=pl.CostEstimate(flops=flops, bytes_accessed=moved, transcendentals=0),
     )(*operands)
+
+
+def is_near(distance, count):
+    return distance not in (0, count // 2)
 
 
 def shaped(shape, dtype):
@@ -171,7 +175,7 @@
     partial_out.send()
 
 
-def hidden_kernel(place_ref, mine_ref, other_ref, back_ref, e_ref, inv_ref, cot_ref, layer_ref, out_ref, *refs):
+def hidden_kernel(place_ref, mine_ref, other_ref, back_ref, e_ref, inv_ref, cot_ref, c_ref, w1_ref, layer_ref, slot_ref, *refs):
     packs, stage, sems = refs[:-2], refs[-2], refs[-1]
     nodes = mine_ref.shape[0]
     width = stage.shape[2]
@@ -183,7 +187,6 @@
     hidden = (values * sigma).astype(BF16)
     slope = sigma * (1.0 + values * (1.0 - sigma))
     back = (back_ref[...] * slope).astype(BF16)
-    out_ref[...] = back
     scale = jnp.concatenate(
         [inv_ref[k * nodes : k * nodes + seeds, 0:1] for k in range(layers)]
         + [jnp.zeros((SEED_ROWS - layers * seeds, 1), F32)],
@@ -205,7 +208,7 @@
     moves = []
     for d, pack in enumerate(packs):
         chosen = stage.at[lax.rem(place_ref[1] + d, len(packs))]
-        if d != len(packs) // 2:
+        if not is_near(d, len(packs)):
             moves.append((chosen, pack))
             continue
         start = 0
@@ -214,38 +217,37 @@
             for lane in range(0, wide, LANES):
                 moves.append((source.at[:, lane : lane + LANES], pack.at[start : start + rows, :]))
                 start += rows
+    layer_ref.get()
     copies = [pltpu.make_async_copy(source, target, sems.at[i]) for i, (source, target) in enumerate(moves)]
     for copy in copies:
         copy.start()
-    for copy in copies:
-        copy.wait()
-
-
-def slot_kernel(back_ref, inv_ref, c_ref, w1_ref, slot_ref):
-    nodes = back_ref.shape[0]
     total = None
-    for k in range(w1_ref.shape[0]):
+    for k in range(layers):
         span = slice(k * nodes, (k + 1) * nodes)
-        back_in = matmul(back_ref[...], w1_ref.get()[k], (1, 1)) * inv_ref.get()[span, 0:1]
+        back_in = matmul(back, w1_ref.get()[k], (1, 1)) * inv_ref[span, 0:1]
         term = matmul(c_ref.get()[:, span], back_in.astype(BF16))
         total = term if total is None else total + term
     slot_ref[...] = total.astype(BF16).reshape(slot_ref.shape)
+    for copy in copies:
+        copy.wait()
 
 
 def weight_kernel(count, place_ref, *refs):
-    layer_refs, pack_refs = list(refs[: count - 1]), list(refs[count - 1 : 2 * count - 1])
-    own_ref, outs, total = refs[2 * count - 1], refs[2 * count : -1], refs[-1]
+    layer_refs, pack_refs = refs[:2], refs[2 : 2 + count]
+    own_ref, outs, total = refs[2 + count], refs[3 + count : -1], refs[-1]
     pack_rows, width = pack_refs[0].shape
     layer_rows, columns = layer_refs[0].shape
-    layer_parts = [r.get()[...] for r in layer_refs]
-    far = pack_refs[count // 2][...]
-    parts, start = [], 0
-    for rows, wide in ((pack_rows, width), (layer_rows, columns)):
-        lanes = [far[start + i * rows : start + (i + 1) * rows] for i in range(wide // LANES)]
-        parts.append(jnp.concatenate(lanes, 1))
-        start += rows * len(lanes)
-    layer_parts.insert(count // 2, parts[1])
-    packs = [parts[0] if d == count // 2 else ref[...] for d, ref in enumerate(pack_refs)]
+    layer_parts, packs = [], []
+    for d, ref in enumerate(pack_refs):
+        if not is_near(d, count):
+            packs.append(ref.get()[...])
+            layer_parts.append(layer_refs[min(d, 1)].get()[...])
+            continue
+        near, start = ref.get()[...], 0
+        for rows, wide, made in ((pack_rows, width, packs), (layer_rows, columns, layer_parts)):
+            lanes = [near[start + i * rows : start + (i + 1) * rows] for i in range(wide // LANES)]
+            made.append(jnp.concatenate(lanes, 1))
+            start += rows * len(lanes)
     nodes = LANES
     relations = layer_rows // nodes
     rows = own_ref.shape[0]
@@ -269,6 +271,7 @@
         [jnp.concatenate([s[k * seeds : (k + 1) * seeds] for s in seconds], 0) for k in range(relations)], 1
     ).astype(BF16)
     group = count * seeds
+    per = columns // (group // COT_ROWS)
     tail = relations * rows
     for d, out in enumerate(outs):
         target = lax.rem(place_ref[0] + d, len(outs))
@@ -286,8 +289,9 @@
         chosen = cots[:, :rows]
         for j in range(1, len(outs)):
             chosen = jnp.where(target == j, cots[:, j * rows : (j + 1) * rows], chosen)
-        chosen = jnp.concatenate([chosen, jnp.zeros((group, columns - rows), F32)], 1)
-        out[out.shape[0] - group :, :] = chosen.astype(BF16)
+        for piece in range(group // COT_ROWS):
+            lanes = slice(piece * per, piece * per + rows)
+            out[out.shape[0] - COT_ROWS :, lanes] = chosen[piece * COT_ROWS : (piece + 1) * COT_ROWS].astype(BF16)
 
 
 def group_kernel(relations, own_ref, *refs):
@@ -297,19 +301,27 @@
     tail = relations * rows
     wide = out_ref.shape[1] - relations * columns
     pieces = wide // columns
-    group = (packs[0].shape[0] - tail) // (pieces + 1)
+    group = (packs[0].shape[0] - tail - COT_ROWS) // pieces
+    per = columns // (group // COT_ROWS)
     for k in range(relations):
         span = slice(k * columns, (k + 1) * columns)
         block = own_ref[:, span]
         for pack in packs[1:]:
             block = block + pack[k * rows : (k + 1) * rows, :].astype(F32)
         out_ref[:, span] = block.astype(BF16)
-    cots = jnp.concatenate([p[tail + pieces * group :, :] for p in packs], 0)
+    cots = jnp.concatenate(
+        [
+            p[tail + pieces * group :, piece * per : piece * per + rows]
+            for p in packs
+            for piece in range(group // COT_ROWS)
+        ],
+        0,
+    )
     for piece in range(pieces):
         first = tail + piece * group
         second = jnp.concatenate([p[first : first + group, :] for p in packs], 0)
         start = (relations + piece) * columns
-        out_ref[:, start : start + columns] = matmul(cots, second, (0, 0))[:rows].astype(BF16)
+        out_ref[:, start : start + columns] = matmul(cots, second, (0, 0)).astype(BF16)
 
 
 def sum_kernel(parts_ref, one_ref, two_ref):
@@ -348,7 +360,7 @@
     return lax.ppermute(array, axis, [(i, (i + by) % size) for i in range(size)])
 
 
-LIMITS = {serve_kernel: 60, index_kernel: 60, first_kernel: 60, hidden_kernel: 60, slot_kernel: 50}
+LIMITS = {serve_kernel: 60, index_kernel: 60, first_kernel: 60, hidden_kernel: 60}
 COSTS = {update_kernel: 0, group_kernel: 0, row_kernel: 0}
 
 
@@ -396,6 +408,7 @@
         ],
         0,
     )
+    idx, place, y = lax.optimization_barrier((idx, jnp.stack([lax.axis_index("col"), x]), y))
     ct, c, inverse, member, back_hidden = call(
         index_kernel,
         [
@@ -418,43 +431,43 @@
         hbm_out=(0, 1),
     )
     other_pre = shift(partial_pre, "col", 1)
-    layer_parts = [layer_in] + [shift(layer_in, "dp", d) for d in range(1, n_x) if d != n_x // 2]
+    layer_parts = [layer_in, shift(layer_in, "dp", n_x // 2)]
 
     pack_rows = nodes + half // width * SEED_ROWS + COT_ROWS
     pack_shape = (pack_rows, width)
-    far = n_x // 2
-    far_shape = ((pack_rows * width + layers * nodes * columns) // LANES, LANES)
-    back, *packs = call(
+    near_shape = ((pack_rows * width + layers * nodes * columns) // LANES, LANES)
+    slot_grad, *packs = call(
         hidden_kernel,
-        [shaped((nodes, hidden_units), BF16)] + [shaped(far_shape if d == far else pack_shape, BF16) for d in range(n_x)],
+        [shaped(blocks_shape, BF16)] + [shaped(near_shape if is_near(d, n_x) else pack_shape, BF16) for d in range(n_x)],
         (
-            jnp.stack([lax.axis_index("col"), x]),
+            place,
             partial_pre,
             other_pre,
             back_hidden,
             member,
             inverse,
             cotangent,
+            c,
+            w_first,
             layer_in,
         ),
         smem=1,
-        scratch=[pltpu.VMEM((n_x, *pack_shape), BF16), pltpu.SemaphoreType.DMA((n_x - 1 + (width + columns) // LANES,))],
-        hbm_in=(1, 2, 3, 4, 5, 7),
+        scratch=[pltpu.VMEM((n_x, *pack_shape), BF16), pltpu.SemaphoreType.DMA((n_x * (width + columns) // LANES,))],
+        hbm_in=(1, 2, 3, 4, 5, 7, 8, 9),
         hbm_raw=range(1, 1 + n_x),
     )
+    packs, layer_parts = lax.optimization_barrier((packs, layer_parts))
     packs = [packs[0]] + [shift(packs[d], "dp", d) for d in range(1, n_x)]
-    back, *layer_parts[1:] = lax.optimization_barrier((back, *layer_parts[1:]))
-    slot_grad = call(slot_kernel, [shaped(blocks_shape, BF16)], (back, inverse, c, w_first), hbm_in=(1, 2, 3))[0]
     arrived = lax.all_to_all(slot_grad, everyone, split_axis=0, concat_axis=0, tiled=True)
 
     block_rows = width // n_y
-    group_rows = layers * block_rows + (layers * half // columns + 1) * n_x * seeds
+    group_rows = layers * block_rows + (layers * half // columns) * n_x * seeds + COT_ROWS
     own, *blocks = call(
         functools.partial(weight_kernel, n_x),
         [shaped((block_rows, layers * columns), F32)] + [shaped((group_rows, columns), BF16)] * n_y,
         (y.reshape(1), *layer_parts, *packs),
         smem=1,
-        hbm_in=range(1, n_x),
+        hbm_in=range(1, 3 + n_x),
         scratch=[pltpu.VMEM((layers, width, columns), F32)],
     )
     blocks = [blocks[0]] + [shift(blocks[d], "y", d) for d in range(1, n_y)]

time: 110 us -> 104 us (0.945)
  waiting for transfers between devices: 33.4 us -> 30.4 us
  Pallas kernels: 28.4 us -> 25.5 us
    pallas_call x10 -> x9, Pallas kernels: 28.4 us -> 25.5 us  [call(): pl.pallas_call(wrapped, out_shape=tuple(outs), in_specs=specs, out_specs=...]
    ppermute x10 -> x9, waiting for transfers between devices: 16.7 us -> 14.4 us  [shift(): lax.ppermute(array, axis, [(i, (i + by) % size) for i in range(size)])]
    ppermute x10 -> x9, starting transfers between devices: 13 us -> 12.4 us  [shift(): lax.ppermute(array, axis, [(i, (i + by) % size) for i in range(size)])]
  transfers between devices with their start and end apart: 13 -> 12, of which waited for: 7 -> 10; matrix products, arithmetic and copies ran while one was open for 2% -> 2% of each run, Pallas kernels for 19% -> 18%
where the time goes in v7:
time: 104 us
  starting transfers between devices  43.3 us (42%)
  waiting for transfers between devices  30.4 us (29%)
  Pallas kernels  25.5 us (25%)
  local copies, waits for them, and re-layouts  2.91 us (3%)
    pallas_call x9, Pallas kernels, call(): pl.pallas_call(wrapped, out_shape=tuple(outs), in_specs=specs, out_specs=...  25.5 us
    all_to_all x1, starting transfers between devices, body(): lax.all_to_all(outgoing, everyone, split_axis=0, concat_axis=0, tiled=True)  15.8 us
    ppermute x9, waiting for transfers between devices, shift(): lax.ppermute(array, axis, [(i, (i + by) % size) for i in range(size)])  14.4 us
    ppermute x9, starting transfers between devices, shift(): lax.ppermute(array, axis, [(i, (i + by) % size) for i in range(size)])  12.4 us
    all_to_all x1, starting transfers between devices, body(): lax.all_to_all(slot_grad, everyone, split_axis=0, concat_axis=0, tiled=True)  9.99 us
    all_to_all x1, waiting for transfers between devices, body(): grads = lax.all_to_all(grads, 'z', split_axis=0, concat_axis=0, tiled=True)  8.74 us
    all_to_all x1, waiting for transfers between devices, body(): lax.all_to_all(outgoing, everyone, split_axis=0, concat_axis=0, tiled=True)  7.26 us
    all_to_all x1, starting transfers between devices, body(): grads = lax.all_to_all(grads, 'z', split_axis=0, concat_axis=0, tiled=True)  5.15 us
  transfers between devices with their start and end apart: 12, of which 10 were waited for; matrix products, arithmetic and copies ran while one was open for 2% of the time, Pallas kernels for 18%

profile of v7, /device:TPU:8, one launch (start us, length us, event | category | flops | bytes accessed | tf_op | source)
XLA Modules:
  0.0 103.8 jit_solution(8816766803147017556)
XLA Ops:
  0.7 2.9 %shard_map.138 = bf16[128,4,384]{2,1,0:T(4,128)(2,1)} custom-call(s32[1,512]{1,0:T(1,128)} %refs_0_.4, f32[1024,384]{1,0:T(8,128)} %refs_0_.5), custom_call_target="tpu_custom_call" | custom-call | flops 999999995904 | bytes 1968128 | tf_op jit(solution)/shard_map/pallas_call | solution.py:89
  3.6 15.8 %all-to-all-start = ((bf16[128,4,384]{2,1,0:T(4,128)(2,1)}), bf16[128,4,384]{2,1,0:T(4,128)(2,1)}, u32[]{:S(2)}, u32[]{:S(2)}) async-start(bf16[128,4,384]{2,1,0:T(4,128)(2,1)} %shard_map.138), calls=%async_computation | async-start | bytes 786432 | tf_op jit(solution)/shard_map/all_to_all | solution.py:397
  19.4 0.0 copy-done.7
  19.4 0.1 reshape.29
  19.5 0.1 copy.32
  19.6 0.1 pad_add_fusion
  19.7 0.1 copy.33
  19.8 0.1 reshape.31
  19.9 0.1 reshape.30
  19.9 0.6 pad_add_fusion.1.refs_0_
  20.5 0.1 add_add_fusion
  20.6 0.8 copy.34.refs_0_
  21.4 6.3 %shard_map.139 = (bf16[384,512]{1,0:T(8,128)(2,1)}, bf16[512,384]{1,0:T(8,128)(2,1)}, f32[384,128]{1,0:T(8,128)}, bf16[32,128]{1,0:T(8,128)(2,1)}, f32[128,1024]{1,0:T(8,128)}) custom-call(s32[128,17]{1,0:T(8,128)} %copy.34.refs_0_, bf16[8,1024]{1,0:T(8,128)(2,1)} %refs_6_.1, bf16[3,1024,1024]{2,1,0:T(8,128)(2,1)} %refs_2_.2), custom_call_target="tpu_custom_call" | custom-call | flops 999999995904 | bytes 7832064 | tf_op jit(solution)/shard_map/pallas_call | solution.py:89
  27.7 7.3 %all-to-all-done.refs_0_ = bf16[128,4,384]{2,1,0:T(4,128)(2,1)} async-done(((bf16[128,4,384]{2,1,0:T(4,128)(2,1)}), bf16[128,4,384]{2,1,0:T(4,128)(2,1)}, u32[]{:S(2)}, u32[]{:S(2)}) %all-to-all-start) | async-done | bytes 393248 | tf_op jit(solution)/shard_map/all_to_all | solution.py:397
  35.0 3.3 %shard_map.140 = (bf16[384,384]{1,0:T(8,128)(2,1)}, f32[128,1024]{1,0:T(8,128)}) custom-call(bf16[128,4,384]{2,1,0:T(4,128)(2,1)} %all-to-all-done.refs_0_, bf16[384,512]{1,0:T(8,128)(2,1)} %get-tuple-element.38.refs_1_, bf16[3,384,1024]{2,1,0:T(8,128)(2,1)} %refs_8_.1), custom_call_target="tpu_custom_call" | custom-call | flops 999999995904 | bytes 3964928 | tf_op jit(solution)/shard_map/pallas_call | solution.py:89
  38.3 0.1 collective-permute-start
  38.4 1.6 %collective-permute-start.2 = (bf16[384,384]{1,0:T(8,128)(2,1)}, bf16[384,384]{1,0:T(8,128)(2,1)}, u32[]{:S(2)}, u32[]{:S(2)}) collective-permute-start(bf16[384,384]{1,0:T(8,128)(2,1)} %get-tuple-element.55.refs_9_.refs_1_), channel_id=1, source_target_pairs={{0,128},{64,192},{128,0},{192,64},{1,129},{65,193},{129,1},{193,65... | collective-permute-start | bytes 884744 | tf_op jit(solution)/shard_map/ppermute | solution.py:360
  40.0 0.5 collective-permute-done.refs_2_
  40.5 0.8 copy-done.10
  41.3 5.9 %shard_map.141 = (bf16[128,4,384]{2,1,0:T(4,128)(2,1)}, bf16[208,256]{1,0:T(8,128)(2,1)}, bf16[1568,128]{1,0:T(8,128)(2,1)}, bf16[208,256]{1,0:T(8,128)(2,1)}, bf16[1568,128]{1,0:T(8,128)(2,1)}) custom-call(s32[2]{0:T(128)} %pad_add_fusion.1.refs_0_, f32[128,1024]{1,0:T(8,128)} %get-tuple-element.39.refs_1_, f32[128,1024]{1,0:T(8,128)} %copy-done.10, ...), custom_call_target="tpu_custom_call" | custom-call | flops 999999995904 | bytes 6250504 | tf_op jit(solution)/shard_map/pallas_call | solution.py:89
  47.2 2.4 %collective-permute-done.2.refs_2_ = bf16[384,384]{1,0:T(8,128)(2,1)} collective-permute-done((bf16[384,384]{1,0:T(8,128)(2,1)}, bf16[384,384]{1,0:T(8,128)(2,1)}, u32[]{:S(2)}, u32[]{:S(2)}) %collective-permute-start.2) | collective-permute-done | bytes 294944 | tf_op jit(solution)/shard_map/ppermute | solution.py:360
  49.6 0.8 collective-permute-start.3
  50.4 2.5 %collective-permute-start.5 = (bf16[1568,128]{1,0:T(8,128)(2,1)}, bf16[1568,128]{1,0:T(8,128)(2,1)S(1)}, u32[]{:S(2)}, u32[]{:S(2)}) collective-permute-start(bf16[1568,128]{1,0:T(8,128)(2,1)} %get-tuple-element.60), channel_id=1, source_target_pairs={{0,192},{64,0},{128,64},{192,128},{1,193},{65,1},{129,65},{193,129... | collective-permute-start | bytes 1204232 | tf_op jit(solution)/shard_map/ppermute | solution.py:360
  52.9 0.3 collective-permute-start.4
  53.2 10.0 %all-to-all-start.1 = ((bf16[128,4,384]{2,1,0:T(4,128)(2,1)}), bf16[128,4,384]{2,1,0:T(4,128)(2,1)}, u32[]{:S(2)}, u32[]{:S(2)}) async-start(bf16[128,4,384]{2,1,0:T(4,128)(2,1)} %get-tuple-element.45), calls=%async_computation.1 | async-start | bytes 786432 | tf_op jit(solution)/shard_map/all_to_all | solution.py:461
  63.2 0.2 collective-permute-done.4.refs_5_
  63.5 0.7 collective-permute-done.3.refs_4_
  64.2 0.0 collective-permute-done.5.refs_6_
  64.2 0.9 copy-done.4
  65.1 1.9 %shard_map.144 = (f32[64,1152]{1,0:T(8,128)S(1)}, bf16[336,384]{1,0:T(8,128)(2,1)S(1)}, bf16[336,384]{1,0:T(8,128)(2,1)S(1)}, bf16[336,384]{1,0:T(8,128)(2,1)S(1)}, bf16[336,384]{1,0:T(8,128)(2,1)S(1)}) custom-call(s32[1]{0:T(128)} %bitcast.5.refs_0_, bf16[384,384]{1,0:T(8,128)(2,1)S(1)} %copy-done.3, bf16[384,384]{1,0:T(8,128)(2,1)} %collective-permute-done.2.refs_2_, ...), custom_call_target="tpu_custom_call" | custom-call | flops 999999995904 | bytes 2932740 | tf_op jit(solution)/shard_map/pallas_call | solution.py:89
  67.0 0.0 copy-start.2
  67.0 0.0 copy-start
  67.0 0.0 copy-start.1
  67.0 1.3 %collective-permute-start.6 = (bf16[336,384]{1,0:T(8,128)(2,1)S(1)}, bf16[336,384]{1,0:T(8,128)(2,1)S(1)}, u32[]{:S(2)}, u32[]{:S(2)}) collective-permute-start(bf16[336,384]{1,0:T(8,128)(2,1)S(1)} %get-tuple-element.63), channel_id=1, source_target_pairs={{0,16},{16,32},{32,48},{48,0},{1,17},{17,33},{33,49},{49,1},{2,18}... | collective-permute-start | bytes 774152 | tf_op jit(solution)/shard_map/ppermute | solution.py:360
  68.3 5.8 %collective-permute-start.7 = (bf16[336,384]{1,0:T(8,128)(2,1)S(1)}, bf16[336,384]{1,0:T(8,128)(2,1)S(1)}, u32[]{:S(2)}, u32[]{:S(2)}) collective-permute-start(bf16[336,384]{1,0:T(8,128)(2,1)S(1)} %get-tuple-element.64), channel_id=1, source_target_pairs={{0,32},{16,48},{32,0},{48,16},{1,33},{17,49},{33,1},{49,17},{2,34}... | collective-permute-start | bytes 774152 | tf_op jit(solution)/shard_map/ppermute | solution.py:360
  74.1 0.0 collective-permute-start.8
  74.1 5.1 %collective-permute-done.6.refs_2_ = bf16[336,384]{1,0:T(8,128)(2,1)S(1)} collective-permute-done((bf16[336,384]{1,0:T(8,128)(2,1)S(1)}, bf16[336,384]{1,0:T(8,128)(2,1)S(1)}, u32[]{:S(2)}, u32[]{:S(2)}) %collective-permute-start.6) | collective-permute-done | bytes 258080 | tf_op jit(solution)/shard_map/ppermute | solution.py:360
  79.1 1.7 %collective-permute-done.7.refs_3_ = bf16[336,384]{1,0:T(8,128)(2,1)S(1)} collective-permute-done((bf16[336,384]{1,0:T(8,128)(2,1)S(1)}, bf16[336,384]{1,0:T(8,128)(2,1)S(1)}, u32[]{:S(2)}, u32[]{:S(2)}) %collective-permute-start.7) | collective-permute-done | bytes 258080 | tf_op jit(solution)/shard_map/ppermute | solution.py:360
  80.9 2.6 %collective-permute-done.8.refs_4_ = bf16[336,384]{1,0:T(8,128)(2,1)S(1)} collective-permute-done((bf16[336,384]{1,0:T(8,128)(2,1)S(1)}, bf16[336,384]{1,0:T(8,128)(2,1)S(1)}, u32[]{:S(2)}, u32[]{:S(2)}) %collective-permute-start.8) | collective-permute-done | bytes 258080 | tf_op jit(solution)/shard_map/ppermute | solution.py:360
  83.5 1.1 %shard_map.145 = bf16[64,2688]{1,0:T(8,128)(2,1)} custom-call(f32[64,1152]{1,0:T(8,128)S(1)} %get-tuple-element.61.refs_0_, bf16[336,384]{1,0:T(8,128)(2,1)S(1)} %get-tuple-element.62.refs_1_, bf16[336,384]{1,0:T(8,128)(2,1)S(1)} %collective-permute-done.6.refs_2_, bf16[336,384]{1,0:T(8,128)(2,1)S(1)} %collective-permute-done.7.refs_3_, ...), custom_call_target="tpu_custom_call" | custom-call | bytes 1671168 | tf_op jit(solution)/shard_map/pallas_call | solution.py:89
  84.5 0.0 all-to-all-done.1.refs_1_
  84.5 5.2 %all-to-all-start.2 = ((bf16[8,8,2688]{2,1,0:T(8,128)(2,1)}), bf16[8,8,2688]{2,1,0:T(8,128)(2,1)S(1)}, u32[]{:S(2)}, u32[]{:S(2)}) async-start(bf16[8,8,2688]{2,1,0:T(8,128)(2,1)} %bitcast.6), calls=%async_computation.2 | async-start | bytes 688128 | tf_op jit(solution)/shard_map/all_to_all | solution.py:481
  89.7 1.8 %shard_map.142 = (f32[1024,384]{1,0:T(8,128)S(1)}, f32[8,128]{1,0:T(8,128)S(1)}) custom-call(s32[1,512]{1,0:T(1,128)S(1)} %copy-done.2, bf16[128,4,384]{2,1,0:T(4,128)(2,1)} %all-to-all-done.1.refs_1_), custom_call_target="tpu_custom_call" | custom-call | bytes 1972224 | tf_op jit(solution)/shard_map/pallas_call | solution.py:89
  91.5 0.1 collective-permute-start.1
  91.6 1.2 %collective-permute-done.1.refs_4_ = f32[8,128]{1,0:T(8,128)S(1)} collective-permute-done((f32[8,128]{1,0:T(8,128)S(1)}, f32[8,128]{1,0:T(8,128)S(1)}, u32[]{:S(2)}, u32[]{:S(2)}) %collective-permute-start.1) | collective-permute-done | bytes 4128 | tf_op jit(solution)/shard_map/ppermute | solution.py:360
  92.8 1.6 %shard_map.143 = (f32[1024,384]{1,0:T(8,128)}, f32[8,128]{1,0:T(8,128)}) custom-call(f32[1024,384]{1,0:T(8,128)S(1)} %copy-done, f32[1024,384]{1,0:T(8,128)S(1)} %get-tuple-element.46.refs_1_, f32[8,128]{1,0:T(8,128)S(1)} %bitcast.11, f32[8,128]{1,0:T(8,128)S(1)} %get-tuple-element.47.refs_3_, f32[8,128]{1,0:T(8,128)S(1)} %collective-permute-done.1.refs_4_), custom_call_target="tpu_custom_call" | custom-call | bytes 4734976 | tf_op jit(solution)/shard_map/pallas_call | solution.py:89
  94.4 8.7 %all-to-all-done.2.refs_0_ = bf16[8,8,2688]{2,1,0:T(8,128)(2,1)S(1)} async-done(((bf16[8,8,2688]{2,1,0:T(8,128)(2,1)}), bf16[8,8,2688]{2,1,0:T(8,128)(2,1)S(1)}, u32[]{:S(2)}, u32[]{:S(2)}) %all-to-all-start.2) | async-done | bytes 344096 | tf_op jit(solution)/shard_map/all_to_all | solution.py:481
  103.1 0.7 shard_map.146
  (20 shorter events, 0.1 us)
Async XLA Ops:
  0.6 18.8 %copy-start.7 = (s32[8,15]{1,0:T(8,128)S(1)}, s32[8,15]{1,0:T(8,128)}, u32[]{:S(2)}) copy-start(s32[8,15]{1,0:T(8,128)} %param.15) | copy-start | bytes 1444
  0.6 18.8 %copy-start.8 = (s32[8,15]{1,0:T(8,128)S(1)}, s32[8,15]{1,0:T(8,128)}, u32[]{:S(2)}) copy-start(s32[8,15]{1,0:T(8,128)} %param.17) | copy-start | bytes 1444
  0.7 18.8 %copy-start.9 = (s32[8]{0:T(128)S(1)}, s32[8]{0:T(128)}, u32[]{:S(2)}) copy-start(s32[8]{0:T(128)} %param.14) | copy-start | bytes 100
  0.7 19.2 %copy-start.5 = (s32[8,15,10]{1,0,2:T(8,128)S(1)}, s32[8,15,10]{1,0,2:T(8,128)}, u32[]{:S(2)}) copy-start(s32[8,15,10]{1,0,2:T(8,128)} %param.16) | copy-start | bytes 14404
  0.7 19.2 %copy-start.6 = (s32[8,15,10]{1,0,2:T(8,128)S(1)}, s32[8,15,10]{1,0,2:T(8,128)}, u32[]{:S(2)}) copy-start(s32[8,15,10]{1,0,2:T(8,128)} %param.18) | copy-start | bytes 14404
  3.6 31.3 %all-to-all-start = ((bf16[128,4,384]{2,1,0:T(4,128)(2,1)}), bf16[128,4,384]{2,1,0:T(4,128)(2,1)}, u32[]{:S(2)}, u32[]{:S(2)}) async-start(bf16[128,4,384]{2,1,0:T(4,128)(2,1)} %shard_map.138), calls=%async_computation | async-start | bytes 786432 | tf_op jit(solution)/shard_map/all_to_all | solution.py:397
  38.3 2.2 %collective-permute-start = (f32[128,1024]{1,0:T(8,128)}, f32[128,1024]{1,0:T(8,128)S(1)}, u32[]{:S(2)}, u32[]{:S(2)}) collective-permute-start(f32[128,1024]{1,0:T(8,128)} %get-tuple-element.39.refs_1_), channel_id=1, source_target_pairs={{0,1},{1,0},{2,3},{3,2},{4,5},{5,4},{6,7},{7,6},{8,9},{9,8},{10,11... | collective-permute-start | bytes 1572872 | tf_op jit(solution)/shard_map/ppermute | solution.py:360
  38.4 11.2 %collective-permute-start.2 = (bf16[384,384]{1,0:T(8,128)(2,1)}, bf16[384,384]{1,0:T(8,128)(2,1)}, u32[]{:S(2)}, u32[]{:S(2)}) collective-permute-start(bf16[384,384]{1,0:T(8,128)(2,1)} %get-tuple-element.55.refs_9_.refs_1_), channel_id=1, source_target_pairs={{0,128},{64,192},{128,0},{192,64},{1,129},{65,193},{129,1},{193,65... | collective-permute-start | bytes 884744 | tf_op jit(solution)/shard_map/ppermute | solution.py:360
  40.5 0.8 copy-start.10
  41.3 22.9 %copy-start.3 = (bf16[384,384]{1,0:T(8,128)(2,1)S(1)}, bf16[384,384]{1,0:T(8,128)(2,1)}, u32[]{:S(2)}) copy-start(bf16[384,384]{1,0:T(8,128)(2,1)} %get-tuple-element.55.refs_9_.refs_1_) | copy-start | bytes 884740
  49.6 14.5 %collective-permute-start.3 = (bf16[1568,128]{1,0:T(8,128)(2,1)}, bf16[1568,128]{1,0:T(8,128)(2,1)S(1)}, u32[]{:S(2)}, u32[]{:S(2)}) collective-permute-start(bf16[1568,128]{1,0:T(8,128)(2,1)} %get-tuple-element.58), channel_id=1, source_target_pairs={{0,64},{64,128},{128,192},{192,0},{1,65},{65,129},{129,193},{193,1... | collective-permute-start | bytes 1204232 | tf_op jit(solution)/shard_map/ppermute | solution.py:360
  50.4 13.8 %collective-permute-start.5 = (bf16[1568,128]{1,0:T(8,128)(2,1)}, bf16[1568,128]{1,0:T(8,128)(2,1)S(1)}, u32[]{:S(2)}, u32[]{:S(2)}) collective-permute-start(bf16[1568,128]{1,0:T(8,128)(2,1)} %get-tuple-element.60), channel_id=1, source_target_pairs={{0,192},{64,0},{128,64},{192,128},{1,193},{65,1},{129,65},{193,129... | collective-permute-start | bytes 1204232 | tf_op jit(solution)/shard_map/ppermute | solution.py:360
  52.9 10.6 %collective-permute-start.4 = (bf16[208,256]{1,0:T(8,128)(2,1)}, bf16[208,256]{1,0:T(8,128)(2,1)S(1)}, u32[]{:S(2)}, u32[]{:S(2)}) collective-permute-start(bf16[208,256]{1,0:T(8,128)(2,1)} %get-tuple-element.59), channel_id=1, source_target_pairs={{0,128},{64,192},{128,0},{192,64},{1,129},{65,193},{129,1},{193,65... | collective-permute-start | bytes 319496 | tf_op jit(solution)/shard_map/ppermute | solution.py:360
  53.2 31.3 %all-to-all-start.1 = ((bf16[128,4,384]{2,1,0:T(4,128)(2,1)}), bf16[128,4,384]{2,1,0:T(4,128)(2,1)}, u32[]{:S(2)}, u32[]{:S(2)}) async-start(bf16[128,4,384]{2,1,0:T(4,128)(2,1)} %get-tuple-element.45), calls=%async_computation.1 | async-start | bytes 786432 | tf_op jit(solution)/shard_map/all_to_all | solution.py:461
  64.2 0.9 copy-start.4
  67.0 22.7 %copy-start.2 = (s32[1,512]{1,0:T(1,128)S(1)}, s32[1,512]{1,0:T(1,128)}, u32[]{:S(2)}) copy-start(s32[1,512]{1,0:T(1,128)} %refs_0_.4) | copy-start | bytes 6148
  67.0 25.8 %copy-start = (f32[1024,384]{1,0:T(8,128)S(1)}, f32[1024,384]{1,0:T(8,128)}, u32[]{:S(2)}) copy-start(f32[1024,384]{1,0:T(8,128)} %refs_0_.5) | copy-start | bytes 4718596
  67.0 25.7 %copy-start.1 = (f32[1024]{0:T(1024)S(1)}, f32[1024]{0:T(1024)}, u32[]{:S(2)}) copy-start(f32[1024]{0:T(1024)} %param.12) | copy-start | bytes 12292
  67.0 12.1 %collective-permute-start.6 = (bf16[336,384]{1,0:T(8,128)(2,1)S(1)}, bf16[336,384]{1,0:T(8,128)(2,1)S(1)}, u32[]{:S(2)}, u32[]{:S(2)}) collective-permute-start(bf16[336,384]{1,0:T(8,128)(2,1)S(1)} %get-tuple-element.63), channel_id=1, source_target_pairs={{0,16},{16,32},{32,48},{48,0},{1,17},{17,33},{33,49},{49,1},{2,18}... | collective-permute-start | bytes 774152 | tf_op jit(solution)/shard_map/ppermute | solution.py:360
  68.3 12.6 %collective-permute-start.7 = (bf16[336,384]{1,0:T(8,128)(2,1)S(1)}, bf16[336,384]{1,0:T(8,128)(2,1)S(1)}, u32[]{:S(2)}, u32[]{:S(2)}) collective-permute-start(bf16[336,384]{1,0:T(8,128)(2,1)S(1)} %get-tuple-element.64), channel_id=1, source_target_pairs={{0,32},{16,48},{32,0},{48,16},{1,33},{17,49},{33,1},{49,17},{2,34}... | collective-permute-start | bytes 774152 | tf_op jit(solution)/shard_map/ppermute | solution.py:360
  74.1 9.4 %collective-permute-start.8 = (bf16[336,384]{1,0:T(8,128)(2,1)S(1)}, bf16[336,384]{1,0:T(8,128)(2,1)S(1)}, u32[]{:S(2)}, u32[]{:S(2)}) collective-permute-start(bf16[336,384]{1,0:T(8,128)(2,1)S(1)} %get-tuple-element.65), channel_id=1, source_target_pairs={{0,48},{16,0},{32,16},{48,32},{1,49},{17,1},{33,17},{49,33},{2,50}... | collective-permute-start | bytes 774152 | tf_op jit(solution)/shard_map/ppermute | solution.py:360
  84.5 18.6 %all-to-all-start.2 = ((bf16[8,8,2688]{2,1,0:T(8,128)(2,1)}), bf16[8,8,2688]{2,1,0:T(8,128)(2,1)S(1)}, u32[]{:S(2)}, u32[]{:S(2)}) async-start(bf16[8,8,2688]{2,1,0:T(8,128)(2,1)} %bitcast.6), calls=%async_computation.2 | async-start | bytes 688128 | tf_op jit(solution)/shard_map/all_to_all | solution.py:481
  91.5 1.2 %collective-permute-start.1 = (f32[8,128]{1,0:T(8,128)S(1)}, f32[8,128]{1,0:T(8,128)S(1)}, u32[]{:S(2)}, u32[]{:S(2)}) collective-permute-start(f32[8,128]{1,0:T(8,128)S(1)} %get-tuple-element.47.refs_3_), channel_id=1, source_target_pairs={{0,1},{1,0},{2,3},{3,2},{4,5},{5,4},{6,7},{7,6},{8,9},{9,8},{10,11... | collective-permute-start | bytes 12296 | tf_op jit(solution)/shard_map/ppermute | solution.py:360

commit v8 on v7

--- a/solution.py
+++ b/solution.py
@@ -51,12 +51,12 @@
         self.copy.start()
 
 
-def call(kernel, outs, operands, smem=0, scratch=(), hbm_in=(), hbm_out=(), hbm_raw=()):
+def call(kernel, outs, operands, smem=0, scratch=(), hbm_in=(), hbm_out=(), raw_in=(), hbm_raw=()):
     name = getattr(kernel, "func", kernel)
     limit, flops = LIMITS.get(name, 12), COSTS.get(name, 10**12)
     moved = sum(o.size * o.dtype.itemsize for o in list(operands) + list(outs))
     specs = [
-        pl.BlockSpec(memory_space=pltpu.SMEM if i < smem else pltpu.HBM if i in hbm_in else pltpu.VMEM)
+        pl.BlockSpec(memory_space=pltpu.SMEM if i < smem else pltpu.HBM if i in hbm_in or i in raw_in else pltpu.VMEM)
         for i in range(len(operands))
     ]
     made = [
@@ -105,14 +105,28 @@
     return jax.ShapeDtypeStruct(shape, dtype)
 
 
-def serve_kernel(serve_ref, table_ref, out_ref, onehot):
+def serve_kernel(serve_ref, table_ref, out_ref, onehot, rows, picked, sems):
+    chunks = range(table_ref.shape[1] // LANES)
+    loads = [
+        pltpu.make_async_copy(table_ref.at[:, i * LANES : (i + 1) * LANES], rows.at[i], sems.at[i]) for i in chunks
+    ]
+    for load in loads:
+        load.start()
     serve = serve_ref.get()[...]
     lanes = lax.broadcasted_iota(jnp.int32, (LANES, onehot.shape[1]), 1)
     for block in range(serve.shape[1] // LANES):
         span = slice(block * LANES, (block + 1) * LANES)
         onehot[span, :] = jnp.where(row_to_column(serve[:, span]) == lanes, 1.0, 0.0).astype(BF16)
-    rows = table_ref.get()[...].astype(BF16)
-    out_ref[...] = matmul(onehot[...], rows).astype(BF16).reshape(out_ref.shape)
+    stores = []
+    for i in chunks:
+        loads[i].wait()
+        found = matmul(onehot[...], rows[i].astype(BF16)).astype(BF16)
+        picked[i] = found.reshape(picked.shape[1:])
+        target = out_ref.at[:, :, i * LANES : (i + 1) * LANES]
+        stores.append(pltpu.make_async_copy(picked.at[i], target, sems.at[len(chunks) + i]))
+        stores[i].start()
+    for store in stores:
+        store.wait()
 
 
 def index_kernel(idx_ref, cot_ref, w2_ref, *refs):
@@ -153,30 +167,36 @@
     outs[-1].send()
 
 
-def first_kernel(fetched_ref, ct_ref, w1_ref, layer_ref, partial_ref):
+def first_kernel(fetched_ref, ct_ref, w1_ref, layer_ref, partial_out, wide, partial_ref, sems):
     layers = w1_ref.shape[0]
-    layer_out, partial_out = layer_ref, partial_ref
-    layer_ref, partial_ref = layer_ref.buffer, partial_ref.buffer
+    layer_out, layer_ref = layer_ref, layer_ref.buffer
     nodes = partial_ref.shape[0]
     fetched = fetched_ref.get()[...].reshape(ct_ref.shape[1], layer_ref.shape[1])
-    total = None
     ct_ref = ct_ref.get()
     ones = jnp.ones((ct_ref.shape[1], LANES), BF16)
+    columns = layer_ref.shape[1]
     for k in range(layers):
         span = slice(k * nodes, (k + 1) * nodes)
         summed = matmul(ct_ref[span, :], fetched)
         inverse = 1.0 / jnp.maximum(matmul(ct_ref[span, :], ones)[:, 0:1], 1.0)
-        layer_ref[span, :] = (summed * inverse).astype(BF16)
+        layer = (summed * inverse).astype(BF16)
+        layer_ref[span, :] = layer
+        wide[:, k * columns : (k + 1) * columns] = layer
     layer_out.send()
-    for k in range(layers):
-        term = matmul(layer_ref[k * nodes : (k + 1) * nodes, :], w1_ref.get()[k])
-        total = term if total is None else total + term
-    partial_ref[...] = total
-    partial_out.send()
+    weights = w1_ref.get()[...].reshape(layers * columns, partial_ref.shape[1])
+    half = partial_ref.shape[1] // 2
+    copies = []
+    for i in range(2):
+        span = slice(i * half, (i + 1) * half)
+        partial_ref[:, span] = matmul(wide[...], weights[:, span])
+        copies.append(pltpu.make_async_copy(partial_ref.at[:, span], partial_out.at[:, span], sems.at[i]))
+        copies[i].start()
+    for copy in copies:
+        copy.wait()
 
 
 def hidden_kernel(place_ref, mine_ref, other_ref, back_ref, e_ref, inv_ref, cot_ref, c_ref, w1_ref, layer_ref, slot_ref, *refs):
-    packs, stage, sems = refs[:-2], refs[-2], refs[-1]
+    packs, (stage, scaled, sems) = refs[:-3], refs[-3:]
     nodes = mine_ref.shape[0]
     width = stage.shape[2]
     seeds = cot_ref.shape[0]
@@ -221,13 +241,12 @@
     copies = [pltpu.make_async_copy(source, target, sems.at[i]) for i, (source, target) in enumerate(moves)]
     for copy in copies:
         copy.start()
-    total = None
+    columns = w1_ref.shape[1]
+    back_in = matmul(back, w1_ref.get()[...].reshape(layers * columns, back.shape[1]), (1, 1))
     for k in range(layers):
         span = slice(k * nodes, (k + 1) * nodes)
-        back_in = matmul(back, w1_ref.get()[k], (1, 1)) * inv_ref[span, 0:1]
-        term = matmul(c_ref.get()[:, span], back_in.astype(BF16))
-        total = term if total is None else total + term
-    slot_ref[...] = total.astype(BF16).reshape(slot_ref.shape)
+        scaled[span, :] = (back_in[:, k * columns : (k + 1) * columns] * inv_ref[span, 0:1]).astype(BF16)
+    slot_ref[...] = matmul(c_ref.get()[...], scaled[...]).astype(BF16).reshape(slot_ref.shape)
     for copy in copies:
         copy.wait()
 
@@ -391,8 +410,20 @@
     width = hidden_units // n_x
 
     blocks_shape = (owners, slots // owners, columns)
+    chunks = columns // LANES
     outgoing = call(
-        serve_kernel, [shaped(blocks_shape, BF16)], (serve_rows, table), scratch=[pltpu.VMEM((slots, table_rows), BF16)], hbm_in=(0, 1)
+        serve_kernel,
+        [shaped(blocks_shape, BF16)],
+        (serve_rows, table),
+        scratch=[
+            pltpu.VMEM((slots, table_rows), BF16),
+            pltpu.VMEM((chunks, table_rows, LANES), F32),
+            pltpu.VMEM((chunks, *blocks_shape[:2], LANES), BF16),
+            pltpu.SemaphoreType.DMA((2 * chunks,)),
+        ],
+        hbm_in=(0,),
+        raw_in=(1,),
+        hbm_raw=(0,),
     )[0]
     fetched = lax.all_to_all(outgoing, everyone, split_axis=0, concat_axis=0, tiled=True)
 
@@ -427,8 +458,14 @@
         first_kernel,
         [shaped((layers * nodes, columns), BF16), shaped((nodes, hidden_units), F32)],
         (fetched, ct, w_first),
+        scratch=[
+            pltpu.VMEM((nodes, layers * columns), BF16),
+            pltpu.VMEM((nodes, hidden_units), F32),
+            pltpu.SemaphoreType.DMA((2,)),
+        ],
         hbm_in=(0, 1, 2),
-        hbm_out=(0, 1),
+        hbm_out=(0,),
+        hbm_raw=(1,),
     )
     other_pre = shift(partial_pre, "col", 1)
     layer_parts = [layer_in, shift(layer_in, "dp", n_x // 2)]
@@ -452,11 +489,15 @@
             layer_in,
         ),
         smem=1,
-        scratch=[pltpu.VMEM((n_x, *pack_shape), BF16), pltpu.SemaphoreType.DMA((n_x * (width + columns) // LANES,))],
-        hbm_in=(1, 2, 3, 4, 5, 7, 8, 9),
+        scratch=[
+            pltpu.VMEM((n_x, *pack_shape), BF16),
+            pltpu.VMEM((layers * nodes, columns), BF16),
+            pltpu.SemaphoreType.DMA((n_x * (width + columns) // LANES,)),
+        ],
+        hbm_in=(1, 2, 3, 4, 5, 9, 8, 7),
         hbm_raw=range(1, 1 + n_x),
     )
-    packs, layer_parts = lax.optimization_barrier((packs, layer_parts))
+    packs[n_x // 2], layer_parts = lax.optimization_barrier((packs[n_x // 2], layer_parts))
     packs = [packs[0]] + [shift(packs[d], "dp", d) for d in range(1, n_x)]
     arrived = lax.all_to_all(slot_grad, everyone, split_axis=0, concat_axis=0, tiled=True)
 

time: 104 us -> 103 us (level)
  transfers between devices with their start and end apart: 12 -> 12, of which waited for: 10 -> 9; matrix products, arithmetic and copies ran while one was open for 2% -> 2% of each run, Pallas kernels for 18% -> 18%
where the time goes in v8:
time: 103 us
  starting transfers between devices  42.6 us (41%)
  waiting for transfers between devices  29.5 us (29%)
  Pallas kernels  26.1 us (25%)
  local copies, waits for them, and re-layouts  2.91 us (3%)
    pallas_call x9, Pallas kernels, call(): pl.pallas_call(wrapped, out_shape=tuple(outs), in_specs=specs, out_specs=...  26.1 us
    all_to_all x1, starting transfers between devices, body(): lax.all_to_all(outgoing, everyone, split_axis=0, concat_axis=0, tiled=True)  15.8 us
    ppermute x9, waiting for transfers between devices, shift(): lax.ppermute(array, axis, [(i, (i + by) % size) for i in range(size)])  13.5 us
    ppermute x9, starting transfers between devices, shift(): lax.ppermute(array, axis, [(i, (i + by) % size) for i in range(size)])  13.1 us
    all_to_all x1, starting transfers between devices, body(): lax.all_to_all(slot_grad, everyone, split_axis=0, concat_axis=0, tiled=True)  9.49 us
    all_to_all x1, waiting for transfers between devices, body(): grads = lax.all_to_all(grads, 'z', split_axis=0, concat_axis=0, tiled=True)  8.76 us
    all_to_all x1, waiting for transfers between devices, body(): lax.all_to_all(outgoing, everyone, split_axis=0, concat_axis=0, tiled=True)  7.27 us
    all_to_all x1, starting transfers between devices, body(): grads = lax.all_to_all(grads, 'z', split_axis=0, concat_axis=0, tiled=True)  4.19 us
  transfers between devices with their start and end apart: 12, of which 9 were waited for; matrix products, arithmetic and copies ran while one was open for 2% of the time, Pallas kernels for 18%

profile of v8, /device:TPU:8, one launch (start us, length us, event | category | flops | bytes accessed | tf_op | source)
XLA Modules:
  0.0 102.7 jit_solution(10845943647723372917)
XLA Ops:
  0.7 4.0 %shard_map.138 = bf16[128,4,384]{2,1,0:T(4,128)(2,1)} custom-call(s32[1,512]{1,0:T(1,128)} %refs_0_.4, f32[1024,384]{1,0:T(8,128)} %refs_0_.5), custom_call_target="tpu_custom_call" | custom-call | flops 999999995904 | bytes 1968128 | tf_op jit(solution)/shard_map/pallas_call | solution.py:89
  4.7 15.8 %all-to-all-start = ((bf16[128,4,384]{2,1,0:T(4,128)(2,1)}), bf16[128,4,384]{2,1,0:T(4,128)(2,1)}, u32[]{:S(2)}, u32[]{:S(2)}) async-start(bf16[128,4,384]{2,1,0:T(4,128)(2,1)} %shard_map.138), calls=%async_computation | async-start | bytes 786432 | tf_op jit(solution)/shard_map/all_to_all | solution.py:428
  20.5 0.1 reshape.29
  20.6 0.0 copy-done.8
  20.6 0.1 copy.32
  20.7 0.1 pad_add_fusion
  20.8 0.1 copy.33
  20.8 0.1 reshape.31
  20.9 0.1 reshape.30
  21.0 0.6 pad_add_fusion.1.refs_0_
  21.6 0.1 add_add_fusion
  21.7 0.8 copy.34.refs_0_
  22.5 6.3 %shard_map.139 = (bf16[384,512]{1,0:T(8,128)(2,1)}, bf16[512,384]{1,0:T(8,128)(2,1)}, f32[384,128]{1,0:T(8,128)}, bf16[32,128]{1,0:T(8,128)(2,1)}, f32[128,1024]{1,0:T(8,128)}) custom-call(s32[128,17]{1,0:T(8,128)} %copy.34.refs_0_, bf16[8,1024]{1,0:T(8,128)(2,1)} %refs_6_.1, bf16[3,1024,1024]{2,1,0:T(8,128)(2,1)} %refs_2_.2), custom_call_target="tpu_custom_call" | custom-call | flops 999999995904 | bytes 7832064 | tf_op jit(solution)/shard_map/pallas_call | solution.py:89
  28.8 7.3 %all-to-all-done.refs_0_ = bf16[128,4,384]{2,1,0:T(4,128)(2,1)} async-done(((bf16[128,4,384]{2,1,0:T(4,128)(2,1)}), bf16[128,4,384]{2,1,0:T(4,128)(2,1)}, u32[]{:S(2)}, u32[]{:S(2)}) %all-to-all-start) | async-done | bytes 393248 | tf_op jit(solution)/shard_map/all_to_all | solution.py:428
  36.0 3.2 %shard_map.140 = (bf16[384,384]{1,0:T(8,128)(2,1)}, f32[128,1024]{1,0:T(8,128)}) custom-call(bf16[128,4,384]{2,1,0:T(4,128)(2,1)} %all-to-all-done.refs_0_, bf16[384,512]{1,0:T(8,128)(2,1)} %get-tuple-element.35.refs_1_, bf16[3,384,1024]{2,1,0:T(8,128)(2,1)} %refs_8_.1), custom_call_target="tpu_custom_call" | custom-call | flops 999999995904 | bytes 3964928 | tf_op jit(solution)/shard_map/pallas_call | solution.py:89
  39.3 0.1 collective-permute-start
  39.4 1.6 %collective-permute-start.2 = (bf16[384,384]{1,0:T(8,128)(2,1)}, bf16[384,384]{1,0:T(8,128)(2,1)}, u32[]{:S(2)}, u32[]{:S(2)}) collective-permute-start(bf16[384,384]{1,0:T(8,128)(2,1)} %get-tuple-element.49.refs_9_.refs_1_), channel_id=1, source_target_pairs={{0,128},{64,192},{128,0},{192,64},{1,129},{65,193},{129,1},{193,65... | collective-permute-start | bytes 884744 | tf_op jit(solution)/shard_map/ppermute | solution.py:379
  41.0 0.5 collective-permute-done.refs_2_
  41.5 0.8 copy-done.10
  42.3 5.5 %shard_map.141 = (bf16[128,4,384]{2,1,0:T(4,128)(2,1)}, bf16[208,256]{1,0:T(8,128)(2,1)}, bf16[1568,128]{1,0:T(8,128)(2,1)}, bf16[208,256]{1,0:T(8,128)(2,1)}, bf16[1568,128]{1,0:T(8,128)(2,1)}) custom-call(s32[2]{0:T(128)} %pad_add_fusion.1.refs_0_, f32[128,1024]{1,0:T(8,128)} %get-tuple-element.36.refs_1_, f32[128,1024]{1,0:T(8,128)} %copy-done.10, ...), custom_call_target="tpu_custom_call" | custom-call | flops 999999995904 | bytes 6250504 | tf_op jit(solution)/shard_map/pallas_call | solution.py:89
  47.8 0.9 collective-permute-start.3
  48.7 2.4 %collective-permute-start.5 = (bf16[1568,128]{1,0:T(8,128)(2,1)}, bf16[1568,128]{1,0:T(8,128)(2,1)S(1)}, u32[]{:S(2)}, u32[]{:S(2)}) collective-permute-start(bf16[1568,128]{1,0:T(8,128)(2,1)} %get-tuple-element.54), channel_id=1, source_target_pairs={{0,192},{64,0},{128,64},{192,128},{1,193},{65,1},{129,65},{193,129... | collective-permute-start | bytes 1204232 | tf_op jit(solution)/shard_map/ppermute | solution.py:379
  51.1 0.0 collective-permute-done.2.refs_2_
  51.1 1.0 %collective-permute-start.4 = (bf16[208,256]{1,0:T(8,128)(2,1)}, bf16[208,256]{1,0:T(8,128)(2,1)S(1)}, u32[]{:S(2)}, u32[]{:S(2)}) collective-permute-start(bf16[208,256]{1,0:T(8,128)(2,1)} %get-tuple-element.53), channel_id=1, source_target_pairs={{0,128},{64,192},{128,0},{192,64},{1,129},{65,193},{129,1},{193,65... | collective-permute-start | bytes 319496 | tf_op jit(solution)/shard_map/ppermute | solution.py:379
  52.2 9.5 %all-to-all-start.1 = ((bf16[128,4,384]{2,1,0:T(4,128)(2,1)}), bf16[128,4,384]{2,1,0:T(4,128)(2,1)}, u32[]{:S(2)}, u32[]{:S(2)}) async-start(bf16[128,4,384]{2,1,0:T(4,128)(2,1)} %get-tuple-element.42), calls=%async_computation.1 | async-start | bytes 786432 | tf_op jit(solution)/shard_map/all_to_all | solution.py:502
  61.7 1.0 %collective-permute-done.4.refs_5_ = bf16[208,256]{1,0:T(8,128)(2,1)S(1)} collective-permute-done((bf16[208,256]{1,0:T(8,128)(2,1)}, bf16[208,256]{1,0:T(8,128)(2,1)S(1)}, u32[]{:S(2)}, u32[]{:S(2)}) %collective-permute-start.4) | collective-permute-done | bytes 106528 | tf_op jit(solution)/shard_map/ppermute | solution.py:379
  62.7 0.2 collective-permute-done.3.refs_4_
  62.9 0.0 collective-permute-done.5.refs_6_
  63.0 0.9 copy-done.4
  63.9 1.9 %shard_map.144 = (f32[64,1152]{1,0:T(8,128)S(1)}, bf16[336,384]{1,0:T(8,128)(2,1)S(1)}, bf16[336,384]{1,0:T(8,128)(2,1)S(1)}, bf16[336,384]{1,0:T(8,128)(2,1)S(1)}, bf16[336,384]{1,0:T(8,128)(2,1)S(1)}) custom-call(s32[1]{0:T(128)} %bitcast.5.refs_0_, bf16[384,384]{1,0:T(8,128)(2,1)S(1)} %copy-done.3, bf16[384,384]{1,0:T(8,128)(2,1)} %collective-permute-done.2.refs_2_, ...), custom_call_target="tpu_custom_call" | custom-call | flops 999999995904 | bytes 2932740 | tf_op jit(solution)/shard_map/pallas_call | solution.py:89
  65.7 0.0 copy-start.2
  65.8 0.0 copy-start
  65.8 0.0 copy-start.1
  65.8 1.3 %collective-permute-start.6 = (bf16[336,384]{1,0:T(8,128)(2,1)S(1)}, bf16[336,384]{1,0:T(8,128)(2,1)S(1)}, u32[]{:S(2)}, u32[]{:S(2)}) collective-permute-start(bf16[336,384]{1,0:T(8,128)(2,1)S(1)} %get-tuple-element.57), channel_id=1, source_target_pairs={{0,16},{16,32},{32,48},{48,0},{1,17},{17,33},{33,49},{49,1},{2,18}... | collective-permute-start | bytes 774152 | tf_op jit(solution)/shard_map/ppermute | solution.py:379
  67.1 5.7 %collective-permute-start.7 = (bf16[336,384]{1,0:T(8,128)(2,1)S(1)}, bf16[336,384]{1,0:T(8,128)(2,1)S(1)}, u32[]{:S(2)}, u32[]{:S(2)}) collective-permute-start(bf16[336,384]{1,0:T(8,128)(2,1)S(1)} %get-tuple-element.58), channel_id=1, source_target_pairs={{0,32},{16,48},{32,0},{48,16},{1,33},{17,49},{33,1},{49,17},{2,34}... | collective-permute-start | bytes 774152 | tf_op jit(solution)/shard_map/ppermute | solution.py:379
  72.8 0.0 collective-permute-start.8
  72.8 5.4 %collective-permute-done.6.refs_2_ = bf16[336,384]{1,0:T(8,128)(2,1)S(1)} collective-permute-done((bf16[336,384]{1,0:T(8,128)(2,1)S(1)}, bf16[336,384]{1,0:T(8,128)(2,1)S(1)}, u32[]{:S(2)}, u32[]{:S(2)}) %collective-permute-start.6) | collective-permute-done | bytes 258080 | tf_op jit(solution)/shard_map/ppermute | solution.py:379
  78.2 2.0 %collective-permute-done.7.refs_3_ = bf16[336,384]{1,0:T(8,128)(2,1)S(1)} collective-permute-done((bf16[336,384]{1,0:T(8,128)(2,1)S(1)}, bf16[336,384]{1,0:T(8,128)(2,1)S(1)}, u32[]{:S(2)}, u32[]{:S(2)}) %collective-permute-start.7) | collective-permute-done | bytes 258080 | tf_op jit(solution)/shard_map/ppermute | solution.py:379
  80.1 3.2 %collective-permute-done.8.refs_4_ = bf16[336,384]{1,0:T(8,128)(2,1)S(1)} collective-permute-done((bf16[336,384]{1,0:T(8,128)(2,1)S(1)}, bf16[336,384]{1,0:T(8,128)(2,1)S(1)}, u32[]{:S(2)}, u32[]{:S(2)}) %collective-permute-start.8) | collective-permute-done | bytes 258080 | tf_op jit(solution)/shard_map/ppermute | solution.py:379
  83.3 1.1 %shard_map.145 = bf16[64,2688]{1,0:T(8,128)(2,1)} custom-call(f32[64,1152]{1,0:T(8,128)S(1)} %get-tuple-element.55.refs_0_, bf16[336,384]{1,0:T(8,128)(2,1)S(1)} %get-tuple-element.56.refs_1_, bf16[336,384]{1,0:T(8,128)(2,1)S(1)} %collective-permute-done.6.refs_2_, bf16[336,384]{1,0:T(8,128)(2,1)S(1)} %collective-permute-done.7.refs_3_, ...), custom_call_target="tpu_custom_call" | custom-call | bytes 1671168 | tf_op jit(solution)/shard_map/pallas_call | solution.py:89
  84.4 0.0 all-to-all-done.1.refs_1_
  84.4 4.2 %all-to-all-start.2 = ((bf16[8,8,2688]{2,1,0:T(8,128)(2,1)}), bf16[8,8,2688]{2,1,0:T(8,128)(2,1)S(1)}, u32[]{:S(2)}, u32[]{:S(2)}) async-start(bf16[8,8,2688]{2,1,0:T(8,128)(2,1)} %bitcast.6), calls=%async_computation.2 | async-start | bytes 688128 | tf_op jit(solution)/shard_map/all_to_all | solution.py:522
  88.6 1.9 %shard_map.142 = (f32[1024,384]{1,0:T(8,128)S(1)}, f32[8,128]{1,0:T(8,128)S(1)}) custom-call(s32[1,512]{1,0:T(1,128)S(1)} %copy-done.2, bf16[128,4,384]{2,1,0:T(4,128)(2,1)} %all-to-all-done.1.refs_1_), custom_call_target="tpu_custom_call" | custom-call | bytes 1972224 | tf_op jit(solution)/shard_map/pallas_call | solution.py:89
  90.4 0.1 collective-permute-start.1
  90.5 1.2 %collective-permute-done.1.refs_4_ = f32[8,128]{1,0:T(8,128)S(1)} collective-permute-done((f32[8,128]{1,0:T(8,128)S(1)}, f32[8,128]{1,0:T(8,128)S(1)}, u32[]{:S(2)}, u32[]{:S(2)}) %collective-permute-start.1) | collective-permute-done | bytes 4128 | tf_op jit(solution)/shard_map/ppermute | solution.py:379
  91.6 1.6 %shard_map.143 = (f32[1024,384]{1,0:T(8,128)}, f32[8,128]{1,0:T(8,128)}) custom-call(f32[1024,384]{1,0:T(8,128)S(1)} %copy-done, f32[1024,384]{1,0:T(8,128)S(1)} %get-tuple-element.43.refs_1_, f32[8,128]{1,0:T(8,128)S(1)} %bitcast.11, f32[8,128]{1,0:T(8,128)S(1)} %get-tuple-element.44.refs_3_, f32[8,128]{1,0:T(8,128)S(1)} %collective-permute-done.1.refs_4_), custom_call_target="tpu_custom_call" | custom-call | bytes 4734976 | tf_op jit(solution)/shard_map/pallas_call | solution.py:89
  93.2 8.8 %all-to-all-done.2.refs_0_ = bf16[8,8,2688]{2,1,0:T(8,128)(2,1)S(1)} async-done(((bf16[8,8,2688]{2,1,0:T(8,128)(2,1)}), bf16[8,8,2688]{2,1,0:T(8,128)(2,1)S(1)}, u32[]{:S(2)}, u32[]{:S(2)}) %all-to-all-start.2) | async-done | bytes 344096 | tf_op jit(solution)/shard_map/all_to_all | solution.py:522
  102.0 0.7 shard_map.146
  (20 shorter events, 0.1 us)
Async XLA Ops:
  0.6 19.9 %copy-start.7 = (s32[8,15]{1,0:T(8,128)S(1)}, s32[8,15]{1,0:T(8,128)}, u32[]{:S(2)}) copy-start(s32[8,15]{1,0:T(8,128)} %param.15) | copy-start | bytes 1444
  0.6 19.9 %copy-start.8 = (s32[8,15]{1,0:T(8,128)S(1)}, s32[8,15]{1,0:T(8,128)}, u32[]{:S(2)}) copy-start(s32[8,15]{1,0:T(8,128)} %param.17) | copy-start | bytes 1444
  0.7 19.9 %copy-start.9 = (s32[8]{0:T(128)S(1)}, s32[8]{0:T(128)}, u32[]{:S(2)}) copy-start(s32[8]{0:T(128)} %param.14) | copy-start | bytes 100
  0.7 20.3 %copy-start.5 = (s32[8,15,10]{1,0,2:T(8,128)S(1)}, s32[8,15,10]{1,0,2:T(8,128)}, u32[]{:S(2)}) copy-start(s32[8,15,10]{1,0,2:T(8,128)} %param.16) | copy-start | bytes 14404
  0.7 20.3 %copy-start.6 = (s32[8,15,10]{1,0,2:T(8,128)S(1)}, s32[8,15,10]{1,0,2:T(8,128)}, u32[]{:S(2)}) copy-start(s32[8,15,10]{1,0,2:T(8,128)} %param.18) | copy-start | bytes 14404
  4.7 31.3 %all-to-all-start = ((bf16[128,4,384]{2,1,0:T(4,128)(2,1)}), bf16[128,4,384]{2,1,0:T(4,128)(2,1)}, u32[]{:S(2)}, u32[]{:S(2)}) async-start(bf16[128,4,384]{2,1,0:T(4,128)(2,1)} %shard_map.138), calls=%async_computation | async-start | bytes 786432 | tf_op jit(solution)/shard_map/all_to_all | solution.py:428
  39.3 2.2 %collective-permute-start = (f32[128,1024]{1,0:T(8,128)}, f32[128,1024]{1,0:T(8,128)S(1)}, u32[]{:S(2)}, u32[]{:S(2)}) collective-permute-start(f32[128,1024]{1,0:T(8,128)} %get-tuple-element.36.refs_1_), channel_id=1, source_target_pairs={{0,1},{1,0},{2,3},{3,2},{4,5},{5,4},{6,7},{7,6},{8,9},{9,8},{10,11... | collective-permute-start | bytes 1572872 | tf_op jit(solution)/shard_map/ppermute | solution.py:379
  39.4 11.8 %collective-permute-start.2 = (bf16[384,384]{1,0:T(8,128)(2,1)}, bf16[384,384]{1,0:T(8,128)(2,1)}, u32[]{:S(2)}, u32[]{:S(2)}) collective-permute-start(bf16[384,384]{1,0:T(8,128)(2,1)} %get-tuple-element.49.refs_9_.refs_1_), channel_id=1, source_target_pairs={{0,128},{64,192},{128,0},{192,64},{1,129},{65,193},{129,1},{193,65... | collective-permute-start | bytes 884744 | tf_op jit(solution)/shard_map/ppermute | solution.py:379
  41.5 0.8 copy-start.10
  42.3 20.7 %copy-start.3 = (bf16[384,384]{1,0:T(8,128)(2,1)S(1)}, bf16[384,384]{1,0:T(8,128)(2,1)}, u32[]{:S(2)}) copy-start(bf16[384,384]{1,0:T(8,128)(2,1)} %get-tuple-element.49.refs_9_.refs_1_) | copy-start | bytes 884740
  47.8 15.1 %collective-permute-start.3 = (bf16[1568,128]{1,0:T(8,128)(2,1)}, bf16[1568,128]{1,0:T(8,128)(2,1)S(1)}, u32[]{:S(2)}, u32[]{:S(2)}) collective-permute-start(bf16[1568,128]{1,0:T(8,128)(2,1)} %get-tuple-element.52), channel_id=1, source_target_pairs={{0,64},{64,128},{128,192},{192,0},{1,65},{65,129},{129,193},{193,1... | collective-permute-start | bytes 1204232 | tf_op jit(solution)/shard_map/ppermute | solution.py:379
  48.7 14.3 %collective-permute-start.5 = (bf16[1568,128]{1,0:T(8,128)(2,1)}, bf16[1568,128]{1,0:T(8,128)(2,1)S(1)}, u32[]{:S(2)}, u32[]{:S(2)}) collective-permute-start(bf16[1568,128]{1,0:T(8,128)(2,1)} %get-tuple-element.54), channel_id=1, source_target_pairs={{0,192},{64,0},{128,64},{192,128},{1,193},{65,1},{129,65},{193,129... | collective-permute-start | bytes 1204232 | tf_op jit(solution)/shard_map/ppermute | solution.py:379
  51.1 11.6 %collective-permute-start.4 = (bf16[208,256]{1,0:T(8,128)(2,1)}, bf16[208,256]{1,0:T(8,128)(2,1)S(1)}, u32[]{:S(2)}, u32[]{:S(2)}) collective-permute-start(bf16[208,256]{1,0:T(8,128)(2,1)} %get-tuple-element.53), channel_id=1, source_target_pairs={{0,128},{64,192},{128,0},{192,64},{1,129},{65,193},{129,1},{193,65... | collective-permute-start | bytes 319496 | tf_op jit(solution)/shard_map/ppermute | solution.py:379
  52.2 32.2 %all-to-all-start.1 = ((bf16[128,4,384]{2,1,0:T(4,128)(2,1)}), bf16[128,4,384]{2,1,0:T(4,128)(2,1)}, u32[]{:S(2)}, u32[]{:S(2)}) async-start(bf16[128,4,384]{2,1,0:T(4,128)(2,1)} %get-tuple-element.42), calls=%async_computation.1 | async-start | bytes 786432 | tf_op jit(solution)/shard_map/all_to_all | solution.py:502
  63.0 0.9 copy-start.4
  65.7 22.8 %copy-start.2 = (s32[1,512]{1,0:T(1,128)S(1)}, s32[1,512]{1,0:T(1,128)}, u32[]{:S(2)}) copy-start(s32[1,512]{1,0:T(1,128)} %refs_0_.4) | copy-start | bytes 6148
  65.8 25.9 %copy-start = (f32[1024,384]{1,0:T(8,128)S(1)}, f32[1024,384]{1,0:T(8,128)}, u32[]{:S(2)}) copy-start(f32[1024,384]{1,0:T(8,128)} %refs_0_.5) | copy-start | bytes 4718596
  65.8 25.9 %copy-start.1 = (f32[1024]{0:T(1024)S(1)}, f32[1024]{0:T(1024)}, u32[]{:S(2)}) copy-start(f32[1024]{0:T(1024)} %param.12) | copy-start | bytes 12292
  65.8 12.4 %collective-permute-start.6 = (bf16[336,384]{1,0:T(8,128)(2,1)S(1)}, bf16[336,384]{1,0:T(8,128)(2,1)S(1)}, u32[]{:S(2)}, u32[]{:S(2)}) collective-permute-start(bf16[336,384]{1,0:T(8,128)(2,1)S(1)} %get-tuple-element.57), channel_id=1, source_target_pairs={{0,16},{16,32},{32,48},{48,0},{1,17},{17,33},{33,49},{49,1},{2,18}... | collective-permute-start | bytes 774152 | tf_op jit(solution)/shard_map/ppermute | solution.py:379
  67.1 13.1 %collective-permute-start.7 = (bf16[336,384]{1,0:T(8,128)(2,1)S(1)}, bf16[336,384]{1,0:T(8,128)(2,1)S(1)}, u32[]{:S(2)}, u32[]{:S(2)}) collective-permute-start(bf16[336,384]{1,0:T(8,128)(2,1)S(1)} %get-tuple-element.58), channel_id=1, source_target_pairs={{0,32},{16,48},{32,0},{48,16},{1,33},{17,49},{33,1},{49,17},{2,34}... | collective-permute-start | bytes 774152 | tf_op jit(solution)/shard_map/ppermute | solution.py:379
  72.8 10.5 %collective-permute-start.8 = (bf16[336,384]{1,0:T(8,128)(2,1)S(1)}, bf16[336,384]{1,0:T(8,128)(2,1)S(1)}, u32[]{:S(2)}, u32[]{:S(2)}) collective-permute-start(bf16[336,384]{1,0:T(8,128)(2,1)S(1)} %get-tuple-element.59), channel_id=1, source_target_pairs={{0,48},{16,0},{32,16},{48,32},{1,49},{17,1},{33,17},{49,33},{2,50}... | collective-permute-start | bytes 774152 | tf_op jit(solution)/shard_map/ppermute | solution.py:379
  84.4 17.6 %all-to-all-start.2 = ((bf16[8,8,2688]{2,1,0:T(8,128)(2,1)}), bf16[8,8,2688]{2,1,0:T(8,128)(2,1)S(1)}, u32[]{:S(2)}, u32[]{:S(2)}) async-start(bf16[8,8,2688]{2,1,0:T(8,128)(2,1)} %bitcast.6), calls=%async_computation.2 | async-start | bytes 688128 | tf_op jit(solution)/shard_map/all_to_all | solution.py:522
  90.4 1.2 %collective-permute-start.1 = (f32[8,128]{1,0:T(8,128)S(1)}, f32[8,128]{1,0:T(8,128)S(1)}, u32[]{:S(2)}, u32[]{:S(2)}) collective-permute-start(f32[8,128]{1,0:T(8,128)S(1)} %get-tuple-element.44.refs_3_), channel_id=1, source_target_pairs={{0,1},{1,0},{2,3},{3,2},{4,5},{5,4},{6,7},{7,6},{8,9},{9,8},{10,11... | collective-permute-start | bytes 12296 | tf_op jit(solution)/shard_map/ppermute | solution.py:379

commit v9 on v8

--- a/solution.py
+++ b/solution.py
@@ -105,11 +105,9 @@
     return jax.ShapeDtypeStruct(shape, dtype)
 
 
-def serve_kernel(serve_ref, table_ref, out_ref, onehot, rows, picked, sems):
-    chunks = range(table_ref.shape[1] // LANES)
-    loads = [
-        pltpu.make_async_copy(table_ref.at[:, i * LANES : (i + 1) * LANES], rows.at[i], sems.at[i]) for i in chunks
-    ]
+def serve_kernel(serve_ref, table_ref, out_ref, onehot, rows, whole, sems):
+    parts = rows.shape[0]
+    loads = [pltpu.make_async_copy(table_ref.at[i], rows.at[i], sems.at[i]) for i in range(parts)]
     for load in loads:
         load.start()
     serve = serve_ref.get()[...]
@@ -117,16 +115,10 @@
     for block in range(serve.shape[1] // LANES):
         span = slice(block * LANES, (block + 1) * LANES)
         onehot[span, :] = jnp.where(row_to_column(serve[:, span]) == lanes, 1.0, 0.0).astype(BF16)
-    stores = []
-    for i in chunks:
-        loads[i].wait()
-        found = matmul(onehot[...], rows[i].astype(BF16)).astype(BF16)
-        picked[i] = found.reshape(picked.shape[1:])
-        target = out_ref.at[:, :, i * LANES : (i + 1) * LANES]
-        stores.append(pltpu.make_async_copy(picked.at[i], target, sems.at[len(chunks) + i]))
-        stores[i].start()
-    for store in stores:
-        store.wait()
+    for i, load in enumerate(loads):
+        load.wait()
+        whole[i * rows.shape[1] : (i + 1) * rows.shape[1], :] = rows[i].astype(BF16)
+    out_ref[...] = matmul(onehot[...], whole[...]).astype(BF16).reshape(out_ref.shape)
 
 
 def index_kernel(idx_ref, cot_ref, w2_ref, *refs):
@@ -410,20 +402,19 @@
     width = hidden_units // n_x
 
     blocks_shape = (owners, slots // owners, columns)
-    chunks = columns // LANES
+    parts = 4
     outgoing = call(
         serve_kernel,
         [shaped(blocks_shape, BF16)],
-        (serve_rows, table),
+        (serve_rows, table.reshape(parts, table_rows // parts, columns)),
         scratch=[
             pltpu.VMEM((slots, table_rows), BF16),
-            pltpu.VMEM((chunks, table_rows, LANES), F32),
-            pltpu.VMEM((chunks, *blocks_shape[:2], LANES), BF16),
-            pltpu.SemaphoreType.DMA((2 * chunks,)),
+            pltpu.VMEM((parts, table_rows // parts, columns), F32),
+            pltpu.VMEM((table_rows, columns), BF16),
+            pltpu.SemaphoreType.DMA((parts,)),
         ],
         hbm_in=(0,),
         raw_in=(1,),
-        hbm_raw=(0,),
     )[0]
     fetched = lax.all_to_all(outgoing, everyone, split_axis=0, concat_axis=0, tiled=True)
 

time: 103 us -> 103 us (level); the launches traced: 103 us -> 102 us
  transfers between devices with their start and end apart: 12 -> 12, of which waited for: 9 -> 10; matrix products, arithmetic and copies ran while one was open for 2% -> 2% of each run, Pallas kernels for 18% -> 18%
where the time goes in v9:
time: 103 us; the launch traced here: 102 us
  starting transfers between devices  42.4 us (41%)
  waiting for transfers between devices  29.5 us (29%)
  Pallas kernels  25.1 us (24%)
  local copies, waits for them, and re-layouts  2.91 us (3%)
    pallas_call x9, Pallas kernels, call(): pl.pallas_call(wrapped, out_shape=tuple(outs), in_specs=specs, out_specs=...  25.1 us
    all_to_all x1, starting transfers between devices, body(): lax.all_to_all(outgoing, everyone, split_axis=0, concat_axis=0, tiled=True)  15.8 us
    ppermute x9, waiting for transfers between devices, shift(): lax.ppermute(array, axis, [(i, (i + by) % size) for i in range(size)])  13.5 us
    ppermute x9, starting transfers between devices, shift(): lax.ppermute(array, axis, [(i, (i + by) % size) for i in range(size)])  13.2 us
    all_to_all x1, starting transfers between devices, body(): lax.all_to_all(slot_grad, everyone, split_axis=0, concat_axis=0, tiled=True)  9.29 us
    all_to_all x1, waiting for transfers between devices, body(): grads = lax.all_to_all(grads, 'z', split_axis=0, concat_axis=0, tiled=True)  8.78 us
    all_to_all x1, waiting for transfers between devices, body(): lax.all_to_all(outgoing, everyone, split_axis=0, concat_axis=0, tiled=True)  7.27 us
    all_to_all x1, starting transfers between devices, body(): grads = lax.all_to_all(grads, 'z', split_axis=0, concat_axis=0, tiled=True)  4.08 us
  transfers between devices with their start and end apart: 12, of which 10 were waited for; matrix products, arithmetic and copies ran while one was open for 2% of the time, Pallas kernels for 18%

profile of v9, /device:TPU:8, one launch (start us, length us, event | category | flops | bytes accessed | tf_op | source)
XLA Modules:
  0.0 101.5 jit_solution(10826064499124920143)
XLA Ops:
  0.7 3.1 %shard_map.138 = bf16[128,4,384]{2,1,0:T(4,128)(2,1)} custom-call(s32[1,512]{1,0:T(1,128)} %refs_0_.4, f32[4,256,384]{2,1,0:T(8,128)} %bitcast.12), custom_call_target="tpu_custom_call" | custom-call | flops 999999995904 | bytes 1968128 | tf_op jit(solution)/shard_map/pallas_call | solution.py:89
  3.7 15.8 %all-to-all-start = ((bf16[128,4,384]{2,1,0:T(4,128)(2,1)}), bf16[128,4,384]{2,1,0:T(4,128)(2,1)}, u32[]{:S(2)}, u32[]{:S(2)}) async-start(bf16[128,4,384]{2,1,0:T(4,128)(2,1)} %shard_map.138), calls=%async_computation | async-start | bytes 786432 | tf_op jit(solution)/shard_map/all_to_all | solution.py:419
  19.5 0.1 reshape.32
  19.6 0.1 copy.32
  19.7 0.1 pad_add_fusion
  19.8 0.1 copy.33
  19.9 0.1 reshape.34
  20.0 0.1 reshape.33
  20.1 0.6 pad_add_fusion.1.refs_0_
  20.7 0.1 add_add_fusion
  20.7 0.8 copy.34.refs_0_
  21.5 6.3 %shard_map.139 = (bf16[384,512]{1,0:T(8,128)(2,1)}, bf16[512,384]{1,0:T(8,128)(2,1)}, f32[384,128]{1,0:T(8,128)}, bf16[32,128]{1,0:T(8,128)(2,1)}, f32[128,1024]{1,0:T(8,128)}) custom-call(s32[128,17]{1,0:T(8,128)} %copy.34.refs_0_, bf16[8,1024]{1,0:T(8,128)(2,1)} %refs_6_.1, bf16[3,1024,1024]{2,1,0:T(8,128)(2,1)} %refs_2_.2), custom_call_target="tpu_custom_call" | custom-call | flops 999999995904 | bytes 7832064 | tf_op jit(solution)/shard_map/pallas_call | solution.py:89
  27.8 7.3 %all-to-all-done.refs_0_ = bf16[128,4,384]{2,1,0:T(4,128)(2,1)} async-done(((bf16[128,4,384]{2,1,0:T(4,128)(2,1)}), bf16[128,4,384]{2,1,0:T(4,128)(2,1)}, u32[]{:S(2)}, u32[]{:S(2)}) %all-to-all-start) | async-done | bytes 393248 | tf_op jit(solution)/shard_map/all_to_all | solution.py:419
  35.1 3.2 %shard_map.140 = (bf16[384,384]{1,0:T(8,128)(2,1)}, f32[128,1024]{1,0:T(8,128)}) custom-call(bf16[128,4,384]{2,1,0:T(4,128)(2,1)} %all-to-all-done.refs_0_, bf16[384,512]{1,0:T(8,128)(2,1)} %get-tuple-element.35.refs_1_, bf16[3,384,1024]{2,1,0:T(8,128)(2,1)} %refs_8_.1), custom_call_target="tpu_custom_call" | custom-call | flops 999999995904 | bytes 3964928 | tf_op jit(solution)/shard_map/pallas_call | solution.py:89
  38.3 0.1 collective-permute-start
  38.4 1.6 %collective-permute-start.2 = (bf16[384,384]{1,0:T(8,128)(2,1)}, bf16[384,384]{1,0:T(8,128)(2,1)}, u32[]{:S(2)}, u32[]{:S(2)}) collective-permute-start(bf16[384,384]{1,0:T(8,128)(2,1)} %get-tuple-element.49.refs_9_.refs_1_), channel_id=1, source_target_pairs={{0,128},{64,192},{128,0},{192,64},{1,129},{65,193},{129,1},{193,65... | collective-permute-start | bytes 884744 | tf_op jit(solution)/shard_map/ppermute | solution.py:371
  40.0 0.5 collective-permute-done.refs_2_
  40.5 0.8 copy-done.10
  41.3 5.5 %shard_map.141 = (bf16[128,4,384]{2,1,0:T(4,128)(2,1)}, bf16[208,256]{1,0:T(8,128)(2,1)}, bf16[1568,128]{1,0:T(8,128)(2,1)}, bf16[208,256]{1,0:T(8,128)(2,1)}, bf16[1568,128]{1,0:T(8,128)(2,1)}) custom-call(s32[2]{0:T(128)} %pad_add_fusion.1.refs_0_, f32[128,1024]{1,0:T(8,128)} %get-tuple-element.36.refs_1_, f32[128,1024]{1,0:T(8,128)} %copy-done.10, ...), custom_call_target="tpu_custom_call" | custom-call | flops 999999995904 | bytes 6250504 | tf_op jit(solution)/shard_map/pallas_call | solution.py:89
  46.9 0.9 collective-permute-start.3
  47.7 2.5 %collective-permute-start.5 = (bf16[1568,128]{1,0:T(8,128)(2,1)}, bf16[1568,128]{1,0:T(8,128)(2,1)S(1)}, u32[]{:S(2)}, u32[]{:S(2)}) collective-permute-start(bf16[1568,128]{1,0:T(8,128)(2,1)} %get-tuple-element.54), channel_id=1, source_target_pairs={{0,192},{64,0},{128,64},{192,128},{1,193},{65,1},{129,65},{193,129... | collective-permute-start | bytes 1204232 | tf_op jit(solution)/shard_map/ppermute | solution.py:371
  50.2 0.0 collective-permute-done.2.refs_2_
  50.2 1.0 %collective-permute-start.4 = (bf16[208,256]{1,0:T(8,128)(2,1)}, bf16[208,256]{1,0:T(8,128)(2,1)S(1)}, u32[]{:S(2)}, u32[]{:S(2)}) collective-permute-start(bf16[208,256]{1,0:T(8,128)(2,1)} %get-tuple-element.53), channel_id=1, source_target_pairs={{0,128},{64,192},{128,0},{192,64},{1,129},{65,193},{129,1},{193,65... | collective-permute-start | bytes 319496 | tf_op jit(solution)/shard_map/ppermute | solution.py:371
  51.2 9.3 %all-to-all-start.1 = ((bf16[128,4,384]{2,1,0:T(4,128)(2,1)}), bf16[128,4,384]{2,1,0:T(4,128)(2,1)}, u32[]{:S(2)}, u32[]{:S(2)}) async-start(bf16[128,4,384]{2,1,0:T(4,128)(2,1)} %get-tuple-element.42), calls=%async_computation.1 | async-start | bytes 786432 | tf_op jit(solution)/shard_map/all_to_all | solution.py:493
  60.5 1.2 %collective-permute-done.4.refs_5_ = bf16[208,256]{1,0:T(8,128)(2,1)S(1)} collective-permute-done((bf16[208,256]{1,0:T(8,128)(2,1)}, bf16[208,256]{1,0:T(8,128)(2,1)S(1)}, u32[]{:S(2)}, u32[]{:S(2)}) %collective-permute-start.4) | collective-permute-done | bytes 106528 | tf_op jit(solution)/shard_map/ppermute | solution.py:371
  61.7 0.2 collective-permute-done.3.refs_4_
  62.0 0.1 collective-permute-done.5.refs_6_
  62.0 0.9 copy-done.4
  62.9 1.9 %shard_map.144 = (f32[64,1152]{1,0:T(8,128)S(1)}, bf16[336,384]{1,0:T(8,128)(2,1)S(1)}, bf16[336,384]{1,0:T(8,128)(2,1)S(1)}, bf16[336,384]{1,0:T(8,128)(2,1)S(1)}, bf16[336,384]{1,0:T(8,128)(2,1)S(1)}) custom-call(s32[1]{0:T(128)} %bitcast.6.refs_0_, bf16[384,384]{1,0:T(8,128)(2,1)S(1)} %copy-done.3, bf16[384,384]{1,0:T(8,128)(2,1)} %collective-permute-done.2.refs_2_, ...), custom_call_target="tpu_custom_call" | custom-call | flops 999999995904 | bytes 2932740 | tf_op jit(solution)/shard_map/pallas_call | solution.py:89
  64.8 0.0 copy-start.2
  64.8 0.0 copy-start
  64.8 0.0 copy-start.1
  64.9 1.2 %collective-permute-start.6 = (bf16[336,384]{1,0:T(8,128)(2,1)S(1)}, bf16[336,384]{1,0:T(8,128)(2,1)S(1)}, u32[]{:S(2)}, u32[]{:S(2)}) collective-permute-start(bf16[336,384]{1,0:T(8,128)(2,1)S(1)} %get-tuple-element.57), channel_id=1, source_target_pairs={{0,16},{16,32},{32,48},{48,0},{1,17},{17,33},{33,49},{49,1},{2,18}... | collective-permute-start | bytes 774152 | tf_op jit(solution)/shard_map/ppermute | solution.py:371
  66.1 5.9 %collective-permute-start.7 = (bf16[336,384]{1,0:T(8,128)(2,1)S(1)}, bf16[336,384]{1,0:T(8,128)(2,1)S(1)}, u32[]{:S(2)}, u32[]{:S(2)}) collective-permute-start(bf16[336,384]{1,0:T(8,128)(2,1)S(1)} %get-tuple-element.58), channel_id=1, source_target_pairs={{0,32},{16,48},{32,0},{48,16},{1,33},{17,49},{33,1},{49,17},{2,34}... | collective-permute-start | bytes 774152 | tf_op jit(solution)/shard_map/ppermute | solution.py:371
  71.9 0.0 collective-permute-start.8
  71.9 5.3 %collective-permute-done.6.refs_2_ = bf16[336,384]{1,0:T(8,128)(2,1)S(1)} collective-permute-done((bf16[336,384]{1,0:T(8,128)(2,1)S(1)}, bf16[336,384]{1,0:T(8,128)(2,1)S(1)}, u32[]{:S(2)}, u32[]{:S(2)}) %collective-permute-start.6) | collective-permute-done | bytes 258080 | tf_op jit(solution)/shard_map/ppermute | solution.py:371
  77.2 2.0 %collective-permute-done.7.refs_3_ = bf16[336,384]{1,0:T(8,128)(2,1)S(1)} collective-permute-done((bf16[336,384]{1,0:T(8,128)(2,1)S(1)}, bf16[336,384]{1,0:T(8,128)(2,1)S(1)}, u32[]{:S(2)}, u32[]{:S(2)}) %collective-permute-start.7) | collective-permute-done | bytes 258080 | tf_op jit(solution)/shard_map/ppermute | solution.py:371
  79.2 3.0 %collective-permute-done.8.refs_4_ = bf16[336,384]{1,0:T(8,128)(2,1)S(1)} collective-permute-done((bf16[336,384]{1,0:T(8,128)(2,1)S(1)}, bf16[336,384]{1,0:T(8,128)(2,1)S(1)}, u32[]{:S(2)}, u32[]{:S(2)}) %collective-permute-start.8) | collective-permute-done | bytes 258080 | tf_op jit(solution)/shard_map/ppermute | solution.py:371
  82.3 1.1 %shard_map.145 = bf16[64,2688]{1,0:T(8,128)(2,1)} custom-call(f32[64,1152]{1,0:T(8,128)S(1)} %get-tuple-element.55.refs_0_, bf16[336,384]{1,0:T(8,128)(2,1)S(1)} %get-tuple-element.56.refs_1_, bf16[336,384]{1,0:T(8,128)(2,1)S(1)} %collective-permute-done.6.refs_2_, bf16[336,384]{1,0:T(8,128)(2,1)S(1)} %collective-permute-done.7.refs_3_, ...), custom_call_target="tpu_custom_call" | custom-call | bytes 1671168 | tf_op jit(solution)/shard_map/pallas_call | solution.py:89
  83.3 0.0 all-to-all-done.1.refs_1_
  83.3 4.1 %all-to-all-start.2 = ((bf16[8,8,2688]{2,1,0:T(8,128)(2,1)}), bf16[8,8,2688]{2,1,0:T(8,128)(2,1)S(1)}, u32[]{:S(2)}, u32[]{:S(2)}) async-start(bf16[8,8,2688]{2,1,0:T(8,128)(2,1)} %bitcast.7), calls=%async_computation.2 | async-start | bytes 688128 | tf_op jit(solution)/shard_map/all_to_all | solution.py:513
  87.4 0.0 copy-done.2
  87.4 1.9 %shard_map.142 = (f32[1024,384]{1,0:T(8,128)S(1)}, f32[8,128]{1,0:T(8,128)S(1)}) custom-call(s32[1,512]{1,0:T(1,128)S(1)} %copy-done.2, bf16[128,4,384]{2,1,0:T(4,128)(2,1)} %all-to-all-done.1.refs_1_), custom_call_target="tpu_custom_call" | custom-call | bytes 1972224 | tf_op jit(solution)/shard_map/pallas_call | solution.py:89
  89.3 0.1 collective-permute-start.1
  89.3 1.2 %collective-permute-done.1.refs_4_ = f32[8,128]{1,0:T(8,128)S(1)} collective-permute-done((f32[8,128]{1,0:T(8,128)S(1)}, f32[8,128]{1,0:T(8,128)S(1)}, u32[]{:S(2)}, u32[]{:S(2)}) %collective-permute-start.1) | collective-permute-done | bytes 4128 | tf_op jit(solution)/shard_map/ppermute | solution.py:371
  90.5 1.6 %shard_map.143 = (f32[1024,384]{1,0:T(8,128)}, f32[8,128]{1,0:T(8,128)}) custom-call(f32[1024,384]{1,0:T(8,128)S(1)} %copy-done, f32[1024,384]{1,0:T(8,128)S(1)} %get-tuple-element.43.refs_1_, f32[8,128]{1,0:T(8,128)S(1)} %bitcast.13, f32[8,128]{1,0:T(8,128)S(1)} %get-tuple-element.44.refs_3_, f32[8,128]{1,0:T(8,128)S(1)} %collective-permute-done.1.refs_4_), custom_call_target="tpu_custom_call" | custom-call | bytes 4734976 | tf_op jit(solution)/shard_map/pallas_call | solution.py:89
  92.1 8.8 %all-to-all-done.2.refs_0_ = bf16[8,8,2688]{2,1,0:T(8,128)(2,1)S(1)} async-done(((bf16[8,8,2688]{2,1,0:T(8,128)(2,1)}), bf16[8,8,2688]{2,1,0:T(8,128)(2,1)S(1)}, u32[]{:S(2)}, u32[]{:S(2)}) %all-to-all-start.2) | async-done | bytes 344096 | tf_op jit(solution)/shard_map/all_to_all | solution.py:513
  100.8 0.7 shard_map.146
  (20 shorter events, 0.1 us)
Async XLA Ops:
  0.6 18.9 %copy-start.7 = (s32[8,15]{1,0:T(8,128)S(1)}, s32[8,15]{1,0:T(8,128)}, u32[]{:S(2)}) copy-start(s32[8,15]{1,0:T(8,128)} %param.15) | copy-start | bytes 1444
  0.6 19.0 %copy-start.8 = (s32[8,15]{1,0:T(8,128)S(1)}, s32[8,15]{1,0:T(8,128)}, u32[]{:S(2)}) copy-start(s32[8,15]{1,0:T(8,128)} %param.17) | copy-start | bytes 1444
  0.7 19.0 %copy-start.9 = (s32[8]{0:T(128)S(1)}, s32[8]{0:T(128)}, u32[]{:S(2)}) copy-start(s32[8]{0:T(128)} %param.14) | copy-start | bytes 100
  0.7 19.3 %copy-start.5 = (s32[8,15,10]{1,0,2:T(8,128)S(1)}, s32[8,15,10]{1,0,2:T(8,128)}, u32[]{:S(2)}) copy-start(s32[8,15,10]{1,0,2:T(8,128)} %param.16) | copy-start | bytes 14404
  0.7 19.3 %copy-start.6 = (s32[8,15,10]{1,0,2:T(8,128)S(1)}, s32[8,15,10]{1,0,2:T(8,128)}, u32[]{:S(2)}) copy-start(s32[8,15,10]{1,0,2:T(8,128)} %param.18) | copy-start | bytes 14404
  3.7 31.3 %all-to-all-start = ((bf16[128,4,384]{2,1,0:T(4,128)(2,1)}), bf16[128,4,384]{2,1,0:T(4,128)(2,1)}, u32[]{:S(2)}, u32[]{:S(2)}) async-start(bf16[128,4,384]{2,1,0:T(4,128)(2,1)} %shard_map.138), calls=%async_computation | async-start | bytes 786432 | tf_op jit(solution)/shard_map/all_to_all | solution.py:419
  38.3 2.2 %collective-permute-start = (f32[128,1024]{1,0:T(8,128)}, f32[128,1024]{1,0:T(8,128)S(1)}, u32[]{:S(2)}, u32[]{:S(2)}) collective-permute-start(f32[128,1024]{1,0:T(8,128)} %get-tuple-element.36.refs_1_), channel_id=1, source_target_pairs={{0,1},{1,0},{2,3},{3,2},{4,5},{5,4},{6,7},{7,6},{8,9},{9,8},{10,11... | collective-permute-start | bytes 1572872 | tf_op jit(solution)/shard_map/ppermute | solution.py:371
  38.4 11.8 %collective-permute-start.2 = (bf16[384,384]{1,0:T(8,128)(2,1)}, bf16[384,384]{1,0:T(8,128)(2,1)}, u32[]{:S(2)}, u32[]{:S(2)}) collective-permute-start(bf16[384,384]{1,0:T(8,128)(2,1)} %get-tuple-element.49.refs_9_.refs_1_), channel_id=1, source_target_pairs={{0,128},{64,192},{128,0},{192,64},{1,129},{65,193},{129,1},{193,65... | collective-permute-start | bytes 884744 | tf_op jit(solution)/shard_map/ppermute | solution.py:371
  40.5 0.8 copy-start.10
  41.3 20.7 %copy-start.3 = (bf16[384,384]{1,0:T(8,128)(2,1)S(1)}, bf16[384,384]{1,0:T(8,128)(2,1)}, u32[]{:S(2)}) copy-start(bf16[384,384]{1,0:T(8,128)(2,1)} %get-tuple-element.49.refs_9_.refs_1_) | copy-start | bytes 884740
  46.9 15.1 %collective-permute-start.3 = (bf16[1568,128]{1,0:T(8,128)(2,1)}, bf16[1568,128]{1,0:T(8,128)(2,1)S(1)}, u32[]{:S(2)}, u32[]{:S(2)}) collective-permute-start(bf16[1568,128]{1,0:T(8,128)(2,1)} %get-tuple-element.52), channel_id=1, source_target_pairs={{0,64},{64,128},{128,192},{192,0},{1,65},{65,129},{129,193},{193,1... | collective-permute-start | bytes 1204232 | tf_op jit(solution)/shard_map/ppermute | solution.py:371
  47.7 14.3 %collective-permute-start.5 = (bf16[1568,128]{1,0:T(8,128)(2,1)}, bf16[1568,128]{1,0:T(8,128)(2,1)S(1)}, u32[]{:S(2)}, u32[]{:S(2)}) collective-permute-start(bf16[1568,128]{1,0:T(8,128)(2,1)} %get-tuple-element.54), channel_id=1, source_target_pairs={{0,192},{64,0},{128,64},{192,128},{1,193},{65,1},{129,65},{193,129... | collective-permute-start | bytes 1204232 | tf_op jit(solution)/shard_map/ppermute | solution.py:371
  50.2 11.6 %collective-permute-start.4 = (bf16[208,256]{1,0:T(8,128)(2,1)}, bf16[208,256]{1,0:T(8,128)(2,1)S(1)}, u32[]{:S(2)}, u32[]{:S(2)}) collective-permute-start(bf16[208,256]{1,0:T(8,128)(2,1)} %get-tuple-element.53), channel_id=1, source_target_pairs={{0,128},{64,192},{128,0},{192,64},{1,129},{65,193},{129,1},{193,65... | collective-permute-start | bytes 319496 | tf_op jit(solution)/shard_map/ppermute | solution.py:371
  51.2 32.1 %all-to-all-start.1 = ((bf16[128,4,384]{2,1,0:T(4,128)(2,1)}), bf16[128,4,384]{2,1,0:T(4,128)(2,1)}, u32[]{:S(2)}, u32[]{:S(2)}) async-start(bf16[128,4,384]{2,1,0:T(4,128)(2,1)} %get-tuple-element.42), calls=%async_computation.1 | async-start | bytes 786432 | tf_op jit(solution)/shard_map/all_to_all | solution.py:493
  62.0 0.9 copy-start.4
  64.8 22.6 %copy-start.2 = (s32[1,512]{1,0:T(1,128)S(1)}, s32[1,512]{1,0:T(1,128)}, u32[]{:S(2)}) copy-start(s32[1,512]{1,0:T(1,128)} %refs_0_.4) | copy-start | bytes 6148
  64.8 25.7 %copy-start = (f32[1024,384]{1,0:T(8,128)S(1)}, f32[1024,384]{1,0:T(8,128)}, u32[]{:S(2)}) copy-start(f32[1024,384]{1,0:T(8,128)} %refs_0_.5) | copy-start | bytes 4718596
  64.8 25.6 %copy-start.1 = (f32[1024]{0:T(1024)S(1)}, f32[1024]{0:T(1024)}, u32[]{:S(2)}) copy-start(f32[1024]{0:T(1024)} %param.12) | copy-start | bytes 12292
  64.9 12.4 %collective-permute-start.6 = (bf16[336,384]{1,0:T(8,128)(2,1)S(1)}, bf16[336,384]{1,0:T(8,128)(2,1)S(1)}, u32[]{:S(2)}, u32[]{:S(2)}) collective-permute-start(bf16[336,384]{1,0:T(8,128)(2,1)S(1)} %get-tuple-element.57), channel_id=1, source_target_pairs={{0,16},{16,32},{32,48},{48,0},{1,17},{17,33},{33,49},{49,1},{2,18}... | collective-permute-start | bytes 774152 | tf_op jit(solution)/shard_map/ppermute | solution.py:371
  66.1 13.2 %collective-permute-start.7 = (bf16[336,384]{1,0:T(8,128)(2,1)S(1)}, bf16[336,384]{1,0:T(8,128)(2,1)S(1)}, u32[]{:S(2)}, u32[]{:S(2)}) collective-permute-start(bf16[336,384]{1,0:T(8,128)(2,1)S(1)} %get-tuple-element.58), channel_id=1, source_target_pairs={{0,32},{16,48},{32,0},{48,16},{1,33},{17,49},{33,1},{49,17},{2,34}... | collective-permute-start | bytes 774152 | tf_op jit(solution)/shard_map/ppermute | solution.py:371
  71.9 10.3 %collective-permute-start.8 = (bf16[336,384]{1,0:T(8,128)(2,1)S(1)}, bf16[336,384]{1,0:T(8,128)(2,1)S(1)}, u32[]{:S(2)}, u32[]{:S(2)}) collective-permute-start(bf16[336,384]{1,0:T(8,128)(2,1)S(1)} %get-tuple-element.59), channel_id=1, source_target_pairs={{0,48},{16,0},{32,16},{48,32},{1,49},{17,1},{33,17},{49,33},{2,50}... | collective-permute-start | bytes 774152 | tf_op jit(solution)/shard_map/ppermute | solution.py:371
  83.3 17.5 %all-to-all-start.2 = ((bf16[8,8,2688]{2,1,0:T(8,128)(2,1)}), bf16[8,8,2688]{2,1,0:T(8,128)(2,1)S(1)}, u32[]{:S(2)}, u32[]{:S(2)}) async-start(bf16[8,8,2688]{2,1,0:T(8,128)(2,1)} %bitcast.7), calls=%async_computation.2 | async-start | bytes 688128 | tf_op jit(solution)/shard_map/all_to_all | solution.py:513
  89.3 1.2 %collective-permute-start.1 = (f32[8,128]{1,0:T(8,128)S(1)}, f32[8,128]{1,0:T(8,128)S(1)}, u32[]{:S(2)}, u32[]{:S(2)}) collective-permute-start(f32[8,128]{1,0:T(8,128)S(1)} %get-tuple-element.44.refs_3_), channel_id=1, source_target_pairs={{0,1},{1,0},{2,3},{3,2},{4,5},{5,4},{6,7},{7,6},{8,9},{9,8},{10,11... | collective-permute-start | bytes 12296 | tf_op jit(solution)/shard_map/ppermute | solution.py:371

commit v10 on v9

--- a/solution.py
+++ b/solution.py
@@ -95,10 +95,6 @@
         compiler_params=pltpu.CompilerParams(vmem_limit_bytes=limit * 1024 * 1024),
         cost_estimate=pl.CostEstimate(flops=flops, bytes_accessed=moved, transcendentals=0),
     )(*operands)
-
-
-def is_near(distance, count):
-    return distance not in (0, count // 2)
 
 
 def shaped(shape, dtype):
@@ -187,7 +183,7 @@
         copy.wait()
 
 
-def hidden_kernel(place_ref, mine_ref, other_ref, back_ref, e_ref, inv_ref, cot_ref, c_ref, w1_ref, layer_ref, slot_ref, *refs):
+def hidden_kernel(place_ref, mine_ref, other_ref, back_ref, e_ref, inv_ref, cot_ref, c_ref, w1_ref, slot_ref, *refs):
     packs, (stage, scaled, sems) = refs[:-3], refs[-3:]
     nodes = mine_ref.shape[0]
     width = stage.shape[2]
@@ -217,20 +213,10 @@
             stage[j, first : first + SEED_ROWS, :] = second[:, part * width : (part + 1) * width]
         first = nodes + half // width * SEED_ROWS
         stage[j, first : first + COT_ROWS, :] = cot[:, span]
-    moves = []
-    for d, pack in enumerate(packs):
-        chosen = stage.at[lax.rem(place_ref[1] + d, len(packs))]
-        if not is_near(d, len(packs)):
-            moves.append((chosen, pack))
-            continue
-        start = 0
-        for source in (chosen, layer_ref.get()):
-            rows, wide = source.shape
-            for lane in range(0, wide, LANES):
-                moves.append((source.at[:, lane : lane + LANES], pack.at[start : start + rows, :]))
-                start += rows
-    layer_ref.get()
-    copies = [pltpu.make_async_copy(source, target, sems.at[i]) for i, (source, target) in enumerate(moves)]
+    copies = [
+        pltpu.make_async_copy(stage.at[lax.rem(place_ref[1] + d, len(packs))], pack, sems.at[d])
+        for d, pack in enumerate(packs)
+    ]
     for copy in copies:
         copy.start()
     columns = w1_ref.shape[1]
@@ -244,21 +230,12 @@
 
 
 def weight_kernel(count, place_ref, *refs):
-    layer_refs, pack_refs = refs[:2], refs[2 : 2 + count]
-    own_ref, outs, total = refs[2 + count], refs[3 + count : -1], refs[-1]
+    layer_refs, pack_refs = refs[:count], refs[count : 2 * count]
+    own_ref, outs, total = refs[2 * count], refs[2 * count + 1 : -1], refs[-1]
     pack_rows, width = pack_refs[0].shape
     layer_rows, columns = layer_refs[0].shape
-    layer_parts, packs = [], []
-    for d, ref in enumerate(pack_refs):
-        if not is_near(d, count):
-            packs.append(ref.get()[...])
-            layer_parts.append(layer_refs[min(d, 1)].get()[...])
-            continue
-        near, start = ref.get()[...], 0
-        for rows, wide, made in ((pack_rows, width, packs), (layer_rows, columns, layer_parts)):
-            lanes = [near[start + i * rows : start + (i + 1) * rows] for i in range(wide // LANES)]
-            made.append(jnp.concatenate(lanes, 1))
-            start += rows * len(lanes)
+    layer_parts = [r.get()[...] for r in layer_refs]
+    packs = [r.get()[...] for r in pack_refs]
     nodes = LANES
     relations = layer_rows // nodes
     rows = own_ref.shape[0]
@@ -371,7 +348,7 @@
     return lax.ppermute(array, axis, [(i, (i + by) % size) for i in range(size)])
 
 
-LIMITS = {serve_kernel: 60, index_kernel: 60, first_kernel: 60, hidden_kernel: 60}
+LIMITS = {serve_kernel: 60, index_kernel: 60, first_kernel: 60, hidden_kernel: 50}
 COSTS = {update_kernel: 0, group_kernel: 0, row_kernel: 0}
 
 
@@ -459,14 +436,15 @@
         hbm_raw=(1,),
     )
     other_pre = shift(partial_pre, "col", 1)
-    layer_parts = [layer_in, shift(layer_in, "dp", n_x // 2)]
+    layer_parts = [layer_in, shift(layer_in, "dp", 1)]
+    if n_x > 2:
+        layer_parts.append(shift(layer_in, "dp", n_x - 1))
 
     pack_rows = nodes + half // width * SEED_ROWS + COT_ROWS
     pack_shape = (pack_rows, width)
-    near_shape = ((pack_rows * width + layers * nodes * columns) // LANES, LANES)
     slot_grad, *packs = call(
         hidden_kernel,
-        [shaped(blocks_shape, BF16)] + [shaped(near_shape if is_near(d, n_x) else pack_shape, BF16) for d in range(n_x)],
+        [shaped(blocks_shape, BF16)] + [shaped(pack_shape, BF16)] * n_x,
         (
             place,
             partial_pre,
@@ -477,18 +455,19 @@
             cotangent,
             c,
             w_first,
-            layer_in,
         ),
         smem=1,
         scratch=[
             pltpu.VMEM((n_x, *pack_shape), BF16),
             pltpu.VMEM((layers * nodes, columns), BF16),
-            pltpu.SemaphoreType.DMA((n_x * (width + columns) // LANES,)),
+            pltpu.SemaphoreType.DMA((n_x,)),
         ],
-        hbm_in=(1, 2, 3, 4, 5, 9, 8, 7),
+        hbm_in=(1, 2, 3, 4, 5, 8, 7),
         hbm_raw=range(1, 1 + n_x),
     )
     packs[n_x // 2], layer_parts = lax.optimization_barrier((packs[n_x // 2], layer_parts))
+    if n_x > 2:
+        layer_parts.insert(2, shift(layer_parts[2], "dp", n_x - 1))
     packs = [packs[0]] + [shift(packs[d], "dp", d) for d in range(1, n_x)]
     arrived = lax.all_to_all(slot_grad, everyone, split_axis=0, concat_axis=0, tiled=True)
 
@@ -499,7 +478,7 @@
         [shaped((block_rows, layers * columns), F32)] + [shaped((group_rows, columns), BF16)] * n_y,
         (y.reshape(1), *layer_parts, *packs),
         smem=1,
-        hbm_in=range(1, 3 + n_x),
+        hbm_in=range(1, 1 + 2 * n_x),
         scratch=[pltpu.VMEM((layers, width, columns), F32)],
     )
     blocks = [blocks[0]] + [shift(blocks[d], "y", d) for d in range(1, n_y)]

time: 103 us -> 105 us (1.019)
  starting transfers between devices: 42.4 us -> 46.2 us
    all_to_all x1, starting transfers between devices: 4.08 us -> 6.12 us  [body(): grads = lax.all_to_all(grads, 'z', split_axis=0, concat_axis=0, tiled=True)]
    ppermute x9 -> x11, starting transfers between devices: 13.2 us -> 15.1 us  [shift(): lax.ppermute(array, axis, [(i, (i + by) % size) for i in range(size)])]
    ppermute x9 -> x11, waiting for transfers between devices: 13.5 us -> 13.9 us  [shift(): lax.ppermute(array, axis, [(i, (i + by) % size) for i in range(size)])]
  transfers between devices with their start and end apart: 12 -> 14, of which waited for: 10 -> 7; matrix products, arithmetic and copies ran while one was open for 2% -> 1% of each run, Pallas kernels for 18% -> 17%
where the time goes in v10:
time: 105 us; the launch traced here: 104 us
  starting transfers between devices  46.2 us (44%)
  waiting for transfers between devices  29.7 us (28%)
  Pallas kernels  24.7 us (24%)
  local copies, waits for them, and re-layouts  2.25 us (2%)
    pallas_call x9, Pallas kernels, call(): pl.pallas_call(wrapped, out_shape=tuple(outs), in_specs=specs, out_specs=...  24.7 us
    all_to_all x1, starting transfers between devices, body(): lax.all_to_all(outgoing, everyone, split_axis=0, concat_axis=0, tiled=True)  15.8 us
    ppermute x11, starting transfers between devices, shift(): lax.ppermute(array, axis, [(i, (i + by) % size) for i in range(size)])  15.1 us
    ppermute x11, waiting for transfers between devices, shift(): lax.ppermute(array, axis, [(i, (i + by) % size) for i in range(size)])  13.9 us
    all_to_all x1, starting transfers between devices, body(): lax.all_to_all(slot_grad, everyone, split_axis=0, concat_axis=0, tiled=True)  9.12 us
    all_to_all x1, waiting for transfers between devices, body(): grads = lax.all_to_all(grads, 'z', split_axis=0, concat_axis=0, tiled=True)  7.96 us
    all_to_all x1, waiting for transfers between devices, body(): lax.all_to_all(outgoing, everyone, split_axis=0, concat_axis=0, tiled=True)  7.79 us
    all_to_all x1, starting transfers between devices, body(): grads = lax.all_to_all(grads, 'z', split_axis=0, concat_axis=0, tiled=True)  6.12 us
  transfers between devices with their start and end apart: 14, of which 7 were waited for; matrix products, arithmetic and copies ran while one was open for 1% of the time, Pallas kernels for 17%

profile of v10, /device:TPU:8, one launch (start us, length us, event | category | flops | bytes accessed | tf_op | source)
XLA Modules:
  0.0 103.9 jit_solution(1137222134390919737)
XLA Ops:
  0.7 3.1 %shard_map.138 = bf16[128,4,384]{2,1,0:T(4,128)(2,1)} custom-call(s32[1,512]{1,0:T(1,128)} %refs_0_.4, f32[4,256,384]{2,1,0:T(8,128)} %bitcast.12), custom_call_target="tpu_custom_call" | custom-call | flops 999999995904 | bytes 1968128 | tf_op jit(solution)/shard_map/pallas_call | solution.py:89
  3.8 15.8 %all-to-all-start = ((bf16[128,4,384]{2,1,0:T(4,128)(2,1)}), bf16[128,4,384]{2,1,0:T(4,128)(2,1)}, u32[]{:S(2)}, u32[]{:S(2)}) async-start(bf16[128,4,384]{2,1,0:T(4,128)(2,1)} %shard_map.138), calls=%async_computation | async-start | bytes 786432 | tf_op jit(solution)/shard_map/all_to_all | solution.py:396
  19.5 0.1 reshape.32
  19.6 0.1 copy.32
  19.7 0.1 pad_add_fusion
  19.8 0.1 copy.33
  19.9 0.1 reshape.34
  20.0 0.1 reshape.33
  20.1 0.1 pad_add_fusion.1.refs_0_
  20.2 0.1 add_add_fusion
  20.2 0.7 copy.34.refs_0_
  21.0 6.3 %shard_map.139 = (bf16[384,512]{1,0:T(8,128)(2,1)}, bf16[512,384]{1,0:T(8,128)(2,1)}, f32[384,128]{1,0:T(8,128)}, bf16[32,128]{1,0:T(8,128)(2,1)}, f32[128,1024]{1,0:T(8,128)}) custom-call(s32[128,17]{1,0:T(8,128)} %copy.34.refs_0_, bf16[8,1024]{1,0:T(8,128)(2,1)} %refs_6_.1, bf16[3,1024,1024]{2,1,0:T(8,128)(2,1)} %refs_2_.2), custom_call_target="tpu_custom_call" | custom-call | flops 999999995904 | bytes 7832064 | tf_op jit(solution)/shard_map/pallas_call | solution.py:89
  27.3 7.8 %all-to-all-done.refs_0_ = bf16[128,4,384]{2,1,0:T(4,128)(2,1)} async-done(((bf16[128,4,384]{2,1,0:T(4,128)(2,1)}), bf16[128,4,384]{2,1,0:T(4,128)(2,1)}, u32[]{:S(2)}, u32[]{:S(2)}) %all-to-all-start) | async-done | bytes 393248 | tf_op jit(solution)/shard_map/all_to_all | solution.py:396
  35.1 0.0 copy-start.9
  35.1 3.3 %shard_map.140 = (bf16[384,384]{1,0:T(8,128)(2,1)}, f32[128,1024]{1,0:T(8,128)}) custom-call(bf16[128,4,384]{2,1,0:T(4,128)(2,1)} %all-to-all-done.refs_0_, bf16[384,512]{1,0:T(8,128)(2,1)} %get-tuple-element.36.refs_1_, bf16[3,384,1024]{2,1,0:T(8,128)(2,1)} %refs_8_.1), custom_call_target="tpu_custom_call" | custom-call | flops 999999995904 | bytes 3964928 | tf_op jit(solution)/shard_map/pallas_call | solution.py:89
  38.4 0.1 collective-permute-start
  38.5 0.9 collective-permute-start.2
  39.4 2.5 %collective-permute-start.3 = (bf16[384,384]{1,0:T(8,128)(2,1)}, bf16[384,384]{1,0:T(8,128)(2,1)}, u32[]{:S(2)}, u32[]{:S(2)}) collective-permute-start(bf16[384,384]{1,0:T(8,128)(2,1)} %get-tuple-element.50.refs_1_), channel_id=1, source_target_pairs={{0,192},{64,0},{128,64},{192,128},{1,193},{65,1},{129,65},{193,129... | collective-permute-start | bytes 884744 | tf_op jit(solution)/shard_map/ppermute | solution.py:348
  41.8 0.0 collective-permute-done.refs_2_
  41.9 1.0 copy-done.3
  42.9 4.8 %shard_map.141 = (bf16[128,4,384]{2,1,0:T(4,128)(2,1)}, bf16[208,256]{1,0:T(8,128)(2,1)S(1)}, bf16[208,256]{1,0:T(8,128)(2,1)S(1)}, bf16[208,256]{1,0:T(8,128)(2,1)S(1)}, bf16[208,256]{1,0:T(8,128)(2,1)S(1)}) custom-call(s32[2]{0:T(128)S(1)} %pad_add_fusion.1.refs_0_, f32[128,1024]{1,0:T(8,128)S(1)} %copy-done.3, ...), custom_call_target="tpu_custom_call" | custom-call | flops 999999995904 | bytes 5365768 | tf_op jit(solution)/shard_map/pallas_call | solution.py:89
  47.7 1.8 %collective-permute-done.2.refs_2_ = bf16[384,384]{1,0:T(8,128)(2,1)} collective-permute-done((bf16[384,384]{1,0:T(8,128)(2,1)}, bf16[384,384]{1,0:T(8,128)(2,1)}, u32[]{:S(2)}, u32[]{:S(2)}) %collective-permute-start.2) | collective-permute-done | bytes 294944 | tf_op jit(solution)/shard_map/ppermute | solution.py:348
  49.5 3.0 %collective-permute-start.4 = (bf16[384,384]{1,0:T(8,128)(2,1)}, bf16[384,384]{1,0:T(8,128)(2,1)S(1)}, u32[]{:S(2)}, u32[]{:S(2)}) collective-permute-start(bf16[384,384]{1,0:T(8,128)(2,1)} %collective-permute-done.3.refs_4_), channel_id=1, source_target_pairs={{0,192},{64,0},{128,64},{192,128},{1,193},{65,1},{129,65},{193,129... | collective-permute-start | bytes 884744 | tf_op jit(solution)/shard_map/ppermute | solution.py:348
  52.4 0.0 collective-permute-start.6
  52.4 0.9 collective-permute-start.5
  53.3 2.4 %collective-permute-start.7 = (bf16[208,256]{1,0:T(8,128)(2,1)S(1)}, bf16[208,256]{1,0:T(8,128)(2,1)S(1)}, u32[]{:S(2)}, u32[]{:S(2)}) collective-permute-start(bf16[208,256]{1,0:T(8,128)(2,1)S(1)} %get-tuple-element.56), channel_id=1, source_target_pairs={{0,192},{64,0},{128,64},{192,128},{1,193},{65,1},{129,65},{193,129... | collective-permute-start | bytes 319496 | tf_op jit(solution)/shard_map/ppermute | solution.py:348
  55.7 9.1 %all-to-all-start.1 = ((bf16[128,4,384]{2,1,0:T(4,128)(2,1)}), bf16[128,4,384]{2,1,0:T(4,128)(2,1)}, u32[]{:S(2)}, u32[]{:S(2)}) async-start(bf16[128,4,384]{2,1,0:T(4,128)(2,1)} %get-tuple-element.42), calls=%async_computation.1 | async-start | bytes 786432 | tf_op jit(solution)/shard_map/all_to_all | solution.py:472
  64.8 0.0 collective-permute-done.5.refs_6_
  64.8 0.0 collective-permute-done.7.refs_8_
  64.8 2.0 %shard_map.144 = (f32[64,1152]{1,0:T(8,128)S(1)}, bf16[336,384]{1,0:T(8,128)(2,1)S(1)}, bf16[336,384]{1,0:T(8,128)(2,1)S(1)}, bf16[336,384]{1,0:T(8,128)(2,1)S(1)}, bf16[336,384]{1,0:T(8,128)(2,1)S(1)}) custom-call(s32[1]{0:T(128)} %bitcast.6.refs_0_, bf16[384,384]{1,0:T(8,128)(2,1)S(1)} %copy-done.4, bf16[384,384]{1,0:T(8,128)(2,1)} %collective-permute-done.2.refs_2_, ...), custom_call_target="tpu_custom_call" | custom-call | flops 999999995904 | bytes 2932740 | tf_op jit(solution)/shard_map/pallas_call | solution.py:89
  66.9 0.0 copy-start.2
  66.9 0.0 copy-start
  66.9 0.0 copy-start.1
  66.9 1.9 %collective-permute-start.10 = (bf16[336,384]{1,0:T(8,128)(2,1)S(1)}, bf16[336,384]{1,0:T(8,128)(2,1)S(1)}, u32[]{:S(2)}, u32[]{:S(2)}) collective-permute-start(bf16[336,384]{1,0:T(8,128)(2,1)S(1)} %get-tuple-element.61), channel_id=1, source_target_pairs={{0,48},{16,0},{32,16},{48,32},{1,49},{17,1},{33,17},{49,33},{2,50}... | collective-permute-start | bytes 774152 | tf_op jit(solution)/shard_map/ppermute | solution.py:348
  68.8 0.2 collective-permute-start.8
  69.0 3.4 %collective-permute-start.9 = (bf16[336,384]{1,0:T(8,128)(2,1)S(1)}, bf16[336,384]{1,0:T(8,128)(2,1)S(1)}, u32[]{:S(2)}, u32[]{:S(2)}) collective-permute-start(bf16[336,384]{1,0:T(8,128)(2,1)S(1)} %get-tuple-element.60), channel_id=1, source_target_pairs={{0,32},{16,48},{32,0},{48,16},{1,33},{17,49},{33,1},{49,17},{2,34}... | collective-permute-start | bytes 774152 | tf_op jit(solution)/shard_map/ppermute | solution.py:348
  72.4 5.4 %collective-permute-done.10.refs_4_ = bf16[336,384]{1,0:T(8,128)(2,1)S(1)} collective-permute-done((bf16[336,384]{1,0:T(8,128)(2,1)S(1)}, bf16[336,384]{1,0:T(8,128)(2,1)S(1)}, u32[]{:S(2)}, u32[]{:S(2)}) %collective-permute-start.10) | collective-permute-done | bytes 258080 | tf_op jit(solution)/shard_map/ppermute | solution.py:348
  77.8 1.4 %collective-permute-done.8.refs_2_ = bf16[336,384]{1,0:T(8,128)(2,1)S(1)} collective-permute-done((bf16[336,384]{1,0:T(8,128)(2,1)S(1)}, bf16[336,384]{1,0:T(8,128)(2,1)S(1)}, u32[]{:S(2)}, u32[]{:S(2)}) %collective-permute-start.8) | collective-permute-done | bytes 258080 | tf_op jit(solution)/shard_map/ppermute | solution.py:348
  79.2 4.1 %collective-permute-done.9.refs_3_ = bf16[336,384]{1,0:T(8,128)(2,1)S(1)} collective-permute-done((bf16[336,384]{1,0:T(8,128)(2,1)S(1)}, bf16[336,384]{1,0:T(8,128)(2,1)S(1)}, u32[]{:S(2)}, u32[]{:S(2)}) %collective-permute-start.9) | collective-permute-done | bytes 258080 | tf_op jit(solution)/shard_map/ppermute | solution.py:348
  83.4 1.1 %shard_map.145 = bf16[64,2688]{1,0:T(8,128)(2,1)} custom-call(f32[64,1152]{1,0:T(8,128)S(1)} %get-tuple-element.57.refs_0_, bf16[336,384]{1,0:T(8,128)(2,1)S(1)} %get-tuple-element.58.refs_1_, bf16[336,384]{1,0:T(8,128)(2,1)S(1)} %collective-permute-done.8.refs_2_, bf16[336,384]{1,0:T(8,128)(2,1)S(1)} %collective-permute-done.9.refs_3_, ...), custom_call_target="tpu_custom_call" | custom-call | bytes 1671168 | tf_op jit(solution)/shard_map/pallas_call | solution.py:89
  84.5 0.0 all-to-all-done.1.refs_1_
  84.5 6.1 %all-to-all-start.2 = ((bf16[8,8,2688]{2,1,0:T(8,128)(2,1)}), bf16[8,8,2688]{2,1,0:T(8,128)(2,1)S(1)}, u32[]{:S(2)}, u32[]{:S(2)}) async-start(bf16[8,8,2688]{2,1,0:T(8,128)(2,1)} %bitcast.7), calls=%async_computation.2 | async-start | bytes 688128 | tf_op jit(solution)/shard_map/all_to_all | solution.py:492
  90.6 1.8 %shard_map.142 = (f32[1024,384]{1,0:T(8,128)S(1)}, f32[8,128]{1,0:T(8,128)S(1)}) custom-call(s32[1,512]{1,0:T(1,128)S(1)} %copy-done.2, bf16[128,4,384]{2,1,0:T(4,128)(2,1)} %all-to-all-done.1.refs_1_), custom_call_target="tpu_custom_call" | custom-call | bytes 1972224 | tf_op jit(solution)/shard_map/pallas_call | solution.py:89
  92.4 0.1 collective-permute-start.1
  92.5 1.2 %collective-permute-done.1.refs_4_ = f32[8,128]{1,0:T(8,128)S(1)} collective-permute-done((f32[8,128]{1,0:T(8,128)S(1)}, f32[8,128]{1,0:T(8,128)S(1)}, u32[]{:S(2)}, u32[]{:S(2)}) %collective-permute-start.1) | collective-permute-done | bytes 4128 | tf_op jit(solution)/shard_map/ppermute | solution.py:348
  93.7 1.6 %shard_map.143 = (f32[1024,384]{1,0:T(8,128)}, f32[8,128]{1,0:T(8,128)}) custom-call(f32[1024,384]{1,0:T(8,128)S(1)} %copy-done, f32[1024,384]{1,0:T(8,128)S(1)} %get-tuple-element.43.refs_1_, f32[8,128]{1,0:T(8,128)S(1)} %bitcast.13, f32[8,128]{1,0:T(8,128)S(1)} %get-tuple-element.44.refs_3_, f32[8,128]{1,0:T(8,128)S(1)} %collective-permute-done.1.refs_4_), custom_call_target="tpu_custom_call" | custom-call | bytes 4734976 | tf_op jit(solution)/shard_map/pallas_call | solution.py:89
  95.3 8.0 %all-to-all-done.2.refs_0_ = bf16[8,8,2688]{2,1,0:T(8,128)(2,1)S(1)} async-done(((bf16[8,8,2688]{2,1,0:T(8,128)(2,1)}), bf16[8,8,2688]{2,1,0:T(8,128)(2,1)S(1)}, u32[]{:S(2)}, u32[]{:S(2)}) %all-to-all-start.2) | async-done | bytes 344096 | tf_op jit(solution)/shard_map/all_to_all | solution.py:492
  103.2 0.7 shard_map.146
  (32 shorter events, 0.1 us)
Async XLA Ops:
  0.6 18.9 %copy-start.12 = (s32[8,15]{1,0:T(8,128)S(1)}, s32[8,15]{1,0:T(8,128)}, u32[]{:S(2)}) copy-start(s32[8,15]{1,0:T(8,128)} %param.15) | copy-start | bytes 1444
  0.6 19.0 %copy-start.13 = (s32[8,15]{1,0:T(8,128)S(1)}, s32[8,15]{1,0:T(8,128)}, u32[]{:S(2)}) copy-start(s32[8,15]{1,0:T(8,128)} %param.17) | copy-start | bytes 1444
  0.7 19.0 %copy-start.14 = (s32[8]{0:T(128)S(1)}, s32[8]{0:T(128)}, u32[]{:S(2)}) copy-start(s32[8]{0:T(128)} %param.14) | copy-start | bytes 100
  0.7 19.3 %copy-start.10 = (s32[8,15,10]{1,0,2:T(8,128)S(1)}, s32[8,15,10]{1,0,2:T(8,128)}, u32[]{:S(2)}) copy-start(s32[8,15,10]{1,0,2:T(8,128)} %param.16) | copy-start | bytes 14404
  0.7 19.3 %copy-start.11 = (s32[8,15,10]{1,0,2:T(8,128)S(1)}, s32[8,15,10]{1,0,2:T(8,128)}, u32[]{:S(2)}) copy-start(s32[8,15,10]{1,0,2:T(8,128)} %param.18) | copy-start | bytes 14404
  3.8 31.3 %all-to-all-start = ((bf16[128,4,384]{2,1,0:T(4,128)(2,1)}), bf16[128,4,384]{2,1,0:T(4,128)(2,1)}, u32[]{:S(2)}, u32[]{:S(2)}) async-start(bf16[128,4,384]{2,1,0:T(4,128)(2,1)} %shard_map.138), calls=%async_computation | async-start | bytes 786432 | tf_op jit(solution)/shard_map/all_to_all | solution.py:396
  35.1 6.7 %copy-start.5 = (bf16[8,1024]{1,0:T(8,128)(2,1)S(1)}, bf16[8,1024]{1,0:T(8,128)(2,1)}, u32[]{:S(2)}) copy-start(bf16[8,1024]{1,0:T(8,128)(2,1)} %refs_6_.1) | copy-start | bytes 49156
  35.1 6.7 %copy-start.6 = (f32[128,1024]{1,0:T(8,128)S(1)}, f32[128,1024]{1,0:T(8,128)}, u32[]{:S(2)}) copy-start(f32[128,1024]{1,0:T(8,128)} %get-tuple-element.38.refs_3_) | copy-start | bytes 1572868
  35.1 6.7 %copy-start.7 = (bf16[512,384]{1,0:T(8,128)(2,1)S(1)}, bf16[512,384]{1,0:T(8,128)(2,1)}, u32[]{:S(2)}) copy-start(bf16[512,384]{1,0:T(8,128)(2,1)} %get-tuple-element.41.refs_7_) | copy-start | bytes 1179652
  35.1 6.7 %copy-start.8 = (f32[384,128]{1,0:T(8,128)S(1)}, f32[384,128]{1,0:T(8,128)}, u32[]{:S(2)}) copy-start(f32[384,128]{1,0:T(8,128)} %get-tuple-element.40.refs_5_) | copy-start | bytes 589828
  35.1 6.8 %copy-start.9 = (bf16[32,128]{1,0:T(8,128)(2,1)S(1)}, bf16[32,128]{1,0:T(8,128)(2,1)}, u32[]{:S(2)}) copy-start(bf16[32,128]{1,0:T(8,128)(2,1)} %get-tuple-element.39.refs_4_) | copy-start | bytes 24580
  38.4 3.4 %collective-permute-start = (f32[128,1024]{1,0:T(8,128)}, f32[128,1024]{1,0:T(8,128)S(1)}, u32[]{:S(2)}, u32[]{:S(2)}) collective-permute-start(f32[128,1024]{1,0:T(8,128)} %get-tuple-element.37.refs_1_), channel_id=1, source_target_pairs={{0,1},{1,0},{2,3},{3,2},{4,5},{5,4},{6,7},{7,6},{8,9},{9,8},{10,11... | collective-permute-start | bytes 1572872 | tf_op jit(solution)/shard_map/ppermute | solution.py:348
  38.5 11.0 %collective-permute-start.2 = (bf16[384,384]{1,0:T(8,128)(2,1)}, bf16[384,384]{1,0:T(8,128)(2,1)}, u32[]{:S(2)}, u32[]{:S(2)}) collective-permute-start(bf16[384,384]{1,0:T(8,128)(2,1)} %get-tuple-element.50.refs_1_), channel_id=1, source_target_pairs={{0,64},{64,128},{128,192},{192,0},{1,65},{65,129},{129,193},{193,1... | collective-permute-start | bytes 884744 | tf_op jit(solution)/shard_map/ppermute | solution.py:348
  39.4 10.1 %collective-permute-start.3 = (bf16[384,384]{1,0:T(8,128)(2,1)}, bf16[384,384]{1,0:T(8,128)(2,1)}, u32[]{:S(2)}, u32[]{:S(2)}) collective-permute-start(bf16[384,384]{1,0:T(8,128)(2,1)} %get-tuple-element.50.refs_1_), channel_id=1, source_target_pairs={{0,192},{64,0},{128,64},{192,128},{1,193},{65,1},{129,65},{193,129... | collective-permute-start | bytes 884744 | tf_op jit(solution)/shard_map/ppermute | solution.py:348
  41.9 1.0 %copy-start.3 = (f32[128,1024]{1,0:T(8,128)S(1)}, f32[128,1024]{1,0:T(8,128)}, u32[]{:S(2)}) copy-start(f32[128,1024]{1,0:T(8,128)} %get-tuple-element.37.refs_1_) | copy-start | bytes 1572868
  42.9 21.9 %copy-start.4 = (bf16[384,384]{1,0:T(8,128)(2,1)S(1)}, bf16[384,384]{1,0:T(8,128)(2,1)}, u32[]{:S(2)}) copy-start(bf16[384,384]{1,0:T(8,128)(2,1)} %get-tuple-element.50.refs_1_) | copy-start | bytes 884740
  49.5 15.4 %collective-permute-start.4 = (bf16[384,384]{1,0:T(8,128)(2,1)}, bf16[384,384]{1,0:T(8,128)(2,1)S(1)}, u32[]{:S(2)}, u32[]{:S(2)}) collective-permute-start(bf16[384,384]{1,0:T(8,128)(2,1)} %collective-permute-done.3.refs_4_), channel_id=1, source_target_pairs={{0,192},{64,0},{128,64},{192,128},{1,193},{65,1},{129,65},{193,129... | collective-permute-start | bytes 884744 | tf_op jit(solution)/shard_map/ppermute | solution.py:348
  52.4 12.4 %collective-permute-start.6 = (bf16[208,256]{1,0:T(8,128)(2,1)S(1)}, bf16[208,256]{1,0:T(8,128)(2,1)S(1)}, u32[]{:S(2)}, u32[]{:S(2)}) collective-permute-start(bf16[208,256]{1,0:T(8,128)(2,1)S(1)} %get-tuple-element.55), channel_id=1, source_target_pairs={{0,128},{64,192},{128,0},{192,64},{1,129},{65,193},{129,1},{193,65... | collective-permute-start | bytes 319496 | tf_op jit(solution)/shard_map/ppermute | solution.py:348
  52.4 12.4 %collective-permute-start.5 = (bf16[208,256]{1,0:T(8,128)(2,1)S(1)}, bf16[208,256]{1,0:T(8,128)(2,1)S(1)}, u32[]{:S(2)}, u32[]{:S(2)}) collective-permute-start(bf16[208,256]{1,0:T(8,128)(2,1)S(1)} %get-tuple-element.54), channel_id=1, source_target_pairs={{0,64},{64,128},{128,192},{192,0},{1,65},{65,129},{129,193},{193,1... | collective-permute-start | bytes 319496 | tf_op jit(solution)/shard_map/ppermute | solution.py:348
  53.3 11.5 %collective-permute-start.7 = (bf16[208,256]{1,0:T(8,128)(2,1)S(1)}, bf16[208,256]{1,0:T(8,128)(2,1)S(1)}, u32[]{:S(2)}, u32[]{:S(2)}) collective-permute-start(bf16[208,256]{1,0:T(8,128)(2,1)S(1)} %get-tuple-element.56), channel_id=1, source_target_pairs={{0,192},{64,0},{128,64},{192,128},{1,193},{65,1},{129,65},{193,129... | collective-permute-start | bytes 319496 | tf_op jit(solution)/shard_map/ppermute | solution.py:348
  55.7 28.8 %all-to-all-start.1 = ((bf16[128,4,384]{2,1,0:T(4,128)(2,1)}), bf16[128,4,384]{2,1,0:T(4,128)(2,1)}, u32[]{:S(2)}, u32[]{:S(2)}) async-start(bf16[128,4,384]{2,1,0:T(4,128)(2,1)} %get-tuple-element.42), calls=%async_computation.1 | async-start | bytes 786432 | tf_op jit(solution)/shard_map/all_to_all | solution.py:472
  66.9 23.7 %copy-start.2 = (s32[1,512]{1,0:T(1,128)S(1)}, s32[1,512]{1,0:T(1,128)}, u32[]{:S(2)}) copy-start(s32[1,512]{1,0:T(1,128)} %refs_0_.4) | copy-start | bytes 6148
  66.9 26.8 %copy-start = (f32[1024,384]{1,0:T(8,128)S(1)}, f32[1024,384]{1,0:T(8,128)}, u32[]{:S(2)}) copy-start(f32[1024,384]{1,0:T(8,128)} %refs_0_.5) | copy-start | bytes 4718596
  66.9 26.8 %copy-start.1 = (f32[1024]{0:T(1024)S(1)}, f32[1024]{0:T(1024)}, u32[]{:S(2)}) copy-start(f32[1024]{0:T(1024)} %param.12) | copy-start | bytes 12292
  66.9 10.9 %collective-permute-start.10 = (bf16[336,384]{1,0:T(8,128)(2,1)S(1)}, bf16[336,384]{1,0:T(8,128)(2,1)S(1)}, u32[]{:S(2)}, u32[]{:S(2)}) collective-permute-start(bf16[336,384]{1,0:T(8,128)(2,1)S(1)} %get-tuple-element.61), channel_id=1, source_target_pairs={{0,48},{16,0},{32,16},{48,32},{1,49},{17,1},{33,17},{49,33},{2,50}... | collective-permute-start | bytes 774152 | tf_op jit(solution)/shard_map/ppermute | solution.py:348
  68.8 10.5 %collective-permute-start.8 = (bf16[336,384]{1,0:T(8,128)(2,1)S(1)}, bf16[336,384]{1,0:T(8,128)(2,1)S(1)}, u32[]{:S(2)}, u32[]{:S(2)}) collective-permute-start(bf16[336,384]{1,0:T(8,128)(2,1)S(1)} %get-tuple-element.59), channel_id=1, source_target_pairs={{0,16},{16,32},{32,48},{48,0},{1,17},{17,33},{33,49},{49,1},{2,18}... | collective-permute-start | bytes 774152 | tf_op jit(solution)/shard_map/ppermute | solution.py:348
  69.0 14.4 %collective-permute-start.9 = (bf16[336,384]{1,0:T(8,128)(2,1)S(1)}, bf16[336,384]{1,0:T(8,128)(2,1)S(1)}, u32[]{:S(2)}, u32[]{:S(2)}) collective-permute-start(bf16[336,384]{1,0:T(8,128)(2,1)S(1)} %get-tuple-element.60), channel_id=1, source_target_pairs={{0,32},{16,48},{32,0},{48,16},{1,33},{17,49},{33,1},{49,17},{2,34}... | collective-permute-start | bytes 774152 | tf_op jit(solution)/shard_map/ppermute | solution.py:348
  84.5 18.8 %all-to-all-start.2 = ((bf16[8,8,2688]{2,1,0:T(8,128)(2,1)}), bf16[8,8,2688]{2,1,0:T(8,128)(2,1)S(1)}, u32[]{:S(2)}, u32[]{:S(2)}) async-start(bf16[8,8,2688]{2,1,0:T(8,128)(2,1)} %bitcast.7), calls=%async_computation.2 | async-start | bytes 688128 | tf_op jit(solution)/shard_map/all_to_all | solution.py:492
  92.4 1.2 %collective-permute-start.1 = (f32[8,128]{1,0:T(8,128)S(1)}, f32[8,128]{1,0:T(8,128)S(1)}, u32[]{:S(2)}, u32[]{:S(2)}) collective-permute-start(f32[8,128]{1,0:T(8,128)S(1)} %get-tuple-element.44.refs_3_), channel_id=1, source_target_pairs={{0,1},{1,0},{2,3},{3,2},{4,5},{5,4},{6,7},{7,6},{8,9},{9,8},{10,11... | collective-permute-start | bytes 12296 | tf_op jit(solution)/shard_map/ppermute | solution.py:348

commit v11 on v9

--- a/solution.py
+++ b/solution.py
@@ -92,7 +92,7 @@
         in_specs=specs,
         out_specs=tuple(made),
         scratch_shapes=buffers + semaphores + list(scratch),
-        compiler_params=pltpu.CompilerParams(vmem_limit_bytes=limit * 1024 * 1024),
+        compiler_params=pltpu.CompilerParams(vmem_limit_bytes=int(limit * 1024 * 1024)),
         cost_estimate=pl.CostEstimate(flops=flops, bytes_accessed=moved, transcendentals=0),
     )(*operands)
 
@@ -245,7 +245,7 @@
 
 def weight_kernel(count, place_ref, *refs):
     layer_refs, pack_refs = refs[:2], refs[2 : 2 + count]
-    own_ref, outs, total = refs[2 + count], refs[3 + count : -1], refs[-1]
+    own_ref, second_ref, outs, total = refs[2 + count], refs[3 + count], refs[4 + count : -1], refs[-1]
     pack_rows, width = pack_refs[0].shape
     layer_rows, columns = layer_refs[0].shape
     layer_parts, packs = [], []
@@ -283,7 +283,8 @@
     ).astype(BF16)
     group = count * seeds
     per = columns // (group // COT_ROWS)
-    tail = relations * rows
+    for piece in range(relations * half // columns):
+        second_ref[piece * group : (piece + 1) * group, :] = second[:, piece * columns : (piece + 1) * columns]
     for d, out in enumerate(outs):
         target = lax.rem(place_ref[0] + d, len(outs))
         start = pl.multiple_of(target * rows, rows)
@@ -293,10 +294,6 @@
                 own_ref[:, k * columns : (k + 1) * columns] = block
             else:
                 out[k * rows : (k + 1) * rows, :] = block.astype(BF16)
-        for piece in range(relations * half // columns):
-            out[tail + piece * group : tail + (piece + 1) * group, :] = second[
-                :, piece * columns : (piece + 1) * columns
-            ]
         chosen = cots[:, :rows]
         for j in range(1, len(outs)):
             chosen = jnp.where(target == j, cots[:, j * rows : (j + 1) * rows], chosen)
@@ -306,13 +303,14 @@
 
 
 def group_kernel(relations, own_ref, *refs):
-    packs, out_ref = refs[:-1], refs[-1]
+    count = len(refs) // 2
+    packs, seconds, out_ref = refs[:count], refs[count:-1], refs[-1]
     rows = own_ref.shape[0]
     columns = packs[0].shape[1]
     tail = relations * rows
     wide = out_ref.shape[1] - relations * columns
     pieces = wide // columns
-    group = (packs[0].shape[0] - tail - COT_ROWS) // pieces
+    group = seconds[0].shape[0] // pieces
     per = columns // (group // COT_ROWS)
     for k in range(relations):
         span = slice(k * columns, (k + 1) * columns)
@@ -322,15 +320,15 @@
         out_ref[:, span] = block.astype(BF16)
     cots = jnp.concatenate(
         [
-            p[tail + pieces * group :, piece * per : piece * per + rows]
+            p[tail:, piece * per : piece * per + rows]
             for p in packs
             for piece in range(group // COT_ROWS)
         ],
         0,
     )
     for piece in range(pieces):
-        first = tail + piece * group
-        second = jnp.concatenate([p[first : first + group, :] for p in packs], 0)
+        first = piece * group
+        second = jnp.concatenate([p[first : first + group, :] for p in seconds], 0)
         start = (relations + piece) * columns
         out_ref[:, start : start + columns] = matmul(cots, second, (0, 0)).astype(BF16)
 
@@ -371,7 +369,7 @@
     return lax.ppermute(array, axis, [(i, (i + by) % size) for i in range(size)])
 
 
-LIMITS = {serve_kernel: 60, index_kernel: 60, first_kernel: 60, hidden_kernel: 60}
+LIMITS = {serve_kernel: 60, index_kernel: 60, first_kernel: 60, hidden_kernel: 51.5}
 COSTS = {update_kernel: 0, group_kernel: 0, row_kernel: 0}
 
 
@@ -493,21 +491,27 @@
     arrived = lax.all_to_all(slot_grad, everyone, split_axis=0, concat_axis=0, tiled=True)
 
     block_rows = width // n_y
-    group_rows = layers * block_rows + (layers * half // columns) * n_x * seeds + COT_ROWS
-    own, *blocks = call(
+    group_rows = layers * block_rows + COT_ROWS
+    second_rows = (layers * half // columns) * n_x * seeds
+    own, second, *blocks = call(
         functools.partial(weight_kernel, n_x),
-        [shaped((block_rows, layers * columns), F32)] + [shaped((group_rows, columns), BF16)] * n_y,
+        [shaped((block_rows, layers * columns), F32), shaped((second_rows, columns), BF16)]
+        + [shaped((group_rows, columns), BF16)] * n_y,
         (y.reshape(1), *layer_parts, *packs),
         smem=1,
         hbm_in=range(1, 3 + n_x),
         scratch=[pltpu.VMEM((layers, width, columns), F32)],
     )
+    seconds = [second, shift(second, "y", 1)]
+    if n_y > 2:
+        last = shift(second, "y", n_y - 1)
+        seconds += [shift(last, "y", n_y - 1), last]
     blocks = [blocks[0]] + [shift(blocks[d], "y", d) for d in range(1, n_y)]
     grad_columns = layers * (columns + half)
     grads = call(
         functools.partial(group_kernel, layers),
         [shaped((block_rows, grad_columns), BF16)],
-        (own, *blocks),
+        (own, *blocks, *seconds),
     )[0]
     grads = grads.reshape(n_z, block_rows // n_z, grad_columns)
     grads = lax.all_to_all(grads, "z", split_axis=0, concat_axis=0, tiled=True)

time: 103 us -> 101 us (0.981)
  waiting for transfers between devices: 29.5 us -> 24.8 us
  starting transfers between devices: 42.4 us -> 46.8 us
    ppermute x9 -> x12, waiting for transfers between devices: 13.5 us -> 8.54 us  [shift(): lax.ppermute(array, axis, [(i, (i + by) % size) for i in range(size)])]
    ppermute x9 -> x12, starting transfers between devices: 13.2 us -> 16.3 us  [shift(): lax.ppermute(array, axis, [(i, (i + by) % size) for i in range(size)])]
  transfers between devices with their start and end apart: 12 -> 15, of which waited for: 10 -> 9; matrix products, arithmetic and copies ran while one was open for 2% -> 1% of each run, Pallas kernels for 18% -> 18%
where the time goes in v11:
time: 101 us; the launch traced here: 100 us
  starting transfers between devices  46.8 us (46%)
  Pallas kernels  24.8 us (25%)
  waiting for transfers between devices  24.8 us (25%)
  local copies, waits for them, and re-layouts  3 us (3%)
    pallas_call x9, Pallas kernels, call(): pl.pallas_call(wrapped, out_shape=tuple(outs), in_specs=specs, out_specs=...  24.8 us
    ppermute x12, starting transfers between devices, shift(): lax.ppermute(array, axis, [(i, (i + by) % size) for i in range(size)])  16.3 us
    all_to_all x1, starting transfers between devices, body(): lax.all_to_all(outgoing, everyone, split_axis=0, concat_axis=0, tiled=True)  15.8 us
    all_to_all x1, starting transfers between devices, body(): lax.all_to_all(slot_grad, everyone, split_axis=0, concat_axis=0, tiled=True)  9.93 us
    ppermute x12, waiting for transfers between devices, shift(): lax.ppermute(array, axis, [(i, (i + by) % size) for i in range(size)])  8.54 us
    all_to_all x1, waiting for transfers between devices, body(): grads = lax.all_to_all(grads, 'z', split_axis=0, concat_axis=0, tiled=True)  8.46 us
    all_to_all x1, waiting for transfers between devices, body(): lax.all_to_all(outgoing, everyone, split_axis=0, concat_axis=0, tiled=True)  7.78 us
    all_to_all x1, starting transfers between devices, body(): grads = lax.all_to_all(grads, 'z', split_axis=0, concat_axis=0, tiled=True)  4.73 us
  transfers between devices with their start and end apart: 15, of which 9 were waited for; matrix products, arithmetic and copies ran while one was open for 1% of the time, Pallas kernels for 18%

profile of v11, /device:TPU:8, one launch (start us, length us, event | category | flops | bytes accessed | tf_op | source)
XLA Modules:
  0.0 100.4 jit_solution(15515548079651481925)
XLA Ops:
  0.7 3.1 %shard_map.138 = bf16[128,4,384]{2,1,0:T(4,128)(2,1)} custom-call(s32[1,512]{1,0:T(1,128)} %refs_0_.4, f32[4,256,384]{2,1,0:T(8,128)} %bitcast.12), custom_call_target="tpu_custom_call" | custom-call | flops 999999995904 | bytes 1968128 | tf_op jit(solution)/shard_map/pallas_call | solution.py:89
  3.7 15.8 %all-to-all-start = ((bf16[128,4,384]{2,1,0:T(4,128)(2,1)}), bf16[128,4,384]{2,1,0:T(4,128)(2,1)}, u32[]{:S(2)}, u32[]{:S(2)}) async-start(bf16[128,4,384]{2,1,0:T(4,128)(2,1)} %shard_map.138), calls=%async_computation | async-start | bytes 786432 | tf_op jit(solution)/shard_map/all_to_all | solution.py:417
  19.5 0.1 reshape.32
  19.6 0.1 copy.32
  19.7 0.1 pad_add_fusion
  19.8 0.1 copy.33
  19.9 0.1 reshape.34
  20.0 0.1 reshape.33
  20.1 0.1 pad_add_fusion.1.refs_0_
  20.1 0.1 add_add_fusion
  20.2 0.8 copy.34.refs_0_
  21.0 6.3 %shard_map.139 = (bf16[384,512]{1,0:T(8,128)(2,1)}, bf16[512,384]{1,0:T(8,128)(2,1)}, f32[384,128]{1,0:T(8,128)}, bf16[32,128]{1,0:T(8,128)(2,1)}, f32[128,1024]{1,0:T(8,128)}) custom-call(s32[128,17]{1,0:T(8,128)} %copy.34.refs_0_, bf16[8,1024]{1,0:T(8,128)(2,1)} %refs_6_.1, bf16[3,1024,1024]{2,1,0:T(8,128)(2,1)} %refs_2_.2), custom_call_target="tpu_custom_call" | custom-call | flops 999999995904 | bytes 7832064 | tf_op jit(solution)/shard_map/pallas_call | solution.py:89
  27.3 7.8 %all-to-all-done.refs_0_ = bf16[128,4,384]{2,1,0:T(4,128)(2,1)} async-done(((bf16[128,4,384]{2,1,0:T(4,128)(2,1)}), bf16[128,4,384]{2,1,0:T(4,128)(2,1)}, u32[]{:S(2)}, u32[]{:S(2)}) %all-to-all-start) | async-done | bytes 393248 | tf_op jit(solution)/shard_map/all_to_all | solution.py:417
  35.1 3.3 %shard_map.140 = (bf16[384,384]{1,0:T(8,128)(2,1)}, f32[128,1024]{1,0:T(8,128)}) custom-call(bf16[128,4,384]{2,1,0:T(4,128)(2,1)} %all-to-all-done.refs_0_, bf16[384,512]{1,0:T(8,128)(2,1)} %get-tuple-element.36.refs_1_, bf16[3,384,1024]{2,1,0:T(8,128)(2,1)} %refs_8_.1), custom_call_target="tpu_custom_call" | custom-call | flops 999999995904 | bytes 3964928 | tf_op jit(solution)/shard_map/pallas_call | solution.py:89
  38.4 0.1 collective-permute-start
  38.5 1.6 %collective-permute-start.2 = (bf16[384,384]{1,0:T(8,128)(2,1)}, bf16[384,384]{1,0:T(8,128)(2,1)}, u32[]{:S(2)}, u32[]{:S(2)}) collective-permute-start(bf16[384,384]{1,0:T(8,128)(2,1)} %get-tuple-element.50.refs_9_.refs_1_), channel_id=1, source_target_pairs={{0,128},{64,192},{128,0},{192,64},{1,129},{65,193},{129,1},{193,65... | collective-permute-start | bytes 884744 | tf_op jit(solution)/shard_map/ppermute | solution.py:369
  40.1 0.5 collective-permute-done.refs_2_
  40.6 0.8 copy-done.14
  41.4 1.0 copy-done.3
  42.4 5.2 %shard_map.141 = (bf16[128,4,384]{2,1,0:T(4,128)(2,1)}, bf16[208,256]{1,0:T(8,128)(2,1)S(1)}, bf16[1568,128]{1,0:T(8,128)(2,1)S(1)}, bf16[208,256]{1,0:T(8,128)(2,1)S(1)}, bf16[1568,128]{1,0:T(8,128)(2,1)S(1)}) custom-call(s32[2]{0:T(128)S(1)} %pad_add_fusion.1.refs_0_, f32[128,1024]{1,0:T(8,128)} %get-tuple-element.37.refs_1_, f32[128,1024]{1,0:T(8,128)} %copy-done.14, ...), custom_call_target="tpu_custom_call" | custom-call | flops 999999995904 | bytes 6250504 | tf_op jit(solution)/shard_map/pallas_call | solution.py:89
  47.5 0.9 collective-permute-start.3
  48.4 2.5 %collective-permute-start.5 = (bf16[1568,128]{1,0:T(8,128)(2,1)S(1)}, bf16[1568,128]{1,0:T(8,128)(2,1)S(1)}, u32[]{:S(2)}, u32[]{:S(2)}) collective-permute-start(bf16[1568,128]{1,0:T(8,128)(2,1)S(1)} %get-tuple-element.55), channel_id=1, source_target_pairs={{0,192},{64,0},{128,64},{192,128},{1,193},{65,1},{129,65},{193,129... | collective-permute-start | bytes 1204232 | tf_op jit(solution)/shard_map/ppermute | solution.py:369
  50.9 0.4 collective-permute-start.4
  51.3 9.9 %all-to-all-start.1 = ((bf16[128,4,384]{2,1,0:T(4,128)(2,1)}), bf16[128,4,384]{2,1,0:T(4,128)(2,1)}, u32[]{:S(2)}, u32[]{:S(2)}) async-start(bf16[128,4,384]{2,1,0:T(4,128)(2,1)} %get-tuple-element.43), calls=%async_computation.1 | async-start | bytes 786432 | tf_op jit(solution)/shard_map/all_to_all | solution.py:491
  61.2 1.0 %collective-permute-done.4.refs_5_ = bf16[208,256]{1,0:T(8,128)(2,1)S(1)} collective-permute-done((bf16[208,256]{1,0:T(8,128)(2,1)S(1)}, bf16[208,256]{1,0:T(8,128)(2,1)S(1)}, u32[]{:S(2)}, u32[]{:S(2)}) %collective-permute-start.4) | collective-permute-done | bytes 106528 | tf_op jit(solution)/shard_map/ppermute | solution.py:369
  62.2 0.2 collective-permute-done.3.refs_4_
  62.4 0.0 collective-permute-done.5.refs_6_
  62.4 1.9 %shard_map.144 = (f32[64,1152]{1,0:T(8,128)S(1)}, bf16[128,384]{1,0:T(8,128)(2,1)S(1)}, bf16[208,384]{1,0:T(8,128)(2,1)S(1)}, bf16[208,384]{1,0:T(8,128)(2,1)S(1...) custom-call(s32[1]{0:T(128)} %bitcast.6.refs_0_, bf16[384,384]{1,0:T(8,128)(2,1)S(1)} %copy-done.4, ...), custom_call_target="tpu_custom_call" | custom-call | flops 999999995904 | bytes 2637828 | tf_op jit(solution)/shard_map/pallas_call | solution.py:89
  64.3 0.0 copy-start.2
  64.3 0.0 copy-start
  64.3 0.0 copy-start.1
  64.3 4.6 %collective-permute-start.10 = (bf16[128,384]{1,0:T(8,128)(2,1)S(1)}, bf16[128,384]{1,0:T(8,128)(2,1)S(1)}, u32[]{:S(2)}, u32[]{:S(2)}) collective-permute-start(bf16[128,384]{1,0:T(8,128)(2,1)S(1)} %get-tuple-element.61.refs_5_), channel_id=1, source_target_pairs={{0,48},{16,0},{32,16},{48,32},{1,49},{17,1},{33,17},{49,33},{2,50}... | collective-permute-start | bytes 294920 | tf_op jit(solution)/shard_map/ppermute | solution.py:369
  69.0 2.2 %collective-permute-start.7 = (bf16[208,384]{1,0:T(8,128)(2,1)S(1)}, bf16[208,384]{1,0:T(8,128)(2,1)S(1)}, u32[]{:S(2)}, u32[]{:S(2)}) collective-permute-start(bf16[208,384]{1,0:T(8,128)(2,1)S(1)} %get-tuple-element.59), channel_id=1, source_target_pairs={{0,32},{16,48},{32,0},{48,16},{1,33},{17,49},{33,1},{49,17},{2,34}... | collective-permute-start | bytes 479240 | tf_op jit(solution)/shard_map/ppermute | solution.py:369
  71.1 0.0 collective-permute-start.8
  71.1 2.0 %collective-permute-start.9 = (bf16[128,384]{1,0:T(8,128)(2,1)S(1)}, bf16[128,384]{1,0:T(8,128)(2,1)S(1)}, u32[]{:S(2)}, u32[]{:S(2)}) collective-permute-start(bf16[128,384]{1,0:T(8,128)(2,1)S(1)} %get-tuple-element.61.refs_5_), channel_id=1, source_target_pairs={{0,16},{16,32},{32,48},{48,0},{1,17},{17,33},{33,49},{49,1},{2,18}... | collective-permute-start | bytes 294920 | tf_op jit(solution)/shard_map/ppermute | solution.py:369
  73.2 0.0 collective-permute-done.10.refs_8_
  73.2 2.0 %collective-permute-start.11 = (bf16[128,384]{1,0:T(8,128)(2,1)S(1)}, bf16[128,384]{1,0:T(8,128)(2,1)S(1)}, u32[]{:S(2)}, u32[]{:S(2)}) collective-permute-start(bf16[128,384]{1,0:T(8,128)(2,1)S(1)} %collective-permute-done.10.refs_8_), channel_id=1, source_target_pairs={{0,48},{16,0},{32,16},{48,32},{1,49},{17,1},{33,17},{49,33},{2,50}... | collective-permute-start | bytes 294920 | tf_op jit(solution)/shard_map/ppermute | solution.py:369
  75.2 4.3 %collective-permute-done.9.refs_6_ = bf16[128,384]{1,0:T(8,128)(2,1)S(1)} collective-permute-done((bf16[128,384]{1,0:T(8,128)(2,1)S(1)}, bf16[128,384]{1,0:T(8,128)(2,1)S(1)}, u32[]{:S(2)}, u32[]{:S(2)}) %collective-permute-start.9) | collective-permute-done | bytes 98336 | tf_op jit(solution)/shard_map/ppermute | solution.py:369
  79.5 0.3 collective-permute-done.8.refs_4_
  79.8 1.1 %collective-permute-done.11.refs_7_ = bf16[128,384]{1,0:T(8,128)(2,1)S(1)} collective-permute-done((bf16[128,384]{1,0:T(8,128)(2,1)S(1)}, bf16[128,384]{1,0:T(8,128)(2,1)S(1)}, u32[]{:S(2)}, u32[]{:S(2)}) %collective-permute-start.11) | collective-permute-done | bytes 98336 | tf_op jit(solution)/shard_map/ppermute | solution.py:369
  80.9 1.1 %shard_map.145 = bf16[64,2688]{1,0:T(8,128)(2,1)} custom-call(f32[64,1152]{1,0:T(8,128)S(1)} %get-tuple-element.56.refs_0_, bf16[208,384]{1,0:T(8,128)(2,1)S(1)} %get-tuple-element.57.refs_1_, bf16[208,384]{1,0:T(8,128)(2,1)S(1)} %collective-permute-done.6.refs_2_, bf16[208,384]{1,0:T(8,128)(2,1)S(1)} %collective-permute-done.7.refs_3_, ...), custom_call_target="tpu_custom_call" | custom-call | bytes 1671168 | tf_op jit(solution)/shard_map/pallas_call | solution.py:89
  81.9 4.7 %all-to-all-start.2 = ((bf16[8,8,2688]{2,1,0:T(8,128)(2,1)}), bf16[8,8,2688]{2,1,0:T(8,128)(2,1)S(1)}, u32[]{:S(2)}, u32[]{:S(2)}) async-start(bf16[8,8,2688]{2,1,0:T(8,128)(2,1)} %bitcast.7), calls=%async_computation.2 | async-start | bytes 688128 | tf_op jit(solution)/shard_map/all_to_all | solution.py:517
  86.7 1.8 %shard_map.142 = (f32[1024,384]{1,0:T(8,128)S(1)}, f32[8,128]{1,0:T(8,128)S(1)}) custom-call(s32[1,512]{1,0:T(1,128)S(1)} %copy-done.2, bf16[128,4,384]{2,1,0:T(4,128)(2,1)} %all-to-all-done.1.refs_1_), custom_call_target="tpu_custom_call" | custom-call | bytes 1972224 | tf_op jit(solution)/shard_map/pallas_call | solution.py:89
  88.5 0.1 collective-permute-start.1
  88.6 1.2 %collective-permute-done.1.refs_4_ = f32[8,128]{1,0:T(8,128)S(1)} collective-permute-done((f32[8,128]{1,0:T(8,128)S(1)}, f32[8,128]{1,0:T(8,128)S(1)}, u32[]{:S(2)}, u32[]{:S(2)}) %collective-permute-start.1) | collective-permute-done | bytes 4128 | tf_op jit(solution)/shard_map/ppermute | solution.py:369
  89.7 1.6 %shard_map.143 = (f32[1024,384]{1,0:T(8,128)}, f32[8,128]{1,0:T(8,128)}) custom-call(f32[1024,384]{1,0:T(8,128)S(1)} %copy-done, f32[1024,384]{1,0:T(8,128)S(1)} %get-tuple-element.44.refs_1_, f32[8,128]{1,0:T(8,128)S(1)} %bitcast.13, f32[8,128]{1,0:T(8,128)S(1)} %get-tuple-element.45.refs_3_, f32[8,128]{1,0:T(8,128)S(1)} %collective-permute-done.1.refs_4_), custom_call_target="tpu_custom_call" | custom-call | bytes 4734976 | tf_op jit(solution)/shard_map/pallas_call | solution.py:89
  91.3 8.5 %all-to-all-done.2.refs_0_ = bf16[8,8,2688]{2,1,0:T(8,128)(2,1)S(1)} async-done(((bf16[8,8,2688]{2,1,0:T(8,128)(2,1)}), bf16[8,8,2688]{2,1,0:T(8,128)(2,1)S(1)}, u32[]{:S(2)}, u32[]{:S(2)}) %all-to-all-start.2) | async-done | bytes 344096 | tf_op jit(solution)/shard_map/all_to_all | solution.py:517
  99.8 0.7 shard_map.146
  (34 shorter events, 0.1 us)
Async XLA Ops:
  0.6 18.9 %copy-start.11 = (s32[8,15]{1,0:T(8,128)S(1)}, s32[8,15]{1,0:T(8,128)}, u32[]{:S(2)}) copy-start(s32[8,15]{1,0:T(8,128)} %param.15) | copy-start | bytes 1444
  0.6 19.0 %copy-start.12 = (s32[8,15]{1,0:T(8,128)S(1)}, s32[8,15]{1,0:T(8,128)}, u32[]{:S(2)}) copy-start(s32[8,15]{1,0:T(8,128)} %param.17) | copy-start | bytes 1444
  0.7 19.0 %copy-start.13 = (s32[8]{0:T(128)S(1)}, s32[8]{0:T(128)}, u32[]{:S(2)}) copy-start(s32[8]{0:T(128)} %param.14) | copy-start | bytes 100
  0.7 19.3 %copy-start.9 = (s32[8,15,10]{1,0,2:T(8,128)S(1)}, s32[8,15,10]{1,0,2:T(8,128)}, u32[]{:S(2)}) copy-start(s32[8,15,10]{1,0,2:T(8,128)} %param.16) | copy-start | bytes 14404
  0.7 19.3 %copy-start.10 = (s32[8,15,10]{1,0,2:T(8,128)S(1)}, s32[8,15,10]{1,0,2:T(8,128)}, u32[]{:S(2)}) copy-start(s32[8,15,10]{1,0,2:T(8,128)} %param.18) | copy-start | bytes 14404
  3.7 31.3 %all-to-all-start = ((bf16[128,4,384]{2,1,0:T(4,128)(2,1)}), bf16[128,4,384]{2,1,0:T(4,128)(2,1)}, u32[]{:S(2)}, u32[]{:S(2)}) async-start(bf16[128,4,384]{2,1,0:T(4,128)(2,1)} %shard_map.138), calls=%async_computation | async-start | bytes 786432 | tf_op jit(solution)/shard_map/all_to_all | solution.py:417
  35.1 6.3 %copy-start.5 = (bf16[8,1024]{1,0:T(8,128)(2,1)S(1)}, bf16[8,1024]{1,0:T(8,128)(2,1)}, u32[]{:S(2)}) copy-start(bf16[8,1024]{1,0:T(8,128)(2,1)} %refs_6_.1) | copy-start | bytes 49156
  35.1 6.3 %copy-start.6 = (bf16[512,384]{1,0:T(8,128)(2,1)S(1)}, bf16[512,384]{1,0:T(8,128)(2,1)}, u32[]{:S(2)}) copy-start(bf16[512,384]{1,0:T(8,128)(2,1)} %get-tuple-element.41.refs_7_) | copy-start | bytes 1179652
  35.1 6.3 %copy-start.7 = (f32[384,128]{1,0:T(8,128)S(1)}, f32[384,128]{1,0:T(8,128)}, u32[]{:S(2)}) copy-start(f32[384,128]{1,0:T(8,128)} %get-tuple-element.40.refs_5_) | copy-start | bytes 589828
  35.1 6.3 %copy-start.8 = (bf16[32,128]{1,0:T(8,128)(2,1)S(1)}, bf16[32,128]{1,0:T(8,128)(2,1)}, u32[]{:S(2)}) copy-start(bf16[32,128]{1,0:T(8,128)(2,1)} %get-tuple-element.39.refs_4_) | copy-start | bytes 24580
  38.4 2.2 %collective-permute-start = (f32[128,1024]{1,0:T(8,128)}, f32[128,1024]{1,0:T(8,128)S(1)}, u32[]{:S(2)}, u32[]{:S(2)}) collective-permute-start(f32[128,1024]{1,0:T(8,128)} %get-tuple-element.37.refs_1_), channel_id=1, source_target_pairs={{0,1},{1,0},{2,3},{3,2},{4,5},{5,4},{6,7},{7,6},{8,9},{9,8},{10,11... | collective-permute-start | bytes 1572872 | tf_op jit(solution)/shard_map/ppermute | solution.py:369
  38.5 12.4 %collective-permute-start.2 = (bf16[384,384]{1,0:T(8,128)(2,1)}, bf16[384,384]{1,0:T(8,128)(2,1)}, u32[]{:S(2)}, u32[]{:S(2)}) collective-permute-start(bf16[384,384]{1,0:T(8,128)(2,1)} %get-tuple-element.50.refs_9_.refs_1_), channel_id=1, source_target_pairs={{0,128},{64,192},{128,0},{192,64},{1,129},{65,193},{129,1},{193,65... | collective-permute-start | bytes 884744 | tf_op jit(solution)/shard_map/ppermute | solution.py:369
  40.6 0.8 copy-start.14
  41.4 1.0 copy-start.3
  42.4 20.1 %copy-start.4 = (bf16[384,384]{1,0:T(8,128)(2,1)S(1)}, bf16[384,384]{1,0:T(8,128)(2,1)}, u32[]{:S(2)}) copy-start(bf16[384,384]{1,0:T(8,128)(2,1)} %get-tuple-element.50.refs_9_.refs_1_) | copy-start | bytes 884740
  47.5 14.9 %collective-permute-start.3 = (bf16[1568,128]{1,0:T(8,128)(2,1)S(1)}, bf16[1568,128]{1,0:T(8,128)(2,1)S(1)}, u32[]{:S(2)}, u32[]{:S(2)}) collective-permute-start(bf16[1568,128]{1,0:T(8,128)(2,1)S(1)} %get-tuple-element.53), channel_id=1, source_target_pairs={{0,64},{64,128},{128,192},{192,0},{1,65},{65,129},{129,193},{193,1... | collective-permute-start | bytes 1204232 | tf_op jit(solution)/shard_map/ppermute | solution.py:369
  48.4 14.0 %collective-permute-start.5 = (bf16[1568,128]{1,0:T(8,128)(2,1)S(1)}, bf16[1568,128]{1,0:T(8,128)(2,1)S(1)}, u32[]{:S(2)}, u32[]{:S(2)}) collective-permute-start(bf16[1568,128]{1,0:T(8,128)(2,1)S(1)} %get-tuple-element.55), channel_id=1, source_target_pairs={{0,192},{64,0},{128,64},{192,128},{1,193},{65,1},{129,65},{193,129... | collective-permute-start | bytes 1204232 | tf_op jit(solution)/shard_map/ppermute | solution.py:369
  50.9 11.4 %collective-permute-start.4 = (bf16[208,256]{1,0:T(8,128)(2,1)S(1)}, bf16[208,256]{1,0:T(8,128)(2,1)S(1)}, u32[]{:S(2)}, u32[]{:S(2)}) collective-permute-start(bf16[208,256]{1,0:T(8,128)(2,1)S(1)} %get-tuple-element.54), channel_id=1, source_target_pairs={{0,128},{64,192},{128,0},{192,64},{1,129},{65,193},{129,1},{193,65... | collective-permute-start | bytes 319496 | tf_op jit(solution)/shard_map/ppermute | solution.py:369
  51.3 30.7 %all-to-all-start.1 = ((bf16[128,4,384]{2,1,0:T(4,128)(2,1)}), bf16[128,4,384]{2,1,0:T(4,128)(2,1)}, u32[]{:S(2)}, u32[]{:S(2)}) async-start(bf16[128,4,384]{2,1,0:T(4,128)(2,1)} %get-tuple-element.43), calls=%async_computation.1 | async-start | bytes 786432 | tf_op jit(solution)/shard_map/all_to_all | solution.py:491
  64.3 22.3 %copy-start.2 = (s32[1,512]{1,0:T(1,128)S(1)}, s32[1,512]{1,0:T(1,128)}, u32[]{:S(2)}) copy-start(s32[1,512]{1,0:T(1,128)} %refs_0_.4) | copy-start | bytes 6148
  64.3 25.4 %copy-start = (f32[1024,384]{1,0:T(8,128)S(1)}, f32[1024,384]{1,0:T(8,128)}, u32[]{:S(2)}) copy-start(f32[1024,384]{1,0:T(8,128)} %refs_0_.5) | copy-start | bytes 4718596
  64.3 25.4 %copy-start.1 = (f32[1024]{0:T(1024)S(1)}, f32[1024]{0:T(1024)}, u32[]{:S(2)}) copy-start(f32[1024]{0:T(1024)} %param.12) | copy-start | bytes 12292
  64.3 8.8 %collective-permute-start.10 = (bf16[128,384]{1,0:T(8,128)(2,1)S(1)}, bf16[128,384]{1,0:T(8,128)(2,1)S(1)}, u32[]{:S(2)}, u32[]{:S(2)}) collective-permute-start(bf16[128,384]{1,0:T(8,128)(2,1)S(1)} %get-tuple-element.61.refs_5_), channel_id=1, source_target_pairs={{0,48},{16,0},{32,16},{48,32},{1,49},{17,1},{33,17},{49,33},{2,50}... | collective-permute-start | bytes 294920 | tf_op jit(solution)/shard_map/ppermute | solution.py:369
  69.0 10.5 %collective-permute-start.6 = (bf16[208,384]{1,0:T(8,128)(2,1)S(1)}, bf16[208,384]{1,0:T(8,128)(2,1)S(1)}, u32[]{:S(2)}, u32[]{:S(2)}) collective-permute-start(bf16[208,384]{1,0:T(8,128)(2,1)S(1)} %get-tuple-element.58), channel_id=1, source_target_pairs={{0,16},{16,32},{32,48},{48,0},{1,17},{17,33},{33,49},{49,1},{2,18}... | collective-permute-start | bytes 479240 | tf_op jit(solution)/shard_map/ppermute | solution.py:369
  69.0 10.5 %collective-permute-start.7 = (bf16[208,384]{1,0:T(8,128)(2,1)S(1)}, bf16[208,384]{1,0:T(8,128)(2,1)S(1)}, u32[]{:S(2)}, u32[]{:S(2)}) collective-permute-start(bf16[208,384]{1,0:T(8,128)(2,1)S(1)} %get-tuple-element.59), channel_id=1, source_target_pairs={{0,32},{16,48},{32,0},{48,16},{1,33},{17,49},{33,1},{49,17},{2,34}... | collective-permute-start | bytes 479240 | tf_op jit(solution)/shard_map/ppermute | solution.py:369
  71.1 8.6 %collective-permute-start.8 = (bf16[208,384]{1,0:T(8,128)(2,1)S(1)}, bf16[208,384]{1,0:T(8,128)(2,1)S(1)}, u32[]{:S(2)}, u32[]{:S(2)}) collective-permute-start(bf16[208,384]{1,0:T(8,128)(2,1)S(1)} %get-tuple-element.60), channel_id=1, source_target_pairs={{0,48},{16,0},{32,16},{48,32},{1,49},{17,1},{33,17},{49,33},{2,50}... | collective-permute-start | bytes 479240 | tf_op jit(solution)/shard_map/ppermute | solution.py:369
  71.1 8.4 %collective-permute-start.9 = (bf16[128,384]{1,0:T(8,128)(2,1)S(1)}, bf16[128,384]{1,0:T(8,128)(2,1)S(1)}, u32[]{:S(2)}, u32[]{:S(2)}) collective-permute-start(bf16[128,384]{1,0:T(8,128)(2,1)S(1)} %get-tuple-element.61.refs_5_), channel_id=1, source_target_pairs={{0,16},{16,32},{32,48},{48,0},{1,17},{17,33},{33,49},{49,1},{2,18}... | collective-permute-start | bytes 294920 | tf_op jit(solution)/shard_map/ppermute | solution.py:369
  73.2 7.7 %collective-permute-start.11 = (bf16[128,384]{1,0:T(8,128)(2,1)S(1)}, bf16[128,384]{1,0:T(8,128)(2,1)S(1)}, u32[]{:S(2)}, u32[]{:S(2)}) collective-permute-start(bf16[128,384]{1,0:T(8,128)(2,1)S(1)} %collective-permute-done.10.refs_8_), channel_id=1, source_target_pairs={{0,48},{16,0},{32,16},{48,32},{1,49},{17,1},{33,17},{49,33},{2,50}... | collective-permute-start | bytes 294920 | tf_op jit(solution)/shard_map/ppermute | solution.py:369
  81.9 17.8 %all-to-all-start.2 = ((bf16[8,8,2688]{2,1,0:T(8,128)(2,1)}), bf16[8,8,2688]{2,1,0:T(8,128)(2,1)S(1)}, u32[]{:S(2)}, u32[]{:S(2)}) async-start(bf16[8,8,2688]{2,1,0:T(8,128)(2,1)} %bitcast.7), calls=%async_computation.2 | async-start | bytes 688128 | tf_op jit(solution)/shard_map/all_to_all | solution.py:517
  88.5 1.2 %collective-permute-start.1 = (f32[8,128]{1,0:T(8,128)S(1)}, f32[8,128]{1,0:T(8,128)S(1)}, u32[]{:S(2)}, u32[]{:S(2)}) collective-permute-start(f32[8,128]{1,0:T(8,128)S(1)} %get-tuple-element.45.refs_3_), channel_id=1, source_target_pairs={{0,1},{1,0},{2,3},{3,2},{4,5},{5,4},{6,7},{7,6},{8,9},{9,8},{10,11... | collective-permute-start | bytes 12296 | tf_op jit(solution)/shard_map/ppermute | solution.py:369

commit v12 on v11

--- a/solution.py
+++ b/solution.py
@@ -98,7 +98,7 @@
 
 
 def is_near(distance, count):
-    return distance not in (0, count // 2)
+    return distance > count // 2
 
 
 def shaped(shape, dtype):
@@ -244,15 +244,17 @@
 
 
 def weight_kernel(count, place_ref, *refs):
-    layer_refs, pack_refs = refs[:2], refs[2 : 2 + count]
-    own_ref, second_ref, outs, total = refs[2 + count], refs[3 + count], refs[4 + count : -1], refs[-1]
+    early = count // 2 + 1
+    layer_refs, pack_refs = refs[:early], refs[early : early + count]
+    refs = refs[early + count :]
+    own_ref, second_ref, outs, total = refs[0], refs[1], refs[2:-1], refs[-1]
     pack_rows, width = pack_refs[0].shape
     layer_rows, columns = layer_refs[0].shape
     layer_parts, packs = [], []
     for d, ref in enumerate(pack_refs):
         if not is_near(d, count):
             packs.append(ref.get()[...])
-            layer_parts.append(layer_refs[min(d, 1)].get()[...])
+            layer_parts.append(layer_refs[d].get()[...])
             continue
         near, start = ref.get()[...], 0
         for rows, wide, made in ((pack_rows, width, packs), (layer_rows, columns, layer_parts)):
@@ -369,7 +371,7 @@
     return lax.ppermute(array, axis, [(i, (i + by) % size) for i in range(size)])
 
 
-LIMITS = {serve_kernel: 60, index_kernel: 60, first_kernel: 60, hidden_kernel: 51.5}
+LIMITS = {serve_kernel: 60, index_kernel: 60, first_kernel: 60, hidden_kernel: 60}
 COSTS = {update_kernel: 0, group_kernel: 0, row_kernel: 0}
 
 
@@ -457,7 +459,7 @@
         hbm_raw=(1,),
     )
     other_pre = shift(partial_pre, "col", 1)
-    layer_parts = [layer_in, shift(layer_in, "dp", n_x // 2)]
+    layer_parts = [layer_in] + [shift(layer_in, "dp", d) for d in range(1, n_x // 2 + 1)]
 
     pack_rows = nodes + half // width * SEED_ROWS + COT_ROWS
     pack_shape = (pack_rows, width)
@@ -499,7 +501,7 @@
         + [shaped((group_rows, columns), BF16)] * n_y,
         (y.reshape(1), *layer_parts, *packs),
         smem=1,
-        hbm_in=range(1, 3 + n_x),
+        hbm_in=range(1, 2 + n_x // 2 + n_x),
         scratch=[pltpu.VMEM((layers, width, columns), F32)],
     )
     seconds = [second, shift(second, "y", 1)]

time: 101 us -> 107 us (1.059)
  waiting for transfers between devices: 24.8 us -> 29.9 us
    ppermute x12 -> x13, waiting for transfers between devices: 8.54 us -> 13.9 us  [shift(): lax.ppermute(array, axis, [(i, (i + by) % size) for i in range(size)])]
    all_to_all x1, starting transfers between devices: 4.73 us -> 5.87 us  [body(): grads = lax.all_to_all(grads, 'z', split_axis=0, concat_axis=0, tiled=True)]
    ppermute x12 -> x13, starting transfers between devices: 16.3 us -> 15.5 us  [shift(): lax.ppermute(array, axis, [(i, (i + by) % size) for i in range(size)])]
  transfers between devices with their start and end apart: 15 -> 16, of which waited for: 9 -> 8; matrix products, arithmetic and copies ran while one was open for 1% -> 2% of each run, Pallas kernels for 18% -> 17%
where the time goes in v12:
time: 107 us
  starting transfers between devices  47.3 us (44%)
  waiting for transfers between devices  29.9 us (28%)
  Pallas kernels  25.1 us (23%)
  local copies, waits for them, and re-layouts  2.88 us (3%)
    pallas_call x9, Pallas kernels, call(): pl.pallas_call(wrapped, out_shape=tuple(outs), in_specs=specs, out_specs=...  25.1 us
    all_to_all x1, starting transfers between devices, body(): lax.all_to_all(outgoing, everyone, split_axis=0, concat_axis=0, tiled=True)  15.8 us
    ppermute x13, starting transfers between devices, shift(): lax.ppermute(array, axis, [(i, (i + by) % size) for i in range(size)])  15.5 us
    ppermute x13, waiting for transfers between devices, shift(): lax.ppermute(array, axis, [(i, (i + by) % size) for i in range(size)])  13.9 us
    all_to_all x1, starting transfers between devices, body(): lax.all_to_all(slot_grad, everyone, split_axis=0, concat_axis=0, tiled=True)  10.2 us
    all_to_all x1, waiting for transfers between devices, body(): grads = lax.all_to_all(grads, 'z', split_axis=0, concat_axis=0, tiled=True)  8.69 us
    all_to_all x1, waiting for transfers between devices, body(): lax.all_to_all(outgoing, everyone, split_axis=0, concat_axis=0, tiled=True)  7.29 us
    all_to_all x1, starting transfers between devices, body(): grads = lax.all_to_all(grads, 'z', split_axis=0, concat_axis=0, tiled=True)  5.87 us
  transfers between devices with their start and end apart: 16, of which 8 were waited for; matrix products, arithmetic and copies ran while one was open for 2% of the time, Pallas kernels for 17%

profile of v12, /device:TPU:8, one launch (start us, length us, event | category | flops | bytes accessed | tf_op | source)
XLA Modules:
  0.0 106.9 jit_solution(4713061130722156638)
XLA Ops:
  0.7 3.1 %shard_map.138 = bf16[128,4,384]{2,1,0:T(4,128)(2,1)} custom-call(s32[1,512]{1,0:T(1,128)} %refs_0_.4, f32[4,256,384]{2,1,0:T(8,128)} %bitcast.12), custom_call_target="tpu_custom_call" | custom-call | flops 999999995904 | bytes 1968128 | tf_op jit(solution)/shard_map/pallas_call | solution.py:89
  3.7 15.8 %all-to-all-start = ((bf16[128,4,384]{2,1,0:T(4,128)(2,1)}), bf16[128,4,384]{2,1,0:T(4,128)(2,1)}, u32[]{:S(2)}, u32[]{:S(2)}) async-start(bf16[128,4,384]{2,1,0:T(4,128)(2,1)} %shard_map.138), calls=%async_computation | async-start | bytes 786432 | tf_op jit(solution)/shard_map/all_to_all | solution.py:419
  19.5 0.1 reshape.32
  19.6 0.1 copy.32
  19.7 0.1 pad_add_fusion
  19.8 0.1 copy.33
  19.9 0.1 reshape.34
  20.0 0.1 reshape.33
  20.1 0.6 pad_add_fusion.1.refs_0_
  20.7 0.1 add_add_fusion
  20.7 0.7 copy.34.refs_0_
  21.5 6.3 %shard_map.139 = (bf16[384,512]{1,0:T(8,128)(2,1)}, bf16[512,384]{1,0:T(8,128)(2,1)}, f32[384,128]{1,0:T(8,128)}, bf16[32,128]{1,0:T(8,128)(2,1)}, f32[128,1024]{1,0:T(8,128)}) custom-call(s32[128,17]{1,0:T(8,128)} %copy.34.refs_0_, bf16[8,1024]{1,0:T(8,128)(2,1)} %refs_6_.1, bf16[3,1024,1024]{2,1,0:T(8,128)(2,1)} %refs_2_.2), custom_call_target="tpu_custom_call" | custom-call | flops 999999995904 | bytes 7832064 | tf_op jit(solution)/shard_map/pallas_call | solution.py:89
  27.8 7.3 %all-to-all-done.refs_0_ = bf16[128,4,384]{2,1,0:T(4,128)(2,1)} async-done(((bf16[128,4,384]{2,1,0:T(4,128)(2,1)}), bf16[128,4,384]{2,1,0:T(4,128)(2,1)}, u32[]{:S(2)}, u32[]{:S(2)}) %all-to-all-start) | async-done | bytes 393248 | tf_op jit(solution)/shard_map/all_to_all | solution.py:419
  35.1 3.2 %shard_map.140 = (bf16[384,384]{1,0:T(8,128)(2,1)}, f32[128,1024]{1,0:T(8,128)}) custom-call(bf16[128,4,384]{2,1,0:T(4,128)(2,1)} %all-to-all-done.refs_0_, bf16[384,512]{1,0:T(8,128)(2,1)} %get-tuple-element.37.refs_1_, bf16[3,384,1024]{2,1,0:T(8,128)(2,1)} %refs_8_.1), custom_call_target="tpu_custom_call" | custom-call | flops 999999995904 | bytes 3964928 | tf_op jit(solution)/shard_map/pallas_call | solution.py:89
  38.3 0.1 collective-permute-start
  38.4 0.9 collective-permute-start.2
  39.3 1.6 %collective-permute-start.3 = (bf16[384,384]{1,0:T(8,128)(2,1)}, bf16[384,384]{1,0:T(8,128)(2,1)}, u32[]{:S(2)}, u32[]{:S(2)}) collective-permute-start(bf16[384,384]{1,0:T(8,128)(2,1)} %get-tuple-element.51.refs_9_.refs_1_), channel_id=1, source_target_pairs={{0,128},{64,192},{128,0},{192,64},{1,129},{65,193},{129,1},{193,65... | collective-permute-start | bytes 884744 | tf_op jit(solution)/shard_map/ppermute | solution.py:371
  40.9 0.0 collective-permute-done.refs_2_
  40.9 0.8 copy-done.10
  41.7 5.5 %shard_map.141 = (bf16[128,4,384]{2,1,0:T(4,128)(2,1)}, bf16[208,256]{1,0:T(8,128)(2,1)}, bf16[208,256]{1,0:T(8,128)(2,1)}, bf16[208,256]{1,0:T(8,128)(2,1)}, bf16[1568,128]{1,0:T(8,128)(2,1)}) custom-call(s32[2]{0:T(128)} %pad_add_fusion.1.refs_0_, f32[128,1024]{1,0:T(8,128)} %get-tuple-element.38.refs_1_, f32[128,1024]{1,0:T(8,128)} %copy-done.10, ...), custom_call_target="tpu_custom_call" | custom-call | flops 999999995904 | bytes 5955592 | tf_op jit(solution)/shard_map/pallas_call | solution.py:89
  47.2 1.8 %collective-permute-start.6 = (bf16[1568,128]{1,0:T(8,128)(2,1)}, bf16[1568,128]{1,0:T(8,128)(2,1)S(1)}, u32[]{:S(2)}, u32[]{:S(2)}) collective-permute-start(bf16[1568,128]{1,0:T(8,128)(2,1)} %get-tuple-element.57), channel_id=1, source_target_pairs={{0,192},{64,0},{128,64},{192,128},{1,193},{65,1},{129,65},{193,129... | collective-permute-start | bytes 1204232 | tf_op jit(solution)/shard_map/ppermute | solution.py:371
  49.0 6.6 %collective-permute-done.2.refs_2_ = bf16[384,384]{1,0:T(8,128)(2,1)} collective-permute-done((bf16[384,384]{1,0:T(8,128)(2,1)}, bf16[384,384]{1,0:T(8,128)(2,1)}, u32[]{:S(2)}, u32[]{:S(2)}) %collective-permute-start.2) | collective-permute-done | bytes 294944 | tf_op jit(solution)/shard_map/ppermute | solution.py:371
  55.7 0.0 collective-permute-done.3.refs_3_
  55.7 1.1 %collective-permute-start.5 = (bf16[208,256]{1,0:T(8,128)(2,1)}, bf16[208,256]{1,0:T(8,128)(2,1)S(1)}, u32[]{:S(2)}, u32[]{:S(2)}) collective-permute-start(bf16[208,256]{1,0:T(8,128)(2,1)} %get-tuple-element.56), channel_id=1, source_target_pairs={{0,128},{64,192},{128,0},{192,64},{1,129},{65,193},{129,1},{193,65... | collective-permute-start | bytes 319496 | tf_op jit(solution)/shard_map/ppermute | solution.py:371
  56.7 10.2 %all-to-all-start.1 = ((bf16[128,4,384]{2,1,0:T(4,128)(2,1)}), bf16[128,4,384]{2,1,0:T(4,128)(2,1)}, u32[]{:S(2)}, u32[]{:S(2)}) async-start(bf16[128,4,384]{2,1,0:T(4,128)(2,1)} %get-tuple-element.44), calls=%async_computation.1 | async-start | bytes 786432 | tf_op jit(solution)/shard_map/all_to_all | solution.py:493
  67.0 0.9 copy-done.4
  67.9 1.9 %shard_map.144 = (f32[64,1152]{1,0:T(8,128)S(1)}, bf16[128,384]{1,0:T(8,128)(2,1)S(1)}, bf16[208,384]{1,0:T(8,128)(2,1)S(1)}, bf16[208,384]{1,0:T(8,128)(2,1)S(1...) custom-call(s32[1]{0:T(128)} %bitcast.6.refs_0_, bf16[384,384]{1,0:T(8,128)(2,1)S(1)} %copy-done.3, ...), custom_call_target="tpu_custom_call" | custom-call | flops 999999995904 | bytes 2637828 | tf_op jit(solution)/shard_map/pallas_call | solution.py:89
  69.9 0.0 copy-start.2
  69.9 0.0 copy-start
  69.9 0.0 copy-start.1
  69.9 1.0 collective-permute-start.11
  70.9 1.1 %collective-permute-start.7 = (bf16[208,384]{1,0:T(8,128)(2,1)S(1)}, bf16[208,384]{1,0:T(8,128)(2,1)S(1)}, u32[]{:S(2)}, u32[]{:S(2)}) collective-permute-start(bf16[208,384]{1,0:T(8,128)(2,1)S(1)} %get-tuple-element.60), channel_id=1, source_target_pairs={{0,16},{16,32},{32,48},{48,0},{1,17},{17,33},{33,49},{49,1},{2,18}... | collective-permute-start | bytes 479240 | tf_op jit(solution)/shard_map/ppermute | solution.py:371
  72.0 3.3 %collective-permute-start.8 = (bf16[208,384]{1,0:T(8,128)(2,1)S(1)}, bf16[208,384]{1,0:T(8,128)(2,1)S(1)}, u32[]{:S(2)}, u32[]{:S(2)}) collective-permute-start(bf16[208,384]{1,0:T(8,128)(2,1)S(1)} %get-tuple-element.61), channel_id=1, source_target_pairs={{0,32},{16,48},{32,0},{48,16},{1,33},{17,49},{33,1},{49,17},{2,34}... | collective-permute-start | bytes 479240 | tf_op jit(solution)/shard_map/ppermute | solution.py:371
  75.3 0.2 collective-permute-start.9
  75.5 1.8 %collective-permute-start.10 = (bf16[128,384]{1,0:T(8,128)(2,1)S(1)}, bf16[128,384]{1,0:T(8,128)(2,1)S(1)}, u32[]{:S(2)}, u32[]{:S(2)}) collective-permute-start(bf16[128,384]{1,0:T(8,128)(2,1)S(1)} %get-tuple-element.63.refs_5_), channel_id=1, source_target_pairs={{0,16},{16,32},{32,48},{48,0},{1,17},{17,33},{33,49},{49,1},{2,18}... | collective-permute-start | bytes 294920 | tf_op jit(solution)/shard_map/ppermute | solution.py:371
  77.3 0.4 collective-permute-done.11.refs_8_
  77.8 2.5 %collective-permute-start.12 = (bf16[128,384]{1,0:T(8,128)(2,1)S(1)}, bf16[128,384]{1,0:T(8,128)(2,1)S(1)}, u32[]{:S(2)}, u32[]{:S(2)}) collective-permute-start(bf16[128,384]{1,0:T(8,128)(2,1)S(1)} %collective-permute-done.11.refs_8_), channel_id=1, source_target_pairs={{0,48},{16,0},{32,16},{48,32},{1,49},{17,1},{33,17},{49,33},{2,50}... | collective-permute-start | bytes 294920 | tf_op jit(solution)/shard_map/ppermute | solution.py:371
  80.2 3.5 %collective-permute-done.10.refs_6_ = bf16[128,384]{1,0:T(8,128)(2,1)S(1)} collective-permute-done((bf16[128,384]{1,0:T(8,128)(2,1)S(1)}, bf16[128,384]{1,0:T(8,128)(2,1)S(1)}, u32[]{:S(2)}, u32[]{:S(2)}) %collective-permute-start.10) | collective-permute-done | bytes 98336 | tf_op jit(solution)/shard_map/ppermute | solution.py:371
  83.8 0.6 collective-permute-done.9.refs_4_
  84.4 1.5 %collective-permute-done.12.refs_7_ = bf16[128,384]{1,0:T(8,128)(2,1)S(1)} collective-permute-done((bf16[128,384]{1,0:T(8,128)(2,1)S(1)}, bf16[128,384]{1,0:T(8,128)(2,1)S(1)}, u32[]{:S(2)}, u32[]{:S(2)}) %collective-permute-start.12) | collective-permute-done | bytes 98336 | tf_op jit(solution)/shard_map/ppermute | solution.py:371
  86.0 1.0 shard_map.145
  87.0 5.9 %all-to-all-start.2 = ((bf16[8,8,2688]{2,1,0:T(8,128)(2,1)}), bf16[8,8,2688]{2,1,0:T(8,128)(2,1)S(1)}, u32[]{:S(2)}, u32[]{:S(2)}) async-start(bf16[8,8,2688]{2,1,0:T(8,128)(2,1)} %bitcast.7), calls=%async_computation.2 | async-start | bytes 688128 | tf_op jit(solution)/shard_map/all_to_all | solution.py:519
  92.9 1.8 %shard_map.142 = (f32[1024,384]{1,0:T(8,128)S(1)}, f32[8,128]{1,0:T(8,128)S(1)}) custom-call(s32[1,512]{1,0:T(1,128)S(1)} %copy-done.2, bf16[128,4,384]{2,1,0:T(4,128)(2,1)} %all-to-all-done.1.refs_1_), custom_call_target="tpu_custom_call" | custom-call | bytes 1972224 | tf_op jit(solution)/shard_map/pallas_call | solution.py:89
  94.7 0.1 collective-permute-start.1
  94.8 1.2 %collective-permute-done.1.refs_4_ = f32[8,128]{1,0:T(8,128)S(1)} collective-permute-done((f32[8,128]{1,0:T(8,128)S(1)}, f32[8,128]{1,0:T(8,128)S(1)}, u32[]{:S(2)}, u32[]{:S(2)}) %collective-permute-start.1) | collective-permute-done | bytes 4128 | tf_op jit(solution)/shard_map/ppermute | solution.py:371
  96.0 1.6 %shard_map.143 = (f32[1024,384]{1,0:T(8,128)}, f32[8,128]{1,0:T(8,128)}) custom-call(f32[1024,384]{1,0:T(8,128)S(1)} %copy-done, f32[1024,384]{1,0:T(8,128)S(1)} %get-tuple-element.45.refs_1_, f32[8,128]{1,0:T(8,128)S(1)} %bitcast.13, f32[8,128]{1,0:T(8,128)S(1)} %get-tuple-element.46.refs_3_, f32[8,128]{1,0:T(8,128)S(1)} %collective-permute-done.1.refs_4_), custom_call_target="tpu_custom_call" | custom-call | bytes 4734976 | tf_op jit(solution)/shard_map/pallas_call | solution.py:89
  97.5 8.7 %all-to-all-done.2.refs_0_ = bf16[8,8,2688]{2,1,0:T(8,128)(2,1)S(1)} async-done(((bf16[8,8,2688]{2,1,0:T(8,128)(2,1)}), bf16[8,8,2688]{2,1,0:T(8,128)(2,1)S(1)}, u32[]{:S(2)}, u32[]{:S(2)}) %all-to-all-start.2) | async-done | bytes 344096 | tf_op jit(solution)/shard_map/all_to_all | solution.py:519
  106.2 0.7 shard_map.146
  (28 shorter events, 0.1 us)
Async XLA Ops:
  0.6 18.9 %copy-start.7 = (s32[8,15]{1,0:T(8,128)S(1)}, s32[8,15]{1,0:T(8,128)}, u32[]{:S(2)}) copy-start(s32[8,15]{1,0:T(8,128)} %param.15) | copy-start | bytes 1444
  0.6 19.0 %copy-start.8 = (s32[8,15]{1,0:T(8,128)S(1)}, s32[8,15]{1,0:T(8,128)}, u32[]{:S(2)}) copy-start(s32[8,15]{1,0:T(8,128)} %param.17) | copy-start | bytes 1444
  0.7 19.0 %copy-start.9 = (s32[8]{0:T(128)S(1)}, s32[8]{0:T(128)}, u32[]{:S(2)}) copy-start(s32[8]{0:T(128)} %param.14) | copy-start | bytes 100
  0.7 19.3 %copy-start.5 = (s32[8,15,10]{1,0,2:T(8,128)S(1)}, s32[8,15,10]{1,0,2:T(8,128)}, u32[]{:S(2)}) copy-start(s32[8,15,10]{1,0,2:T(8,128)} %param.16) | copy-start | bytes 14404
  0.7 19.3 %copy-start.6 = (s32[8,15,10]{1,0,2:T(8,128)S(1)}, s32[8,15,10]{1,0,2:T(8,128)}, u32[]{:S(2)}) copy-start(s32[8,15,10]{1,0,2:T(8,128)} %param.18) | copy-start | bytes 14404
  3.7 31.3 %all-to-all-start = ((bf16[128,4,384]{2,1,0:T(4,128)(2,1)}), bf16[128,4,384]{2,1,0:T(4,128)(2,1)}, u32[]{:S(2)}, u32[]{:S(2)}) async-start(bf16[128,4,384]{2,1,0:T(4,128)(2,1)} %shard_map.138), calls=%async_computation | async-start | bytes 786432 | tf_op jit(solution)/shard_map/all_to_all | solution.py:419
  38.3 2.6 %collective-permute-start = (f32[128,1024]{1,0:T(8,128)}, f32[128,1024]{1,0:T(8,128)S(1)}, u32[]{:S(2)}, u32[]{:S(2)}) collective-permute-start(f32[128,1024]{1,0:T(8,128)} %get-tuple-element.38.refs_1_), channel_id=1, source_target_pairs={{0,1},{1,0},{2,3},{3,2},{4,5},{5,4},{6,7},{7,6},{8,9},{9,8},{10,11... | collective-permute-start | bytes 1572872 | tf_op jit(solution)/shard_map/ppermute | solution.py:371
  38.4 17.3 %collective-permute-start.2 = (bf16[384,384]{1,0:T(8,128)(2,1)}, bf16[384,384]{1,0:T(8,128)(2,1)}, u32[]{:S(2)}, u32[]{:S(2)}) collective-permute-start(bf16[384,384]{1,0:T(8,128)(2,1)} %get-tuple-element.51.refs_9_.refs_1_), channel_id=1, source_target_pairs={{0,64},{64,128},{128,192},{192,0},{1,65},{65,129},{129,193},{193,1... | collective-permute-start | bytes 884744 | tf_op jit(solution)/shard_map/ppermute | solution.py:371
  39.3 16.4 %collective-permute-start.3 = (bf16[384,384]{1,0:T(8,128)(2,1)}, bf16[384,384]{1,0:T(8,128)(2,1)}, u32[]{:S(2)}, u32[]{:S(2)}) collective-permute-start(bf16[384,384]{1,0:T(8,128)(2,1)} %get-tuple-element.51.refs_9_.refs_1_), channel_id=1, source_target_pairs={{0,128},{64,192},{128,0},{192,64},{1,129},{65,193},{129,1},{193,65... | collective-permute-start | bytes 884744 | tf_op jit(solution)/shard_map/ppermute | solution.py:371
  40.9 0.8 copy-start.10
  41.7 25.3 %copy-start.3 = (bf16[384,384]{1,0:T(8,128)(2,1)S(1)}, bf16[384,384]{1,0:T(8,128)(2,1)}, u32[]{:S(2)}) copy-start(bf16[384,384]{1,0:T(8,128)(2,1)} %get-tuple-element.51.refs_9_.refs_1_) | copy-start | bytes 884740
  47.2 19.8 %collective-permute-start.6 = (bf16[1568,128]{1,0:T(8,128)(2,1)}, bf16[1568,128]{1,0:T(8,128)(2,1)S(1)}, u32[]{:S(2)}, u32[]{:S(2)}) collective-permute-start(bf16[1568,128]{1,0:T(8,128)(2,1)} %get-tuple-element.57), channel_id=1, source_target_pairs={{0,192},{64,0},{128,64},{192,128},{1,193},{65,1},{129,65},{193,129... | collective-permute-start | bytes 1204232 | tf_op jit(solution)/shard_map/ppermute | solution.py:371
  55.7 11.3 %collective-permute-start.5 = (bf16[208,256]{1,0:T(8,128)(2,1)}, bf16[208,256]{1,0:T(8,128)(2,1)S(1)}, u32[]{:S(2)}, u32[]{:S(2)}) collective-permute-start(bf16[208,256]{1,0:T(8,128)(2,1)} %get-tuple-element.56), channel_id=1, source_target_pairs={{0,128},{64,192},{128,0},{192,64},{1,129},{65,193},{129,1},{193,65... | collective-permute-start | bytes 319496 | tf_op jit(solution)/shard_map/ppermute | solution.py:371
  56.7 10.2 %collective-permute-start.4 = (bf16[208,256]{1,0:T(8,128)(2,1)}, bf16[208,256]{1,0:T(8,128)(2,1)S(1)}, u32[]{:S(2)}, u32[]{:S(2)}) collective-permute-start(bf16[208,256]{1,0:T(8,128)(2,1)} %get-tuple-element.55), channel_id=1, source_target_pairs={{0,64},{64,128},{128,192},{192,0},{1,65},{65,129},{129,193},{193,1... | collective-permute-start | bytes 319496 | tf_op jit(solution)/shard_map/ppermute | solution.py:371
  56.7 30.3 %all-to-all-start.1 = ((bf16[128,4,384]{2,1,0:T(4,128)(2,1)}), bf16[128,4,384]{2,1,0:T(4,128)(2,1)}, u32[]{:S(2)}, u32[]{:S(2)}) async-start(bf16[128,4,384]{2,1,0:T(4,128)(2,1)} %get-tuple-element.44), calls=%async_computation.1 | async-start | bytes 786432 | tf_op jit(solution)/shard_map/all_to_all | solution.py:493
  67.0 0.9 copy-start.4
  69.9 23.0 %copy-start.2 = (s32[1,512]{1,0:T(1,128)S(1)}, s32[1,512]{1,0:T(1,128)}, u32[]{:S(2)}) copy-start(s32[1,512]{1,0:T(1,128)} %refs_0_.4) | copy-start | bytes 6148
  69.9 26.1 %copy-start = (f32[1024,384]{1,0:T(8,128)S(1)}, f32[1024,384]{1,0:T(8,128)}, u32[]{:S(2)}) copy-start(f32[1024,384]{1,0:T(8,128)} %refs_0_.5) | copy-start | bytes 4718596
  69.9 26.1 %copy-start.1 = (f32[1024]{0:T(1024)S(1)}, f32[1024]{0:T(1024)}, u32[]{:S(2)}) copy-start(f32[1024]{0:T(1024)} %param.12) | copy-start | bytes 12292
  69.9 7.9 %collective-permute-start.11 = (bf16[128,384]{1,0:T(8,128)(2,1)S(1)}, bf16[128,384]{1,0:T(8,128)(2,1)S(1)}, u32[]{:S(2)}, u32[]{:S(2)}) collective-permute-start(bf16[128,384]{1,0:T(8,128)(2,1)S(1)} %get-tuple-element.63.refs_5_), channel_id=1, source_target_pairs={{0,48},{16,0},{32,16},{48,32},{1,49},{17,1},{33,17},{49,33},{2,50}... | collective-permute-start | bytes 294920 | tf_op jit(solution)/shard_map/ppermute | solution.py:371
  70.9 12.9 %collective-permute-start.7 = (bf16[208,384]{1,0:T(8,128)(2,1)S(1)}, bf16[208,384]{1,0:T(8,128)(2,1)S(1)}, u32[]{:S(2)}, u32[]{:S(2)}) collective-permute-start(bf16[208,384]{1,0:T(8,128)(2,1)S(1)} %get-tuple-element.60), channel_id=1, source_target_pairs={{0,16},{16,32},{32,48},{48,0},{1,17},{17,33},{33,49},{49,1},{2,18}... | collective-permute-start | bytes 479240 | tf_op jit(solution)/shard_map/ppermute | solution.py:371
  72.0 11.8 %collective-permute-start.8 = (bf16[208,384]{1,0:T(8,128)(2,1)S(1)}, bf16[208,384]{1,0:T(8,128)(2,1)S(1)}, u32[]{:S(2)}, u32[]{:S(2)}) collective-permute-start(bf16[208,384]{1,0:T(8,128)(2,1)S(1)} %get-tuple-element.61), channel_id=1, source_target_pairs={{0,32},{16,48},{32,0},{48,16},{1,33},{17,49},{33,1},{49,17},{2,34}... | collective-permute-start | bytes 479240 | tf_op jit(solution)/shard_map/ppermute | solution.py:371
  75.3 9.1 %collective-permute-start.9 = (bf16[208,384]{1,0:T(8,128)(2,1)S(1)}, bf16[208,384]{1,0:T(8,128)(2,1)S(1)}, u32[]{:S(2)}, u32[]{:S(2)}) collective-permute-start(bf16[208,384]{1,0:T(8,128)(2,1)S(1)} %get-tuple-element.62), channel_id=1, source_target_pairs={{0,48},{16,0},{32,16},{48,32},{1,49},{17,1},{33,17},{49,33},{2,50}... | collective-permute-start | bytes 479240 | tf_op jit(solution)/shard_map/ppermute | solution.py:371
  75.5 8.2 %collective-permute-start.10 = (bf16[128,384]{1,0:T(8,128)(2,1)S(1)}, bf16[128,384]{1,0:T(8,128)(2,1)S(1)}, u32[]{:S(2)}, u32[]{:S(2)}) collective-permute-start(bf16[128,384]{1,0:T(8,128)(2,1)S(1)} %get-tuple-element.63.refs_5_), channel_id=1, source_target_pairs={{0,16},{16,32},{32,48},{48,0},{1,17},{17,33},{33,49},{49,1},{2,18}... | collective-permute-start | bytes 294920 | tf_op jit(solution)/shard_map/ppermute | solution.py:371
  77.8 8.2 %collective-permute-start.12 = (bf16[128,384]{1,0:T(8,128)(2,1)S(1)}, bf16[128,384]{1,0:T(8,128)(2,1)S(1)}, u32[]{:S(2)}, u32[]{:S(2)}) collective-permute-start(bf16[128,384]{1,0:T(8,128)(2,1)S(1)} %collective-permute-done.11.refs_8_), channel_id=1, source_target_pairs={{0,48},{16,0},{32,16},{48,32},{1,49},{17,1},{33,17},{49,33},{2,50}... | collective-permute-start | bytes 294920 | tf_op jit(solution)/shard_map/ppermute | solution.py:371
  87.0 19.2 %all-to-all-start.2 = ((bf16[8,8,2688]{2,1,0:T(8,128)(2,1)}), bf16[8,8,2688]{2,1,0:T(8,128)(2,1)S(1)}, u32[]{:S(2)}, u32[]{:S(2)}) async-start(bf16[8,8,2688]{2,1,0:T(8,128)(2,1)} %bitcast.7), calls=%async_computation.2 | async-start | bytes 688128 | tf_op jit(solution)/shard_map/all_to_all | solution.py:519
  94.7 1.2 %collective-permute-start.1 = (f32[8,128]{1,0:T(8,128)S(1)}, f32[8,128]{1,0:T(8,128)S(1)}, u32[]{:S(2)}, u32[]{:S(2)}) collective-permute-start(f32[8,128]{1,0:T(8,128)S(1)} %get-tuple-element.46.refs_3_), channel_id=1, source_target_pairs={{0,1},{1,0},{2,3},{3,2},{4,5},{5,4},{6,7},{7,6},{8,9},{9,8},{10,11... | collective-permute-start | bytes 12296 | tf_op jit(solution)/shard_map/ppermute | solution.py:371

commit v13 on v11

--- a/solution.py
+++ b/solution.py
@@ -187,8 +187,8 @@
         copy.wait()
 
 
-def hidden_kernel(place_ref, mine_ref, other_ref, back_ref, e_ref, inv_ref, cot_ref, c_ref, w1_ref, layer_ref, slot_ref, *refs):
-    packs, (stage, scaled, sems) = refs[:-3], refs[-3:]
+def hidden_kernel(place_ref, mine_ref, other_ref, back_ref, e_ref, inv_ref, cot_ref, layer_ref, out_ref, *refs):
+    packs, (stage, sems) = refs[:-2], refs[-2:]
     nodes = mine_ref.shape[0]
     width = stage.shape[2]
     seeds = cot_ref.shape[0]
@@ -199,6 +199,7 @@
     hidden = (values * sigma).astype(BF16)
     slope = sigma * (1.0 + values * (1.0 - sigma))
     back = (back_ref[...] * slope).astype(BF16)
+    out_ref[...] = back
     scale = jnp.concatenate(
         [inv_ref[k * nodes : k * nodes + seeds, 0:1] for k in range(layers)]
         + [jnp.zeros((SEED_ROWS - layers * seeds, 1), F32)],
@@ -233,14 +234,18 @@
     copies = [pltpu.make_async_copy(source, target, sems.at[i]) for i, (source, target) in enumerate(moves)]
     for copy in copies:
         copy.start()
-    columns = w1_ref.shape[1]
-    back_in = matmul(back, w1_ref.get()[...].reshape(layers * columns, back.shape[1]), (1, 1))
+    for copy in copies:
+        copy.wait()
+
+
+def slot_kernel(back_ref, inv_ref, c_ref, w1_ref, slot_ref, scaled):
+    layers, columns, hidden = w1_ref.shape
+    nodes = back_ref.shape[0]
+    back_in = matmul(back_ref.get()[...], w1_ref.get()[...].reshape(layers * columns, hidden), (1, 1))
     for k in range(layers):
         span = slice(k * nodes, (k + 1) * nodes)
-        scaled[span, :] = (back_in[:, k * columns : (k + 1) * columns] * inv_ref[span, 0:1]).astype(BF16)
+        scaled[span, :] = (back_in[:, k * columns : (k + 1) * columns] * inv_ref.get()[span, 0:1]).astype(BF16)
     slot_ref[...] = matmul(c_ref.get()[...], scaled[...]).astype(BF16).reshape(slot_ref.shape)
-    for copy in copies:
-        copy.wait()
 
 
 def weight_kernel(count, place_ref, *refs):
@@ -369,7 +374,7 @@
     return lax.ppermute(array, axis, [(i, (i + by) % size) for i in range(size)])
 
 
-LIMITS = {serve_kernel: 60, index_kernel: 60, first_kernel: 60, hidden_kernel: 51.5}
+LIMITS = {serve_kernel: 60, index_kernel: 60, first_kernel: 60, hidden_kernel: 60, slot_kernel: 60}
 COSTS = {update_kernel: 0, group_kernel: 0, row_kernel: 0}
 
 
@@ -462,9 +467,9 @@
     pack_rows = nodes + half // width * SEED_ROWS + COT_ROWS
     pack_shape = (pack_rows, width)
     near_shape = ((pack_rows * width + layers * nodes * columns) // LANES, LANES)
-    slot_grad, *packs = call(
+    back, *packs = call(
         hidden_kernel,
-        [shaped(blocks_shape, BF16)] + [shaped(near_shape if is_near(d, n_x) else pack_shape, BF16) for d in range(n_x)],
+        [shaped((nodes, hidden_units), BF16)] + [shaped(near_shape if is_near(d, n_x) else pack_shape, BF16) for d in range(n_x)],
         (
             place,
             partial_pre,
@@ -473,21 +478,25 @@
             member,
             inverse,
             cotangent,
-            c,
-            w_first,
             layer_in,
         ),
         smem=1,
         scratch=[
             pltpu.VMEM((n_x, *pack_shape), BF16),
-            pltpu.VMEM((layers * nodes, columns), BF16),
             pltpu.SemaphoreType.DMA((n_x * (width + columns) // LANES,)),
         ],
-        hbm_in=(1, 2, 3, 4, 5, 9, 8, 7),
+        hbm_in=(1, 2, 3, 4, 5, 7),
         hbm_raw=range(1, 1 + n_x),
     )
-    packs[n_x // 2], layer_parts = lax.optimization_barrier((packs[n_x // 2], layer_parts))
     packs = [packs[0]] + [shift(packs[d], "dp", d) for d in range(1, n_x)]
+    slot_grad = call(
+        slot_kernel,
+        [shaped(blocks_shape, BF16)],
+        (back, inverse, c, w_first),
+        scratch=[pltpu.VMEM((layers * nodes, columns), BF16)],
+        hbm_in=(0, 3, 1, 2),
+    )[0]
+    slot_grad, layer_parts = lax.optimization_barrier((slot_grad, layer_parts))
     arrived = lax.all_to_all(slot_grad, everyone, split_axis=0, concat_axis=0, tiled=True)
 
     block_rows = width // n_y

time: 101 us -> 103 us (1.020)
  Pallas kernels: 24.8 us -> 28.4 us
    pallas_call x9 -> x10, Pallas kernels: 24.8 us -> 28.4 us  [call(): pl.pallas_call(wrapped, out_shape=tuple(outs), in_specs=specs, out_specs=...]
    all_to_all x1, starting transfers between devices: 4.73 us -> 5.81 us  [body(): grads = lax.all_to_all(grads, 'z', split_axis=0, concat_axis=0, tiled=True)]
  transfers between devices with their start and end apart: 15 -> 15, of which waited for: 9 -> 8; matrix products, arithmetic and copies ran while one was open for 1% -> 2% of each run, Pallas kernels for 18% -> 21%
where the time goes in v13:
time: 103 us
  starting transfers between devices  46.9 us (46%)
  Pallas kernels  28.4 us (28%)
  waiting for transfers between devices  24 us (23%)
  local copies, waits for them, and re-layouts  2.02 us (2%)
    pallas_call x10, Pallas kernels, call(): pl.pallas_call(wrapped, out_shape=tuple(outs), in_specs=specs, out_specs=...  28.4 us
    all_to_all x1, starting transfers between devices, body(): lax.all_to_all(outgoing, everyone, split_axis=0, concat_axis=0, tiled=True)  15.8 us
    ppermute x12, starting transfers between devices, shift(): lax.ppermute(array, axis, [(i, (i + by) % size) for i in range(size)])  15.4 us
    all_to_all x1, starting transfers between devices, body(): lax.all_to_all(slot_grad, everyone, split_axis=0, concat_axis=0, tiled=True)  10 us
    all_to_all x1, waiting for transfers between devices, body(): grads = lax.all_to_all(grads, 'z', split_axis=0, concat_axis=0, tiled=True)  8.51 us
    ppermute x12, waiting for transfers between devices, shift(): lax.ppermute(array, axis, [(i, (i + by) % size) for i in range(size)])  8.19 us
    all_to_all x1, waiting for transfers between devices, body(): lax.all_to_all(outgoing, everyone, split_axis=0, concat_axis=0, tiled=True)  7.27 us
    all_to_all x1, starting transfers between devices, body(): grads = lax.all_to_all(grads, 'z', split_axis=0, concat_axis=0, tiled=True)  5.81 us
  transfers between devices with their start and end apart: 15, of which 8 were waited for; matrix products, arithmetic and copies ran while one was open for 2% of the time, Pallas kernels for 21%

profile of v13, /device:TPU:8, one launch (start us, length us, event | category | flops | bytes accessed | tf_op | source)
XLA Modules:
  0.0 102.9 jit_solution(13855686897515483825)
XLA Ops:
  0.7 3.1 %shard_map.138 = bf16[128,4,384]{2,1,0:T(4,128)(2,1)} custom-call(s32[1,512]{1,0:T(1,128)} %refs_0_.4, f32[4,256,384]{2,1,0:T(8,128)} %bitcast.12), custom_call_target="tpu_custom_call" | custom-call | flops 999999995904 | bytes 1968128 | tf_op jit(solution)/shard_map/pallas_call | solution.py:89
  3.7 15.8 %all-to-all-start = ((bf16[128,4,384]{2,1,0:T(4,128)(2,1)}), bf16[128,4,384]{2,1,0:T(4,128)(2,1)}, u32[]{:S(2)}, u32[]{:S(2)}) async-start(bf16[128,4,384]{2,1,0:T(4,128)(2,1)} %shard_map.138), calls=%async_computation | async-start | bytes 786432 | tf_op jit(solution)/shard_map/all_to_all | solution.py:422
  19.5 0.1 reshape.32
  19.6 0.1 copy.32
  19.7 0.1 pad_add_fusion
  19.8 0.1 copy.33
  19.9 0.1 reshape.34
  20.0 0.1 reshape.33
  20.1 0.6 pad_add_fusion.1.refs_0_
  20.7 0.1 add_add_fusion
  20.7 0.7 copy.34.refs_0_
  21.5 6.3 %shard_map.139 = (bf16[384,512]{1,0:T(8,128)(2,1)}, bf16[512,384]{1,0:T(8,128)(2,1)}, f32[384,128]{1,0:T(8,128)}, bf16[32,128]{1,0:T(8,128)(2,1)}, f32[128,1024]{1,0:T(8,128)}) custom-call(s32[128,17]{1,0:T(8,128)} %copy.34.refs_0_, bf16[8,1024]{1,0:T(8,128)(2,1)} %refs_6_.1, bf16[3,1024,1024]{2,1,0:T(8,128)(2,1)} %refs_2_.2), custom_call_target="tpu_custom_call" | custom-call | flops 999999995904 | bytes 7832064 | tf_op jit(solution)/shard_map/pallas_call | solution.py:89
  27.8 7.3 %all-to-all-done.refs_0_ = bf16[128,4,384]{2,1,0:T(4,128)(2,1)} async-done(((bf16[128,4,384]{2,1,0:T(4,128)(2,1)}), bf16[128,4,384]{2,1,0:T(4,128)(2,1)}, u32[]{:S(2)}, u32[]{:S(2)}) %all-to-all-start) | async-done | bytes 393248 | tf_op jit(solution)/shard_map/all_to_all | solution.py:422
  35.1 3.2 %shard_map.140 = (bf16[384,384]{1,0:T(8,128)(2,1)}, f32[128,1024]{1,0:T(8,128)}) custom-call(bf16[128,4,384]{2,1,0:T(4,128)(2,1)} %all-to-all-done.refs_0_, bf16[384,512]{1,0:T(8,128)(2,1)} %get-tuple-element.36.refs_1_, bf16[3,384,1024]{2,1,0:T(8,128)(2,1)} %refs_3_.1), custom_call_target="tpu_custom_call" | custom-call | flops 999999995904 | bytes 3964928 | tf_op jit(solution)/shard_map/pallas_call | solution.py:89
  38.3 0.1 collective-permute-start
  38.4 1.6 %collective-permute-start.1 = (bf16[384,384]{1,0:T(8,128)(2,1)}, bf16[384,384]{1,0:T(8,128)(2,1)}, u32[]{:S(2)}, u32[]{:S(2)}) collective-permute-start(bf16[384,384]{1,0:T(8,128)(2,1)} %get-tuple-element.50.refs_7_.refs_1_), channel_id=1, source_target_pairs={{0,128},{64,192},{128,0},{192,64},{1,129},{65,193},{129,1},{193,65... | collective-permute-start | bytes 884744 | tf_op jit(solution)/shard_map/ppermute | solution.py:374
  40.0 0.5 collective-permute-done.refs_2_
  40.5 0.8 copy-done.10
  41.3 4.4 %shard_map.141 = (bf16[128,1024]{1,0:T(8,128)(2,1)}, bf16[208,256]{1,0:T(8,128)(2,1)}, bf16[1568,128]{1,0:T(8,128)(2,1)}, bf16[208,256]{1,0:T(8,128)(2,1)}, bf16[1568,128]{1,0:T(8,128)(2,1)}) custom-call(s32[2]{0:T(128)} %pad_add_fusion.1.refs_0_, f32[128,1024]{1,0:T(8,128)} %get-tuple-element.37.refs_1_, f32[128,1024]{1,0:T(8,128)} %copy-done.10, ...), custom_call_target="tpu_custom_call" | custom-call | flops 999999995904 | bytes 3366920 | tf_op jit(solution)/shard_map/pallas_call | solution.py:89
  45.7 0.9 collective-permute-start.3
  46.5 2.5 %collective-permute-start.5 = (bf16[1568,128]{1,0:T(8,128)(2,1)}, bf16[1568,128]{1,0:T(8,128)(2,1)}, u32[]{:S(2)}, u32[]{:S(2)}) collective-permute-start(bf16[1568,128]{1,0:T(8,128)(2,1)} %get-tuple-element.55), channel_id=1, source_target_pairs={{0,192},{64,0},{128,64},{192,128},{1,193},{65,1},{129,65},{193,129... | collective-permute-start | bytes 1204232 | tf_op jit(solution)/shard_map/ppermute | solution.py:374
  49.0 0.3 collective-permute-start.4
  49.3 4.1 %shard_map.142 = bf16[128,4,384]{2,1,0:T(4,128)(2,1)} custom-call(bf16[128,1024]{1,0:T(8,128)(2,1)} %get-tuple-element.42.refs_0_, f32[384,128]{1,0:T(8,128)} %get-tuple-element.40.refs_5_.refs_1_, bf16[512,384]{1,0:T(8,128)(2,1)} %get-tuple-element.43.refs_2_, bf16[3,384,1024]{2,1,0:T(8,128)(2,1)} %refs_3_.1), custom_call_target="tpu_custom_call" | custom-call | flops 999999995904 | bytes 3604480 | tf_op jit(solution)/shard_map/pallas_call | solution.py:89
  53.4 0.0 collective-permute-done.1.refs_2_
  53.4 10.0 %all-to-all-start.1 = ((bf16[128,4,384]{2,1,0:T(4,128)(2,1)}), bf16[128,4,384]{2,1,0:T(4,128)(2,1)}, u32[]{:S(2)}, u32[]{:S(2)}) async-start(bf16[128,4,384]{2,1,0:T(4,128)(2,1)} %shard_map.142), calls=%async_computation.1 | async-start | bytes 786432 | tf_op jit(solution)/shard_map/all_to_all | solution.py:500
  63.4 0.0 collective-permute-done.4.refs_5_
  63.5 2.2 %shard_map.145 = (f32[64,1152]{1,0:T(8,128)S(1)}, bf16[128,384]{1,0:T(8,128)(2,1)S(1)}, bf16[208,384]{1,0:T(8,128)(2,1)S(1)}, bf16[208,384]{1,0:T(8,128)(2,1)S(1...) custom-call(s32[1]{0:T(128)} %bitcast.6.refs_0_, bf16[384,384]{1,0:T(8,128)(2,1)S(1)} %copy-done.3, ...), custom_call_target="tpu_custom_call" | custom-call | flops 999999995904 | bytes 2637828 | tf_op jit(solution)/shard_map/pallas_call | solution.py:89
  65.7 0.0 copy-start.2
  65.7 0.0 copy-start
  65.7 0.0 copy-start.1
  65.8 1.0 collective-permute-start.10
  66.8 1.1 %collective-permute-start.6 = (bf16[208,384]{1,0:T(8,128)(2,1)S(1)}, bf16[208,384]{1,0:T(8,128)(2,1)S(1)}, u32[]{:S(2)}, u32[]{:S(2)}) collective-permute-start(bf16[208,384]{1,0:T(8,128)(2,1)S(1)} %get-tuple-element.58), channel_id=1, source_target_pairs={{0,16},{16,32},{32,48},{48,0},{1,17},{17,33},{33,49},{49,1},{2,18}... | collective-permute-start | bytes 479240 | tf_op jit(solution)/shard_map/ppermute | solution.py:374
  67.9 3.3 %collective-permute-start.7 = (bf16[208,384]{1,0:T(8,128)(2,1)S(1)}, bf16[208,384]{1,0:T(8,128)(2,1)S(1)}, u32[]{:S(2)}, u32[]{:S(2)}) collective-permute-start(bf16[208,384]{1,0:T(8,128)(2,1)S(1)} %get-tuple-element.59), channel_id=1, source_target_pairs={{0,32},{16,48},{32,0},{48,16},{1,33},{17,49},{33,1},{49,17},{2,34}... | collective-permute-start | bytes 479240 | tf_op jit(solution)/shard_map/ppermute | solution.py:374
  71.2 0.2 collective-permute-start.8
  71.4 1.8 %collective-permute-start.9 = (bf16[128,384]{1,0:T(8,128)(2,1)S(1)}, bf16[128,384]{1,0:T(8,128)(2,1)S(1)}, u32[]{:S(2)}, u32[]{:S(2)}) collective-permute-start(bf16[128,384]{1,0:T(8,128)(2,1)S(1)} %get-tuple-element.61.refs_5_), channel_id=1, source_target_pairs={{0,16},{16,32},{32,48},{48,0},{1,17},{17,33},{33,49},{49,1},{2,18}... | collective-permute-start | bytes 294920 | tf_op jit(solution)/shard_map/ppermute | solution.py:374
  73.2 0.5 collective-permute-done.10.refs_8_
  73.7 2.5 %collective-permute-start.11 = (bf16[128,384]{1,0:T(8,128)(2,1)S(1)}, bf16[128,384]{1,0:T(8,128)(2,1)S(1)}, u32[]{:S(2)}, u32[]{:S(2)}) collective-permute-start(bf16[128,384]{1,0:T(8,128)(2,1)S(1)} %collective-permute-done.10.refs_8_), channel_id=1, source_target_pairs={{0,48},{16,0},{32,16},{48,32},{1,49},{17,1},{33,17},{49,33},{2,50}... | collective-permute-start | bytes 294920 | tf_op jit(solution)/shard_map/ppermute | solution.py:374
  76.1 3.9 %collective-permute-done.9.refs_6_ = bf16[128,384]{1,0:T(8,128)(2,1)S(1)} collective-permute-done((bf16[128,384]{1,0:T(8,128)(2,1)S(1)}, bf16[128,384]{1,0:T(8,128)(2,1)S(1)}, u32[]{:S(2)}, u32[]{:S(2)}) %collective-permute-start.9) | collective-permute-done | bytes 98336 | tf_op jit(solution)/shard_map/ppermute | solution.py:374
  80.1 0.5 collective-permute-done.8.refs_4_
  80.6 1.6 %collective-permute-done.11.refs_7_ = bf16[128,384]{1,0:T(8,128)(2,1)S(1)} collective-permute-done((bf16[128,384]{1,0:T(8,128)(2,1)S(1)}, bf16[128,384]{1,0:T(8,128)(2,1)S(1)}, u32[]{:S(2)}, u32[]{:S(2)}) %collective-permute-start.11) | collective-permute-done | bytes 98336 | tf_op jit(solution)/shard_map/ppermute | solution.py:374
  82.2 1.0 %shard_map.146 = bf16[64,2688]{1,0:T(8,128)(2,1)} custom-call(f32[64,1152]{1,0:T(8,128)S(1)} %get-tuple-element.56.refs_0_, bf16[208,384]{1,0:T(8,128)(2,1)S(1)} %get-tuple-element.57.refs_1_, bf16[208,384]{1,0:T(8,128)(2,1)S(1)} %collective-permute-done.6.refs_2_, bf16[208,384]{1,0:T(8,128)(2,1)S(1)} %collective-permute-done.7.refs_3_, ...), custom_call_target="tpu_custom_call" | custom-call | bytes 1671168 | tf_op jit(solution)/shard_map/pallas_call | solution.py:89
  83.3 5.8 %all-to-all-start.2 = ((bf16[8,8,2688]{2,1,0:T(8,128)(2,1)}), bf16[8,8,2688]{2,1,0:T(8,128)(2,1)S(1)}, u32[]{:S(2)}, u32[]{:S(2)}) async-start(bf16[8,8,2688]{2,1,0:T(8,128)(2,1)} %bitcast.7), calls=%async_computation.2 | async-start | bytes 688128 | tf_op jit(solution)/shard_map/all_to_all | solution.py:526
  89.1 1.8 %shard_map.143 = (f32[1024,384]{1,0:T(8,128)S(1)}, f32[8,128]{1,0:T(8,128)S(1)}) custom-call(s32[1,512]{1,0:T(1,128)S(1)} %copy-done.2, bf16[128,4,384]{2,1,0:T(4,128)(2,1)} %all-to-all-done.1.refs_1_), custom_call_target="tpu_custom_call" | custom-call | bytes 1972224 | tf_op jit(solution)/shard_map/pallas_call | solution.py:89
  91.0 0.1 collective-permute-start.2
  91.0 1.2 %collective-permute-done.2.refs_4_ = f32[8,128]{1,0:T(8,128)S(1)} collective-permute-done((f32[8,128]{1,0:T(8,128)S(1)}, f32[8,128]{1,0:T(8,128)S(1)}, u32[]{:S(2)}, u32[]{:S(2)}) %collective-permute-start.2) | collective-permute-done | bytes 4128 | tf_op jit(solution)/shard_map/ppermute | solution.py:374
  92.2 1.6 %shard_map.144 = (f32[1024,384]{1,0:T(8,128)}, f32[8,128]{1,0:T(8,128)}) custom-call(f32[1024,384]{1,0:T(8,128)S(1)} %copy-done, f32[1024,384]{1,0:T(8,128)S(1)} %get-tuple-element.45.refs_1_, f32[8,128]{1,0:T(8,128)S(1)} %bitcast.13, f32[8,128]{1,0:T(8,128)S(1)} %get-tuple-element.46.refs_3_, f32[8,128]{1,0:T(8,128)S(1)} %collective-permute-done.2.refs_4_), custom_call_target="tpu_custom_call" | custom-call | bytes 4734976 | tf_op jit(solution)/shard_map/pallas_call | solution.py:89
  93.8 8.5 %all-to-all-done.2.refs_0_ = bf16[8,8,2688]{2,1,0:T(8,128)(2,1)S(1)} async-done(((bf16[8,8,2688]{2,1,0:T(8,128)(2,1)}), bf16[8,8,2688]{2,1,0:T(8,128)(2,1)S(1)}, u32[]{:S(2)}, u32[]{:S(2)}) %all-to-all-start.2) | async-done | bytes 344096 | tf_op jit(solution)/shard_map/all_to_all | solution.py:526
  102.3 0.7 shard_map.147
  (27 shorter events, 0.1 us)
Async XLA Ops:
  0.6 18.9 %copy-start.7 = (s32[8,15]{1,0:T(8,128)S(1)}, s32[8,15]{1,0:T(8,128)}, u32[]{:S(2)}) copy-start(s32[8,15]{1,0:T(8,128)} %param.15) | copy-start | bytes 1444
  0.6 19.0 %copy-start.8 = (s32[8,15]{1,0:T(8,128)S(1)}, s32[8,15]{1,0:T(8,128)}, u32[]{:S(2)}) copy-start(s32[8,15]{1,0:T(8,128)} %param.17) | copy-start | bytes 1444
  0.7 19.0 %copy-start.9 = (s32[8]{0:T(128)S(1)}, s32[8]{0:T(128)}, u32[]{:S(2)}) copy-start(s32[8]{0:T(128)} %param.14) | copy-start | bytes 100
  0.7 19.3 %copy-start.5 = (s32[8,15,10]{1,0,2:T(8,128)S(1)}, s32[8,15,10]{1,0,2:T(8,128)}, u32[]{:S(2)}) copy-start(s32[8,15,10]{1,0,2:T(8,128)} %param.16) | copy-start | bytes 14404
  0.7 19.3 %copy-start.6 = (s32[8,15,10]{1,0,2:T(8,128)S(1)}, s32[8,15,10]{1,0,2:T(8,128)}, u32[]{:S(2)}) copy-start(s32[8,15,10]{1,0,2:T(8,128)} %param.18) | copy-start | bytes 14404
  3.7 31.3 %all-to-all-start = ((bf16[128,4,384]{2,1,0:T(4,128)(2,1)}), bf16[128,4,384]{2,1,0:T(4,128)(2,1)}, u32[]{:S(2)}, u32[]{:S(2)}) async-start(bf16[128,4,384]{2,1,0:T(4,128)(2,1)} %shard_map.138), calls=%async_computation | async-start | bytes 786432 | tf_op jit(solution)/shard_map/all_to_all | solution.py:422
  38.3 2.2 %collective-permute-start = (f32[128,1024]{1,0:T(8,128)}, f32[128,1024]{1,0:T(8,128)S(1)}, u32[]{:S(2)}, u32[]{:S(2)}) collective-permute-start(f32[128,1024]{1,0:T(8,128)} %get-tuple-element.37.refs_1_), channel_id=1, source_target_pairs={{0,1},{1,0},{2,3},{3,2},{4,5},{5,4},{6,7},{7,6},{8,9},{9,8},{10,11... | collective-permute-start | bytes 1572872 | tf_op jit(solution)/shard_map/ppermute | solution.py:374
  38.4 15.0 %collective-permute-start.1 = (bf16[384,384]{1,0:T(8,128)(2,1)}, bf16[384,384]{1,0:T(8,128)(2,1)}, u32[]{:S(2)}, u32[]{:S(2)}) collective-permute-start(bf16[384,384]{1,0:T(8,128)(2,1)} %get-tuple-element.50.refs_7_.refs_1_), channel_id=1, source_target_pairs={{0,128},{64,192},{128,0},{192,64},{1,129},{65,193},{129,1},{193,65... | collective-permute-start | bytes 884744 | tf_op jit(solution)/shard_map/ppermute | solution.py:374
  40.5 0.8 copy-start.10
  45.7 17.8 %collective-permute-start.3 = (bf16[1568,128]{1,0:T(8,128)(2,1)}, bf16[1568,128]{1,0:T(8,128)(2,1)}, u32[]{:S(2)}, u32[]{:S(2)}) collective-permute-start(bf16[1568,128]{1,0:T(8,128)(2,1)} %get-tuple-element.53), channel_id=1, source_target_pairs={{0,64},{64,128},{128,192},{192,0},{1,65},{65,129},{129,193},{193,1... | collective-permute-start | bytes 1204232 | tf_op jit(solution)/shard_map/ppermute | solution.py:374
  46.5 16.9 %collective-permute-start.5 = (bf16[1568,128]{1,0:T(8,128)(2,1)}, bf16[1568,128]{1,0:T(8,128)(2,1)}, u32[]{:S(2)}, u32[]{:S(2)}) collective-permute-start(bf16[1568,128]{1,0:T(8,128)(2,1)} %get-tuple-element.55), channel_id=1, source_target_pairs={{0,192},{64,0},{128,64},{192,128},{1,193},{65,1},{129,65},{193,129... | collective-permute-start | bytes 1204232 | tf_op jit(solution)/shard_map/ppermute | solution.py:374
  49.0 14.4 %collective-permute-start.4 = (bf16[208,256]{1,0:T(8,128)(2,1)}, bf16[208,256]{1,0:T(8,128)(2,1)}, u32[]{:S(2)}, u32[]{:S(2)}) collective-permute-start(bf16[208,256]{1,0:T(8,128)(2,1)} %get-tuple-element.54), channel_id=1, source_target_pairs={{0,128},{64,192},{128,0},{192,64},{1,129},{65,193},{129,1},{193,65... | collective-permute-start | bytes 319496 | tf_op jit(solution)/shard_map/ppermute | solution.py:374
  49.3 14.1 %copy-start.3 = (bf16[384,384]{1,0:T(8,128)(2,1)S(1)}, bf16[384,384]{1,0:T(8,128)(2,1)}, u32[]{:S(2)}) copy-start(bf16[384,384]{1,0:T(8,128)(2,1)} %get-tuple-element.50.refs_7_.refs_1_) | copy-start | bytes 884740
  49.3 14.1 %copy-start.4 = (bf16[208,256]{1,0:T(8,128)(2,1)S(1)}, bf16[208,256]{1,0:T(8,128)(2,1)}, u32[]{:S(2)}) copy-start(bf16[208,256]{1,0:T(8,128)(2,1)} %get-tuple-element.52.refs_3_) | copy-start | bytes 319492
  53.4 29.9 %all-to-all-start.1 = ((bf16[128,4,384]{2,1,0:T(4,128)(2,1)}), bf16[128,4,384]{2,1,0:T(4,128)(2,1)}, u32[]{:S(2)}, u32[]{:S(2)}) async-start(bf16[128,4,384]{2,1,0:T(4,128)(2,1)} %shard_map.142), calls=%async_computation.1 | async-start | bytes 786432 | tf_op jit(solution)/shard_map/all_to_all | solution.py:500
  65.7 23.4 %copy-start.2 = (s32[1,512]{1,0:T(1,128)S(1)}, s32[1,512]{1,0:T(1,128)}, u32[]{:S(2)}) copy-start(s32[1,512]{1,0:T(1,128)} %refs_0_.4) | copy-start | bytes 6148
  65.7 26.5 %copy-start = (f32[1024,384]{1,0:T(8,128)S(1)}, f32[1024,384]{1,0:T(8,128)}, u32[]{:S(2)}) copy-start(f32[1024,384]{1,0:T(8,128)} %refs_0_.5) | copy-start | bytes 4718596
  65.7 26.4 %copy-start.1 = (f32[1024]{0:T(1024)S(1)}, f32[1024]{0:T(1024)}, u32[]{:S(2)}) copy-start(f32[1024]{0:T(1024)} %param.12) | copy-start | bytes 12292
  65.8 7.9 %collective-permute-start.10 = (bf16[128,384]{1,0:T(8,128)(2,1)S(1)}, bf16[128,384]{1,0:T(8,128)(2,1)S(1)}, u32[]{:S(2)}, u32[]{:S(2)}) collective-permute-start(bf16[128,384]{1,0:T(8,128)(2,1)S(1)} %get-tuple-element.61.refs_5_), channel_id=1, source_target_pairs={{0,48},{16,0},{32,16},{48,32},{1,49},{17,1},{33,17},{49,33},{2,50}... | collective-permute-start | bytes 294920 | tf_op jit(solution)/shard_map/ppermute | solution.py:374
  66.8 13.3 %collective-permute-start.6 = (bf16[208,384]{1,0:T(8,128)(2,1)S(1)}, bf16[208,384]{1,0:T(8,128)(2,1)S(1)}, u32[]{:S(2)}, u32[]{:S(2)}) collective-permute-start(bf16[208,384]{1,0:T(8,128)(2,1)S(1)} %get-tuple-element.58), channel_id=1, source_target_pairs={{0,16},{16,32},{32,48},{48,0},{1,17},{17,33},{33,49},{49,1},{2,18}... | collective-permute-start | bytes 479240 | tf_op jit(solution)/shard_map/ppermute | solution.py:374
  67.9 12.2 %collective-permute-start.7 = (bf16[208,384]{1,0:T(8,128)(2,1)S(1)}, bf16[208,384]{1,0:T(8,128)(2,1)S(1)}, u32[]{:S(2)}, u32[]{:S(2)}) collective-permute-start(bf16[208,384]{1,0:T(8,128)(2,1)S(1)} %get-tuple-element.59), channel_id=1, source_target_pairs={{0,32},{16,48},{32,0},{48,16},{1,33},{17,49},{33,1},{49,17},{2,34}... | collective-permute-start | bytes 479240 | tf_op jit(solution)/shard_map/ppermute | solution.py:374
  71.2 9.4 %collective-permute-start.8 = (bf16[208,384]{1,0:T(8,128)(2,1)S(1)}, bf16[208,384]{1,0:T(8,128)(2,1)S(1)}, u32[]{:S(2)}, u32[]{:S(2)}) collective-permute-start(bf16[208,384]{1,0:T(8,128)(2,1)S(1)} %get-tuple-element.60), channel_id=1, source_target_pairs={{0,48},{16,0},{32,16},{48,32},{1,49},{17,1},{33,17},{49,33},{2,50}... | collective-permute-start | bytes 479240 | tf_op jit(solution)/shard_map/ppermute | solution.py:374
  71.4 8.7 %collective-permute-start.9 = (bf16[128,384]{1,0:T(8,128)(2,1)S(1)}, bf16[128,384]{1,0:T(8,128)(2,1)S(1)}, u32[]{:S(2)}, u32[]{:S(2)}) collective-permute-start(bf16[128,384]{1,0:T(8,128)(2,1)S(1)} %get-tuple-element.61.refs_5_), channel_id=1, source_target_pairs={{0,16},{16,32},{32,48},{48,0},{1,17},{17,33},{33,49},{49,1},{2,18}... | collective-permute-start | bytes 294920 | tf_op jit(solution)/shard_map/ppermute | solution.py:374
  73.7 8.6 %collective-permute-start.11 = (bf16[128,384]{1,0:T(8,128)(2,1)S(1)}, bf16[128,384]{1,0:T(8,128)(2,1)S(1)}, u32[]{:S(2)}, u32[]{:S(2)}) collective-permute-start(bf16[128,384]{1,0:T(8,128)(2,1)S(1)} %collective-permute-done.10.refs_8_), channel_id=1, source_target_pairs={{0,48},{16,0},{32,16},{48,32},{1,49},{17,1},{33,17},{49,33},{2,50}... | collective-permute-start | bytes 294920 | tf_op jit(solution)/shard_map/ppermute | solution.py:374
  83.3 19.0 %all-to-all-start.2 = ((bf16[8,8,2688]{2,1,0:T(8,128)(2,1)}), bf16[8,8,2688]{2,1,0:T(8,128)(2,1)S(1)}, u32[]{:S(2)}, u32[]{:S(2)}) async-start(bf16[8,8,2688]{2,1,0:T(8,128)(2,1)} %bitcast.7), calls=%async_computation.2 | async-start | bytes 688128 | tf_op jit(solution)/shard_map/all_to_all | solution.py:526
  91.0 1.2 %collective-permute-start.2 = (f32[8,128]{1,0:T(8,128)S(1)}, f32[8,128]{1,0:T(8,128)S(1)}, u32[]{:S(2)}, u32[]{:S(2)}) collective-permute-start(f32[8,128]{1,0:T(8,128)S(1)} %get-tuple-element.46.refs_3_), channel_id=1, source_target_pairs={{0,1},{1,0},{2,3},{3,2},{4,5},{5,4},{6,7},{7,6},{8,9},{9,8},{10,11... | collective-permute-start | bytes 12296 | tf_op jit(solution)/shard_map/ppermute | solution.py:374
